TPU v7x, 128 devices: a whole 4x4x4 slice. The times are simulated.
128 devices in a mesh: vocab: 32 (over x, z, core), tok: 4 (over y).
Axes of the slice: x: 4, y: 4, z: 4, core: 2. Of those that a mesh axis runs over, the one named last changes fastest.
Arguments:
- comp_hidden: bfloat16 [4, 512, 4096], P(None, 'tok', 'vocab')
- embed: bfloat16 [65536, 4096], P('vocab')
- mix_logits: float32 [4, 512], P(None, 'tok')
- targets: int32 [512], P('tok'), may hold values from 0 to 65535
- loss_weight: float32 [512], P('tok'), may hold values from 1 to 10
Outputs:
- grad_hidden: float32 [4, 512, 4096], P(None, 'tok', 'vocab')
- grad_embed: bfloat16 [65536, 4096], P('vocab', 'tok')
- grad_mix: float32 [4, 512], P(None, 'tok')
All inputs are finite; a program needn't handle non-finite values.
Results may differ from a plain program's by a relative error of at most 0.0049.
Values may be sent and summed in bfloat16 or wider, within the bound.
No kernel may reach another device: no remote copies, remote signals or barrier semaphores. Data moves between devices by JAX's collectives and lax.ppermute only.
A program may use at most 192 MiB of HBM per device.

v0:
```python
import jax
import jax.numpy as jnp
from jax import lax
from jax.sharding import PartitionSpec as P


def local(comp_hidden, embed, mix_logits, targets, loss_weight):
    voc_dev = embed.shape[0]
    features = lax.all_gather(comp_hidden, "vocab", axis=2, tiled=True)
    logits = jnp.einsum("kth,vh->ktv", features, embed, preferred_element_type=jnp.float32)
    local_ids = targets - lax.axis_index("vocab") * voc_dev
    vocab_iota = lax.broadcasted_iota(jnp.int32, (1, local_ids.shape[0], voc_dev), 2)
    target_mask = vocab_iota == local_ids[None, :, None]
    local_target = jnp.sum(jnp.where(target_mask, logits, 0.0), axis=2)
    local_max = jnp.max(logits, axis=2)
    global_max = lax.pmax(local_max, "vocab")
    local_sum = jnp.sum(jnp.exp(logits - global_max[..., None]), axis=2)
    total, target_logit = lax.psum((local_sum, local_target), "vocab")
    lse = global_max + jnp.log(total)
    log_mix = jax.nn.log_softmax(mix_logits, axis=0)
    resp = jax.nn.softmax(log_mix + target_logit - lse, axis=0)
    grad_mix = loss_weight[None, :] * (jnp.exp(log_mix) - resp)
    weighting = loss_weight[None, :] * resp
    probs = jnp.exp(logits - lse[..., None])
    token_grad = (weighting[..., None] * (probs - target_mask.astype(jnp.float32))).astype(
        jnp.bfloat16
    )
    hidden_terms = jnp.einsum("ktv,vh->kth", token_grad, embed, preferred_element_type=jnp.float32)
    grad_hidden = lax.psum_scatter(hidden_terms, "vocab", scatter_dimension=2, tiled=True)
    columns = lax.all_to_all(features, "tok", split_axis=2, concat_axis=1, tiled=True)
    grad_embed = jnp.einsum(
        "ktv,kth->vh",
        lax.all_gather(token_grad, "tok", axis=1, tiled=True),
        columns,
        preferred_element_type=jnp.float32,
    )
    return (grad_hidden, grad_embed.astype(jnp.bfloat16), grad_mix)


def solution(mesh):
    return jax.shard_map(
        local,
        mesh=mesh,
        in_specs=(P(None, "tok", "vocab"), P("vocab", None), P(None, "tok"), P("tok"), P("tok")),
        out_specs=(P(None, "tok", "vocab"), P("vocab", "tok"), P(None, "tok")),
        check_vma=False,
    )
```

profile of v0, /device:TPU:0, one launch (start us, length us, event | category | flops | bytes accessed | tf_op | source)
XLA Modules:
  0.0 442.3 jit_solution(11893379937335671078)
XLA Ops:
  7.2 0.0 all-gather.3.cloned.1.call-start
  7.2 0.7 all-gather.3.cloned.1.call-update
  7.9 0.0 all-gather.5.cloned.1.call-start
  7.9 0.7 reduce_max.28
  8.6 0.7 exponential_reduce_fusion.1
  9.4 0.7 broadcast_subtract_fusion
  10.0 0.2 iota_compare_fusion
  10.3 51.8 %all-gather.3.cloned.1.call-done = bf16[4,128,4096]{2,1,0:T(8,128)(2,1)} async-done(((bf16[4,128,128]{2,1,0:T(8,128)(2,1)}), bf16[4,128,4096]{2,1,0:T(8,128)(2,1)}) %all-gather.3.cloned.1.call-update) | async-done | bytes 4194320 | tf_op jit(solution)/shard_map/all_gather | solution.py:9
  62.0 15.0 %fusion.8 = (f32[4,128]{1,0:T(4,128)S(1)}, f32[4,128,2048]{2,1,0:T(8,128)}) fusion(bf16[4,128,4096]{2,1,0:T(8,128)(2,1)} %all-gather.3.cloned.1.call-done, bf16[2048,4096]{1,0:T(8,128)(2,1)} %param.6), kind=kOutput, calls=%fused_computation.20 | convolution fusion | flops 8590983168 | bytes 25167872 | tf_op jit(solution)/shard_map/kth,vh->ktv/dot_general | solution.py:10
  77.1 0.0 copy-start
  77.1 0.0 copy-start.1
  77.1 65.2 %pmax.7 = f32[4,128]{1,0:T(4,128)S(1)} all-reduce(f32[4,128]{1,0:T(4,128)S(1)} %get-tuple-element.14), channel_id=1, replica_groups=mesh['vocab'=32,'tok'=4] {'vocab'}, use_global_device_ids=true, to_apply=%region_5.6 | all-reduce | flops 512 | bytes 4096 | tf_op jit(solution)/shard_map/pmax | solution.py:16
  142.3 3.4 select_reduce_fusion
  145.7 62.7 %all-reduce = (f32[4,128]{1,0:T(4,128)S(1)}, f32[4,128]{1,0:T(4,128)S(1)}) all-reduce(f32[4,128]{1,0:T(4,128)S(1)} %get-tuple-element.4, f32[4,128]{1,0:T(4,128)S(1)} %get-tuple-element.3), channel_id=1, replica_groups=mesh['vocab'=32,'tok'=4] {'vocab'}, use_global_device_ids=true, to_apply=%region_7.8 | all-reduce | flops 1024 | bytes 8192 | tf_op jit(solution)/shard_map/psum | solution.py:18
  208.4 0.0 copy-done
  208.5 0.0 copy-done.1
  208.5 0.6 subtract_multiply_fusion
  209.1 4.5 %multiply_convert_fusion = bf16[4,128,2048]{2,1,0:T(8,128)(2,1)} fusion(f32[4,128,2048]{2,1,0:T(8,128)} %get-tuple-element.15, f32[128,2048]{1,0:T(8,128)S(1)} %get-tuple-element.13, f32[4,128]{1,0:T(4,128)S(1)} %get-tuple-element.9, f32[4,128]{1,0:T(4,128)S(1)} %get-tuple-element.11), kind=kLoop, calls=%fused_computation.5 | loop fusion | flops 4194304 | bytes 7344128 | tf_op jit(solution)/shard_map/convert_element_type | solution.py:25
  213.5 0.0 all-gather.5.cloned.1.call-update
  213.5 0.0 reduce-scatter.2.cloned.1.call-start
  213.6 15.0 %fusion = f32[4,128,4096]{2,1,0:T(8,128)} fusion(bf16[4,128,2048]{2,1,0:T(8,128)(2,1)} %multiply_convert_fusion, bf16[2048,4096]{1,0:T(8,128)(2,1)} %param.6), kind=kOutput, calls=%fused_computation | convolution fusion | flops 8589934592 | bytes 27262976 | tf_op jit(solution)/shard_map/ktv,vh->kth/dot_general | solution.py:28
  228.6 0.0 reduce-scatter.2.cloned.1.call-update
  228.6 7.5 %copy.10 = bf16[4,128,4096]{1,0,2:T(4,128)(2,1)} copy(bf16[4,128,4096]{2,1,0:T(8,128)(2,1)} %all-gather.3.cloned.1.call-done) | data formatting | bytes 8388608 | tf_op jit(solution)/shard_map/all_gather | solution.py:9
  236.1 100.5 %all_to_all.18 = bf16[4,128,4096]{1,0,2:T(4,128)(2,1)} all-to-all(bf16[4,128,4096]{1,0,2:T(4,128)(2,1)} %copy.10), channel_id=1, replica_groups=mesh['vocab'=32,'tok'=4] {'tok'}, dimensions={2} | all-to-all | bytes 8388608 | tf_op jit(solution)/shard_map/all_to_all | solution.py:30
  336.6 7.5 %copy.11 = bf16[4,128,4,1024]{3,1,2,0:T(8,128)(2,1)} copy(bf16[4,128,4,1024]{1,0,3,2:T(4,128)(2,1)} %bitcast.17) | data formatting | bytes 8388608 | tf_op jit(solution)/shard_map/all_to_all | solution.py:30
  344.1 0.0 all-gather.5.cloned.1.call-done
  344.1 14.0 %bitcast_convert_fusion = bf16[2048,1024]{1,0:T(8,128)(2,1)} fusion(bf16[4,512,2048]{2,1,0:T(8,128)(2,1)} %all-gather.5.cloned.1.call-done, bf16[4,512,1024]{2,1,0:T(8,128)(2,1)} %bitcast.18), kind=kOutput, calls=%fused_computation.4 | convolution fusion | flops 8592031744 | bytes 16777216 | tf_op jit(solution)/shard_map/ktv,kth->vh/dot_general | solution.py:31
  358.0 77.7 %reduce-scatter.2.cloned.1.call-done = f32[4,128,128]{2,1,0:T(8,128)} async-done(((f32[4,128,4096]{2,1,0:T(8,128)}), f32[4,128,128]{2,1,0:T(8,128)}) %reduce-scatter.2.cloned.1.call-update) | async-done | bytes 262160 | tf_op jit(solution)/shard_map/reduce_scatter | solution.py:29
  (3 shorter events, 0.1 us)
Async XLA Ops:
  7.2 54.9 %all-gather.3.cloned.1.call-start = ((), (), s32[]{:S(2)}) async-start(), calls=%async_computation.2 | async-start | bytes 4325376 | tf_op jit(solution)/shard_map/all_gather | solution.py:9
  7.9 336.2 %all-gather.5.cloned.1.call-start = ((), (), s32[]{:S(2)}) async-start(), calls=%async_computation.4 | async-start | bytes 10485760 | tf_op jit(solution)/shard_map/all_gather | solution.py:33
  77.1 131.3 %copy-start = (f32[4,128]{1,0:T(4,128)S(1)}, f32[4,128]{1,0:T(4,128)}, u32[]{:S(2)}) copy-start(f32[4,128]{1,0:T(4,128)} %param.7) | copy-start | bytes 6148
  77.1 131.4 %copy-start.1 = (f32[128]{0:T(128)S(1)}, f32[128]{0:T(128)}, u32[]{:S(2)}) copy-start(f32[128]{0:T(128)} %param.9) | copy-start | bytes 1540
  213.5 222.2 %reduce-scatter.2.cloned.1.call-start = ((), (), s32[]{:S(2)}) async-start(), calls=%async_computation.3 | async-start | bytes 8650752 | tf_op jit(solution)/shard_map/reduce_scatter | solution.py:29
Sparse Core Ops, SparseCore 0:
  10.2 51.8 all-gather.2
  213.7 124.3 all-gather.4
  342.3 93.3 reduce-scatter.1
where the time goes:
time: 443 us; the launch traced here: 442 us
  blocking collectives  228 us (51%)
  waiting for transfers between devices  130 us (29%)
  matrix products  44 us (10%)
  local copies, waits for them, and re-layouts  15 us (3%)
  between operations  13.8 us (3%)
  other arithmetic  10.8 us (2%)
    all_to_all x1, blocking collectives, local(): lax.all_to_all(features, 'tok', split_axis=2, concat_axis=1, tiled=True)  100 us
    reduce_scatter x1, waiting for transfers between devices, local(): lax.psum_scatter(hidden_terms, 'vocab', scatter_dimension=2, tiled=True)  77.7 us
    pmax x1, blocking collectives, local(): global_max = lax.pmax(local_max, 'vocab')  65.2 us
    psum x1, blocking collectives, local(): total, target_logit = lax.psum((local_sum, local_target), 'vocab')  62.7 us
    all_gather x1, waiting for transfers between devices, local(): features = lax.all_gather(comp_hidden, 'vocab', axis=2, tiled=True)  51.8 us
    dot_general x1, matrix products, local(): jnp.einsum('ktv,vh->kth', token_grad, embed, preferred_element_type=jnp.f...  15 us
    dot_general x1, matrix products, local(): jnp.einsum('kth,vh->ktv', features, embed, preferred_element_type=jnp.flo...  15 us
    dot_general x1, matrix products, local(): jnp.einsum('ktv,kth->vh', lax.all_gather(token_grad, 'tok', axis=1, tiled...  14 us
  transfers between devices with their start and end apart: 3, of which 2 were waited for; matrix products, arithmetic and copies ran while one was open for 10% of the time, Pallas kernels for 0%

commit v1 on v0

v1 whole, which is shorter than its diff:
```python
import functools

import jax
import jax.numpy as jnp
from jax import lax
from jax.experimental import pallas as pl
from jax.experimental.pallas import tpu as pltpu
from jax.sharding import Mesh, PartitionSpec as P

BF, F32 = jnp.bfloat16, jnp.float32
ROWS = 512
HALF = 256
WIDTH = 4096
VOC = 2048
TILE = 512
TILES = VOC // TILE
VMEM = 56 * 2**20


def shift(a, axis, d):
    return lax.ppermute(a, axis, [((i + d) % 4, i) for i in range(4)])


def sibling(a):
    return lax.ppermute(a, "c", [(0, 1), (1, 0)])


def cross(a, which, d):
    pairs = []
    for x in range(4):
        for z in range(4):
            for c in range(2):
                along_x = (c + which) % 2 == 0
                sx, sz = ((x + d) % 4, z) if along_x else (x, (z + d) % 4)
                pairs.append(((sx * 4 + sz) * 2 + c, (x * 4 + z) * 2 + c))
    return lax.ppermute(a, ("x", "z", "c"), pairs)


def dot_nt(a, b):
    return lax.dot_general(a, b, (((1,), (1,)), ((), ())), preferred_element_type=F32)


def dot_nn(a, b):
    return lax.dot_general(a, b, (((1,), (0,)), ((), ())), preferred_element_type=F32)


def params(**kw):
    return pltpu.CompilerParams(vmem_limit_bytes=VMEM, **kw)


SMALL = pl.CostEstimate(flops=1000, bytes_accessed=1000, transcendentals=0)
HBM = pl.BlockSpec(memory_space=pltpu.HBM)


def gate_body(*refs):
    pass


def gate(*arrays):
    n = len(arrays)
    return pl.pallas_call(
        gate_body,
        in_specs=[HBM] * n,
        out_specs=[HBM] * n,
        out_shape=[jax.ShapeDtypeStruct(a.shape, a.dtype) for a in arrays],
        input_output_aliases={i: i for i in range(n)},
        compiler_params=params(),
        cost_estimate=SMALL,
        name="gate",
    )(*arrays)


LOW = pl.BlockSpec((TILE, ROWS), lambda i, at: (0, 0))
HIGH = pl.BlockSpec((TILE, ROWS), lambda i, at: (jnp.maximum(i - 1, 0), 0))


def pick(i, low, high):
    return jnp.where(i == 0, low[...], high[...])


def gather_pieces(block):
    s = jnp.stack([block] + [cross(block, 0, d) for d in (1, 2, 3)])
    p, m = cross(s, 1, 1), cross(s, 1, 3)
    dp, dm = cross(p[:2], 1, 1), cross(m[2:], 1, 3)
    return [s, p, m, dp, dm]


PLACES = [
    [(a, 0) for a in range(4)],
    [(a, 1) for a in range(4)],
    [(a, 3) for a in range(4)],
    [(0, 2), (1, 2)],
    [(2, 2), (3, 2)],
]


def logits_body(at, *refs):
    pieces, refs = refs[:10], refs[10:]
    tid, emb, e0_out, e1_out, st_out, loc_out, full, sem = refs
    step = pl.program_id(0)
    x, z, c = at[0], at[1], at[2]

    @pl.when(step == 0)
    def _():
        copies = []
        for n in range(10):
            core = c if n < 5 else 1 - c
            row = pl.multiple_of(core * HALF, HALF)
            for b, (o1, o2) in enumerate(PLACES[n % 5]):
                dx = jnp.where(core == 0, o1, o2)
                dz = jnp.where(core == 0, o2, o1)
                col = pl.multiple_of((((x + dx) & 3) * 4 + ((z + dz) & 3)) * 256, 256)
                copies.append((pieces[n].at[b], full.at[pl.ds(row, HALF), pl.ds(col, 256)], sem.at[len(copies)]))
        for copy in copies:
            pltpu.make_async_copy(*copy).start()
        for copy in copies:
            pltpu.make_async_copy(*copy).wait()
        st_out[...] = jnp.zeros((8, ROWS), F32)
        loc_out[...] = jnp.zeros((8, ROWS), F32)

    logits = dot_nt(emb[...], full[...])
    top = jnp.max(logits, axis=0, keepdims=True)
    ids = lax.broadcasted_iota(jnp.int32, logits.shape, 0) + step * TILE
    hit = jnp.sum(jnp.where(ids == tid[...], logits, 0.0), axis=0, keepdims=True)
    e = jnp.exp(logits - top)
    total = jnp.sum(e, axis=0, keepdims=True)
    e = e.astype(BF)

    @pl.when(step == 0)
    def _():
        e0_out[...] = e

    @pl.when(step > 0)
    def _():
        e1_out[...] = e

    for s in range(TILES):

        @pl.when(step == s)
        def _():
            st_out[pl.ds(s, 1), :] = top

    @pl.when(step == 0)
    def _():
        loc_out[pl.ds(0, 1), :] = top
        loc_out[pl.ds(1, 1), :] = total
        loc_out[pl.ds(2, 1), :] = hit

    @pl.when(step > 0)
    def _():
        old = loc_out[pl.ds(0, 1), :]
        new = jnp.maximum(old, top)
        loc_out[pl.ds(1, 1), :] = loc_out[pl.ds(1, 1), :] * jnp.exp(old - new) + total * jnp.exp(top - new)
        loc_out[pl.ds(0, 1), :] = new
        loc_out[pl.ds(2, 1), :] = loc_out[pl.ds(2, 1), :] + hit


def logits_call(at, pieces, tid, emb, name):
    whole = pl.BlockSpec((8, ROWS), lambda i, at: (0, 0))
    return pl.pallas_call(
        logits_body,
        grid_spec=pltpu.PrefetchScalarGridSpec(
            num_scalar_prefetch=1,
            grid=(TILES,),
            in_specs=[HBM] * 10
            + [pl.BlockSpec((1, ROWS), lambda i, at: (0, 0)), pl.BlockSpec((TILE, WIDTH), lambda i, at: (i, 0))],
            out_specs=[LOW, HIGH, whole, whole],
            scratch_shapes=[pltpu.VMEM((ROWS, WIDTH), BF), pltpu.SemaphoreType.DMA((32,))],
        ),
        out_shape=[
            jax.ShapeDtypeStruct((TILE, ROWS), BF),
            jax.ShapeDtypeStruct((VOC - TILE, ROWS), BF),
            jax.ShapeDtypeStruct((8, ROWS), F32),
            jax.ShapeDtypeStruct((8, ROWS), F32),
        ],
        compiler_params=params(),
        cost_estimate=SMALL,
        name=name,
    )(at, *pieces, tid, emb)


def merge(parts):
    top = functools.reduce(jnp.maximum, [p[0:1] for p in parts])
    total = sum(p[1:2] * jnp.exp(p[0:1] - top) for p in parts)
    hit = sum(p[2:3] for p in parts)
    return top, total, hit


def merge_body(*refs):
    top, total, hit = merge([r[...] for r in refs[:-1]])
    out = refs[-1]
    out[...] = jnp.zeros((8, ROWS), F32)
    out[pl.ds(0, 1), :] = top
    out[pl.ds(1, 1), :] = total
    out[pl.ds(2, 1), :] = hit


def merge_call(*parts):
    return pl.pallas_call(
        merge_body,
        out_shape=jax.ShapeDtypeStruct((8, ROWS), F32),
        compiler_params=params(),
        cost_estimate=SMALL,
        name="merge",
    )(*parts)


def finish_body(a, b, st, tid, mix, weight, feats, ep0, em0, pack, grad_mix):
    top, total, hit = merge([a[...], b[...]])
    lse = top + jnp.log(total)
    gap = hit - lse
    mixes = [mix[pl.ds(k, 1), :] for k in range(4)]
    big = functools.reduce(jnp.maximum, mixes)
    norm = big + jnp.log(sum(jnp.exp(m - big) for m in mixes))
    logm = [m - norm for m in mixes]
    score = [logm[k] + gap[:, k * 128 : (k + 1) * 128] for k in range(4)]
    big = functools.reduce(jnp.maximum, score)
    ex = [jnp.exp(s - big) for s in score]
    den = sum(ex)
    w = weight[...]
    scaled = []
    for k in range(4):
        resp = ex[k] / den
        grad_mix[pl.ds(k, 1), :] = w * (jnp.exp(logm[k]) - resp)
        scaled.append(w * resp)
    d = jnp.concatenate(scaled, axis=1)
    pack[...] = jnp.zeros((8, ROWS), F32)
    pack[pl.ds(0, TILES), :] = jnp.exp(st[pl.ds(0, TILES), :] - lse) * d
    pack[pl.ds(4, 1), :] = d
    pack[pl.ds(5, 1), :] = lse
    pack[pl.ds(6, 1), :] = tid[...].astype(F32)


def finish_call(a, b, st, tid, mix, weight, *awaited):
    return pl.pallas_call(
        finish_body,
        in_specs=[pl.BlockSpec(memory_space=pltpu.VMEM)] * 6 + [HBM] * 3,
        out_shape=[jax.ShapeDtypeStruct((8, ROWS), F32), jax.ShapeDtypeStruct((4, 128), F32)],
        compiler_params=params(),
        cost_estimate=SMALL,
        name="finish",
    )(a, b, st, tid, mix, weight, *awaited)


def token_grad(e, pack, scale, base):
    ids = lax.broadcasted_iota(jnp.int32, e.shape, 0) + base
    tid = pack[pl.ds(6, 1), :].astype(jnp.int32)
    g = e.astype(F32) * scale
    return (g - jnp.where(ids == tid, pack[pl.ds(4, 1), :], 0.0)).astype(BF)


def hidden_body(at, e0, e1, pack, w0, w1, w2, w3, keep, send0, send1, tgt_out, tg):
    @pl.when(pl.program_id(0) == 0)
    def _():
        for t in range(TILES):
            rows = pl.ds(t * TILE, TILE)
            e = e0[...] if t == 0 else e1[pl.ds((t - 1) * TILE, TILE), :]
            g = token_grad(e, pack, pack[pl.ds(t, 1), :], t * TILE)
            tgt_out[rows, :] = g
            tg[:, rows] = g.T

    w = jnp.concatenate([w0[...], w1[...], w2[...], w3[...]], axis=1)
    r = dot_nn(tg[...], w)
    first = at[2] == 0
    for k in range(4):
        cols = slice(k * 256, (k + 1) * 256)
        a, b = r[:HALF, cols], r[HALF:, cols]
        keep[0, k] = jnp.where(first, a, b)
        (send0, send1)[k // 2][k % 2, 0] = jnp.where(first, b, a).astype(BF)


def hidden_call(at, e0, e1, pack, emb):
    whole = lambda s: pl.BlockSpec(s, lambda i, at: (0,) * len(s))

    def weight(k):
        def index(i, at):
            dx = jnp.where(at[2] == 0, i, k)
            dz = jnp.where(at[2] == 0, k, i)
            return (0, ((at[0] + dx) & 3) * 4 + ((at[1] + dz) & 3))

        return pl.BlockSpec((VOC, 256), index)

    return pl.pallas_call(
        hidden_body,
        grid_spec=pltpu.PrefetchScalarGridSpec(
            num_scalar_prefetch=1,
            grid=(4,),
            in_specs=[whole((TILE, ROWS)), whole((VOC - TILE, ROWS)), whole((8, ROWS))] + [weight(k) for k in range(4)],
            out_specs=[
                pl.BlockSpec((1, 4, HALF, 256), lambda i, at: (i, 0, 0, 0)),
                pl.BlockSpec((2, 1, HALF, 256), lambda i, at: (0, i, 0, 0)),
                pl.BlockSpec((2, 1, HALF, 256), lambda i, at: (0, i, 0, 0)),
                whole((VOC, ROWS)),
            ],
            scratch_shapes=[pltpu.VMEM((ROWS, VOC), BF)],
        ),
        out_shape=[
            jax.ShapeDtypeStruct((4, 4, HALF, 256), F32),
            jax.ShapeDtypeStruct((2, 4, HALF, 256), BF),
            jax.ShapeDtypeStruct((2, 4, HALF, 256), BF),
            jax.ShapeDtypeStruct((VOC, ROWS), BF),
        ],
        compiler_params=params(),
        cost_estimate=SMALL,
        name="hidden",
    )(at, e0, e1, pack, emb, emb, emb, emb)


def add(*xs):
    return sum(x.astype(F32) for x in xs)


def scatter(keep, recv, c):
    b = [add(keep[d], recv[d // 2][d % 2]) for d in range(4)]
    n = HALF // 2
    r1 = cross(b[2][:, :n].astype(BF), 0, 3)
    r3 = cross(b[2][:, n:].astype(BF), 0, 1)
    s1 = jnp.concatenate([add(b[1][:, :n], r1).astype(BF), b[1][:, n:].astype(BF)], axis=1)
    s3 = jnp.concatenate([b[3][:, :n].astype(BF), add(b[3][:, n:], r3).astype(BF)], axis=1)
    t = add(b[0], cross(s1, 0, 3), cross(s3, 0, 1))
    u = [cross(t[d].astype(BF), 1, 4 - d) for d in (1, 2, 3)]
    f = add(t[0], *u)
    low, high = f[:, :128], f[:, 128:]
    mine, other = jnp.where(c == 0, low, high), jnp.where(c == 0, high, low)
    got = sibling(other)
    return jnp.where(c == 0, jnp.concatenate([mine, got]), jnp.concatenate([got, mine]))


def quarter_copies(at, feats, offsets, q, sem):
    copies = []
    for n, d in enumerate(offsets):
        group = (at[3] + d) & 3
        for k in range(8):
            dst = q.at[pl.ds(n * ROWS, ROWS), pl.ds(k * 128, 128)]
            copies.append(pltpu.make_async_copy(feats.at[group, k // 2, k % 2], dst, sem.at[n * 8 + k]))
    return copies


def embed_a_body(at, tgt, ep0, ep1, em0, em1, pack_p, pack_m, feats, acc, q, sem):
    i = pl.program_id(0)

    @pl.when(i == 0)
    def _():
        copies = quarter_copies(at, feats, (0, 1, 3), q, sem)
        for copy in copies:
            copy.start()
        for copy in copies:
            copy.wait()

    parts = [tgt[...]]
    for e, pack in ((pick(i, ep0, ep1), pack_p), (pick(i, em0, em1), pack_m)):
        parts.append(token_grad(e, pack, pack[pl.ds(i, 1), :], i * TILE))
    acc[...] = dot_nn(jnp.concatenate(parts, axis=1), q[...])


def embed_a_call(at, tgt, ep0, ep1, em0, em1, pack_p, pack_m, feats):
    tile = pl.BlockSpec((TILE, ROWS), lambda i, at: (i, 0))
    pack = pl.BlockSpec((8, ROWS), lambda i, at: (0, 0))
    return pl.pallas_call(
        embed_a_body,
        grid_spec=pltpu.PrefetchScalarGridSpec(
            num_scalar_prefetch=1,
            grid=(TILES,),
            in_specs=[tile, LOW, HIGH, LOW, HIGH, pack, pack, HBM],
            out_specs=pl.BlockSpec((TILE, 1024), lambda i, at: (i, 0)),
            scratch_shapes=[pltpu.VMEM((3 * ROWS, 1024), BF), pltpu.SemaphoreType.DMA((24,))],
        ),
        out_shape=jax.ShapeDtypeStruct((VOC, 1024), F32),
        compiler_params=params(),
        cost_estimate=SMALL,
        name="embed_a",
    )(at, tgt, ep0, ep1, em0, em1, pack_p, pack_m, feats)


def embed_b_body(at, acc, ea, eb, ec, pack_d, feats, out, q, sem):
    i = pl.program_id(0)

    @pl.when(i == 0)
    def _():
        copies = quarter_copies(at, feats, (2,), q, sem)
        for copy in copies:
            copy.start()
        for copy in copies:
            copy.wait()

    g = token_grad(jnp.where(i == 0, ea[...], jnp.where(i == 1, eb[...], ec[...])), pack_d, pack_d[pl.ds(i, 1), :], i * TILE)
    out[...] = (acc[...] + dot_nn(g, q[...])).astype(BF)


def embed_b_call(at, acc, ea, eb, ec, pack_d, feats):
    tile = pl.BlockSpec((TILE, 1024), lambda i, at: (i, 0))
    return pl.pallas_call(
        embed_b_body,
        grid_spec=pltpu.PrefetchScalarGridSpec(
            num_scalar_prefetch=1,
            grid=(TILES,),
            in_specs=[
                tile,
                LOW,
                LOW,
                pl.BlockSpec((TILE, ROWS), lambda i, at: (jnp.maximum(i - 2, 0), 0)),
                pl.BlockSpec((8, ROWS), lambda i, at: (0, 0)),
                HBM,
            ],
            out_specs=tile,
            scratch_shapes=[pltpu.VMEM((ROWS, 1024), BF), pltpu.SemaphoreType.DMA((8,))],
        ),
        out_shape=jax.ShapeDtypeStruct((VOC, 1024), BF),
        compiler_params=params(),
        cost_estimate=SMALL,
        name="embed_b",
    )(at, acc, ea, eb, ec, pack_d, feats)


def local(comp_hidden, embed, mix, targets, weight):
    x, z, c, y = (lax.axis_index(a).astype(jnp.int32) for a in ("x", "z", "c", "y"))
    at = jnp.stack([x, z, c, y])
    own = comp_hidden.reshape(ROWS, 128)
    tid = jnp.tile(targets - ((x * 4 + z) * 2 + c) * VOC, 4).reshape(1, ROWS)

    swap = [(a * 4 + b, b * 4 + a) for a in range(4) for b in range(4)]
    turned = lax.ppermute(own, ("x", "y"), swap)

    low, high = own[:HALF], own[HALF:]
    mine, other = jnp.where(c == 0, low, high), jnp.where(c == 0, high, low)
    got = sibling(other)
    block = jnp.where(c == 0, jnp.concatenate([mine, got], axis=1), jnp.concatenate([got, mine], axis=1))
    pieces = gather_pieces(block)
    pieces = pieces + [sibling(p) for p in pieces]
    feats = lax.all_gather(turned, ("x", "z", "c")).reshape(4, 4, 2, ROWS, 128)

    e0, e1, st, loc = logits_call(at, pieces, tid, embed, "logits")
    ep0, em0 = shift(e0, "y", 1), shift(e0, "y", 3)
    ep1, em1 = shift(e1, "y", 1), shift(e1, "y", 3)

    s = merge_call(loc, *(shift(loc, "x", d) for d in (1, 2, 3)))
    s = merge_call(s, *(shift(s, "z", d) for d in (1, 2, 3)))
    pack, grad_mix = finish_call(s, sibling(s), st, tid, mix, weight.reshape(1, 128), feats, ep0, em0)
    pack_p, pack_m, pack_d = shift(pack, "y", 1), shift(pack, "y", 3), shift(pack, "y", 2)

    keep, send0, send1, tgt = hidden_call(at, e0, e1, pack, embed)
    recv0, recv1, ep1, em1 = gate(sibling(send0), sibling(send1), ep1, em1)
    diag = [shift(ep0, "y", 1), shift(ep1[:TILE], "y", 1), shift(em1[TILE:], "y", 3)]
    grad_hidden = scatter(keep, (recv0, recv1), c)

    acc = embed_a_call(at, tgt, ep0, ep1, em0, em1, pack_p, pack_m, feats)
    grad_embed = embed_b_call(at, acc, *diag, pack_d, feats)
    return grad_hidden.reshape(4, 128, 128), grad_embed, grad_mix


def solution(mesh):
    fine = Mesh(mesh.devices.reshape(4, 4, 2, 4), ("x", "z", "c", "y"))
    v = ("x", "z", "c")
    return jax.shard_map(
        local,
        mesh=fine,
        in_specs=(P(None, "y", v), P(v, None), P(None, "y"), P("y"), P("y")),
        out_specs=(P(None, "y", v), P(v, "y"), P(None, "y")),
        check_vma=False,
    )
```

time: 443 us -> 239 us (0.54)
  blocking collectives: 228 us -> 0 us
  Pallas kernels: 0 us -> 61.7 us
  starting transfers between devices: 0.12 us -> 54.7 us
  matrix products: 44 us -> 0 us
  waiting for transfers between devices: 130 us -> 89.9 us
  local copies, waits for them, and re-layouts: 15 us -> 8.76 us
    all_to_all x1 -> x0, blocking collectives: 100 us -> none  [local(): lax.all_to_all(features, 'tok', split_axis=2, concat_axis=1, tiled=True)]
    ppermute x0 -> x41, waiting for transfers between devices: none -> 89.9 us  [the longest x16 43.9 us: shift(): return lax.ppermute(a, axis, [((i + d) % 4, i) for i in range(4)])]
    reduce_scatter x1 -> x0, waiting for transfers between devices: 77.7 us -> none  [local(): lax.psum_scatter(hidden_terms, 'vocab', scatter_dimension=2, tiled=True)]
    pmax x1 -> x0, blocking collectives: 65.2 us -> none  [local(): global_max = lax.pmax(local_max, 'vocab')]
    psum x1 -> x0, blocking collectives: 62.7 us -> none  [local(): total, target_logit = lax.psum((local_sum, local_target), 'vocab')]
    pallas_call x0 -> x8, Pallas kernels: none -> 61.7 us  [the longest x1 17.7 us: logits_call(): pl.pallas_call(logits_body, grid_spec=pltpu.PrefetchScalarGridSpec(num_sc...]
    ppermute x0 -> x41, starting transfers between devices: none -> 54.6 us  [the longest x14 33.6 us: cross(): return lax.ppermute(a, ('x', 'z', 'c'), pairs)]
    all_gather x2 -> x1, waiting for transfers between devices: 51.8 us -> 0.02 us  [local(): feats = lax.all_gather(turned, ('x', 'z', 'c')).reshape(4, 4, 2, ROWS, 128)]
  transfers between devices with their start and end apart: 3 -> 42, of which waited for: 2 -> 21; matrix products, arithmetic and copies ran while one was open for 10% -> 3% of each run, Pallas kernels for 0% -> 26%
where the time goes in v1:
time: 239 us; the launch traced here: 237 us
  waiting for transfers between devices  89.9 us (38%)
  Pallas kernels  61.7 us (26%)
  starting transfers between devices  54.7 us (23%)
  between operations  14.5 us (6%)
  local copies, waits for them, and re-layouts  8.76 us (4%)
  other arithmetic  7.55 us (3%)
    ppermute x16, waiting for transfers between devices, shift(): return lax.ppermute(a, axis, [((i + d) % 4, i) for i in range(4)])  43.9 us
    ppermute x14, waiting for transfers between devices, cross(): return lax.ppermute(a, ('x', 'z', 'c'), pairs)  39 us
    ppermute x14, starting transfers between devices, cross(): return lax.ppermute(a, ('x', 'z', 'c'), pairs)  33.6 us
    ppermute x16, starting transfers between devices, shift(): return lax.ppermute(a, axis, [((i + d) % 4, i) for i in range(4)])  18.2 us
    pallas_call x1, Pallas kernels, logits_call(): pl.pallas_call(logits_body, grid_spec=pltpu.PrefetchScalarGridSpec(num_sc...  17.7 us
    pallas_call x1, Pallas kernels, hidden_call(): pl.pallas_call(hidden_body, grid_spec=pltpu.PrefetchScalarGridSpec(num_sc...  16.7 us
    pallas_call x1, Pallas kernels, embed_a_call(): pl.pallas_call(embed_a_body, grid_spec=pltpu.PrefetchScalarGridSpec(num_s...  13.4 us
    pallas_call x1, Pallas kernels, embed_b_call(): pl.pallas_call(embed_b_body, grid_spec=pltpu.PrefetchScalarGridSpec(num_s...  9.67 us
  transfers between devices with their start and end apart: 42, of which 21 were waited for; matrix products, arithmetic and copies ran while one was open for 3% of the time, Pallas kernels for 26%

profile of v1, /device:TPU:0, one launch (start us, length us, event | category | flops | bytes accessed | tf_op | source)
XLA Modules:
  0.0 237.1 jit_solution(1523179876866771832)
XLA Ops:
  7.2 1.6 collective-permute-start.20
  8.8 0.6 copy-done.16
  9.5 0.9 broadcast_select_fusion.1
  10.4 1.2 collective-permute-done
  11.7 8.3 %collective-permute-start.3 = (bf16[256,256]{1,0:T(8,128)(2,1)S(1)}, bf16[256,256]{1,0:T(8,128)(2,1)S(1)}, u32[]{:S(2)}, u32[]{:S(2)}) collective-permute-start(bf16[256,256]{1,0:T(8,128)(2,1)S(1)} %maximum_select_fusion.2), channel_id=1, source_target_pairs={{96,0},{28,4},{104,8},{4,12},{112,16},{12,20},{120,24},{20,28},{0,... | collective-permute-start | bytes 393224 | tf_op jit(solution)/shard_map/ppermute | solution.py:36
  20.0 8.0 %collective-permute-start.2 = (bf16[256,256]{1,0:T(8,128)(2,1)S(1)}, bf16[256,256]{1,0:T(8,128)(2,1)S(1)}, u32[]{:S(2)}, u32[]{:S(2)}) collective-permute-start(bf16[256,256]{1,0:T(8,128)(2,1)S(1)} %maximum_select_fusion.2), channel_id=1, source_target_pairs={{64,0},{20,4},{72,8},{28,12},{80,16},{4,20},{88,24},{12,28},{96,32... | collective-permute-start | bytes 393224 | tf_op jit(solution)/shard_map/ppermute | solution.py:36
  28.0 1.5 collective-permute-start.1
  29.5 2.8 %collective-permute-done.2 = bf16[256,256]{1,0:T(8,128)(2,1)S(1)} collective-permute-done((bf16[256,256]{1,0:T(8,128)(2,1)S(1)}, bf16[256,256]{1,0:T(8,128)(2,1)S(1)}, u32[]{:S(2)}, u32[]{:S(2)}) %collective-permute-start.2) | collective-permute-done | bytes 131104 | tf_op jit(solution)/shard_map/ppermute | solution.py:36
  32.3 2.6 %collective-permute-done.1 = bf16[256,256]{1,0:T(8,128)(2,1)S(1)} collective-permute-done((bf16[256,256]{1,0:T(8,128)(2,1)S(1)}, bf16[256,256]{1,0:T(8,128)(2,1)S(1)}, u32[]{:S(2)}, u32[]{:S(2)}) %collective-permute-start.1) | collective-permute-done | bytes 131104 | tf_op jit(solution)/shard_map/ppermute | solution.py:36
  35.0 4.5 %collective-permute-start.4 = (bf16[4,256,256]{2,1,0:T(8,128)(2,1)S(1)}, bf16[4,256,256]{2,1,0:T(8,128)(2,1)S(1)}, u32[]{:S(2)}, u32[]{:S(2)}) collective-permute-start(bf16[4,256,256]{2,1,0:T(8,128)(2,1)S(1)} %pad_maximum_fusion.refs_0_), channel_id=1, source_target_pairs={{8,0},{36,4},{16,8},{44,12},{24,16},{52,20},{0,24},{60,28},{40,32}... | collective-permute-start | bytes 1572872 | tf_op jit(solution)/shard_map/ppermute | solution.py:36
  39.5 7.0 %collective-permute-done.4.refs_1_ = bf16[4,256,256]{2,1,0:T(8,128)(2,1)S(1)} collective-permute-done((bf16[4,256,256]{2,1,0:T(8,128)(2,1)S(1)}, bf16[4,256,256]{2,1,0:T(8,128)(2,1)S(1)}, u32[]{:S(2)}, u32[]{:S(2)}) %collective-permute-start.4) | collective-permute-done | bytes 524320 | tf_op jit(solution)/shard_map/ppermute | solution.py:36
  46.6 0.8 slice.113
  47.3 3.7 %collective-permute-start.6 = (bf16[2,256,256]{2,1,0:T(8,128)(2,1)}, bf16[2,256,256]{2,1,0:T(8,128)(2,1)S(1)}, u32[]{:S(2)}, u32[]{:S(2)}) collective-permute-start(bf16[2,256,256]{2,1,0:T(8,128)(2,1)} %slice.113), channel_id=1, source_target_pairs={{8,0},{36,4},{16,8},{44,12},{24,16},{52,20},{0,24},{60,28},{40,32}... | collective-permute-start | bytes 786440 | tf_op jit(solution)/shard_map/ppermute | solution.py:36
  51.0 0.8 slice.114
  52.3 5.5 %collective-permute-done.6.refs_3_ = bf16[2,256,256]{2,1,0:T(8,128)(2,1)S(1)} collective-permute-done((bf16[2,256,256]{2,1,0:T(8,128)(2,1)}, bf16[2,256,256]{2,1,0:T(8,128)(2,1)S(1)}, u32[]{:S(2)}, u32[]{:S(2)}) %collective-permute-start.6) | collective-permute-done | bytes 262176 | tf_op jit(solution)/shard_map/ppermute | solution.py:36
  57.9 6.6 %collective-permute-done.7.refs_4_ = bf16[2,256,256]{2,1,0:T(8,128)(2,1)} collective-permute-done((bf16[2,256,256]{2,1,0:T(8,128)(2,1)}, bf16[2,256,256]{2,1,0:T(8,128)(2,1)}, u32[]{:S(2)}, u32[]{:S(2)}) %collective-permute-start.7) | collective-permute-done | bytes 262176 | tf_op jit(solution)/shard_map/ppermute | solution.py:36
  64.5 0.7 pad_add_fusion.at
  65.1 0.7 broadcast_subtract_fusion
  66.4 0.6 tile.2
  67.0 17.7 %logits.1 = (bf16[512,512]{1,0:T(8,128)(2,1)}, bf16[1536,512]{1,0:T(8,128)(2,1)}, f32[8,512]{1,0:T(8,128)}, f32[8,512]{1,0:T(8,128)}) custom-call(s32[4]{0:T(128)} %pad_add_fusion.at, bf16[4,256,256]{2,1,0:T(8,128)(2,1)} %copy-done.6, bf16[4,256,256]{2,1,0:T(8,128)(2,1)} %copy-done.7, bf16[4,256,256]{2,1,0:T(8,128)(2,1)} %copy-done.8, ...), custom_call_target="tpu_custom_call" | custom-call | flops 1000 | bytes 1000 | tf_op jit(solution)/shard_map/logits/pallas_call | solution.py:160
  84.8 2.0 collective-permute-start.22
  86.8 1.3 collective-permute-start.25
  88.1 0.7 collective-permute-start.26
  88.8 2.2 collective-permute-start.13
  91.1 1.7 collective-permute-done.13.refs_1_
  92.8 1.7 collective-permute-start.14
  94.5 3.8 %collective-permute-done.14.refs_2_ = f32[8,512]{1,0:T(8,128)S(1)} collective-permute-done((f32[8,512]{1,0:T(8,128)}, f32[8,512]{1,0:T(8,128)S(1)}, u32[]{:S(2)}, u32[]{:S(2)}) %collective-permute-start.14) | collective-permute-done | bytes 16416 | tf_op jit(solution)/shard_map/ppermute | solution.py:21
  98.2 0.8 collective-permute-start.15
  99.0 4.6 %collective-permute-done.15.refs_3_ = f32[8,512]{1,0:T(8,128)S(1)} collective-permute-done((f32[8,512]{1,0:T(8,128)}, f32[8,512]{1,0:T(8,128)S(1)}, u32[]{:S(2)}, u32[]{:S(2)}) %collective-permute-start.15) | collective-permute-done | bytes 16416 | tf_op jit(solution)/shard_map/ppermute | solution.py:21
  103.6 0.6 copy-done.23
  104.2 1.4 merge.2.refs_0_
  105.6 3.9 %collective-permute-done.16.refs_1_ = f32[8,512]{1,0:T(8,128)S(1)} collective-permute-done((f32[8,512]{1,0:T(8,128)}, f32[8,512]{1,0:T(8,128)S(1)}, u32[]{:S(2)}, u32[]{:S(2)}) %collective-permute-start.16) | collective-permute-done | bytes 16416 | tf_op jit(solution)/shard_map/ppermute | solution.py:21
  109.6 5.5 %collective-permute-done.17.refs_2_ = f32[8,512]{1,0:T(8,128)S(1)} collective-permute-done((f32[8,512]{1,0:T(8,128)}, f32[8,512]{1,0:T(8,128)S(1)}, u32[]{:S(2)}, u32[]{:S(2)}) %collective-permute-start.17) | collective-permute-done | bytes 16416 | tf_op jit(solution)/shard_map/ppermute | solution.py:21
  115.0 5.2 %collective-permute-done.18.refs_3_ = f32[8,512]{1,0:T(8,128)S(1)} collective-permute-done((f32[8,512]{1,0:T(8,128)}, f32[8,512]{1,0:T(8,128)S(1)}, u32[]{:S(2)}, u32[]{:S(2)}) %collective-permute-start.18) | collective-permute-done | bytes 16416 | tf_op jit(solution)/shard_map/ppermute | solution.py:21
  120.2 0.6 copy-done.24
  120.8 1.4 merge.3.a
  122.2 1.4 collective-permute-done.19.b
  123.6 0.6 copy-done.18
  124.2 1.4 finish.1
  125.6 16.7 %hidden.1 = (f32[4,4,256,256]{3,2,1,0:T(8,128)}, bf16[2,4,256,256]{3,2,1,0:T(8,128)(2,1)}, bf16[2,4,256,256]{3,2,1,0:T(8,128)(2,1)}, bf16[2048,512]{1,0:T(8,128)(2,1)}) custom-call(s32[4]{0:T(128)} %pad_add_fusion.at, bf16[512,512]{1,0:T(8,128)(2,1)} %get-tuple-element.17.e0, bf16[1536,512]{1,0:T(8,128)(2,1)} %get-tuple-element.18.e1, ...), custom_call_target="tpu_custom_call" | custom-call | flops 1000 | bytes 1000 | tf_op jit(solution)/shard_map/hidden/pallas_call | solution.py:283
  142.9 2.3 collective-permute-done.23.refs_0_
  145.3 1.5 collective-permute-done.24.refs_1_
  146.8 1.0 copy-done.5
  147.7 2.7 %fusion.1 = (bf16[4,256,256]{2,1,0:T(8,128)(2,1)S(1)}, f32[4,256,256]{2,1,0:T(8,128)S(1)}, f32[4,256,256]{2,1,0:T(8,128)S(1)}) fusion(f32[4,4,256,256]{3,2,1,0:T(8,128)} %get-tuple-element.22, bf16[2,4,256,256]{3,2,1,0:T(8,128)(2,1)} %get-tuple-element.26, bf16[2,4,256,256]{3,2,1,0:T(8,128)(2,1)} %get-tuple-element.25), kind=kLoop, calls=%fused_computation.5 | loop fusion | flops 1835008 | bytes 7340032 | tf_op jit(solution)/shard_map/convert.6
  150.5 2.1 collective-permute-start.29
  152.7 4.2 %collective-permute-done.29 = bf16[4,128,256]{2,1,0:T(8,128)(2,1)S(1)} collective-permute-done((bf16[4,128,256]{2,1,0:T(8,128)(2,1)S(1)}, bf16[4,128,256]{2,1,0:T(8,128)(2,1)S(1)}, u32[]{:S(2)}, u32[]{:S(2)}) %collective-permute-start.29) | collective-permute-done | bytes 262176 | tf_op jit(solution)/shard_map/ppermute | solution.py:36
  157.0 3.3 %collective-permute-start.30 = (bf16[4,256,256]{2,1,0:T(8,128)(2,1)S(1)}, bf16[4,256,256]{2,1,0:T(8,128)(2,1)S(1)}, u32[]{:S(2)}, u32[]{:S(2)}) collective-permute-start(bf16[4,256,256]{2,1,0:T(8,128)(2,1)S(1)} %pad_maximum_fusion.2), channel_id=1, source_target_pairs={{32,0},{12,4},{40,8},{20,12},{48,16},{28,20},{56,24},{4,28},{64,32... | collective-permute-start | bytes 1572872 | tf_op jit(solution)/shard_map/ppermute | solution.py:36
  160.7 6.3 %collective-permute-done.30 = bf16[4,256,256]{2,1,0:T(8,128)(2,1)S(1)} collective-permute-done((bf16[4,256,256]{2,1,0:T(8,128)(2,1)S(1)}, bf16[4,256,256]{2,1,0:T(8,128)(2,1)S(1)}, u32[]{:S(2)}, u32[]{:S(2)}) %collective-permute-start.30) | collective-permute-done | bytes 524320 | tf_op jit(solution)/shard_map/ppermute | solution.py:36
  167.0 3.9 %collective-permute-done.28 = bf16[4,256,256]{2,1,0:T(8,128)(2,1)S(1)} collective-permute-done((bf16[4,256,256]{2,1,0:T(8,128)(2,1)S(1)}, bf16[4,256,256]{2,1,0:T(8,128)(2,1)S(1)}, u32[]{:S(2)}, u32[]{:S(2)}) %collective-permute-start.28) | collective-permute-done | bytes 524320 | tf_op jit(solution)/shard_map/ppermute | solution.py:36
  170.9 1.5 fusion.7
  172.6 0.8 collective-permute-start.32
  173.4 1.2 collective-permute-start.31
  174.6 3.2 %collective-permute-start.37 = (bf16[512,512]{1,0:T(8,128)(2,1)}, bf16[512,512]{1,0:T(8,128)(2,1)S(1)}, u32[]{:S(2)}, u32[]{:S(2)}) collective-permute-start(bf16[512,512]{1,0:T(8,128)(2,1)} %collective-permute-done.21.ep0), channel_id=1, source_target_pairs={{1,0},{2,1},{3,2},{0,3},{5,4},{6,5},{7,6},{4,7},{9,8},{10,9},{11,1... | collective-permute-start | bytes 1572872 | tf_op jit(solution)/shard_map/ppermute | solution.py:21
  177.8 1.1 slice.111
  178.9 1.8 collective-permute-start.38
  181.0 3.1 %collective-permute-start.35 = (f32[8,512]{1,0:T(8,128)S(1)}, f32[8,512]{1,0:T(8,128)S(1)}, u32[]{:S(2)}, u32[]{:S(2)}) collective-permute-start(f32[8,512]{1,0:T(8,128)S(1)} %copy-done.27), channel_id=1, source_target_pairs={{1,0},{2,1},{3,2},{0,3},{5,4},{6,5},{7,6},{4,7},{9,8},{10,9},{11,1... | collective-permute-start | bytes 49160 | tf_op jit(solution)/shard_map/ppermute | solution.py:21
  184.0 13.8 %collective-permute-done.35.pack_p = f32[8,512]{1,0:T(8,128)S(1)} collective-permute-done((f32[8,512]{1,0:T(8,128)S(1)}, f32[8,512]{1,0:T(8,128)S(1)}, u32[]{:S(2)}, u32[]{:S(2)}) %collective-permute-start.35) | collective-permute-done | bytes 16416 | tf_op jit(solution)/shard_map/ppermute | solution.py:21
  197.8 5.4 %collective-permute-done.36.pack_m = f32[8,512]{1,0:T(8,128)S(1)} collective-permute-done((f32[8,512]{1,0:T(8,128)S(1)}, f32[8,512]{1,0:T(8,128)S(1)}, u32[]{:S(2)}, u32[]{:S(2)}) %collective-permute-start.36) | collective-permute-done | bytes 16416 | tf_op jit(solution)/shard_map/ppermute | solution.py:21
  203.2 1.2 collective-permute-start.40
  204.4 13.4 %embed_a.1.acc = f32[2048,1024]{1,0:T(8,128)} custom-call(s32[4]{0:T(128)} %pad_add_fusion.at, bf16[2048,512]{1,0:T(8,128)(2,1)} %get-tuple-element.27.tgt, bf16[512,512]{1,0:T(8,128)(2,1)} %collective-permute-done.21.ep0, bf16[1536,512]{1,0:T(8,128)(2,1)} %get-tuple-element.28.ep1, bf16[512,512]{1,0:T(8,128)(2,1)} %collective-permute-done.22.em0, ...), custom_call_target="tpu_custom_call" | custom-call | flops 1000 | bytes 1000 | tf_op jit(solution)/shard_map/embed_a/pallas_call | solution.py:359
  217.9 0.7 copy-done.13
  218.9 1.0 copy-done.9
  219.8 9.7 %embed_b.1 = bf16[2048,1024]{1,0:T(8,128)(2,1)} custom-call(s32[4]{0:T(128)} %pad_add_fusion.at, f32[2048,1024]{1,0:T(8,128)} %embed_a.1.acc, bf16[512,512]{1,0:T(8,128)(2,1)} %copy-done.13, bf16[512,512]{1,0:T(8,128)(2,1)} %copy-done.14, bf16[1024,512]{1,0:T(8,128)(2,1)} %copy-done.9, f32[8,512]{1,0:T(8,128)} %copy-done.17, ...), custom_call_target="tpu_custom_call" | custom-call | flops 1000 | bytes 1000 | tf_op jit(solution)/shard_map/embed_b/pallas_call | solution.py:392
  229.5 0.7 maximum_select_fusion
  (109 shorter events, 3.3 us)
Async XLA Ops:
  7.2 116.5 %all-gather.3.cloned.1.call-start = ((), (), s32[]{:S(2)}) async-start(), calls=%async_computation | async-start | bytes 4325376 | tf_op jit(solution)/shard_map/all_gather | solution.py:430
  7.2 1.6 collective-permute-start.20
  10.3 1.3 collective-permute-start
  11.7 17.8 %collective-permute-start.3 = (bf16[256,256]{1,0:T(8,128)(2,1)S(1)}, bf16[256,256]{1,0:T(8,128)(2,1)S(1)}, u32[]{:S(2)}, u32[]{:S(2)}) collective-permute-start(bf16[256,256]{1,0:T(8,128)(2,1)S(1)} %maximum_select_fusion.2), channel_id=1, source_target_pairs={{96,0},{28,4},{104,8},{4,12},{112,16},{12,20},{120,24},{20,28},{0,... | collective-permute-start | bytes 393224 | tf_op jit(solution)/shard_map/ppermute | solution.py:36
  20.0 12.3 %collective-permute-start.2 = (bf16[256,256]{1,0:T(8,128)(2,1)S(1)}, bf16[256,256]{1,0:T(8,128)(2,1)S(1)}, u32[]{:S(2)}, u32[]{:S(2)}) collective-permute-start(bf16[256,256]{1,0:T(8,128)(2,1)S(1)} %maximum_select_fusion.2), channel_id=1, source_target_pairs={{64,0},{20,4},{72,8},{28,12},{80,16},{4,20},{88,24},{12,28},{96,32... | collective-permute-start | bytes 393224 | tf_op jit(solution)/shard_map/ppermute | solution.py:36
  28.0 6.9 %collective-permute-start.1 = (bf16[256,256]{1,0:T(8,128)(2,1)S(1)}, bf16[256,256]{1,0:T(8,128)(2,1)S(1)}, u32[]{:S(2)}, u32[]{:S(2)}) collective-permute-start(bf16[256,256]{1,0:T(8,128)(2,1)S(1)} %maximum_select_fusion.2), channel_id=1, source_target_pairs={{32,0},{12,4},{40,8},{20,12},{48,16},{28,20},{56,24},{4,28},{64,32... | collective-permute-start | bytes 393224 | tf_op jit(solution)/shard_map/ppermute | solution.py:36
  35.0 32.0 %copy-start.6 = (bf16[4,256,256]{2,1,0:T(8,128)(2,1)}, bf16[4,256,256]{2,1,0:T(8,128)(2,1)S(1)}, u32[]{:S(2)}) copy-start(bf16[4,256,256]{2,1,0:T(8,128)(2,1)S(1)} %pad_maximum_fusion.refs_0_) | copy-start | bytes 1572868
  35.0 11.6 %collective-permute-start.4 = (bf16[4,256,256]{2,1,0:T(8,128)(2,1)S(1)}, bf16[4,256,256]{2,1,0:T(8,128)(2,1)S(1)}, u32[]{:S(2)}, u32[]{:S(2)}) collective-permute-start(bf16[4,256,256]{2,1,0:T(8,128)(2,1)S(1)} %pad_maximum_fusion.refs_0_), channel_id=1, source_target_pairs={{8,0},{36,4},{16,8},{44,12},{24,16},{52,20},{0,24},{60,28},{40,32}... | collective-permute-start | bytes 1572872 | tf_op jit(solution)/shard_map/ppermute | solution.py:36
  39.5 11.5 %collective-permute-start.5 = (bf16[4,256,256]{2,1,0:T(8,128)(2,1)S(1)}, bf16[4,256,256]{2,1,0:T(8,128)(2,1)S(1)}, u32[]{:S(2)}, u32[]{:S(2)}) collective-permute-start(bf16[4,256,256]{2,1,0:T(8,128)(2,1)S(1)} %pad_maximum_fusion.refs_0_), channel_id=1, source_target_pairs={{24,0},{100,4},{0,8},{108,12},{8,16},{116,20},{16,24},{124,28},{56... | collective-permute-start | bytes 1572872 | tf_op jit(solution)/shard_map/ppermute | solution.py:36
  46.6 20.4 %copy-start.7 = (bf16[4,256,256]{2,1,0:T(8,128)(2,1)}, bf16[4,256,256]{2,1,0:T(8,128)(2,1)S(1)}, u32[]{:S(2)}) copy-start(bf16[4,256,256]{2,1,0:T(8,128)(2,1)S(1)} %collective-permute-done.4.refs_1_) | copy-start | bytes 1572868
  47.3 10.5 %collective-permute-start.6 = (bf16[2,256,256]{2,1,0:T(8,128)(2,1)}, bf16[2,256,256]{2,1,0:T(8,128)(2,1)S(1)}, u32[]{:S(2)}, u32[]{:S(2)}) collective-permute-start(bf16[2,256,256]{2,1,0:T(8,128)(2,1)} %slice.113), channel_id=1, source_target_pairs={{8,0},{36,4},{16,8},{44,12},{24,16},{52,20},{0,24},{60,28},{40,32}... | collective-permute-start | bytes 786440 | tf_op jit(solution)/shard_map/ppermute | solution.py:36
  51.0 15.9 %copy-start.8 = (bf16[4,256,256]{2,1,0:T(8,128)(2,1)}, bf16[4,256,256]{2,1,0:T(8,128)(2,1)S(1)}, u32[]{:S(2)}) copy-start(bf16[4,256,256]{2,1,0:T(8,128)(2,1)S(1)} %collective-permute-done.5.refs_2_) | copy-start | bytes 1572868
  51.8 12.7 %collective-permute-start.7 = (bf16[2,256,256]{2,1,0:T(8,128)(2,1)}, bf16[2,256,256]{2,1,0:T(8,128)(2,1)}, u32[]{:S(2)}, u32[]{:S(2)}) collective-permute-start(bf16[2,256,256]{2,1,0:T(8,128)(2,1)} %slice.114), channel_id=1, source_target_pairs={{24,0},{100,4},{0,8},{108,12},{8,16},{116,20},{16,24},{124,28},{56... | collective-permute-start | bytes 786440 | tf_op jit(solution)/shard_map/ppermute | solution.py:36
  51.8 14.0 %collective-permute-start.8 = (bf16[4,256,256]{2,1,0:T(8,128)(2,1)S(1)}, bf16[4,256,256]{2,1,0:T(8,128)(2,1)S(1)}, u32[]{:S(2)}, u32[]{:S(2)}) collective-permute-start(bf16[4,256,256]{2,1,0:T(8,128)(2,1)S(1)} %pad_maximum_fusion.refs_0_), channel_id=1, source_target_pairs={{0,4},{4,0},{1,5},{5,1},{2,6},{6,2},{3,7},{7,3},{8,12},{12,8},{9,1... | collective-permute-start | bytes 1572872 | tf_op jit(solution)/shard_map/ppermute | solution.py:25
  51.8 14.0 %collective-permute-start.9 = (bf16[4,256,256]{2,1,0:T(8,128)(2,1)S(1)}, bf16[4,256,256]{2,1,0:T(8,128)(2,1)S(1)}, u32[]{:S(2)}, u32[]{:S(2)}) collective-permute-start(bf16[4,256,256]{2,1,0:T(8,128)(2,1)S(1)} %collective-permute-done.4.refs_1_), channel_id=1, source_target_pairs={{0,4},{4,0},{1,5},{5,1},{2,6},{6,2},{3,7},{7,3},{8,12},{12,8},{9,1... | collective-permute-start | bytes 1572872 | tf_op jit(solution)/shard_map/ppermute | solution.py:25
  52.3 13.5 %collective-permute-start.10 = (bf16[4,256,256]{2,1,0:T(8,128)(2,1)S(1)}, bf16[4,256,256]{2,1,0:T(8,128)(2,1)S(1)}, u32[]{:S(2)}, u32[]{:S(2)}) collective-permute-start(bf16[4,256,256]{2,1,0:T(8,128)(2,1)S(1)} %collective-permute-done.5.refs_2_), channel_id=1, source_target_pairs={{0,4},{4,0},{1,5},{5,1},{2,6},{6,2},{3,7},{7,3},{8,12},{12,8},{9,1... | collective-permute-start | bytes 1572872 | tf_op jit(solution)/shard_map/ppermute | solution.py:25
  57.9 9.1 %copy-start.15 = (bf16[2,256,256]{2,1,0:T(8,128)(2,1)}, bf16[2,256,256]{2,1,0:T(8,128)(2,1)S(1)}, u32[]{:S(2)}) copy-start(bf16[2,256,256]{2,1,0:T(8,128)(2,1)S(1)} %collective-permute-done.6.refs_3_) | copy-start | bytes 786436
  57.9 8.0 %collective-permute-start.11 = (bf16[2,256,256]{2,1,0:T(8,128)(2,1)S(1)}, bf16[2,256,256]{2,1,0:T(8,128)(2,1)}, u32[]{:S(2)}, u32[]{:S(2)}) collective-permute-start(bf16[2,256,256]{2,1,0:T(8,128)(2,1)S(1)} %collective-permute-done.6.refs_3_), channel_id=1, source_target_pairs={{0,4},{4,0},{1,5},{5,1},{2,6},{6,2},{3,7},{7,3},{8,12},{12,8},{9,1... | collective-permute-start | bytes 786440 | tf_op jit(solution)/shard_map/ppermute | solution.py:25
  64.5 1.9 collective-permute-start.12
  65.8 1.2 copy-start.10
  65.8 1.2 copy-start.11
  65.8 1.2 copy-start.12
  84.7 38.9 %collective-permute-start.21 = (bf16[512,512]{1,0:T(8,128)(2,1)}, bf16[512,512]{1,0:T(8,128)(2,1)}, u32[]{:S(2)}, u32[]{:S(2)}) collective-permute-start(bf16[512,512]{1,0:T(8,128)(2,1)} %get-tuple-element.17.e0), channel_id=1, source_target_pairs={{1,0},{2,1},{3,2},{0,3},{5,4},{6,5},{7,6},{4,7},{9,8},{10,9},{11,1... | collective-permute-start | bytes 1572872 | tf_op jit(solution)/shard_map/ppermute | solution.py:21
  84.8 38.8 %collective-permute-start.22 = (bf16[512,512]{1,0:T(8,128)(2,1)}, bf16[512,512]{1,0:T(8,128)(2,1)}, u32[]{:S(2)}, u32[]{:S(2)}) collective-permute-start(bf16[512,512]{1,0:T(8,128)(2,1)} %get-tuple-element.17.e0), channel_id=1, source_target_pairs={{3,0},{0,1},{1,2},{2,3},{7,4},{4,5},{5,6},{6,7},{11,8},{8,9},{9,10... | collective-permute-start | bytes 1572872 | tf_op jit(solution)/shard_map/ppermute | solution.py:21
  86.8 56.1 %collective-permute-start.25 = (bf16[1536,512]{1,0:T(8,128)(2,1)}, bf16[1536,512]{1,0:T(8,128)(2,1)S(1)}, u32[]{:S(2)}, u32[]{:S(2)}) collective-permute-start(bf16[1536,512]{1,0:T(8,128)(2,1)} %get-tuple-element.18.e1), channel_id=1, source_target_pairs={{1,0},{2,1},{3,2},{0,3},{5,4},{6,5},{7,6},{4,7},{9,8},{10,9},{11,1... | collective-permute-start | bytes 4718600 | tf_op jit(solution)/shard_map/ppermute | solution.py:21
  88.1 54.8 %collective-permute-start.26 = (bf16[1536,512]{1,0:T(8,128)(2,1)}, bf16[1536,512]{1,0:T(8,128)(2,1)S(1)}, u32[]{:S(2)}, u32[]{:S(2)}) collective-permute-start(bf16[1536,512]{1,0:T(8,128)(2,1)} %get-tuple-element.18.e1), channel_id=1, source_target_pairs={{3,0},{0,1},{1,2},{2,3},{7,4},{4,5},{5,6},{6,7},{11,8},{8,9},{9,10... | collective-permute-start | bytes 4718600 | tf_op jit(solution)/shard_map/ppermute | solution.py:21
  88.8 3.9 %collective-permute-start.13 = (f32[8,512]{1,0:T(8,128)}, f32[8,512]{1,0:T(8,128)S(1)}, u32[]{:S(2)}, u32[]{:S(2)}) collective-permute-start(f32[8,512]{1,0:T(8,128)} %get-tuple-element.19.refs_0_), channel_id=1, source_target_pairs={{32,0},{64,32},{96,64},{0,96},{33,1},{65,33},{97,65},{1,97},{34,2}... | collective-permute-start | bytes 49160 | tf_op jit(solution)/shard_map/ppermute | solution.py:21
  92.8 10.8 %copy-start.19 = (f32[8,512]{1,0:T(8,128)}, f32[8,512]{1,0:T(8,128)S(1)}, u32[]{:S(2)}) copy-start(f32[8,512]{1,0:T(8,128)S(1)} %collective-permute-done.13.refs_1_) | copy-start | bytes 49156
  92.8 5.5 %collective-permute-start.14 = (f32[8,512]{1,0:T(8,128)}, f32[8,512]{1,0:T(8,128)S(1)}, u32[]{:S(2)}, u32[]{:S(2)}) collective-permute-start(f32[8,512]{1,0:T(8,128)} %get-tuple-element.19.refs_0_), channel_id=1, source_target_pairs={{64,0},{96,32},{0,64},{32,96},{65,1},{97,33},{1,65},{33,97},{66,2}... | collective-permute-start | bytes 49160 | tf_op jit(solution)/shard_map/ppermute | solution.py:21
  98.2 5.4 %copy-start.21 = (f32[8,512]{1,0:T(8,128)}, f32[8,512]{1,0:T(8,128)S(1)}, u32[]{:S(2)}) copy-start(f32[8,512]{1,0:T(8,128)S(1)} %collective-permute-done.14.refs_2_) | copy-start | bytes 49156
  98.2 5.4 %collective-permute-start.15 = (f32[8,512]{1,0:T(8,128)}, f32[8,512]{1,0:T(8,128)S(1)}, u32[]{:S(2)}, u32[]{:S(2)}) collective-permute-start(f32[8,512]{1,0:T(8,128)} %get-tuple-element.19.refs_0_), channel_id=1, source_target_pairs={{96,0},{0,32},{32,64},{64,96},{97,1},{1,33},{33,65},{65,97},{98,2}... | collective-permute-start | bytes 49160 | tf_op jit(solution)/shard_map/ppermute | solution.py:21
  105.6 3.9 %collective-permute-start.16 = (f32[8,512]{1,0:T(8,128)}, f32[8,512]{1,0:T(8,128)S(1)}, u32[]{:S(2)}, u32[]{:S(2)}) collective-permute-start(f32[8,512]{1,0:T(8,128)} %merge.2.refs_0_), channel_id=1, source_target_pairs={{8,0},{16,8},{24,16},{0,24},{9,1},{17,9},{25,17},{1,25},{10,2},{18... | collective-permute-start | bytes 49160 | tf_op jit(solution)/shard_map/ppermute | solution.py:21
  109.6 10.6 %copy-start.20 = (f32[8,512]{1,0:T(8,128)}, f32[8,512]{1,0:T(8,128)S(1)}, u32[]{:S(2)}) copy-start(f32[8,512]{1,0:T(8,128)S(1)} %collective-permute-done.16.refs_1_) | copy-start | bytes 49156
  109.6 5.5 %collective-permute-start.17 = (f32[8,512]{1,0:T(8,128)}, f32[8,512]{1,0:T(8,128)S(1)}, u32[]{:S(2)}, u32[]{:S(2)}) collective-permute-start(f32[8,512]{1,0:T(8,128)} %merge.2.refs_0_), channel_id=1, source_target_pairs={{16,0},{24,8},{0,16},{8,24},{17,1},{25,9},{1,17},{9,25},{18,2},{26... | collective-permute-start | bytes 49160 | tf_op jit(solution)/shard_map/ppermute | solution.py:21
  115.0 5.2 %copy-start.22 = (f32[8,512]{1,0:T(8,128)}, f32[8,512]{1,0:T(8,128)S(1)}, u32[]{:S(2)}) copy-start(f32[8,512]{1,0:T(8,128)S(1)} %collective-permute-done.17.refs_2_) | copy-start | bytes 49156
  115.0 5.2 %collective-permute-start.18 = (f32[8,512]{1,0:T(8,128)}, f32[8,512]{1,0:T(8,128)S(1)}, u32[]{:S(2)}, u32[]{:S(2)}) collective-permute-start(f32[8,512]{1,0:T(8,128)} %merge.2.refs_0_), channel_id=1, source_target_pairs={{24,0},{0,8},{8,16},{16,24},{25,1},{1,9},{9,17},{17,25},{26,2},{2,... | collective-permute-start | bytes 49160 | tf_op jit(solution)/shard_map/ppermute | solution.py:21
  122.2 1.4 collective-permute-start.19
  142.3 3.0 %collective-permute-start.23 = (bf16[2,4,256,256]{3,2,1,0:T(8,128)(2,1)}, bf16[2,4,256,256]{3,2,1,0:T(8,128)(2,1)S(1)}, u32[]{:S(2)}, u32[]{:S(2)}) collective-permute-start(bf16[2,4,256,256]{3,2,1,0:T(8,128)(2,1)} %get-tuple-element.23), channel_id=1, source_target_pairs={{0,4},{4,0},{1,5},{5,1},{2,6},{6,2},{3,7},{7,3},{8,12},{12,8},{9,1... | collective-permute-start | bytes 3145736 | tf_op jit(solution)/shard_map/ppermute | solution.py:25
  142.6 4.2 %collective-permute-start.24 = (bf16[2,4,256,256]{3,2,1,0:T(8,128)(2,1)}, bf16[2,4,256,256]{3,2,1,0:T(8,128)(2,1)S(1)}, u32[]{:S(2)}, u32[]{:S(2)}) collective-permute-start(bf16[2,4,256,256]{3,2,1,0:T(8,128)(2,1)} %get-tuple-element.24), channel_id=1, source_target_pairs={{0,4},{4,0},{1,5},{5,1},{2,6},{6,2},{3,7},{7,3},{8,12},{12,8},{9,1... | collective-permute-start | bytes 3145736 | tf_op jit(solution)/shard_map/ppermute | solution.py:25
  142.9 3.9 %copy-start.2 = (bf16[1536,512]{1,0:T(8,128)(2,1)}, bf16[1536,512]{1,0:T(8,128)(2,1)S(1)}, u32[]{:S(2)}) copy-start(bf16[1536,512]{1,0:T(8,128)(2,1)S(1)} %collective-permute-done.25.refs_2_) | copy-start | bytes 4718596
  142.9 3.9 %copy-start = (bf16[1536,512]{1,0:T(8,128)(2,1)}, bf16[1536,512]{1,0:T(8,128)(2,1)S(1)}, u32[]{:S(2)}) copy-start(bf16[1536,512]{1,0:T(8,128)(2,1)S(1)} %collective-permute-done.26.refs_3_) | copy-start | bytes 4718596
  145.3 1.5 copy-start.3
  146.8 1.0 copy-start.5
  150.4 10.2 %copy-start.1 = (bf16[1536,512]{1,0:T(8,128)(2,1)S(1)}, bf16[1536,512]{1,0:T(8,128)(2,1)}, u32[]{:S(2)}) copy-start(bf16[1536,512]{1,0:T(8,128)(2,1)} %get-tuple-element.29.em1) | copy-start | bytes 4718596
  150.4 20.5 %copy-start.4 = (bf16[2,4,256,256]{3,2,1,0:T(8,128)(2,1)S(1)}, bf16[2,4,256,256]{3,2,1,0:T(8,128)(2,1)}, u32[]{:S(2)}) copy-start(bf16[2,4,256,256]{3,2,1,0:T(8,128)(2,1)} %get-tuple-element.25) | copy-start | bytes 3145732
  150.5 6.4 %collective-permute-start.29 = (bf16[4,128,256]{2,1,0:T(8,128)(2,1)S(1)}, bf16[4,128,256]{2,1,0:T(8,128)(2,1)S(1)}, u32[]{:S(2)}, u32[]{:S(2)}) collective-permute-start(bf16[4,128,256]{2,1,0:T(8,128)(2,1)S(1)} %get-tuple-element.40), channel_id=1, source_target_pairs={{32,0},{12,4},{40,8},{20,12},{48,16},{28,20},{56,24},{4,28},{64,32... | collective-permute-start | bytes 786440 | tf_op jit(solution)/shard_map/ppermute | solution.py:36
  152.6 7.7 %collective-permute-start.27 = (bf16[4,128,256]{2,1,0:T(8,128)(2,1)S(1)}, bf16[4,128,256]{2,1,0:T(8,128)(2,1)S(1)}, u32[]{:S(2)}, u32[]{:S(2)}) collective-permute-start(bf16[4,128,256]{2,1,0:T(8,128)(2,1)S(1)} %get-tuple-element.39), channel_id=1, source_target_pairs={{96,0},{28,4},{104,8},{4,12},{112,16},{12,20},{120,24},{20,28},{0,... | collective-permute-start | bytes 786440 | tf_op jit(solution)/shard_map/ppermute | solution.py:36
  157.0 10.0 %collective-permute-start.30 = (bf16[4,256,256]{2,1,0:T(8,128)(2,1)S(1)}, bf16[4,256,256]{2,1,0:T(8,128)(2,1)S(1)}, u32[]{:S(2)}, u32[]{:S(2)}) collective-permute-start(bf16[4,256,256]{2,1,0:T(8,128)(2,1)S(1)} %pad_maximum_fusion.2), channel_id=1, source_target_pairs={{32,0},{12,4},{40,8},{20,12},{48,16},{28,20},{56,24},{4,28},{64,32... | collective-permute-start | bytes 1572872 | tf_op jit(solution)/shard_map/ppermute | solution.py:36
  160.5 10.5 %collective-permute-start.28 = (bf16[4,256,256]{2,1,0:T(8,128)(2,1)S(1)}, bf16[4,256,256]{2,1,0:T(8,128)(2,1)S(1)}, u32[]{:S(2)}, u32[]{:S(2)}) collective-permute-start(bf16[4,256,256]{2,1,0:T(8,128)(2,1)S(1)} %pad_maximum_fusion.1), channel_id=1, source_target_pairs={{96,0},{28,4},{104,8},{4,12},{112,16},{12,20},{120,24},{20,28},{0,... | collective-permute-start | bytes 1572872 | tf_op jit(solution)/shard_map/ppermute | solution.py:36
  160.6 20.3 %copy-start.27 = (f32[8,512]{1,0:T(8,128)S(1)}, f32[8,512]{1,0:T(8,128)}, u32[]{:S(2)}) copy-start(f32[8,512]{1,0:T(8,128)} %get-tuple-element.21.pack) | copy-start | bytes 49156
  160.7 57.3 %collective-permute-start.39 = (bf16[1024,512]{1,0:T(8,128)(2,1)S(1)}, bf16[1024,512]{1,0:T(8,128)(2,1)S(1)}, u32[]{:S(2)}, u32[]{:S(2)}) collective-permute-start(bf16[1024,512]{1,0:T(8,128)(2,1)S(1)} %slice.112), channel_id=1, source_target_pairs={{3,0},{0,1},{1,2},{2,3},{7,4},{4,5},{5,6},{6,7},{11,8},{8,9},{9,10... | collective-permute-start | bytes 3145736 | tf_op jit(solution)/shard_map/ppermute | solution.py:21
  172.5 6.4 %collective-permute-start.33 = (bf16[256,256]{1,0:T(8,128)(2,1)S(1)}, bf16[256,256]{1,0:T(8,128)(2,1)S(1)}, u32[]{:S(2)}, u32[]{:S(2)}) collective-permute-start(bf16[256,256]{1,0:T(8,128)(2,1)S(1)} %get-tuple-element.37), channel_id=1, source_target_pairs={{8,0},{36,4},{16,8},{44,12},{24,16},{52,20},{0,24},{60,28},{40,32}... | collective-permute-start | bytes 393224 | tf_op jit(solution)/shard_map/ppermute | solution.py:36
  172.6 8.2 %collective-permute-start.32 = (bf16[256,256]{1,0:T(8,128)(2,1)S(1)}, bf16[256,256]{1,0:T(8,128)(2,1)S(1)}, u32[]{:S(2)}, u32[]{:S(2)}) collective-permute-start(bf16[256,256]{1,0:T(8,128)(2,1)S(1)} %get-tuple-element.38), channel_id=1, source_target_pairs={{16,0},{68,4},{24,8},{76,12},{0,16},{84,20},{8,24},{92,28},{48,32}... | collective-permute-start | bytes 393224 | tf_op jit(solution)/shard_map/ppermute | solution.py:36
  173.4 7.3 %collective-permute-start.31 = (bf16[256,256]{1,0:T(8,128)(2,1)S(1)}, bf16[256,256]{1,0:T(8,128)(2,1)S(1)}, u32[]{:S(2)}, u32[]{:S(2)}) collective-permute-start(bf16[256,256]{1,0:T(8,128)(2,1)S(1)} %get-tuple-element.36), channel_id=1, source_target_pairs={{24,0},{100,4},{0,8},{108,12},{8,16},{116,20},{16,24},{124,28},{56... | collective-permute-start | bytes 393224 | tf_op jit(solution)/shard_map/ppermute | solution.py:36
  174.6 43.3 %collective-permute-start.37 = (bf16[512,512]{1,0:T(8,128)(2,1)}, bf16[512,512]{1,0:T(8,128)(2,1)S(1)}, u32[]{:S(2)}, u32[]{:S(2)}) collective-permute-start(bf16[512,512]{1,0:T(8,128)(2,1)} %collective-permute-done.21.ep0), channel_id=1, source_target_pairs={{1,0},{2,1},{3,2},{0,3},{5,4},{6,5},{7,6},{4,7},{9,8},{10,9},{11,1... | collective-permute-start | bytes 1572872 | tf_op jit(solution)/shard_map/ppermute | solution.py:21
  178.9 39.0 %collective-permute-start.38 = (bf16[512,512]{1,0:T(8,128)(2,1)S(1)}, bf16[512,512]{1,0:T(8,128)(2,1)S(1)}, u32[]{:S(2)}, u32[]{:S(2)}) collective-permute-start(bf16[512,512]{1,0:T(8,128)(2,1)S(1)} %slice.111), channel_id=1, source_target_pairs={{1,0},{2,1},{3,2},{0,3},{5,4},{6,5},{7,6},{4,7},{9,8},{10,9},{11,1... | collective-permute-start | bytes 1572872 | tf_op jit(solution)/shard_map/ppermute | solution.py:21
  180.8 48.7 %collective-permute-start.34 = (f32[256,128]{1,0:T(8,128)S(1)}, f32[256,128]{1,0:T(8,128)S(1)}, u32[]{:S(2)}, u32[]{:S(2)}) collective-permute-start(f32[256,128]{1,0:T(8,128)S(1)} %get-tuple-element.42), channel_id=1, source_target_pairs={{0,4},{4,0},{1,5},{5,1},{2,6},{6,2},{3,7},{7,3},{8,12},{12,8},{9,1... | collective-permute-start | bytes 393224 | tf_op jit(solution)/shard_map/ppermute | solution.py:25
  181.0 16.9 %collective-permute-start.35 = (f32[8,512]{1,0:T(8,128)S(1)}, f32[8,512]{1,0:T(8,128)S(1)}, u32[]{:S(2)}, u32[]{:S(2)}) collective-permute-start(f32[8,512]{1,0:T(8,128)S(1)} %copy-done.27), channel_id=1, source_target_pairs={{1,0},{2,1},{3,2},{0,3},{5,4},{6,5},{7,6},{4,7},{9,8},{10,9},{11,1... | collective-permute-start | bytes 49160 | tf_op jit(solution)/shard_map/ppermute | solution.py:21
  197.8 6.6 %copy-start.25 = (f32[8,512]{1,0:T(8,128)}, f32[8,512]{1,0:T(8,128)S(1)}, u32[]{:S(2)}) copy-start(f32[8,512]{1,0:T(8,128)S(1)} %collective-permute-done.35.pack_p) | copy-start | bytes 49156
  197.8 5.4 %collective-permute-start.36 = (f32[8,512]{1,0:T(8,128)S(1)}, f32[8,512]{1,0:T(8,128)S(1)}, u32[]{:S(2)}, u32[]{:S(2)}) collective-permute-start(f32[8,512]{1,0:T(8,128)S(1)} %copy-done.27), channel_id=1, source_target_pairs={{3,0},{0,1},{1,2},{2,3},{7,4},{4,5},{5,6},{6,7},{11,8},{8,9},{9,10... | collective-permute-start | bytes 49160 | tf_op jit(solution)/shard_map/ppermute | solution.py:21
  203.2 1.2 copy-start.26
  203.2 14.7 %collective-permute-start.40 = (f32[8,512]{1,0:T(8,128)S(1)}, f32[8,512]{1,0:T(8,128)S(1)}, u32[]{:S(2)}, u32[]{:S(2)}) collective-permute-start(f32[8,512]{1,0:T(8,128)S(1)} %copy-done.27), channel_id=1, source_target_pairs={{2,0},{3,1},{0,2},{1,3},{6,4},{7,5},{4,6},{5,7},{10,8},{11,9},{8,1... | collective-permute-start | bytes 49160 | tf_op jit(solution)/shard_map/ppermute | solution.py:21
  217.9 1.0 copy-start.14
  218.9 1.0 copy-start.9
  (6 other events, 4.0 us)
Sparse Core Ops, SparseCore 0:
  10.3 59.9 all-gather.2

commit v2 on v1

--- a/solution.py
+++ b/solution.py
@@ -70,12 +70,21 @@
     )(*arrays)
 
 
-LOW = pl.BlockSpec((TILE, ROWS), lambda i, at: (0, 0))
-HIGH = pl.BlockSpec((TILE, ROWS), lambda i, at: (jnp.maximum(i - 1, 0), 0))
-
-
-def pick(i, low, high):
-    return jnp.where(i == 0, low[...], high[...])
+CUT = 768
+SUB = 256
+
+
+def sub_specs():
+    low = [pl.BlockSpec((SUB, ROWS), lambda i, at, k=k: (jnp.minimum(2 * i + k, CUT // SUB - 1), 0)) for k in (0, 1)]
+    high = [pl.BlockSpec((SUB, ROWS), lambda i, at, k=k: (jnp.maximum(2 * i + k - CUT // SUB, 0), 0)) for k in (0, 1)]
+    return low + high
+
+
+def pick(i, low0, low1, high0, high1):
+    n = CUT // SUB
+    return jnp.concatenate(
+        [jnp.where(2 * i < n, low0[...], high0[...]), jnp.where(2 * i + 1 < n, low1[...], high1[...])], axis=0
+    )
 
 
 def gather_pieces(block):
@@ -96,7 +105,7 @@
 
 def logits_body(at, *refs):
     pieces, refs = refs[:10], refs[10:]
-    tid, emb, e0_out, e1_out, st_out, loc_out, full, sem = refs
+    tid, emb, _, e0_out, e1_out, st_out, loc_out, _, full, sem = refs
     step = pl.program_id(0)
     x, z, c = at[0], at[1], at[2]
 
@@ -126,19 +135,15 @@
     total = jnp.sum(e, axis=0, keepdims=True)
     e = e.astype(BF)
 
-    @pl.when(step == 0)
-    def _():
-        e0_out[...] = e
-
-    @pl.when(step > 0)
-    def _():
-        e1_out[...] = e
-
     for s in range(TILES):
 
         @pl.when(step == s)
         def _():
             st_out[pl.ds(s, 1), :] = top
+            for k in (0, 1):
+                row = s * TILE + k * SUB
+                ref, row = (e0_out, row) if row < CUT else (e1_out, row - CUT)
+                ref[pl.ds(row, SUB), :] = e[k * SUB : (k + 1) * SUB]
 
     @pl.when(step == 0)
     def _():
@@ -155,7 +160,7 @@
         loc_out[pl.ds(2, 1), :] = loc_out[pl.ds(2, 1), :] + hit
 
 
-def logits_call(at, pieces, tid, emb, name):
+def logits_call(at, pieces, tid, emb, later):
     whole = pl.BlockSpec((8, ROWS), lambda i, at: (0, 0))
     return pl.pallas_call(
         logits_body,
@@ -163,20 +168,28 @@
             num_scalar_prefetch=1,
             grid=(TILES,),
             in_specs=[HBM] * 10
-            + [pl.BlockSpec((1, ROWS), lambda i, at: (0, 0)), pl.BlockSpec((TILE, WIDTH), lambda i, at: (i, 0))],
-            out_specs=[LOW, HIGH, whole, whole],
+            + [pl.BlockSpec((1, ROWS), lambda i, at: (0, 0)), pl.BlockSpec((TILE, WIDTH), lambda i, at: (i, 0)), HBM],
+            out_specs=[
+                pl.BlockSpec((CUT, ROWS), lambda i, at: (0, 0)),
+                pl.BlockSpec((VOC - CUT, ROWS), lambda i, at: (0, 0)),
+                whole,
+                whole,
+                HBM,
+            ],
             scratch_shapes=[pltpu.VMEM((ROWS, WIDTH), BF), pltpu.SemaphoreType.DMA((32,))],
         ),
         out_shape=[
-            jax.ShapeDtypeStruct((TILE, ROWS), BF),
-            jax.ShapeDtypeStruct((VOC - TILE, ROWS), BF),
+            jax.ShapeDtypeStruct((CUT, ROWS), BF),
+            jax.ShapeDtypeStruct((VOC - CUT, ROWS), BF),
             jax.ShapeDtypeStruct((8, ROWS), F32),
             jax.ShapeDtypeStruct((8, ROWS), F32),
+            jax.ShapeDtypeStruct(later.shape, later.dtype),
         ],
-        compiler_params=params(),
-        cost_estimate=SMALL,
-        name=name,
-    )(at, *pieces, tid, emb)
+        input_output_aliases={13: 4},
+        compiler_params=params(),
+        cost_estimate=SMALL,
+        name="logits",
+    )(at, *pieces, tid, emb, later)
 
 
 def merge(parts):
@@ -205,7 +218,7 @@
     )(*parts)
 
 
-def finish_body(a, b, st, tid, mix, weight, feats, ep0, em0, pack, grad_mix):
+def finish_body(a, b, st, tid, mix, weight, ep0, em0, e1, pack, grad_mix, e1_out):
     top, total, hit = merge([a[...], b[...]])
     lse = top + jnp.log(total)
     gap = hit - lse
@@ -235,7 +248,13 @@
     return pl.pallas_call(
         finish_body,
         in_specs=[pl.BlockSpec(memory_space=pltpu.VMEM)] * 6 + [HBM] * 3,
-        out_shape=[jax.ShapeDtypeStruct((8, ROWS), F32), jax.ShapeDtypeStruct((4, 128), F32)],
+        out_specs=[pl.BlockSpec(memory_space=pltpu.VMEM)] * 2 + [HBM],
+        out_shape=[
+            jax.ShapeDtypeStruct((8, ROWS), F32),
+            jax.ShapeDtypeStruct((4, 128), F32),
+            jax.ShapeDtypeStruct((VOC - CUT, ROWS), BF),
+        ],
+        input_output_aliases={8: 2},
         compiler_params=params(),
         cost_estimate=SMALL,
         name="finish",
@@ -252,10 +271,10 @@
 def hidden_body(at, e0, e1, pack, w0, w1, w2, w3, keep, send0, send1, tgt_out, tg):
     @pl.when(pl.program_id(0) == 0)
     def _():
-        for t in range(TILES):
-            rows = pl.ds(t * TILE, TILE)
-            e = e0[...] if t == 0 else e1[pl.ds((t - 1) * TILE, TILE), :]
-            g = token_grad(e, pack, pack[pl.ds(t, 1), :], t * TILE)
+        for t in range(VOC // SUB):
+            rows = pl.ds(t * SUB, SUB)
+            e = e0[rows, :] if t * SUB < CUT else e1[pl.ds(t * SUB - CUT, SUB), :]
+            g = token_grad(e, pack, pack[pl.ds(t * SUB // TILE, 1), :], t * SUB)
             tgt_out[rows, :] = g
             tg[:, rows] = g.T
 
@@ -285,21 +304,21 @@
         grid_spec=pltpu.PrefetchScalarGridSpec(
             num_scalar_prefetch=1,
             grid=(4,),
-            in_specs=[whole((TILE, ROWS)), whole((VOC - TILE, ROWS)), whole((8, ROWS))] + [weight(k) for k in range(4)],
+            in_specs=[whole((CUT, ROWS)), whole((VOC - CUT, ROWS)), whole((8, ROWS))] + [weight(k) for k in range(4)],
             out_specs=[
                 pl.BlockSpec((1, 4, HALF, 256), lambda i, at: (i, 0, 0, 0)),
-                pl.BlockSpec((2, 1, HALF, 256), lambda i, at: (0, i, 0, 0)),
-                pl.BlockSpec((2, 1, HALF, 256), lambda i, at: (0, i, 0, 0)),
+            ]
+            + [pl.BlockSpec((2, 1, HALF, 256), lambda i, at: (0, i, 0, 0))] * 2
+            + [
                 whole((VOC, ROWS)),
             ],
             scratch_shapes=[pltpu.VMEM((ROWS, VOC), BF)],
         ),
         out_shape=[
             jax.ShapeDtypeStruct((4, 4, HALF, 256), F32),
-            jax.ShapeDtypeStruct((2, 4, HALF, 256), BF),
-            jax.ShapeDtypeStruct((2, 4, HALF, 256), BF),
-            jax.ShapeDtypeStruct((VOC, ROWS), BF),
-        ],
+        ]
+        + [jax.ShapeDtypeStruct((2, 4, HALF, 256), BF)] * 2
+        + [jax.ShapeDtypeStruct((VOC, ROWS), BF)],
         compiler_params=params(),
         cost_estimate=SMALL,
         name="hidden",
@@ -336,7 +355,8 @@
     return copies
 
 
-def embed_a_body(at, tgt, ep0, ep1, em0, em1, pack_p, pack_m, feats, acc, q, sem):
+def embed_a_body(at, tgt, *refs):
+    ep, em, (pack_p, pack_m, feats, acc, q, sem) = refs[:4], refs[4:8], refs[8:]
     i = pl.program_id(0)
 
     @pl.when(i == 0)
@@ -348,7 +368,7 @@
             copy.wait()
 
     parts = [tgt[...]]
-    for e, pack in ((pick(i, ep0, ep1), pack_p), (pick(i, em0, em1), pack_m)):
+    for e, pack in ((pick(i, *ep), pack_p), (pick(i, *em), pack_m)):
         parts.append(token_grad(e, pack, pack[pl.ds(i, 1), :], i * TILE))
     acc[...] = dot_nn(jnp.concatenate(parts, axis=1), q[...])
 
@@ -361,7 +381,7 @@
         grid_spec=pltpu.PrefetchScalarGridSpec(
             num_scalar_prefetch=1,
             grid=(TILES,),
-            in_specs=[tile, LOW, HIGH, LOW, HIGH, pack, pack, HBM],
+            in_specs=[tile, *sub_specs(), *sub_specs(), pack, pack, HBM],
             out_specs=pl.BlockSpec((TILE, 1024), lambda i, at: (i, 0)),
             scratch_shapes=[pltpu.VMEM((3 * ROWS, 1024), BF), pltpu.SemaphoreType.DMA((24,))],
         ),
@@ -369,10 +389,10 @@
         compiler_params=params(),
         cost_estimate=SMALL,
         name="embed_a",
-    )(at, tgt, ep0, ep1, em0, em1, pack_p, pack_m, feats)
-
-
-def embed_b_body(at, acc, ea, eb, ec, pack_d, feats, out, q, sem):
+    )(at, tgt, ep0, ep0, ep1, ep1, em0, em0, em1, em1, pack_p, pack_m, feats)
+
+
+def embed_b_body(at, acc, ea0, ea1, eb0, eb1, pack_d, feats, out, q, sem):
     i = pl.program_id(0)
 
     @pl.when(i == 0)
@@ -383,11 +403,11 @@
         for copy in copies:
             copy.wait()
 
-    g = token_grad(jnp.where(i == 0, ea[...], jnp.where(i == 1, eb[...], ec[...])), pack_d, pack_d[pl.ds(i, 1), :], i * TILE)
+    g = token_grad(pick(i, ea0, ea1, eb0, eb1), pack_d, pack_d[pl.ds(i, 1), :], i * TILE)
     out[...] = (acc[...] + dot_nn(g, q[...])).astype(BF)
 
 
-def embed_b_call(at, acc, ea, eb, ec, pack_d, feats):
+def embed_b_call(at, acc, ea, eb, pack_d, feats):
     tile = pl.BlockSpec((TILE, 1024), lambda i, at: (i, 0))
     return pl.pallas_call(
         embed_b_body,
@@ -396,9 +416,7 @@
             grid=(TILES,),
             in_specs=[
                 tile,
-                LOW,
-                LOW,
-                pl.BlockSpec((TILE, ROWS), lambda i, at: (jnp.maximum(i - 2, 0), 0)),
+                *sub_specs(),
                 pl.BlockSpec((8, ROWS), lambda i, at: (0, 0)),
                 HBM,
             ],
@@ -409,7 +427,7 @@
         compiler_params=params(),
         cost_estimate=SMALL,
         name="embed_b",
-    )(at, acc, ea, eb, ec, pack_d, feats)
+    )(at, acc, ea, ea, eb, eb, pack_d, feats)
 
 
 def local(comp_hidden, embed, mix, targets, weight):
@@ -427,21 +445,21 @@
     block = jnp.where(c == 0, jnp.concatenate([mine, got], axis=1), jnp.concatenate([got, mine], axis=1))
     pieces = gather_pieces(block)
     pieces = pieces + [sibling(p) for p in pieces]
+
+    e0, e1, st, loc, turned = logits_call(at, pieces, tid, embed, turned)
     feats = lax.all_gather(turned, ("x", "z", "c")).reshape(4, 4, 2, ROWS, 128)
-
-    e0, e1, st, loc = logits_call(at, pieces, tid, embed, "logits")
     ep0, em0 = shift(e0, "y", 1), shift(e0, "y", 3)
-    ep1, em1 = shift(e1, "y", 1), shift(e1, "y", 3)
 
     s = merge_call(loc, *(shift(loc, "x", d) for d in (1, 2, 3)))
     s = merge_call(s, *(shift(s, "z", d) for d in (1, 2, 3)))
-    pack, grad_mix = finish_call(s, sibling(s), st, tid, mix, weight.reshape(1, 128), feats, ep0, em0)
-    pack_p, pack_m, pack_d = shift(pack, "y", 1), shift(pack, "y", 3), shift(pack, "y", 2)
-
-    keep, send0, send1, tgt = hidden_call(at, e0, e1, pack, embed)
-    recv0, recv1, ep1, em1 = gate(sibling(send0), sibling(send1), ep1, em1)
-    diag = [shift(ep0, "y", 1), shift(ep1[:TILE], "y", 1), shift(em1[TILE:], "y", 3)]
-    grad_hidden = scatter(keep, (recv0, recv1), c)
+    pack, grad_mix, e1 = finish_call(s, sibling(s), st, tid, mix, weight.reshape(1, 128), ep0, em0, e1)
+    pack, pack_p, pack_m, pack_d, e1 = gate(pack, shift(pack, "y", 1), shift(pack, "y", 3), shift(pack, "y", 2), e1)
+    ep1, em1 = shift(e1, "y", 1), shift(e1, "y", 3)
+
+    keep, *send, tgt = hidden_call(at, e0, e1, pack, embed)
+    *recv, ep1, em1, feats = gate(*(sibling(t) for t in send), ep1, em1, feats)
+    diag = shift(ep0, "y", 1), shift(em1, "y", 3)
+    grad_hidden = scatter(keep, recv, c)
 
     acc = embed_a_call(at, tgt, ep0, ep1, em0, em1, pack_p, pack_m, feats)
     grad_embed = embed_b_call(at, acc, *diag, pack_d, feats)

time: 239 us -> 203 us (0.85)
  waiting for transfers between devices: 89.9 us -> 61.8 us
  starting transfers between devices: 54.7 us -> 46.2 us
    ppermute x16 -> x15, waiting for transfers between devices: 43.9 us -> 22.9 us  [shift(): return lax.ppermute(a, axis, [((i + d) % 4, i) for i in range(4)])]
    ppermute x14, waiting for transfers between devices: 39 us -> 31.1 us  [cross(): return lax.ppermute(a, ('x', 'z', 'c'), pairs)]
    ppermute x14, starting transfers between devices: 33.6 us -> 27 us  [cross(): return lax.ppermute(a, ('x', 'z', 'c'), pairs)]
    unnamed x56 -> x62, local copies, waits for them, and re-layouts: 5.35 us -> 7.69 us
    ppermute x16 -> x15, starting transfers between devices: 18.2 us -> 16.3 us  [shift(): return lax.ppermute(a, axis, [((i + d) % 4, i) for i in range(4)])]
  transfers between devices with their start and end apart: 42 -> 41, of which waited for: 21 -> 26; matrix products, arithmetic and copies ran while one was open for 3% -> 2% of each run, Pallas kernels for 26% -> 17%
where the time goes in v2:
time: 203 us; the launch traced here: 201 us
  Pallas kernels  63 us (31%)
  waiting for transfers between devices  61.8 us (30%)
  starting transfers between devices  46.2 us (23%)
  between operations  14.4 us (7%)
  local copies, waits for them, and re-layouts  10 us (5%)
  other arithmetic  5.94 us (3%)
    ppermute x14, waiting for transfers between devices, cross(): return lax.ppermute(a, ('x', 'z', 'c'), pairs)  31.1 us
    ppermute x14, starting transfers between devices, cross(): return lax.ppermute(a, ('x', 'z', 'c'), pairs)  27 us
    ppermute x15, waiting for transfers between devices, shift(): return lax.ppermute(a, axis, [((i + d) % 4, i) for i in range(4)])  22.9 us
    pallas_call x1, Pallas kernels, logits_call(): pl.pallas_call(logits_body, grid_spec=pltpu.PrefetchScalarGridSpec(num_sc...  17.9 us
    pallas_call x1, Pallas kernels, hidden_call(): pl.pallas_call(hidden_body, grid_spec=pltpu.PrefetchScalarGridSpec(num_sc...  16.9 us
    ppermute x15, starting transfers between devices, shift(): return lax.ppermute(a, axis, [((i + d) % 4, i) for i in range(4)])  16.3 us
    pallas_call x1, Pallas kernels, embed_a_call(): pl.pallas_call(embed_a_body, grid_spec=pltpu.PrefetchScalarGridSpec(num_s...  13.8 us
    pallas_call x1, Pallas kernels, embed_b_call(): pl.pallas_call(embed_b_body, grid_spec=pltpu.PrefetchScalarGridSpec(num_s...  10.2 us
  transfers between devices with their start and end apart: 41, of which 26 were waited for; matrix products, arithmetic and copies ran while one was open for 2% of the time, Pallas kernels for 17%

profile of v2, /device:TPU:0, one launch (start us, length us, event | category | flops | bytes accessed | tf_op | source)
XLA Modules:
  0.0 201.3 jit_solution(4256891863249002827)
XLA Ops:
  7.2 0.9 broadcast_select_fusion.1
  8.2 1.2 collective-permute-done
  9.5 1.6 collective-permute-start.3
  11.1 1.7 collective-permute-start.1
  12.8 1.9 collective-permute-start.2
  14.7 1.0 collective-permute-done.3
  16.1 3.2 %collective-permute-done.2 = bf16[256,256]{1,0:T(8,128)(2,1)S(1)} collective-permute-done((bf16[256,256]{1,0:T(8,128)(2,1)S(1)}, bf16[256,256]{1,0:T(8,128)(2,1)S(1)}, u32[]{:S(2)}, u32[]{:S(2)}) %collective-permute-start.2) | collective-permute-done | bytes 131104 | tf_op jit(solution)/shard_map/ppermute | solution.py:36
  19.4 4.2 %collective-permute-start.4 = (bf16[4,256,256]{2,1,0:T(8,128)(2,1)S(1)}, bf16[4,256,256]{2,1,0:T(8,128)(2,1)S(1)}, u32[]{:S(2)}, u32[]{:S(2)}) collective-permute-start(bf16[4,256,256]{2,1,0:T(8,128)(2,1)S(1)} %pad_maximum_fusion.refs_0_), channel_id=1, source_target_pairs={{8,0},{36,4},{16,8},{44,12},{24,16},{52,20},{0,24},{60,28},{40,32}... | collective-permute-start | bytes 1572872 | tf_op jit(solution)/shard_map/ppermute | solution.py:36
  23.5 1.6 collective-permute-start.13
  25.1 5.1 %collective-permute-done.4.refs_1_ = bf16[4,256,256]{2,1,0:T(8,128)(2,1)S(1)} collective-permute-done((bf16[4,256,256]{2,1,0:T(8,128)(2,1)S(1)}, bf16[4,256,256]{2,1,0:T(8,128)(2,1)S(1)}, u32[]{:S(2)}, u32[]{:S(2)}) %collective-permute-start.4) | collective-permute-done | bytes 524320 | tf_op jit(solution)/shard_map/ppermute | solution.py:36
  30.2 0.8 slice.105
  31.0 3.7 %collective-permute-start.6 = (bf16[2,256,256]{2,1,0:T(8,128)(2,1)}, bf16[2,256,256]{2,1,0:T(8,128)(2,1)S(1)}, u32[]{:S(2)}, u32[]{:S(2)}) collective-permute-start(bf16[2,256,256]{2,1,0:T(8,128)(2,1)} %slice.105), channel_id=1, source_target_pairs={{8,0},{36,4},{16,8},{44,12},{24,16},{52,20},{0,24},{60,28},{40,32}... | collective-permute-start | bytes 786440 | tf_op jit(solution)/shard_map/ppermute | solution.py:36
  34.7 0.8 slice.106
  36.1 2.8 %collective-permute-done.6.refs_3_ = bf16[2,256,256]{2,1,0:T(8,128)(2,1)S(1)} collective-permute-done((bf16[2,256,256]{2,1,0:T(8,128)(2,1)}, bf16[2,256,256]{2,1,0:T(8,128)(2,1)S(1)}, u32[]{:S(2)}, u32[]{:S(2)}) %collective-permute-start.6) | collective-permute-done | bytes 262176 | tf_op jit(solution)/shard_map/ppermute | solution.py:36
  38.9 4.5 %collective-permute-done.7.refs_4_ = bf16[2,256,256]{2,1,0:T(8,128)(2,1)} collective-permute-done((bf16[2,256,256]{2,1,0:T(8,128)(2,1)}, bf16[2,256,256]{2,1,0:T(8,128)(2,1)}, u32[]{:S(2)}, u32[]{:S(2)}) %collective-permute-start.7) | collective-permute-done | bytes 262176 | tf_op jit(solution)/shard_map/ppermute | solution.py:36
  43.4 0.6 pad_add_fusion.at
  44.1 1.2 collective-permute-done.12.refs_9_
  45.3 0.7 tile.2
  46.3 17.9 %logits.1 = (bf16[768,512]{1,0:T(8,128)(2,1)}, bf16[1280,512]{1,0:T(8,128)(2,1)}, f32[8,512]{1,0:T(8,128)}, f32[8,512]{1,0:T(8,128)}, bf16[512,128]{1,0:T(8,128)(2,1)}) custom-call(s32[4]{0:T(128)} %pad_add_fusion.at, bf16[4,256,256]{2,1,0:T(8,128)(2,1)} %copy-done.12, bf16[4,256,256]{2,1,0:T(8,128)(2,1)} %copy-done.13, ...), custom_call_target="tpu_custom_call", output_to_operand_aliasing={{4}: (13, {})} | custom-call | flops 1000 | bytes 1000 | tf_op jit(solution)/shard_map/logits/pallas_call | solution.py:165
  64.2 3.1 %collective-permute-start.21 = (bf16[768,512]{1,0:T(8,128)(2,1)}, bf16[768,512]{1,0:T(8,128)(2,1)S(1)}, u32[]{:S(2)}, u32[]{:S(2)}) collective-permute-start(bf16[768,512]{1,0:T(8,128)(2,1)} %get-tuple-element.25.e0), channel_id=1, source_target_pairs={{1,0},{2,1},{3,2},{0,3},{5,4},{6,5},{7,6},{4,7},{9,8},{10,9},{11,1... | collective-permute-start | bytes 2359304 | tf_op jit(solution)/shard_map/ppermute | solution.py:21
  67.3 1.5 collective-permute-start.14
  68.8 0.8 collective-permute-start.15
  69.6 0.9 collective-permute-start.16
  70.5 0.7 collective-permute-done.14.refs_1_
  71.2 3.0 %collective-permute-done.15.refs_2_ = f32[8,512]{1,0:T(8,128)S(1)} collective-permute-done((f32[8,512]{1,0:T(8,128)}, f32[8,512]{1,0:T(8,128)S(1)}, u32[]{:S(2)}, u32[]{:S(2)}) %collective-permute-start.15) | collective-permute-done | bytes 16416 | tf_op jit(solution)/shard_map/ppermute | solution.py:21
  74.9 0.6 copy-done.28
  75.5 1.4 merge.2.refs_0_
  76.9 0.9 collective-permute-start.18
  77.8 1.1 collective-permute-start.19
  78.9 1.9 collective-permute-done.17.refs_1_
  80.8 1.5 collective-permute-done.18.refs_2_
  82.3 1.2 collective-permute-done.19.refs_3_
  83.5 0.6 copy-done.29
  84.1 1.4 merge.3.a
  85.5 1.4 collective-permute-done.20.b
  86.9 1.1 collective-permute-done.22.em0.refs_4_.refs_5_
  88.0 0.9 copy-done.5
  88.9 1.4 finish.1
  90.3 2.6 %collective-permute-start.23 = (f32[8,512]{1,0:T(8,128)}, f32[8,512]{1,0:T(8,128)S(1)}, u32[]{:S(2)}, u32[]{:S(2)}) collective-permute-start(f32[8,512]{1,0:T(8,128)} %get-tuple-element.29.refs_0_), channel_id=1, source_target_pairs={{1,0},{2,1},{3,2},{0,3},{5,4},{6,5},{7,6},{4,7},{9,8},{10,9},{11,1... | collective-permute-start | bytes 49160 | tf_op jit(solution)/shard_map/ppermute | solution.py:21
  92.8 1.5 collective-permute-start.25
  94.5 3.5 %collective-permute-done.24.refs_2_ = f32[8,512]{1,0:T(8,128)S(1)} collective-permute-done((f32[8,512]{1,0:T(8,128)}, f32[8,512]{1,0:T(8,128)S(1)}, u32[]{:S(2)}, u32[]{:S(2)}) %collective-permute-start.24) | collective-permute-done | bytes 16416 | tf_op jit(solution)/shard_map/ppermute | solution.py:21
  98.9 3.2 %collective-permute-start.28 = (bf16[1280,512]{1,0:T(8,128)(2,1)}, bf16[1280,512]{1,0:T(8,128)(2,1)S(1)}, u32[]{:S(2)}, u32[]{:S(2)}) collective-permute-start(bf16[1280,512]{1,0:T(8,128)(2,1)} %get-tuple-element.31.e1), channel_id=1, source_target_pairs={{1,0},{2,1},{3,2},{0,3},{5,4},{6,5},{7,6},{4,7},{9,8},{10,9},{11,1... | collective-permute-start | bytes 3932168 | tf_op jit(solution)/shard_map/ppermute | solution.py:21
  102.1 16.9 %hidden.1 = (f32[4,4,256,256]{3,2,1,0:T(8,128)}, bf16[2,4,256,256]{3,2,1,0:T(8,128)(2,1)}, bf16[2,4,256,256]{3,2,1,0:T(8,128)(2,1)}, bf16[2048,512]{1,0:T(8,128)(2,1)}) custom-call(s32[4]{0:T(128)} %pad_add_fusion.at, bf16[768,512]{1,0:T(8,128)(2,1)} %get-tuple-element.25.e0, bf16[1280,512]{1,0:T(8,128)(2,1)} %get-tuple-element.31.e1, ...), custom_call_target="tpu_custom_call" | custom-call | flops 1000 | bytes 1000 | tf_op jit(solution)/shard_map/hidden/pallas_call | solution.py:302
  119.6 2.4 %collective-permute-done.26.refs_0_ = bf16[2,4,256,256]{3,2,1,0:T(8,128)(2,1)S(1)} collective-permute-done((bf16[2,4,256,256]{3,2,1,0:T(8,128)(2,1)}, bf16[2,4,256,256]{3,2,1,0:T(8,128)(2,1)S(1)}, u32[]{:S(2)}, u32[]{:S(2)}) %collective-permute-start.26) | collective-permute-done | bytes 1048608 | tf_op jit(solution)/shard_map/ppermute | solution.py:25
  122.0 1.5 collective-permute-done.27.refs_1_
  123.5 5.7 %collective-permute-done.28.refs_2_ = bf16[1280,512]{1,0:T(8,128)(2,1)S(1)} collective-permute-done((bf16[1280,512]{1,0:T(8,128)(2,1)}, bf16[1280,512]{1,0:T(8,128)(2,1)S(1)}, u32[]{:S(2)}, u32[]{:S(2)}) %collective-permute-start.28) | collective-permute-done | bytes 1310752 | tf_op jit(solution)/shard_map/ppermute | solution.py:21
  129.2 3.3 %collective-permute-done.29.refs_3_ = bf16[1280,512]{1,0:T(8,128)(2,1)S(1)} collective-permute-done((bf16[1280,512]{1,0:T(8,128)(2,1)}, bf16[1280,512]{1,0:T(8,128)(2,1)S(1)}, u32[]{:S(2)}, u32[]{:S(2)}) %collective-permute-start.29) | collective-permute-done | bytes 1310752 | tf_op jit(solution)/shard_map/ppermute | solution.py:21
  132.5 1.1 copy-done.1
  133.5 2.2 %copy-done.10 = f32[4,4,256,256]{3,2,1,0:T(8,128)S(1)} copy-done((f32[4,4,256,256]{3,2,1,0:T(8,128)S(1)}, f32[4,4,256,256]{3,2,1,0:T(8,128)}, u32[]{:S(2)}) %copy-start.10) | copy-done | bytes 4194328
  135.7 1.7 fusion.1
  137.5 0.7 collective-permute-start.30
  138.3 2.6 %collective-permute-start.32 = (bf16[4,128,256]{2,1,0:T(8,128)(2,1)S(1)}, bf16[4,128,256]{2,1,0:T(8,128)(2,1)S(1)}, u32[]{:S(2)}, u32[]{:S(2)}) collective-permute-start(bf16[4,128,256]{2,1,0:T(8,128)(2,1)S(1)} %get-tuple-element.56), channel_id=1, source_target_pairs={{32,0},{12,4},{40,8},{20,12},{48,16},{28,20},{56,24},{4,28},{64,32... | collective-permute-start | bytes 786440 | tf_op jit(solution)/shard_map/ppermute | solution.py:36
  141.0 4.2 %collective-permute-done.30 = bf16[4,128,256]{2,1,0:T(8,128)(2,1)S(1)} collective-permute-done((bf16[4,128,256]{2,1,0:T(8,128)(2,1)S(1)}, bf16[4,128,256]{2,1,0:T(8,128)(2,1)S(1)}, u32[]{:S(2)}, u32[]{:S(2)}) %collective-permute-start.30) | collective-permute-done | bytes 262176 | tf_op jit(solution)/shard_map/ppermute | solution.py:36
  145.5 3.3 %collective-permute-start.33 = (bf16[4,256,256]{2,1,0:T(8,128)(2,1)S(1)}, bf16[4,256,256]{2,1,0:T(8,128)(2,1)S(1)}, u32[]{:S(2)}, u32[]{:S(2)}) collective-permute-start(bf16[4,256,256]{2,1,0:T(8,128)(2,1)S(1)} %pad_maximum_fusion.2), channel_id=1, source_target_pairs={{32,0},{12,4},{40,8},{20,12},{48,16},{28,20},{56,24},{4,28},{64,32... | collective-permute-start | bytes 1572872 | tf_op jit(solution)/shard_map/ppermute | solution.py:36
  148.8 6.9 %collective-permute-done.31 = bf16[4,256,256]{2,1,0:T(8,128)(2,1)S(1)} collective-permute-done((bf16[4,256,256]{2,1,0:T(8,128)(2,1)S(1)}, bf16[4,256,256]{2,1,0:T(8,128)(2,1)S(1)}, u32[]{:S(2)}, u32[]{:S(2)}) %collective-permute-start.31) | collective-permute-done | bytes 524320 | tf_op jit(solution)/shard_map/ppermute | solution.py:36
  155.7 1.5 fusion.7
  157.3 4.4 %collective-permute-start.34 = (bf16[256,256]{1,0:T(8,128)(2,1)S(1)}, bf16[256,256]{1,0:T(8,128)(2,1)S(1)}, u32[]{:S(2)}, u32[]{:S(2)}) collective-permute-start(bf16[256,256]{1,0:T(8,128)(2,1)S(1)} %get-tuple-element.52), channel_id=1, source_target_pairs={{24,0},{100,4},{0,8},{108,12},{8,16},{116,20},{16,24},{124,28},{56... | collective-permute-start | bytes 393224 | tf_op jit(solution)/shard_map/ppermute | solution.py:36
  161.7 2.8 %collective-permute-start.36 = (bf16[256,256]{1,0:T(8,128)(2,1)S(1)}, bf16[256,256]{1,0:T(8,128)(2,1)S(1)}, u32[]{:S(2)}, u32[]{:S(2)}) collective-permute-start(bf16[256,256]{1,0:T(8,128)(2,1)S(1)} %get-tuple-element.53), channel_id=1, source_target_pairs={{8,0},{36,4},{16,8},{44,12},{24,16},{52,20},{0,24},{60,28},{40,32}... | collective-permute-start | bytes 393224 | tf_op jit(solution)/shard_map/ppermute | solution.py:36
  164.4 0.7 collective-permute-start.38
  165.1 3.0 %collective-permute-done.35 = bf16[256,256]{1,0:T(8,128)(2,1)S(1)} collective-permute-done((bf16[256,256]{1,0:T(8,128)(2,1)S(1)}, bf16[256,256]{1,0:T(8,128)(2,1)S(1)}, u32[]{:S(2)}, u32[]{:S(2)}) %collective-permute-start.35) | collective-permute-done | bytes 131104 | tf_op jit(solution)/shard_map/ppermute | solution.py:36
  168.3 13.8 %embed_a.1.acc = f32[2048,1024]{1,0:T(8,128)} custom-call(s32[4]{0:T(128)} %pad_add_fusion.at, bf16[2048,512]{1,0:T(8,128)(2,1)} %get-tuple-element.39.tgt, bf16[768,512]{1,0:T(8,128)(2,1)} %copy-done.3, bf16[768,512]{1,0:T(8,128)(2,1)} %copy-done.3, bf16[1280,512]{1,0:T(8,128)(2,1)} %get-tuple-element.40.refs_2_.refs_3_, ...), custom_call_target="tpu_custom_call" | custom-call | flops 1000 | bytes 1000 | tf_op jit(solution)/shard_map/embed_a/pallas_call | solution.py:379
  182.2 0.7 maximum_select_fusion
  182.9 0.9 copy-done.11
  184.2 10.2 %embed_b.1 = bf16[2048,1024]{1,0:T(8,128)(2,1)} custom-call(s32[4]{0:T(128)} %pad_add_fusion.at, f32[2048,1024]{1,0:T(8,128)} %embed_a.1.acc, bf16[768,512]{1,0:T(8,128)(2,1)} %copy-done.11, bf16[768,512]{1,0:T(8,128)(2,1)} %copy-done.11, bf16[1280,512]{1,0:T(8,128)(2,1)} %copy-done.6, bf16[1280,512]{1,0:T(8,128)(2,1)} %copy-done.6, ...), custom_call_target="tpu_custom_call" | custom-call | flops 1000 | bytes 1000 | tf_op jit(solution)/shard_map/embed_b/pallas_call | solution.py:412
  (112 shorter events, 5.0 us)
Async XLA Ops:
  7.2 36.9 %copy-start.30 = (s32[128]{0:T(128)S(1)}, s32[128]{0:T(128)}, u32[]{:S(2)}) copy-start(s32[128]{0:T(128)} %param.8) | copy-start | bytes 1540
  7.2 125.3 %all-gather.3.cloned.1.call-start = ((), (), s32[]{:S(2)}) async-start(), calls=%async_computation | async-start | bytes 4325376 | tf_op jit(solution)/shard_map/all_gather | solution.py:450
  8.1 1.3 collective-permute-start
  9.5 6.2 %collective-permute-start.3 = (bf16[256,256]{1,0:T(8,128)(2,1)S(1)}, bf16[256,256]{1,0:T(8,128)(2,1)S(1)}, u32[]{:S(2)}, u32[]{:S(2)}) collective-permute-start(bf16[256,256]{1,0:T(8,128)(2,1)S(1)} %maximum_select_fusion.2), channel_id=1, source_target_pairs={{96,0},{28,4},{104,8},{4,12},{112,16},{12,20},{120,24},{20,28},{0,... | collective-permute-start | bytes 393224 | tf_op jit(solution)/shard_map/ppermute | solution.py:36
  11.1 5.0 %collective-permute-start.1 = (bf16[256,256]{1,0:T(8,128)(2,1)S(1)}, bf16[256,256]{1,0:T(8,128)(2,1)S(1)}, u32[]{:S(2)}, u32[]{:S(2)}) collective-permute-start(bf16[256,256]{1,0:T(8,128)(2,1)S(1)} %maximum_select_fusion.2), channel_id=1, source_target_pairs={{32,0},{12,4},{40,8},{20,12},{48,16},{28,20},{56,24},{4,28},{64,32... | collective-permute-start | bytes 393224 | tf_op jit(solution)/shard_map/ppermute | solution.py:36
  12.8 6.5 %collective-permute-start.2 = (bf16[256,256]{1,0:T(8,128)(2,1)S(1)}, bf16[256,256]{1,0:T(8,128)(2,1)S(1)}, u32[]{:S(2)}, u32[]{:S(2)}) collective-permute-start(bf16[256,256]{1,0:T(8,128)(2,1)S(1)} %maximum_select_fusion.2), channel_id=1, source_target_pairs={{64,0},{20,4},{72,8},{28,12},{80,16},{4,20},{88,24},{12,28},{96,32... | collective-permute-start | bytes 393224 | tf_op jit(solution)/shard_map/ppermute | solution.py:36
  19.3 26.6 %copy-start.12 = (bf16[4,256,256]{2,1,0:T(8,128)(2,1)}, bf16[4,256,256]{2,1,0:T(8,128)(2,1)S(1)}, u32[]{:S(2)}) copy-start(bf16[4,256,256]{2,1,0:T(8,128)(2,1)S(1)} %pad_maximum_fusion.refs_0_) | copy-start | bytes 1572868
  19.4 10.9 %collective-permute-start.4 = (bf16[4,256,256]{2,1,0:T(8,128)(2,1)S(1)}, bf16[4,256,256]{2,1,0:T(8,128)(2,1)S(1)}, u32[]{:S(2)}, u32[]{:S(2)}) collective-permute-start(bf16[4,256,256]{2,1,0:T(8,128)(2,1)S(1)} %pad_maximum_fusion.refs_0_), channel_id=1, source_target_pairs={{8,0},{36,4},{16,8},{44,12},{24,16},{52,20},{0,24},{60,28},{40,32}... | collective-permute-start | bytes 1572872 | tf_op jit(solution)/shard_map/ppermute | solution.py:36
  23.5 11.2 %collective-permute-start.5 = (bf16[4,256,256]{2,1,0:T(8,128)(2,1)S(1)}, bf16[4,256,256]{2,1,0:T(8,128)(2,1)S(1)}, u32[]{:S(2)}, u32[]{:S(2)}) collective-permute-start(bf16[4,256,256]{2,1,0:T(8,128)(2,1)S(1)} %pad_maximum_fusion.refs_0_), channel_id=1, source_target_pairs={{24,0},{100,4},{0,8},{108,12},{8,16},{116,20},{16,24},{124,28},{56... | collective-permute-start | bytes 1572872 | tf_op jit(solution)/shard_map/ppermute | solution.py:36
  23.5 12.5 %collective-permute-start.13 = (bf16[512,128]{1,0:T(8,128)(2,1)}, bf16[512,128]{1,0:T(8,128)(2,1)S(1)}, u32[]{:S(2)}, u32[]{:S(2)}) collective-permute-start(bf16[512,128]{1,0:T(8,128)(2,1)} %bitcast.46), channel_id=1, source_target_pairs={{0,0},{1,32},{2,64},{3,96},{32,1},{33,33},{34,65},{35,97},{64,2},{... | collective-permute-start | bytes 393224 | tf_op jit(solution)/shard_map/ppermute | solution.py:440
  30.2 15.7 %copy-start.13 = (bf16[4,256,256]{2,1,0:T(8,128)(2,1)}, bf16[4,256,256]{2,1,0:T(8,128)(2,1)S(1)}, u32[]{:S(2)}) copy-start(bf16[4,256,256]{2,1,0:T(8,128)(2,1)S(1)} %collective-permute-done.4.refs_1_) | copy-start | bytes 1572868
  31.0 7.9 %collective-permute-start.6 = (bf16[2,256,256]{2,1,0:T(8,128)(2,1)}, bf16[2,256,256]{2,1,0:T(8,128)(2,1)S(1)}, u32[]{:S(2)}, u32[]{:S(2)}) collective-permute-start(bf16[2,256,256]{2,1,0:T(8,128)(2,1)} %slice.105), channel_id=1, source_target_pairs={{8,0},{36,4},{16,8},{44,12},{24,16},{52,20},{0,24},{60,28},{40,32}... | collective-permute-start | bytes 786440 | tf_op jit(solution)/shard_map/ppermute | solution.py:36
  34.7 11.3 %copy-start.14 = (bf16[4,256,256]{2,1,0:T(8,128)(2,1)}, bf16[4,256,256]{2,1,0:T(8,128)(2,1)S(1)}, u32[]{:S(2)}) copy-start(bf16[4,256,256]{2,1,0:T(8,128)(2,1)S(1)} %collective-permute-done.5.refs_2_) | copy-start | bytes 1572868
  35.5 7.9 %collective-permute-start.7 = (bf16[2,256,256]{2,1,0:T(8,128)(2,1)}, bf16[2,256,256]{2,1,0:T(8,128)(2,1)}, u32[]{:S(2)}, u32[]{:S(2)}) collective-permute-start(bf16[2,256,256]{2,1,0:T(8,128)(2,1)} %slice.106), channel_id=1, source_target_pairs={{24,0},{100,4},{0,8},{108,12},{8,16},{116,20},{16,24},{124,28},{56... | collective-permute-start | bytes 786440 | tf_op jit(solution)/shard_map/ppermute | solution.py:36
  35.5 8.5 %collective-permute-start.8 = (bf16[4,256,256]{2,1,0:T(8,128)(2,1)S(1)}, bf16[4,256,256]{2,1,0:T(8,128)(2,1)S(1)}, u32[]{:S(2)}, u32[]{:S(2)}) collective-permute-start(bf16[4,256,256]{2,1,0:T(8,128)(2,1)S(1)} %pad_maximum_fusion.refs_0_), channel_id=1, source_target_pairs={{0,4},{4,0},{1,5},{5,1},{2,6},{6,2},{3,7},{7,3},{8,12},{12,8},{9,1... | collective-permute-start | bytes 1572872 | tf_op jit(solution)/shard_map/ppermute | solution.py:25
  35.5 9.8 %collective-permute-start.10 = (bf16[4,256,256]{2,1,0:T(8,128)(2,1)S(1)}, bf16[4,256,256]{2,1,0:T(8,128)(2,1)S(1)}, u32[]{:S(2)}, u32[]{:S(2)}) collective-permute-start(bf16[4,256,256]{2,1,0:T(8,128)(2,1)S(1)} %collective-permute-done.5.refs_2_), channel_id=1, source_target_pairs={{0,4},{4,0},{1,5},{5,1},{2,6},{6,2},{3,7},{7,3},{8,12},{12,8},{9,1... | collective-permute-start | bytes 1572872 | tf_op jit(solution)/shard_map/ppermute | solution.py:25
  36.0 9.9 %copy-start.15 = (bf16[512,128]{1,0:T(8,128)(2,1)}, bf16[512,128]{1,0:T(8,128)(2,1)S(1)}, u32[]{:S(2)}) copy-start(bf16[512,128]{1,0:T(8,128)(2,1)S(1)} %collective-permute-done.13.refs_12_) | copy-start | bytes 393220
  36.0 9.3 %collective-permute-start.9 = (bf16[4,256,256]{2,1,0:T(8,128)(2,1)S(1)}, bf16[4,256,256]{2,1,0:T(8,128)(2,1)S(1)}, u32[]{:S(2)}, u32[]{:S(2)}) collective-permute-start(bf16[4,256,256]{2,1,0:T(8,128)(2,1)S(1)} %collective-permute-done.4.refs_1_), channel_id=1, source_target_pairs={{0,4},{4,0},{1,5},{5,1},{2,6},{6,2},{3,7},{7,3},{8,12},{12,8},{9,1... | collective-permute-start | bytes 1572872 | tf_op jit(solution)/shard_map/ppermute | solution.py:25
  38.9 7.1 %copy-start.19 = (bf16[2,256,256]{2,1,0:T(8,128)(2,1)}, bf16[2,256,256]{2,1,0:T(8,128)(2,1)S(1)}, u32[]{:S(2)}) copy-start(bf16[2,256,256]{2,1,0:T(8,128)(2,1)S(1)} %collective-permute-done.6.refs_3_) | copy-start | bytes 786436
  38.9 5.2 %collective-permute-start.11 = (bf16[2,256,256]{2,1,0:T(8,128)(2,1)S(1)}, bf16[2,256,256]{2,1,0:T(8,128)(2,1)}, u32[]{:S(2)}, u32[]{:S(2)}) collective-permute-start(bf16[2,256,256]{2,1,0:T(8,128)(2,1)S(1)} %collective-permute-done.6.refs_3_), channel_id=1, source_target_pairs={{0,4},{4,0},{1,5},{5,1},{2,6},{6,2},{3,7},{7,3},{8,12},{12,8},{9,1... | collective-permute-start | bytes 786440 | tf_op jit(solution)/shard_map/ppermute | solution.py:25
  43.4 1.9 collective-permute-start.12
  44.1 1.9 copy-start.16
  45.3 1.0 copy-start.18
  64.2 22.8 %collective-permute-start.21 = (bf16[768,512]{1,0:T(8,128)(2,1)}, bf16[768,512]{1,0:T(8,128)(2,1)S(1)}, u32[]{:S(2)}, u32[]{:S(2)}) collective-permute-start(bf16[768,512]{1,0:T(8,128)(2,1)} %get-tuple-element.25.e0), channel_id=1, source_target_pairs={{1,0},{2,1},{3,2},{0,3},{5,4},{6,5},{7,6},{4,7},{9,8},{10,9},{11,1... | collective-permute-start | bytes 2359304 | tf_op jit(solution)/shard_map/ppermute | solution.py:21
  67.3 20.7 %collective-permute-start.22 = (bf16[768,512]{1,0:T(8,128)(2,1)}, bf16[768,512]{1,0:T(8,128)(2,1)S(1)}, u32[]{:S(2)}, u32[]{:S(2)}) collective-permute-start(bf16[768,512]{1,0:T(8,128)(2,1)} %get-tuple-element.25.e0), channel_id=1, source_target_pairs={{3,0},{0,1},{1,2},{2,3},{7,4},{4,5},{5,6},{6,7},{11,8},{8,9},{9,10... | collective-permute-start | bytes 2359304 | tf_op jit(solution)/shard_map/ppermute | solution.py:21
  67.3 3.9 %collective-permute-start.14 = (f32[8,512]{1,0:T(8,128)}, f32[8,512]{1,0:T(8,128)S(1)}, u32[]{:S(2)}, u32[]{:S(2)}) collective-permute-start(f32[8,512]{1,0:T(8,128)} %get-tuple-element.26.refs_0_), channel_id=1, source_target_pairs={{32,0},{64,32},{96,64},{0,96},{33,1},{65,33},{97,65},{1,97},{34,2}... | collective-permute-start | bytes 49160 | tf_op jit(solution)/shard_map/ppermute | solution.py:21
  68.8 5.5 %collective-permute-start.15 = (f32[8,512]{1,0:T(8,128)}, f32[8,512]{1,0:T(8,128)S(1)}, u32[]{:S(2)}, u32[]{:S(2)}) collective-permute-start(f32[8,512]{1,0:T(8,128)} %get-tuple-element.26.refs_0_), channel_id=1, source_target_pairs={{64,0},{96,32},{0,64},{32,96},{65,1},{97,33},{1,65},{33,97},{66,2}... | collective-permute-start | bytes 49160 | tf_op jit(solution)/shard_map/ppermute | solution.py:21
  69.6 5.2 %collective-permute-start.16 = (f32[8,512]{1,0:T(8,128)}, f32[8,512]{1,0:T(8,128)S(1)}, u32[]{:S(2)}, u32[]{:S(2)}) collective-permute-start(f32[8,512]{1,0:T(8,128)} %get-tuple-element.26.refs_0_), channel_id=1, source_target_pairs={{96,0},{0,32},{32,64},{64,96},{97,1},{1,33},{33,65},{65,97},{98,2}... | collective-permute-start | bytes 49160 | tf_op jit(solution)/shard_map/ppermute | solution.py:21
  71.2 3.6 %copy-start.24 = (f32[8,512]{1,0:T(8,128)}, f32[8,512]{1,0:T(8,128)S(1)}, u32[]{:S(2)}) copy-start(f32[8,512]{1,0:T(8,128)S(1)} %collective-permute-done.14.refs_1_) | copy-start | bytes 49156
  76.9 3.9 %collective-permute-start.17 = (f32[8,512]{1,0:T(8,128)}, f32[8,512]{1,0:T(8,128)S(1)}, u32[]{:S(2)}, u32[]{:S(2)}) collective-permute-start(f32[8,512]{1,0:T(8,128)} %merge.2.refs_0_), channel_id=1, source_target_pairs={{8,0},{16,8},{24,16},{0,24},{9,1},{17,9},{25,17},{1,25},{10,2},{18... | collective-permute-start | bytes 49160 | tf_op jit(solution)/shard_map/ppermute | solution.py:21
  76.9 5.5 %collective-permute-start.18 = (f32[8,512]{1,0:T(8,128)}, f32[8,512]{1,0:T(8,128)S(1)}, u32[]{:S(2)}, u32[]{:S(2)}) collective-permute-start(f32[8,512]{1,0:T(8,128)} %merge.2.refs_0_), channel_id=1, source_target_pairs={{16,0},{24,8},{0,16},{8,24},{17,1},{25,9},{1,17},{9,25},{18,2},{26... | collective-permute-start | bytes 49160 | tf_op jit(solution)/shard_map/ppermute | solution.py:21
  77.8 5.8 %collective-permute-start.19 = (f32[8,512]{1,0:T(8,128)}, f32[8,512]{1,0:T(8,128)S(1)}, u32[]{:S(2)}, u32[]{:S(2)}) collective-permute-start(f32[8,512]{1,0:T(8,128)} %merge.2.refs_0_), channel_id=1, source_target_pairs={{24,0},{0,8},{8,16},{16,24},{25,1},{1,9},{9,17},{17,25},{26,2},{2,... | collective-permute-start | bytes 49160 | tf_op jit(solution)/shard_map/ppermute | solution.py:21
  80.8 2.7 %copy-start.25 = (f32[8,512]{1,0:T(8,128)}, f32[8,512]{1,0:T(8,128)S(1)}, u32[]{:S(2)}) copy-start(f32[8,512]{1,0:T(8,128)S(1)} %collective-permute-done.17.refs_1_) | copy-start | bytes 49156
  82.3 1.2 copy-start.27
  85.5 1.4 collective-permute-start.20
  86.9 1.1 copy-start.23
  86.9 1.1 copy-start.3
  90.3 4.2 %collective-permute-start.23 = (f32[8,512]{1,0:T(8,128)}, f32[8,512]{1,0:T(8,128)S(1)}, u32[]{:S(2)}, u32[]{:S(2)}) collective-permute-start(f32[8,512]{1,0:T(8,128)} %get-tuple-element.29.refs_0_), channel_id=1, source_target_pairs={{1,0},{2,1},{3,2},{0,3},{5,4},{6,5},{7,6},{4,7},{9,8},{10,9},{11,1... | collective-permute-start | bytes 49160 | tf_op jit(solution)/shard_map/ppermute | solution.py:21
  92.8 5.2 %collective-permute-start.24 = (f32[8,512]{1,0:T(8,128)}, f32[8,512]{1,0:T(8,128)S(1)}, u32[]{:S(2)}, u32[]{:S(2)}) collective-permute-start(f32[8,512]{1,0:T(8,128)} %get-tuple-element.29.refs_0_), channel_id=1, source_target_pairs={{3,0},{0,1},{1,2},{2,3},{7,4},{4,5},{5,6},{6,7},{11,8},{8,9},{9,10... | collective-permute-start | bytes 49160 | tf_op jit(solution)/shard_map/ppermute | solution.py:21
  92.8 5.5 %collective-permute-start.25 = (f32[8,512]{1,0:T(8,128)}, f32[8,512]{1,0:T(8,128)S(1)}, u32[]{:S(2)}, u32[]{:S(2)}) collective-permute-start(f32[8,512]{1,0:T(8,128)} %get-tuple-element.29.refs_0_), channel_id=1, source_target_pairs={{2,0},{3,1},{0,2},{1,3},{6,4},{7,5},{4,6},{5,7},{10,8},{11,9},{8,1... | collective-permute-start | bytes 49160 | tf_op jit(solution)/shard_map/ppermute | solution.py:21
  94.5 3.8 %copy-start.20 = (f32[8,512]{1,0:T(8,128)}, f32[8,512]{1,0:T(8,128)S(1)}, u32[]{:S(2)}) copy-start(f32[8,512]{1,0:T(8,128)S(1)} %collective-permute-done.23.refs_1_) | copy-start | bytes 49156
  98.9 30.3 %collective-permute-start.28 = (bf16[1280,512]{1,0:T(8,128)(2,1)}, bf16[1280,512]{1,0:T(8,128)(2,1)S(1)}, u32[]{:S(2)}, u32[]{:S(2)}) collective-permute-start(bf16[1280,512]{1,0:T(8,128)(2,1)} %get-tuple-element.31.e1), channel_id=1, source_target_pairs={{1,0},{2,1},{3,2},{0,3},{5,4},{6,5},{7,6},{4,7},{9,8},{10,9},{11,1... | collective-permute-start | bytes 3932168 | tf_op jit(solution)/shard_map/ppermute | solution.py:21
  102.1 30.3 %collective-permute-start.29 = (bf16[1280,512]{1,0:T(8,128)(2,1)}, bf16[1280,512]{1,0:T(8,128)(2,1)S(1)}, u32[]{:S(2)}, u32[]{:S(2)}) collective-permute-start(bf16[1280,512]{1,0:T(8,128)(2,1)} %get-tuple-element.31.e1), channel_id=1, source_target_pairs={{3,0},{0,1},{1,2},{2,3},{7,4},{4,5},{5,6},{6,7},{11,8},{8,9},{9,10... | collective-permute-start | bytes 3932168 | tf_op jit(solution)/shard_map/ppermute | solution.py:21
  119.0 3.0 %collective-permute-start.26 = (bf16[2,4,256,256]{3,2,1,0:T(8,128)(2,1)}, bf16[2,4,256,256]{3,2,1,0:T(8,128)(2,1)S(1)}, u32[]{:S(2)}, u32[]{:S(2)}) collective-permute-start(bf16[2,4,256,256]{3,2,1,0:T(8,128)(2,1)} %get-tuple-element.34), channel_id=1, source_target_pairs={{0,4},{4,0},{1,5},{5,1},{2,6},{6,2},{3,7},{7,3},{8,12},{12,8},{9,1... | collective-permute-start | bytes 3145736 | tf_op jit(solution)/shard_map/ppermute | solution.py:25
  119.1 4.4 %collective-permute-start.27 = (bf16[2,4,256,256]{3,2,1,0:T(8,128)(2,1)}, bf16[2,4,256,256]{3,2,1,0:T(8,128)(2,1)S(1)}, u32[]{:S(2)}, u32[]{:S(2)}) collective-permute-start(bf16[2,4,256,256]{3,2,1,0:T(8,128)(2,1)} %get-tuple-element.35), channel_id=1, source_target_pairs={{0,4},{4,0},{1,5},{5,1},{2,6},{6,2},{3,7},{7,3},{8,12},{12,8},{9,1... | collective-permute-start | bytes 3145736 | tf_op jit(solution)/shard_map/ppermute | solution.py:25
  122.0 7.2 %copy-start.7 = (bf16[2,4,256,256]{3,2,1,0:T(8,128)(2,1)}, bf16[2,4,256,256]{3,2,1,0:T(8,128)(2,1)S(1)}, u32[]{:S(2)}) copy-start(bf16[2,4,256,256]{3,2,1,0:T(8,128)(2,1)S(1)} %collective-permute-done.26.refs_0_) | copy-start | bytes 3145732
  123.5 5.7 %copy-start.9 = (bf16[2,4,256,256]{3,2,1,0:T(8,128)(2,1)}, bf16[2,4,256,256]{3,2,1,0:T(8,128)(2,1)S(1)}, u32[]{:S(2)}) copy-start(bf16[2,4,256,256]{3,2,1,0:T(8,128)(2,1)S(1)} %collective-permute-done.27.refs_1_) | copy-start | bytes 3145732
  129.2 3.3 %copy-start = (bf16[1280,512]{1,0:T(8,128)(2,1)}, bf16[1280,512]{1,0:T(8,128)(2,1)S(1)}, u32[]{:S(2)}) copy-start(bf16[1280,512]{1,0:T(8,128)(2,1)S(1)} %collective-permute-done.28.refs_2_) | copy-start | bytes 3932164
  132.5 1.1 copy-start.1
  133.5 2.2 %copy-start.10 = (f32[4,4,256,256]{3,2,1,0:T(8,128)S(1)}, f32[4,4,256,256]{3,2,1,0:T(8,128)}, u32[]{:S(2)}) copy-start(f32[4,4,256,256]{3,2,1,0:T(8,128)} %get-tuple-element.33) | copy-start | bytes 12582916
  137.5 7.7 %collective-permute-start.30 = (bf16[4,128,256]{2,1,0:T(8,128)(2,1)S(1)}, bf16[4,128,256]{2,1,0:T(8,128)(2,1)S(1)}, u32[]{:S(2)}, u32[]{:S(2)}) collective-permute-start(bf16[4,128,256]{2,1,0:T(8,128)(2,1)S(1)} %get-tuple-element.55), channel_id=1, source_target_pairs={{96,0},{28,4},{104,8},{4,12},{112,16},{12,20},{120,24},{20,28},{0,... | collective-permute-start | bytes 786440 | tf_op jit(solution)/shard_map/ppermute | solution.py:36
  138.3 7.1 %collective-permute-start.32 = (bf16[4,128,256]{2,1,0:T(8,128)(2,1)S(1)}, bf16[4,128,256]{2,1,0:T(8,128)(2,1)S(1)}, u32[]{:S(2)}, u32[]{:S(2)}) collective-permute-start(bf16[4,128,256]{2,1,0:T(8,128)(2,1)S(1)} %get-tuple-element.56), channel_id=1, source_target_pairs={{32,0},{12,4},{40,8},{20,12},{48,16},{28,20},{56,24},{4,28},{64,32... | collective-permute-start | bytes 786440 | tf_op jit(solution)/shard_map/ppermute | solution.py:36
  140.9 7.9 %copy-start.2 = (bf16[1280,512]{1,0:T(8,128)(2,1)S(1)}, bf16[1280,512]{1,0:T(8,128)(2,1)}, u32[]{:S(2)}) copy-start(bf16[1280,512]{1,0:T(8,128)(2,1)} %get-tuple-element.41.refs_6_.refs_7_) | copy-start | bytes 3932164
  140.9 14.8 %copy-start.8 = (bf16[2,4,256,256]{3,2,1,0:T(8,128)(2,1)S(1)}, bf16[2,4,256,256]{3,2,1,0:T(8,128)(2,1)}, u32[]{:S(2)}) copy-start(bf16[2,4,256,256]{3,2,1,0:T(8,128)(2,1)} %get-tuple-element.37) | copy-start | bytes 3145732
  145.3 10.5 %collective-permute-start.31 = (bf16[4,256,256]{2,1,0:T(8,128)(2,1)S(1)}, bf16[4,256,256]{2,1,0:T(8,128)(2,1)S(1)}, u32[]{:S(2)}, u32[]{:S(2)}) collective-permute-start(bf16[4,256,256]{2,1,0:T(8,128)(2,1)S(1)} %pad_maximum_fusion.1), channel_id=1, source_target_pairs={{96,0},{28,4},{104,8},{4,12},{112,16},{12,20},{120,24},{20,28},{0,... | collective-permute-start | bytes 1572872 | tf_op jit(solution)/shard_map/ppermute | solution.py:36
  145.5 10.2 %collective-permute-start.33 = (bf16[4,256,256]{2,1,0:T(8,128)(2,1)S(1)}, bf16[4,256,256]{2,1,0:T(8,128)(2,1)S(1)}, u32[]{:S(2)}, u32[]{:S(2)}) collective-permute-start(bf16[4,256,256]{2,1,0:T(8,128)(2,1)S(1)} %pad_maximum_fusion.2), channel_id=1, source_target_pairs={{32,0},{12,4},{40,8},{20,12},{48,16},{28,20},{56,24},{4,28},{64,32... | collective-permute-start | bytes 1572872 | tf_op jit(solution)/shard_map/ppermute | solution.py:36
  148.8 15.6 %copy-start.4 = (bf16[768,512]{1,0:T(8,128)(2,1)S(1)}, bf16[768,512]{1,0:T(8,128)(2,1)}, u32[]{:S(2)}) copy-start(bf16[768,512]{1,0:T(8,128)(2,1)} %copy-done.3) | copy-start | bytes 2359300
  148.8 34.1 %collective-permute-start.39 = (bf16[1280,512]{1,0:T(8,128)(2,1)S(1)}, bf16[1280,512]{1,0:T(8,128)(2,1)S(1)}, u32[]{:S(2)}, u32[]{:S(2)}) collective-permute-start(bf16[1280,512]{1,0:T(8,128)(2,1)S(1)} %copy-done.2), channel_id=1, source_target_pairs={{3,0},{0,1},{1,2},{2,3},{7,4},{4,5},{5,6},{6,7},{11,8},{8,9},{9,10... | collective-permute-start | bytes 3932168 | tf_op jit(solution)/shard_map/ppermute | solution.py:21
  157.3 7.8 %collective-permute-start.34 = (bf16[256,256]{1,0:T(8,128)(2,1)S(1)}, bf16[256,256]{1,0:T(8,128)(2,1)S(1)}, u32[]{:S(2)}, u32[]{:S(2)}) collective-permute-start(bf16[256,256]{1,0:T(8,128)(2,1)S(1)} %get-tuple-element.52), channel_id=1, source_target_pairs={{24,0},{100,4},{0,8},{108,12},{8,16},{116,20},{16,24},{124,28},{56... | collective-permute-start | bytes 393224 | tf_op jit(solution)/shard_map/ppermute | solution.py:36
  161.7 6.5 %collective-permute-start.35 = (bf16[256,256]{1,0:T(8,128)(2,1)S(1)}, bf16[256,256]{1,0:T(8,128)(2,1)S(1)}, u32[]{:S(2)}, u32[]{:S(2)}) collective-permute-start(bf16[256,256]{1,0:T(8,128)(2,1)S(1)} %get-tuple-element.54), channel_id=1, source_target_pairs={{16,0},{68,4},{24,8},{76,12},{0,16},{84,20},{8,24},{92,28},{48,32}... | collective-permute-start | bytes 393224 | tf_op jit(solution)/shard_map/ppermute | solution.py:36
  161.7 6.5 %collective-permute-start.36 = (bf16[256,256]{1,0:T(8,128)(2,1)S(1)}, bf16[256,256]{1,0:T(8,128)(2,1)S(1)}, u32[]{:S(2)}, u32[]{:S(2)}) collective-permute-start(bf16[256,256]{1,0:T(8,128)(2,1)S(1)} %get-tuple-element.53), channel_id=1, source_target_pairs={{8,0},{36,4},{16,8},{44,12},{24,16},{52,20},{0,24},{60,28},{40,32}... | collective-permute-start | bytes 393224 | tf_op jit(solution)/shard_map/ppermute | solution.py:36
  164.4 18.5 %collective-permute-start.38 = (bf16[768,512]{1,0:T(8,128)(2,1)S(1)}, bf16[768,512]{1,0:T(8,128)(2,1)S(1)}, u32[]{:S(2)}, u32[]{:S(2)}) collective-permute-start(bf16[768,512]{1,0:T(8,128)(2,1)S(1)} %copy-done.4), channel_id=1, source_target_pairs={{1,0},{2,1},{3,2},{0,3},{5,4},{6,5},{7,6},{4,7},{9,8},{10,9},{11,1... | collective-permute-start | bytes 2359304 | tf_op jit(solution)/shard_map/ppermute | solution.py:21
  168.2 13.9 %collective-permute-start.37 = (f32[256,128]{1,0:T(8,128)S(1)}, f32[256,128]{1,0:T(8,128)S(1)}, u32[]{:S(2)}, u32[]{:S(2)}) collective-permute-start(f32[256,128]{1,0:T(8,128)S(1)} %get-tuple-element.58), channel_id=1, source_target_pairs={{0,4},{4,0},{1,5},{5,1},{2,6},{6,2},{3,7},{7,3},{8,12},{12,8},{9,1... | collective-permute-start | bytes 393224 | tf_op jit(solution)/shard_map/ppermute | solution.py:25
  182.9 1.3 copy-start.6
  (8 other events, 5.6 us)
Sparse Core Ops, SparseCore 0:
  64.3 44.0 all-gather.2

commit v3 on v2

--- a/solution.py
+++ b/solution.py
@@ -70,7 +70,7 @@
     )(*arrays)
 
 
-CUT = 768
+CUT = 1024
 SUB = 256
 
 
@@ -89,22 +89,11 @@
 
 def gather_pieces(block):
     s = jnp.stack([block] + [cross(block, 0, d) for d in (1, 2, 3)])
-    p, m = cross(s, 1, 1), cross(s, 1, 3)
-    dp, dm = cross(p[:2], 1, 1), cross(m[2:], 1, 3)
-    return [s, p, m, dp, dm]
-
-
-PLACES = [
-    [(a, 0) for a in range(4)],
-    [(a, 1) for a in range(4)],
-    [(a, 3) for a in range(4)],
-    [(0, 2), (1, 2)],
-    [(2, 2), (3, 2)],
-]
+    return [s] + [cross(s, 1, d) for d in (1, 2, 3)]
 
 
 def logits_body(at, *refs):
-    pieces, refs = refs[:10], refs[10:]
+    pieces, refs = refs[:8], refs[8:]
     tid, emb, _, e0_out, e1_out, st_out, loc_out, _, full, sem = refs
     step = pl.program_id(0)
     x, z, c = at[0], at[1], at[2]
@@ -112,12 +101,12 @@
     @pl.when(step == 0)
     def _():
         copies = []
-        for n in range(10):
-            core = c if n < 5 else 1 - c
+        for n in range(8):
+            core = c if n < 4 else 1 - c
             row = pl.multiple_of(core * HALF, HALF)
-            for b, (o1, o2) in enumerate(PLACES[n % 5]):
-                dx = jnp.where(core == 0, o1, o2)
-                dz = jnp.where(core == 0, o2, o1)
+            for b in range(4):
+                dx = jnp.where(core == 0, b, n % 4)
+                dz = jnp.where(core == 0, n % 4, b)
                 col = pl.multiple_of((((x + dx) & 3) * 4 + ((z + dz) & 3)) * 256, 256)
                 copies.append((pieces[n].at[b], full.at[pl.ds(row, HALF), pl.ds(col, 256)], sem.at[len(copies)]))
         for copy in copies:
@@ -167,7 +156,7 @@
         grid_spec=pltpu.PrefetchScalarGridSpec(
             num_scalar_prefetch=1,
             grid=(TILES,),
-            in_specs=[HBM] * 10
+            in_specs=[HBM] * 8
             + [pl.BlockSpec((1, ROWS), lambda i, at: (0, 0)), pl.BlockSpec((TILE, WIDTH), lambda i, at: (i, 0)), HBM],
             out_specs=[
                 pl.BlockSpec((CUT, ROWS), lambda i, at: (0, 0)),
@@ -185,7 +174,7 @@
             jax.ShapeDtypeStruct((8, ROWS), F32),
             jax.ShapeDtypeStruct(later.shape, later.dtype),
         ],
-        input_output_aliases={13: 4},
+        input_output_aliases={11: 4},
         compiler_params=params(),
         cost_estimate=SMALL,
         name="logits",
@@ -329,20 +318,17 @@
     return sum(x.astype(F32) for x in xs)
 
 
-def scatter(keep, recv, c):
+def scatter(keep, recv, c, acc):
     b = [add(keep[d], recv[d // 2][d % 2]) for d in range(4)]
-    n = HALF // 2
-    r1 = cross(b[2][:, :n].astype(BF), 0, 3)
-    r3 = cross(b[2][:, n:].astype(BF), 0, 1)
-    s1 = jnp.concatenate([add(b[1][:, :n], r1).astype(BF), b[1][:, n:].astype(BF)], axis=1)
-    s3 = jnp.concatenate([b[3][:, :n].astype(BF), add(b[3][:, n:], r3).astype(BF)], axis=1)
-    t = add(b[0], cross(s1, 0, 3), cross(s3, 0, 1))
+    u = [cross(b[d].astype(BF), 0, 4 - d) for d in (1, 2, 3)]
+    *u, acc = gate(*u, acc)
+    t = add(b[0], *u)
     u = [cross(t[d].astype(BF), 1, 4 - d) for d in (1, 2, 3)]
     f = add(t[0], *u)
     low, high = f[:, :128], f[:, 128:]
     mine, other = jnp.where(c == 0, low, high), jnp.where(c == 0, high, low)
     got = sibling(other)
-    return jnp.where(c == 0, jnp.concatenate([mine, got]), jnp.concatenate([got, mine]))
+    return jnp.where(c == 0, jnp.concatenate([mine, got]), jnp.concatenate([got, mine])), acc
 
 
 def quarter_copies(at, feats, offsets, q, sem):
@@ -453,15 +439,16 @@
     s = merge_call(loc, *(shift(loc, "x", d) for d in (1, 2, 3)))
     s = merge_call(s, *(shift(s, "z", d) for d in (1, 2, 3)))
     pack, grad_mix, e1 = finish_call(s, sibling(s), st, tid, mix, weight.reshape(1, 128), ep0, em0, e1)
-    pack, pack_p, pack_m, pack_d, e1 = gate(pack, shift(pack, "y", 1), shift(pack, "y", 3), shift(pack, "y", 2), e1)
     ep1, em1 = shift(e1, "y", 1), shift(e1, "y", 3)
-
-    keep, *send, tgt = hidden_call(at, e0, e1, pack, embed)
-    *recv, ep1, em1, feats = gate(*(sibling(t) for t in send), ep1, em1, feats)
+    keep, send0, send1, tgt = hidden_call(at, e0, e1, pack, embed)
+    send0, send1, pack, ep1, em1 = gate(send0, send1, pack, ep1, em1)
+    recv0, recv1, pack_p, pack_m, pack_d, ep0, em1 = gate(
+        sibling(send0), sibling(send1), *(shift(pack, "y", d) for d in (1, 3, 2)), ep0, em1
+    )
     diag = shift(ep0, "y", 1), shift(em1, "y", 3)
-    grad_hidden = scatter(keep, recv, c)
 
     acc = embed_a_call(at, tgt, ep0, ep1, em0, em1, pack_p, pack_m, feats)
+    grad_hidden, acc = scatter(keep, (recv0, recv1), c, acc)
     grad_embed = embed_b_call(at, acc, *diag, pack_d, feats)
     return grad_hidden.reshape(4, 128, 128), grad_embed, grad_mix
 

time: 203 us -> 192 us (0.946)
  waiting for transfers between devices: 61.8 us -> 36.8 us
  starting transfers between devices: 46.2 us -> 58.6 us
    ppermute x15, starting transfers between devices: 16.3 us -> 35.2 us  [shift(): return lax.ppermute(a, axis, [((i + d) % 4, i) for i in range(4)])]
    ppermute x14 -> x12, waiting for transfers between devices: 31.1 us -> 19.6 us  [cross(): return lax.ppermute(a, ('x', 'z', 'c'), pairs)]
    ppermute x15, waiting for transfers between devices: 22.9 us -> 14.5 us  [shift(): return lax.ppermute(a, axis, [((i + d) % 4, i) for i in range(4)])]
    ppermute x14 -> x12, starting transfers between devices: 27 us -> 20.7 us  [cross(): return lax.ppermute(a, ('x', 'z', 'c'), pairs)]
    ppermute x10 -> x9, waiting for transfers between devices: 7.7 us -> 2.65 us  [sibling(): return lax.ppermute(a, 'c', [(0, 1), (1, 0)])]
    convert_element_type x2 -> x1, other arithmetic: 0.17 us -> 2.87 us  [scatter(): u = [cross(b[d].astype(BF), 0, 4 - d) for d in (1, 2, 3)]]
    unnamed x62 -> x56, local copies, waits for them, and re-layouts: 7.69 us -> 8.04 us
  transfers between devices with their start and end apart: 41 -> 38, of which waited for: 26 -> 20; matrix products, arithmetic and copies ran while one was open for 2% -> 3% of each run, Pallas kernels for 17% -> 24%
where the time goes in v3:
time: 192 us; the launch traced here: 190 us
  Pallas kernels  63.3 us (33%)
  starting transfers between devices  58.6 us (31%)
  waiting for transfers between devices  36.8 us (19%)
  between operations  14.3 us (7%)
  local copies, waits for them, and re-layouts  8.72 us (5%)
  other arithmetic  7.97 us (4%)
    ppermute x15, starting transfers between devices, shift(): return lax.ppermute(a, axis, [((i + d) % 4, i) for i in range(4)])  35.2 us
    ppermute x12, starting transfers between devices, cross(): return lax.ppermute(a, ('x', 'z', 'c'), pairs)  20.7 us
    ppermute x12, waiting for transfers between devices, cross(): return lax.ppermute(a, ('x', 'z', 'c'), pairs)  19.6 us
    pallas_call x1, Pallas kernels, logits_call(): pl.pallas_call(logits_body, grid_spec=pltpu.PrefetchScalarGridSpec(num_sc...  17.9 us
    pallas_call x1, Pallas kernels, hidden_call(): pl.pallas_call(hidden_body, grid_spec=pltpu.PrefetchScalarGridSpec(num_sc...  17.1 us
    ppermute x15, waiting for transfers between devices, shift(): return lax.ppermute(a, axis, [((i + d) % 4, i) for i in range(4)])  14.5 us
    pallas_call x1, Pallas kernels, embed_a_call(): pl.pallas_call(embed_a_body, grid_spec=pltpu.PrefetchScalarGridSpec(num_s...  13.8 us
    pallas_call x1, Pallas kernels, embed_b_call(): pl.pallas_call(embed_b_body, grid_spec=pltpu.PrefetchScalarGridSpec(num_s...  10.3 us
  transfers between devices with their start and end apart: 38, of which 20 were waited for; matrix products, arithmetic and copies ran while one was open for 3% of the time, Pallas kernels for 24%

profile of v3, /device:TPU:0, one launch (start us, length us, event | category | flops | bytes accessed | tf_op | source)
XLA Modules:
  0.0 189.7 jit_solution(3404446515227659350)
XLA Ops:
  7.2 0.9 broadcast_select_fusion.1
  8.2 1.2 collective-permute-done
  9.5 1.6 collective-permute-start.3
  11.1 2.7 %collective-permute-start.2 = (bf16[256,256]{1,0:T(8,128)(2,1)S(1)}, bf16[256,256]{1,0:T(8,128)(2,1)S(1)}, u32[]{:S(2)}, u32[]{:S(2)}) collective-permute-start(bf16[256,256]{1,0:T(8,128)(2,1)S(1)} %maximum_select_fusion.2), channel_id=1, source_target_pairs={{64,0},{20,4},{72,8},{28,12},{80,16},{4,20},{88,24},{12,28},{96,32... | collective-permute-start | bytes 393224 | tf_op jit(solution)/shard_map/ppermute | solution.py:36
  13.9 1.4 collective-permute-start.1
  15.3 0.4 collective-permute-done.3
  15.7 2.5 %collective-permute-done.2 = bf16[256,256]{1,0:T(8,128)(2,1)S(1)} collective-permute-done((bf16[256,256]{1,0:T(8,128)(2,1)S(1)}, bf16[256,256]{1,0:T(8,128)(2,1)S(1)}, u32[]{:S(2)}, u32[]{:S(2)}) %collective-permute-start.2) | collective-permute-done | bytes 131104 | tf_op jit(solution)/shard_map/ppermute | solution.py:36
  18.2 0.6 collective-permute-done.1
  18.9 2.0 %collective-permute-start.6 = (bf16[4,256,256]{2,1,0:T(8,128)(2,1)S(1)}, bf16[4,256,256]{2,1,0:T(8,128)(2,1)S(1)}, u32[]{:S(2)}, u32[]{:S(2)}) collective-permute-start(bf16[4,256,256]{2,1,0:T(8,128)(2,1)S(1)} %pad_maximum_fusion.refs_0_), channel_id=1, source_target_pairs={{24,0},{100,4},{0,8},{108,12},{8,16},{116,20},{16,24},{124,28},{56... | collective-permute-start | bytes 1572872 | tf_op jit(solution)/shard_map/ppermute | solution.py:36
  20.9 3.6 %collective-permute-start.5 = (bf16[4,256,256]{2,1,0:T(8,128)(2,1)S(1)}, bf16[4,256,256]{2,1,0:T(8,128)(2,1)S(1)}, u32[]{:S(2)}, u32[]{:S(2)}) collective-permute-start(bf16[4,256,256]{2,1,0:T(8,128)(2,1)S(1)} %pad_maximum_fusion.refs_0_), channel_id=1, source_target_pairs={{16,0},{68,4},{24,8},{76,12},{0,16},{84,20},{8,24},{92,28},{48,32}... | collective-permute-start | bytes 1572872 | tf_op jit(solution)/shard_map/ppermute | solution.py:36
  24.5 1.0 collective-permute-start.4
  25.5 4.7 %collective-permute-done.6.refs_3_ = bf16[4,256,256]{2,1,0:T(8,128)(2,1)S(1)} collective-permute-done((bf16[4,256,256]{2,1,0:T(8,128)(2,1)S(1)}, bf16[4,256,256]{2,1,0:T(8,128)(2,1)S(1)}, u32[]{:S(2)}, u32[]{:S(2)}) %collective-permute-start.6) | collective-permute-done | bytes 524320 | tf_op jit(solution)/shard_map/ppermute | solution.py:36
  30.2 7.1 %collective-permute-done.5.refs_2_ = bf16[4,256,256]{2,1,0:T(8,128)(2,1)S(1)} collective-permute-done((bf16[4,256,256]{2,1,0:T(8,128)(2,1)S(1)}, bf16[4,256,256]{2,1,0:T(8,128)(2,1)S(1)}, u32[]{:S(2)}, u32[]{:S(2)}) %collective-permute-start.5) | collective-permute-done | bytes 524320 | tf_op jit(solution)/shard_map/ppermute | solution.py:36
  37.3 0.5 collective-permute-start.8
  37.8 1.6 collective-permute-start.11
  39.3 0.7 broadcast_subtract_fusion
  40.0 0.6 pad_add_fusion.at
  40.6 0.7 tile.2
  41.6 17.9 %logits.1 = (bf16[1024,512]{1,0:T(8,128)(2,1)}, bf16[1024,512]{1,0:T(8,128)(2,1)}, f32[8,512]{1,0:T(8,128)}, f32[8,512]{1,0:T(8,128)}, bf16[512,128]{1,0:T(8,128)(2,1)}) custom-call(s32[4]{0:T(128)} %pad_add_fusion.at, bf16[4,256,256]{2,1,0:T(8,128)(2,1)} %copy-done.11, bf16[4,256,256]{2,1,0:T(8,128)(2,1)} %copy-done.15, ...), custom_call_target="tpu_custom_call", output_to_operand_aliasing={{4}: (11, {})} | custom-call | flops 1000 | bytes 1000 | tf_op jit(solution)/shard_map/logits/pallas_call | solution.py:154
  59.5 7.4 %collective-permute-start.20 = (bf16[1024,512]{1,0:T(8,128)(2,1)}, bf16[1024,512]{1,0:T(8,128)(2,1)S(1)}, u32[]{:S(2)}, u32[]{:S(2)}) collective-permute-start(bf16[1024,512]{1,0:T(8,128)(2,1)} %get-tuple-element.31.e0), channel_id=1, source_target_pairs={{3,0},{0,1},{1,2},{2,3},{7,4},{4,5},{5,6},{6,7},{11,8},{8,9},{9,10... | collective-permute-start | bytes 3145736 | tf_op jit(solution)/shard_map/ppermute | solution.py:21
  66.8 6.8 %collective-permute-start.19 = (bf16[1024,512]{1,0:T(8,128)(2,1)}, bf16[1024,512]{1,0:T(8,128)(2,1)S(1)}, u32[]{:S(2)}, u32[]{:S(2)}) collective-permute-start(bf16[1024,512]{1,0:T(8,128)(2,1)} %get-tuple-element.31.e0), channel_id=1, source_target_pairs={{1,0},{2,1},{3,2},{0,3},{5,4},{6,5},{7,6},{4,7},{9,8},{10,9},{11,1... | collective-permute-start | bytes 3145736 | tf_op jit(solution)/shard_map/ppermute | solution.py:21
  73.6 4.2 %collective-permute-start.13 = (f32[8,512]{1,0:T(8,128)}, f32[8,512]{1,0:T(8,128)S(1)}, u32[]{:S(2)}, u32[]{:S(2)}) collective-permute-start(f32[8,512]{1,0:T(8,128)} %get-tuple-element.32.refs_0_), channel_id=1, source_target_pairs={{64,0},{96,32},{0,64},{32,96},{65,1},{97,33},{1,65},{33,97},{66,2}... | collective-permute-start | bytes 49160 | tf_op jit(solution)/shard_map/ppermute | solution.py:21
  77.8 0.9 collective-permute-start.12
  78.7 1.2 collective-permute-done.13.refs_2_
  79.9 2.0 %collective-permute-done.12.refs_1_ = f32[8,512]{1,0:T(8,128)S(1)} collective-permute-done((f32[8,512]{1,0:T(8,128)}, f32[8,512]{1,0:T(8,128)S(1)}, u32[]{:S(2)}, u32[]{:S(2)}) %collective-permute-start.12) | collective-permute-done | bytes 16416 | tf_op jit(solution)/shard_map/ppermute | solution.py:21
  82.0 0.6 copy-done.26
  82.6 1.4 merge.2.refs_0_
  83.9 1.6 collective-permute-start.17
  85.5 1.8 collective-permute-start.16
  87.3 1.5 collective-permute-start.15
  89.2 1.9 collective-permute-done.16.refs_2_
  91.3 0.4 copy-done.25
  91.7 0.6 copy-done.27
  92.3 1.4 merge.3.a
  93.7 1.4 collective-permute-done.18.b
  95.1 1.5 collective-permute-done.20.em0.refs_4_.refs_5_
  96.6 1.0 copy-done.4
  97.9 1.4 finish.1
  99.3 0.8 collective-permute-start.22
  100.2 2.4 %collective-permute-start.21 = (bf16[1024,512]{1,0:T(8,128)(2,1)}, bf16[1024,512]{1,0:T(8,128)(2,1)S(1)}, u32[]{:S(2)}, u32[]{:S(2)}) collective-permute-start(bf16[1024,512]{1,0:T(8,128)(2,1)} %get-tuple-element.35.e1), channel_id=1, source_target_pairs={{1,0},{2,1},{3,2},{0,3},{5,4},{6,5},{7,6},{4,7},{9,8},{10,9},{11,1... | collective-permute-start | bytes 3145736 | tf_op jit(solution)/shard_map/ppermute | solution.py:21
  102.6 17.1 %hidden.1 = (f32[4,4,256,256]{3,2,1,0:T(8,128)}, bf16[2,4,256,256]{3,2,1,0:T(8,128)(2,1)}, bf16[2,4,256,256]{3,2,1,0:T(8,128)(2,1)}, bf16[2048,512]{1,0:T(8,128)(2,1)}) custom-call(s32[4]{0:T(128)} %pad_add_fusion.at, bf16[1024,512]{1,0:T(8,128)(2,1)} %get-tuple-element.31.e0, bf16[1024,512]{1,0:T(8,128)(2,1)} %get-tuple-element.35.e1, ...), custom_call_target="tpu_custom_call" | custom-call | flops 1000 | bytes 1000 | tf_op jit(solution)/shard_map/hidden/pallas_call | solution.py:291
  119.6 5.1 %collective-permute-done.22.refs_4_ = bf16[1024,512]{1,0:T(8,128)(2,1)S(1)} collective-permute-done((bf16[1024,512]{1,0:T(8,128)(2,1)}, bf16[1024,512]{1,0:T(8,128)(2,1)S(1)}, u32[]{:S(2)}, u32[]{:S(2)}) %collective-permute-start.22) | collective-permute-done | bytes 1048608 | tf_op jit(solution)/shard_map/ppermute | solution.py:21
  124.8 1.0 copy-done.2
  126.2 0.5 collective-permute-start.24
  126.7 2.0 %collective-permute-start.27 = (f32[8,512]{1,0:T(8,128)}, f32[8,512]{1,0:T(8,128)S(1)}, u32[]{:S(2)}, u32[]{:S(2)}) collective-permute-start(f32[8,512]{1,0:T(8,128)} %get-tuple-element.42), channel_id=1, source_target_pairs={{2,0},{3,1},{0,2},{1,3},{6,4},{7,5},{4,6},{5,7},{10,8},{11,9},{8,1... | collective-permute-start | bytes 49160 | tf_op jit(solution)/shard_map/ppermute | solution.py:21
  128.6 1.5 collective-permute-start.26
  130.1 1.8 collective-permute-start.25
  132.1 1.7 collective-permute-done.26.refs_3_
  135.4 2.9 %fusion.4 = (bf16[4,256,256]{2,1,0:T(8,128)(2,1)}, bf16[4,256,256]{2,1,0:T(8,128)(2,1)}, bf16[4,256,256]{2,1,0:T(8,128)(2,1)}) fusion(f32[4,4,256,256]{3,2,1,0:T(8,128)S(1)} %copy-done.6, bf16[2,4,256,256]{3,2,1,0:T(8,128)(2,1)} %get-tuple-element.45, bf16[2,4,256,256]{3,2,1,0:T(8,128)(2,1)} %get-tuple-element.44), kind=kLoop, calls=%fused_computation.8 | loop fusion | flops 2359296 | bytes 6291456 | tf_op jit(solution)/shard_map/convert_element_type | solution.py:323
  138.3 1.6 collective-permute-start.30
  139.9 1.2 collective-permute-start.28
  141.1 2.6 %collective-permute-start.35 = (bf16[1024,512]{1,0:T(8,128)(2,1)S(1)}, bf16[1024,512]{1,0:T(8,128)(2,1)S(1)}, u32[]{:S(2)}, u32[]{:S(2)}) collective-permute-start(bf16[1024,512]{1,0:T(8,128)(2,1)S(1)} %copy-done.1), channel_id=1, source_target_pairs={{1,0},{2,1},{3,2},{0,3},{5,4},{6,5},{7,6},{4,7},{9,8},{10,9},{11,1... | collective-permute-start | bytes 3145736 | tf_op jit(solution)/shard_map/ppermute | solution.py:21
  143.7 13.8 %embed_a.1.refs_3_ = f32[2048,1024]{1,0:T(8,128)} custom-call(s32[4]{0:T(128)} %pad_add_fusion.at, bf16[2048,512]{1,0:T(8,128)(2,1)} %get-tuple-element.46.tgt, bf16[1024,512]{1,0:T(8,128)(2,1)} %get-tuple-element.47.refs_0_.refs_1_, bf16[1024,512]{1,0:T(8,128)(2,1)} %get-tuple-element.47.refs_0_.refs_1_, ...), custom_call_target="tpu_custom_call" | custom-call | flops 1000 | bytes 1000 | tf_op jit(solution)/shard_map/embed_a/pallas_call | solution.py:365
  157.6 1.2 copy-done.8
  158.7 2.0 %fusion.8 = (bf16[4,256,256]{2,1,0:T(8,128)(2,1)S(1)}, f32[4,256,256]{2,1,0:T(8,128)S(1)}) fusion(bf16[4,256,256]{2,1,0:T(8,128)(2,1)} %get-tuple-element.55, bf16[4,256,256]{2,1,0:T(8,128)(2,1)} %get-tuple-element.54, bf16[4,256,256]{2,1,0:T(8,128)(2,1)} %get-tuple-element.53, bf16[2,4,256,256]{3,2,1,0:T(8,128)(2,1)S(1)} %copy-done.8, ...), kind=kLoop, calls=%fused_computation.26 | loop fusion | flops 2359296 | bytes 4718592 | tf_op jit(solution)/shard_map/convert.2
  160.8 2.4 %collective-permute-start.31 = (bf16[256,256]{1,0:T(8,128)(2,1)S(1)}, bf16[256,256]{1,0:T(8,128)(2,1)S(1)}, u32[]{:S(2)}, u32[]{:S(2)}) collective-permute-start(bf16[256,256]{1,0:T(8,128)(2,1)S(1)} %get-tuple-element.64), channel_id=1, source_target_pairs={{24,0},{100,4},{0,8},{108,12},{8,16},{116,20},{16,24},{124,28},{56... | collective-permute-start | bytes 393224 | tf_op jit(solution)/shard_map/ppermute | solution.py:36
  163.3 0.9 collective-permute-start.33
  164.1 2.2 %collective-permute-start.32 = (bf16[256,256]{1,0:T(8,128)(2,1)S(1)}, bf16[256,256]{1,0:T(8,128)(2,1)S(1)}, u32[]{:S(2)}, u32[]{:S(2)}) collective-permute-start(bf16[256,256]{1,0:T(8,128)(2,1)S(1)} %get-tuple-element.66), channel_id=1, source_target_pairs={{16,0},{68,4},{24,8},{76,12},{0,16},{84,20},{8,24},{92,28},{48,32}... | collective-permute-start | bytes 393224 | tf_op jit(solution)/shard_map/ppermute | solution.py:36
  166.3 0.8 collective-permute-done.31
  167.1 1.2 collective-permute-done.33
  168.2 2.4 %collective-permute-done.32 = bf16[256,256]{1,0:T(8,128)(2,1)S(1)} collective-permute-done((bf16[256,256]{1,0:T(8,128)(2,1)S(1)}, bf16[256,256]{1,0:T(8,128)(2,1)S(1)}, u32[]{:S(2)}, u32[]{:S(2)}) %collective-permute-start.32) | collective-permute-done | bytes 131104 | tf_op jit(solution)/shard_map/ppermute | solution.py:36
  170.8 1.0 copy-done.10
  171.8 10.3 %embed_b.1 = bf16[2048,1024]{1,0:T(8,128)(2,1)} custom-call(s32[4]{0:T(128)} %pad_add_fusion.at, f32[2048,1024]{1,0:T(8,128)} %get-tuple-element.56.acc, bf16[1024,512]{1,0:T(8,128)(2,1)} %copy-done.10, bf16[1024,512]{1,0:T(8,128)(2,1)} %copy-done.10, bf16[1024,512]{1,0:T(8,128)(2,1)} %collective-permute-done.36.eb0.eb1, ...), custom_call_target="tpu_custom_call" | custom-call | flops 1000 | bytes 1000 | tf_op jit(solution)/shard_map/embed_b/pallas_call | solution.py:398
  182.1 0.7 maximum_select_fusion
  (92 shorter events, 4.0 us)
Async XLA Ops:
  7.2 136.5 %all-gather.3.cloned.1.call-start = ((), (), s32[]{:S(2)}) async-start(), calls=%async_computation | async-start | bytes 4325376 | tf_op jit(solution)/shard_map/all_gather | solution.py:436
  8.1 1.3 collective-permute-start
  9.5 6.2 %collective-permute-start.3 = (bf16[256,256]{1,0:T(8,128)(2,1)S(1)}, bf16[256,256]{1,0:T(8,128)(2,1)S(1)}, u32[]{:S(2)}, u32[]{:S(2)}) collective-permute-start(bf16[256,256]{1,0:T(8,128)(2,1)S(1)} %maximum_select_fusion.2), channel_id=1, source_target_pairs={{96,0},{28,4},{104,8},{4,12},{112,16},{12,20},{120,24},{20,28},{0,... | collective-permute-start | bytes 393224 | tf_op jit(solution)/shard_map/ppermute | solution.py:36
  11.1 7.1 %collective-permute-start.2 = (bf16[256,256]{1,0:T(8,128)(2,1)S(1)}, bf16[256,256]{1,0:T(8,128)(2,1)S(1)}, u32[]{:S(2)}, u32[]{:S(2)}) collective-permute-start(bf16[256,256]{1,0:T(8,128)(2,1)S(1)} %maximum_select_fusion.2), channel_id=1, source_target_pairs={{64,0},{20,4},{72,8},{28,12},{80,16},{4,20},{88,24},{12,28},{96,32... | collective-permute-start | bytes 393224 | tf_op jit(solution)/shard_map/ppermute | solution.py:36
  13.9 5.0 %collective-permute-start.1 = (bf16[256,256]{1,0:T(8,128)(2,1)S(1)}, bf16[256,256]{1,0:T(8,128)(2,1)S(1)}, u32[]{:S(2)}, u32[]{:S(2)}) collective-permute-start(bf16[256,256]{1,0:T(8,128)(2,1)S(1)} %maximum_select_fusion.2), channel_id=1, source_target_pairs={{32,0},{12,4},{40,8},{20,12},{48,16},{28,20},{56,24},{4,28},{64,32... | collective-permute-start | bytes 393224 | tf_op jit(solution)/shard_map/ppermute | solution.py:36
  18.9 22.4 %copy-start.11 = (bf16[4,256,256]{2,1,0:T(8,128)(2,1)}, bf16[4,256,256]{2,1,0:T(8,128)(2,1)S(1)}, u32[]{:S(2)}) copy-start(bf16[4,256,256]{2,1,0:T(8,128)(2,1)S(1)} %pad_maximum_fusion.refs_0_) | copy-start | bytes 1572868
  18.9 11.3 %collective-permute-start.6 = (bf16[4,256,256]{2,1,0:T(8,128)(2,1)S(1)}, bf16[4,256,256]{2,1,0:T(8,128)(2,1)S(1)}, u32[]{:S(2)}, u32[]{:S(2)}) collective-permute-start(bf16[4,256,256]{2,1,0:T(8,128)(2,1)S(1)} %pad_maximum_fusion.refs_0_), channel_id=1, source_target_pairs={{24,0},{100,4},{0,8},{108,12},{8,16},{116,20},{16,24},{124,28},{56... | collective-permute-start | bytes 1572872 | tf_op jit(solution)/shard_map/ppermute | solution.py:36
  20.9 16.4 %collective-permute-start.5 = (bf16[4,256,256]{2,1,0:T(8,128)(2,1)S(1)}, bf16[4,256,256]{2,1,0:T(8,128)(2,1)S(1)}, u32[]{:S(2)}, u32[]{:S(2)}) collective-permute-start(bf16[4,256,256]{2,1,0:T(8,128)(2,1)S(1)} %pad_maximum_fusion.refs_0_), channel_id=1, source_target_pairs={{16,0},{68,4},{24,8},{76,12},{0,16},{84,20},{8,24},{92,28},{48,32}... | collective-permute-start | bytes 1572872 | tf_op jit(solution)/shard_map/ppermute | solution.py:36
  24.5 12.8 %collective-permute-start.4 = (bf16[4,256,256]{2,1,0:T(8,128)(2,1)S(1)}, bf16[4,256,256]{2,1,0:T(8,128)(2,1)S(1)}, u32[]{:S(2)}, u32[]{:S(2)}) collective-permute-start(bf16[4,256,256]{2,1,0:T(8,128)(2,1)S(1)} %pad_maximum_fusion.refs_0_), channel_id=1, source_target_pairs={{8,0},{36,4},{16,8},{44,12},{24,16},{52,20},{0,24},{60,28},{40,32}... | collective-permute-start | bytes 1572872 | tf_op jit(solution)/shard_map/ppermute | solution.py:36
  25.5 15.1 %collective-permute-start.7 = (bf16[4,256,256]{2,1,0:T(8,128)(2,1)S(1)}, bf16[4,256,256]{2,1,0:T(8,128)(2,1)S(1)}, u32[]{:S(2)}, u32[]{:S(2)}) collective-permute-start(bf16[4,256,256]{2,1,0:T(8,128)(2,1)S(1)} %pad_maximum_fusion.refs_0_), channel_id=1, source_target_pairs={{0,4},{4,0},{1,5},{5,1},{2,6},{6,2},{3,7},{7,3},{8,12},{12,8},{9,1... | collective-permute-start | bytes 1572872 | tf_op jit(solution)/shard_map/ppermute | solution.py:25
  30.2 11.1 %copy-start.13 = (bf16[4,256,256]{2,1,0:T(8,128)(2,1)}, bf16[4,256,256]{2,1,0:T(8,128)(2,1)S(1)}, u32[]{:S(2)}) copy-start(bf16[4,256,256]{2,1,0:T(8,128)(2,1)S(1)} %collective-permute-done.6.refs_3_) | copy-start | bytes 1572868
  30.2 10.4 %collective-permute-start.10 = (bf16[4,256,256]{2,1,0:T(8,128)(2,1)S(1)}, bf16[4,256,256]{2,1,0:T(8,128)(2,1)S(1)}, u32[]{:S(2)}, u32[]{:S(2)}) collective-permute-start(bf16[4,256,256]{2,1,0:T(8,128)(2,1)S(1)} %collective-permute-done.6.refs_3_), channel_id=1, source_target_pairs={{0,4},{4,0},{1,5},{5,1},{2,6},{6,2},{3,7},{7,3},{8,12},{12,8},{9,1... | collective-permute-start | bytes 1572872 | tf_op jit(solution)/shard_map/ppermute | solution.py:25
  37.2 4.0 %copy-start.14 = (bf16[4,256,256]{2,1,0:T(8,128)(2,1)}, bf16[4,256,256]{2,1,0:T(8,128)(2,1)S(1)}, u32[]{:S(2)}) copy-start(bf16[4,256,256]{2,1,0:T(8,128)(2,1)S(1)} %collective-permute-done.5.refs_2_) | copy-start | bytes 1572868
  37.3 3.3 %collective-permute-start.9 = (bf16[4,256,256]{2,1,0:T(8,128)(2,1)S(1)}, bf16[4,256,256]{2,1,0:T(8,128)(2,1)}, u32[]{:S(2)}, u32[]{:S(2)}) collective-permute-start(bf16[4,256,256]{2,1,0:T(8,128)(2,1)S(1)} %collective-permute-done.5.refs_2_), channel_id=1, source_target_pairs={{0,4},{4,0},{1,5},{5,1},{2,6},{6,2},{3,7},{7,3},{8,12},{12,8},{9,1... | collective-permute-start | bytes 1572872 | tf_op jit(solution)/shard_map/ppermute | solution.py:25
  37.3 4.0 %copy-start.15 = (bf16[4,256,256]{2,1,0:T(8,128)(2,1)}, bf16[4,256,256]{2,1,0:T(8,128)(2,1)S(1)}, u32[]{:S(2)}) copy-start(bf16[4,256,256]{2,1,0:T(8,128)(2,1)S(1)} %collective-permute-done.4.refs_1_) | copy-start | bytes 1572868
  37.3 3.3 %collective-permute-start.8 = (bf16[4,256,256]{2,1,0:T(8,128)(2,1)S(1)}, bf16[4,256,256]{2,1,0:T(8,128)(2,1)}, u32[]{:S(2)}, u32[]{:S(2)}) collective-permute-start(bf16[4,256,256]{2,1,0:T(8,128)(2,1)S(1)} %collective-permute-done.4.refs_1_), channel_id=1, source_target_pairs={{0,4},{4,0},{1,5},{5,1},{2,6},{6,2},{3,7},{7,3},{8,12},{12,8},{9,1... | collective-permute-start | bytes 1572872 | tf_op jit(solution)/shard_map/ppermute | solution.py:25
  37.8 2.8 %collective-permute-start.11 = (bf16[512,128]{1,0:T(8,128)(2,1)}, bf16[512,128]{1,0:T(8,128)(2,1)S(1)}, u32[]{:S(2)}, u32[]{:S(2)}) collective-permute-start(bf16[512,128]{1,0:T(8,128)(2,1)} %bitcast.49), channel_id=1, source_target_pairs={{0,0},{1,32},{2,64},{3,96},{32,1},{33,33},{34,65},{35,97},{64,2},{... | collective-permute-start | bytes 393224 | tf_op jit(solution)/shard_map/ppermute | solution.py:426
  40.5 0.7 copy-start.12
  40.5 0.8 copy-start.16
  40.6 1.0 copy-start.17
  59.5 37.1 %collective-permute-start.20 = (bf16[1024,512]{1,0:T(8,128)(2,1)}, bf16[1024,512]{1,0:T(8,128)(2,1)S(1)}, u32[]{:S(2)}, u32[]{:S(2)}) collective-permute-start(bf16[1024,512]{1,0:T(8,128)(2,1)} %get-tuple-element.31.e0), channel_id=1, source_target_pairs={{3,0},{0,1},{1,2},{2,3},{7,4},{4,5},{5,6},{6,7},{11,8},{8,9},{9,10... | collective-permute-start | bytes 3145736 | tf_op jit(solution)/shard_map/ppermute | solution.py:21
  66.8 29.8 %collective-permute-start.19 = (bf16[1024,512]{1,0:T(8,128)(2,1)}, bf16[1024,512]{1,0:T(8,128)(2,1)S(1)}, u32[]{:S(2)}, u32[]{:S(2)}) collective-permute-start(bf16[1024,512]{1,0:T(8,128)(2,1)} %get-tuple-element.31.e0), channel_id=1, source_target_pairs={{1,0},{2,1},{3,2},{0,3},{5,4},{6,5},{7,6},{4,7},{9,8},{10,9},{11,1... | collective-permute-start | bytes 3145736 | tf_op jit(solution)/shard_map/ppermute | solution.py:21
  73.6 5.2 %collective-permute-start.14 = (f32[8,512]{1,0:T(8,128)}, f32[8,512]{1,0:T(8,128)S(1)}, u32[]{:S(2)}, u32[]{:S(2)}) collective-permute-start(f32[8,512]{1,0:T(8,128)} %get-tuple-element.32.refs_0_), channel_id=1, source_target_pairs={{96,0},{0,32},{32,64},{64,96},{97,1},{1,33},{33,65},{65,97},{98,2}... | collective-permute-start | bytes 49160 | tf_op jit(solution)/shard_map/ppermute | solution.py:21
  73.6 6.3 %collective-permute-start.13 = (f32[8,512]{1,0:T(8,128)}, f32[8,512]{1,0:T(8,128)S(1)}, u32[]{:S(2)}, u32[]{:S(2)}) collective-permute-start(f32[8,512]{1,0:T(8,128)} %get-tuple-element.32.refs_0_), channel_id=1, source_target_pairs={{64,0},{96,32},{0,64},{32,96},{65,1},{97,33},{1,65},{33,97},{66,2}... | collective-permute-start | bytes 49160 | tf_op jit(solution)/shard_map/ppermute | solution.py:21
  77.8 4.1 %collective-permute-start.12 = (f32[8,512]{1,0:T(8,128)}, f32[8,512]{1,0:T(8,128)S(1)}, u32[]{:S(2)}, u32[]{:S(2)}) collective-permute-start(f32[8,512]{1,0:T(8,128)} %get-tuple-element.32.refs_0_), channel_id=1, source_target_pairs={{32,0},{64,32},{96,64},{0,96},{33,1},{65,33},{97,65},{1,97},{34,2}... | collective-permute-start | bytes 49160 | tf_op jit(solution)/shard_map/ppermute | solution.py:21
  78.7 3.2 %copy-start.22 = (f32[8,512]{1,0:T(8,128)}, f32[8,512]{1,0:T(8,128)S(1)}, u32[]{:S(2)}) copy-start(f32[8,512]{1,0:T(8,128)S(1)} %collective-permute-done.14.refs_3_) | copy-start | bytes 49156
  79.9 2.0 %copy-start.24 = (f32[8,512]{1,0:T(8,128)}, f32[8,512]{1,0:T(8,128)S(1)}, u32[]{:S(2)}) copy-start(f32[8,512]{1,0:T(8,128)S(1)} %collective-permute-done.13.refs_2_) | copy-start | bytes 49156
  81.9 0.6 copy-start.26
  83.9 5.2 %collective-permute-start.17 = (f32[8,512]{1,0:T(8,128)}, f32[8,512]{1,0:T(8,128)S(1)}, u32[]{:S(2)}, u32[]{:S(2)}) collective-permute-start(f32[8,512]{1,0:T(8,128)} %merge.2.refs_0_), channel_id=1, source_target_pairs={{24,0},{0,8},{8,16},{16,24},{25,1},{1,9},{9,17},{17,25},{26,2},{2,... | collective-permute-start | bytes 49160 | tf_op jit(solution)/shard_map/ppermute | solution.py:21
  85.5 5.5 %collective-permute-start.16 = (f32[8,512]{1,0:T(8,128)}, f32[8,512]{1,0:T(8,128)S(1)}, u32[]{:S(2)}, u32[]{:S(2)}) collective-permute-start(f32[8,512]{1,0:T(8,128)} %merge.2.refs_0_), channel_id=1, source_target_pairs={{16,0},{24,8},{0,16},{8,24},{17,1},{25,9},{1,17},{9,25},{18,2},{26... | collective-permute-start | bytes 49160 | tf_op jit(solution)/shard_map/ppermute | solution.py:21
  87.3 3.9 %collective-permute-start.15 = (f32[8,512]{1,0:T(8,128)}, f32[8,512]{1,0:T(8,128)S(1)}, u32[]{:S(2)}, u32[]{:S(2)}) collective-permute-start(f32[8,512]{1,0:T(8,128)} %merge.2.refs_0_), channel_id=1, source_target_pairs={{8,0},{16,8},{24,16},{0,24},{9,1},{17,9},{25,17},{1,25},{10,2},{18... | collective-permute-start | bytes 49160 | tf_op jit(solution)/shard_map/ppermute | solution.py:21
  89.2 2.1 %copy-start.23 = (f32[8,512]{1,0:T(8,128)}, f32[8,512]{1,0:T(8,128)S(1)}, u32[]{:S(2)}) copy-start(f32[8,512]{1,0:T(8,128)S(1)} %collective-permute-done.17.refs_3_) | copy-start | bytes 49156
  91.7 0.6 copy-start.27
  93.7 1.4 collective-permute-start.18
  95.1 1.5 copy-start.21
  96.6 1.0 copy-start.4
  96.6 1.3 copy-start
  99.3 25.5 %collective-permute-start.22 = (bf16[1024,512]{1,0:T(8,128)(2,1)}, bf16[1024,512]{1,0:T(8,128)(2,1)S(1)}, u32[]{:S(2)}, u32[]{:S(2)}) collective-permute-start(bf16[1024,512]{1,0:T(8,128)(2,1)} %get-tuple-element.35.e1), channel_id=1, source_target_pairs={{3,0},{0,1},{1,2},{2,3},{7,4},{4,5},{5,6},{6,7},{11,8},{8,9},{9,10... | collective-permute-start | bytes 3145736 | tf_op jit(solution)/shard_map/ppermute | solution.py:21
  100.2 24.6 %collective-permute-start.21 = (bf16[1024,512]{1,0:T(8,128)(2,1)}, bf16[1024,512]{1,0:T(8,128)(2,1)S(1)}, u32[]{:S(2)}, u32[]{:S(2)}) collective-permute-start(bf16[1024,512]{1,0:T(8,128)(2,1)} %get-tuple-element.35.e1), channel_id=1, source_target_pairs={{1,0},{2,1},{3,2},{0,3},{5,4},{6,5},{7,6},{4,7},{9,8},{10,9},{11,1... | collective-permute-start | bytes 3145736 | tf_op jit(solution)/shard_map/ppermute | solution.py:21
  124.8 1.0 copy-start.2
  124.8 1.4 copy-start.5
  126.2 9.2 %copy-start.6 = (f32[4,4,256,256]{3,2,1,0:T(8,128)S(1)}, f32[4,4,256,256]{3,2,1,0:T(8,128)}, u32[]{:S(2)}) copy-start(f32[4,4,256,256]{3,2,1,0:T(8,128)} %get-tuple-element.37) | copy-start | bytes 12582916
  126.2 7.9 %collective-permute-start.23 = (bf16[2,4,256,256]{3,2,1,0:T(8,128)(2,1)}, bf16[2,4,256,256]{3,2,1,0:T(8,128)(2,1)S(1)}, u32[]{:S(2)}, u32[]{:S(2)}) collective-permute-start(bf16[2,4,256,256]{3,2,1,0:T(8,128)(2,1)} %get-tuple-element.40), channel_id=1, source_target_pairs={{0,4},{4,0},{1,5},{5,1},{2,6},{6,2},{3,7},{7,3},{8,12},{12,8},{9,1... | collective-permute-start | bytes 3145736 | tf_op jit(solution)/shard_map/ppermute | solution.py:25
  126.2 7.9 %collective-permute-start.24 = (bf16[2,4,256,256]{3,2,1,0:T(8,128)(2,1)}, bf16[2,4,256,256]{3,2,1,0:T(8,128)(2,1)S(1)}, u32[]{:S(2)}, u32[]{:S(2)}) collective-permute-start(bf16[2,4,256,256]{3,2,1,0:T(8,128)(2,1)} %get-tuple-element.41), channel_id=1, source_target_pairs={{0,4},{4,0},{1,5},{5,1},{2,6},{6,2},{3,7},{7,3},{8,12},{12,8},{9,1... | collective-permute-start | bytes 3145736 | tf_op jit(solution)/shard_map/ppermute | solution.py:25
  126.7 5.5 %collective-permute-start.27 = (f32[8,512]{1,0:T(8,128)}, f32[8,512]{1,0:T(8,128)S(1)}, u32[]{:S(2)}, u32[]{:S(2)}) collective-permute-start(f32[8,512]{1,0:T(8,128)} %get-tuple-element.42), channel_id=1, source_target_pairs={{2,0},{3,1},{0,2},{1,3},{6,4},{7,5},{4,6},{5,7},{10,8},{11,9},{8,1... | collective-permute-start | bytes 49160 | tf_op jit(solution)/shard_map/ppermute | solution.py:21
  128.6 5.2 %collective-permute-start.26 = (f32[8,512]{1,0:T(8,128)}, f32[8,512]{1,0:T(8,128)S(1)}, u32[]{:S(2)}, u32[]{:S(2)}) collective-permute-start(f32[8,512]{1,0:T(8,128)} %get-tuple-element.42), channel_id=1, source_target_pairs={{3,0},{0,1},{1,2},{2,3},{7,4},{4,5},{5,6},{6,7},{11,8},{8,9},{9,10... | collective-permute-start | bytes 49160 | tf_op jit(solution)/shard_map/ppermute | solution.py:21
  130.1 3.9 %collective-permute-start.25 = (f32[8,512]{1,0:T(8,128)}, f32[8,512]{1,0:T(8,128)S(1)}, u32[]{:S(2)}, u32[]{:S(2)}) collective-permute-start(f32[8,512]{1,0:T(8,128)} %get-tuple-element.42), channel_id=1, source_target_pairs={{1,0},{2,1},{3,2},{0,3},{5,4},{6,5},{7,6},{4,7},{9,8},{10,9},{11,1... | collective-permute-start | bytes 49160 | tf_op jit(solution)/shard_map/ppermute | solution.py:21
  132.1 1.9 %copy-start.20 = (f32[8,512]{1,0:T(8,128)}, f32[8,512]{1,0:T(8,128)S(1)}, u32[]{:S(2)}) copy-start(f32[8,512]{1,0:T(8,128)S(1)} %collective-permute-done.27.refs_4_) | copy-start | bytes 49156
  133.8 0.6 copy-start.18
  134.1 1.0 copy-start.7
  134.1 1.3 copy-start.9
  135.4 5.7 %copy-start.1 = (bf16[1024,512]{1,0:T(8,128)(2,1)S(1)}, bf16[1024,512]{1,0:T(8,128)(2,1)}, u32[]{:S(2)}) copy-start(bf16[1024,512]{1,0:T(8,128)(2,1)} %get-tuple-element.47.refs_0_.refs_1_) | copy-start | bytes 3145732
  135.4 8.3 %copy-start.3 = (bf16[1024,512]{1,0:T(8,128)(2,1)S(1)}, bf16[1024,512]{1,0:T(8,128)(2,1)}, u32[]{:S(2)}) copy-start(bf16[1024,512]{1,0:T(8,128)(2,1)} %get-tuple-element.49.refs_6_.refs_7_) | copy-start | bytes 3145732
  138.3 19.3 %collective-permute-start.30 = (bf16[4,256,256]{2,1,0:T(8,128)(2,1)}, bf16[4,256,256]{2,1,0:T(8,128)(2,1)}, u32[]{:S(2)}, u32[]{:S(2)}) collective-permute-start(bf16[4,256,256]{2,1,0:T(8,128)(2,1)} %get-tuple-element.61), channel_id=1, source_target_pairs={{32,0},{12,4},{40,8},{20,12},{48,16},{28,20},{56,24},{4,28},{64,32... | collective-permute-start | bytes 1572872 | tf_op jit(solution)/shard_map/ppermute | solution.py:36
  139.9 17.7 %collective-permute-start.29 = (bf16[4,256,256]{2,1,0:T(8,128)(2,1)}, bf16[4,256,256]{2,1,0:T(8,128)(2,1)}, u32[]{:S(2)}, u32[]{:S(2)}) collective-permute-start(bf16[4,256,256]{2,1,0:T(8,128)(2,1)} %get-tuple-element.62), channel_id=1, source_target_pairs={{64,0},{20,4},{72,8},{28,12},{80,16},{4,20},{88,24},{12,28},{96,32... | collective-permute-start | bytes 1572872 | tf_op jit(solution)/shard_map/ppermute | solution.py:36
  139.9 17.6 %collective-permute-start.28 = (bf16[4,256,256]{2,1,0:T(8,128)(2,1)}, bf16[4,256,256]{2,1,0:T(8,128)(2,1)}, u32[]{:S(2)}, u32[]{:S(2)}) collective-permute-start(bf16[4,256,256]{2,1,0:T(8,128)(2,1)} %get-tuple-element.63), channel_id=1, source_target_pairs={{96,0},{28,4},{104,8},{4,12},{112,16},{12,20},{120,24},{20,28},{0,... | collective-permute-start | bytes 1572872 | tf_op jit(solution)/shard_map/ppermute | solution.py:36
  141.1 29.7 %collective-permute-start.35 = (bf16[1024,512]{1,0:T(8,128)(2,1)S(1)}, bf16[1024,512]{1,0:T(8,128)(2,1)S(1)}, u32[]{:S(2)}, u32[]{:S(2)}) collective-permute-start(bf16[1024,512]{1,0:T(8,128)(2,1)S(1)} %copy-done.1), channel_id=1, source_target_pairs={{1,0},{2,1},{3,2},{0,3},{5,4},{6,5},{7,6},{4,7},{9,8},{10,9},{11,1... | collective-permute-start | bytes 3145736 | tf_op jit(solution)/shard_map/ppermute | solution.py:21
  143.7 27.1 %collective-permute-start.36 = (bf16[1024,512]{1,0:T(8,128)(2,1)S(1)}, bf16[1024,512]{1,0:T(8,128)(2,1)}, u32[]{:S(2)}, u32[]{:S(2)}) collective-permute-start(bf16[1024,512]{1,0:T(8,128)(2,1)S(1)} %copy-done.3), channel_id=1, source_target_pairs={{3,0},{0,1},{1,2},{2,3},{7,4},{4,5},{5,6},{6,7},{11,8},{8,9},{9,10... | collective-permute-start | bytes 3145736 | tf_op jit(solution)/shard_map/ppermute | solution.py:21
  157.5 1.2 copy-start.8
  160.8 6.2 %collective-permute-start.31 = (bf16[256,256]{1,0:T(8,128)(2,1)S(1)}, bf16[256,256]{1,0:T(8,128)(2,1)S(1)}, u32[]{:S(2)}, u32[]{:S(2)}) collective-permute-start(bf16[256,256]{1,0:T(8,128)(2,1)S(1)} %get-tuple-element.64), channel_id=1, source_target_pairs={{24,0},{100,4},{0,8},{108,12},{8,16},{116,20},{16,24},{124,28},{56... | collective-permute-start | bytes 393224 | tf_op jit(solution)/shard_map/ppermute | solution.py:36
  163.3 5.0 %collective-permute-start.33 = (bf16[256,256]{1,0:T(8,128)(2,1)S(1)}, bf16[256,256]{1,0:T(8,128)(2,1)S(1)}, u32[]{:S(2)}, u32[]{:S(2)}) collective-permute-start(bf16[256,256]{1,0:T(8,128)(2,1)S(1)} %get-tuple-element.65), channel_id=1, source_target_pairs={{8,0},{36,4},{16,8},{44,12},{24,16},{52,20},{0,24},{60,28},{40,32}... | collective-permute-start | bytes 393224 | tf_op jit(solution)/shard_map/ppermute | solution.py:36
  164.1 6.5 %collective-permute-start.32 = (bf16[256,256]{1,0:T(8,128)(2,1)S(1)}, bf16[256,256]{1,0:T(8,128)(2,1)S(1)}, u32[]{:S(2)}, u32[]{:S(2)}) collective-permute-start(bf16[256,256]{1,0:T(8,128)(2,1)S(1)} %get-tuple-element.66), channel_id=1, source_target_pairs={{16,0},{68,4},{24,8},{76,12},{0,16},{84,20},{8,24},{92,28},{48,32}... | collective-permute-start | bytes 393224 | tf_op jit(solution)/shard_map/ppermute | solution.py:36
  170.7 11.4 %collective-permute-start.34 = (f32[256,128]{1,0:T(8,128)S(1)}, f32[256,128]{1,0:T(8,128)S(1)}, u32[]{:S(2)}, u32[]{:S(2)}) collective-permute-start(f32[256,128]{1,0:T(8,128)S(1)} %get-tuple-element.68), channel_id=1, source_target_pairs={{0,4},{4,0},{1,5},{5,1},{2,6},{6,2},{3,7},{7,3},{8,12},{12,8},{9,1... | collective-permute-start | bytes 393224 | tf_op jit(solution)/shard_map/ppermute | solution.py:25
  170.8 1.0 copy-start.10
  (2 other events, 1.2 us)
Sparse Core Ops, SparseCore 0:
  59.6 55.4 all-gather.2

commit v4 on v3

--- a/solution.py
+++ b/solution.py
@@ -70,26 +70,14 @@
     )(*arrays)
 
 
-CUT = 1024
+CUT = VOC // 2
 SUB = 256
 
 
-def sub_specs():
-    low = [pl.BlockSpec((SUB, ROWS), lambda i, at, k=k: (jnp.minimum(2 * i + k, CUT // SUB - 1), 0)) for k in (0, 1)]
-    high = [pl.BlockSpec((SUB, ROWS), lambda i, at, k=k: (jnp.maximum(2 * i + k - CUT // SUB, 0), 0)) for k in (0, 1)]
-    return low + high
-
-
-def pick(i, low0, low1, high0, high1):
-    n = CUT // SUB
-    return jnp.concatenate(
-        [jnp.where(2 * i < n, low0[...], high0[...]), jnp.where(2 * i + 1 < n, low1[...], high1[...])], axis=0
-    )
-
-
-def gather_pieces(block):
-    s = jnp.stack([block] + [cross(block, 0, d) for d in (1, 2, 3)])
-    return [s] + [cross(s, 1, d) for d in (1, 2, 3)]
+def gather_pieces(block, other):
+    *ring, other = gate(*(cross(block, 0, d) for d in (1, 2, 3)), other)
+    s = jnp.stack([block, *ring])
+    return [s] + [cross(s, 1, d) for d in (1, 2, 3)], other
 
 
 def logits_body(at, *refs):
@@ -331,89 +319,53 @@
     return jnp.where(c == 0, jnp.concatenate([mine, got]), jnp.concatenate([got, mine])), acc
 
 
-def quarter_copies(at, feats, offsets, q, sem):
-    copies = []
-    for n, d in enumerate(offsets):
+def embed_body(base, at, tgt, ep, em, ed, pack_p, pack_m, pack_d, feats, *refs):
+    out, q, sem = refs[-3:]
+    i = pl.program_id(0)
+
+    def copies(n, d):
         group = (at[3] + d) & 3
         for k in range(8):
             dst = q.at[pl.ds(n * ROWS, ROWS), pl.ds(k * 128, 128)]
-            copies.append(pltpu.make_async_copy(feats.at[group, k // 2, k % 2], dst, sem.at[n * 8 + k]))
-    return copies
-
-
-def embed_a_body(at, tgt, *refs):
-    ep, em, (pack_p, pack_m, feats, acc, q, sem) = refs[:4], refs[4:8], refs[8:]
-    i = pl.program_id(0)
+            yield pltpu.make_async_copy(feats.at[group, k // 2, k % 2], dst, sem.at[n * 8 + k])
 
     @pl.when(i == 0)
     def _():
-        copies = quarter_copies(at, feats, (0, 1, 3), q, sem)
-        for copy in copies:
-            copy.start()
-        for copy in copies:
-            copy.wait()
+        for n, d in enumerate((0, 1, 3, 2)):
+            for copy in copies(n, d):
+                copy.start()
+        for n, d in enumerate((0, 1, 3, 2)):
+            for copy in copies(n, d):
+                copy.wait()
 
     parts = [tgt[...]]
-    for e, pack in ((pick(i, *ep), pack_p), (pick(i, *em), pack_m)):
-        parts.append(token_grad(e, pack, pack[pl.ds(i, 1), :], i * TILE))
-    acc[...] = dot_nn(jnp.concatenate(parts, axis=1), q[...])
-
-
-def embed_a_call(at, tgt, ep0, ep1, em0, em1, pack_p, pack_m, feats):
+    tile = base // TILE + i
+    for e, pack in ((ep, pack_p), (em, pack_m), (ed, pack_d)):
+        parts.append(token_grad(e[...], pack, pack[pl.ds(tile, 1), :], tile * TILE))
+    out[...] = dot_nn(jnp.concatenate(parts, axis=1), q[...]).astype(BF)
+
+
+def embed_call(at, base, tgt, ep, em, ed, packs, feats, into, name):
+    first = base // TILE
     tile = pl.BlockSpec((TILE, ROWS), lambda i, at: (i, 0))
     pack = pl.BlockSpec((8, ROWS), lambda i, at: (0, 0))
-    return pl.pallas_call(
-        embed_a_body,
+    more = [] if into is None else [into]
+    return pl.pallas_call(
+        functools.partial(embed_body, base),
         grid_spec=pltpu.PrefetchScalarGridSpec(
             num_scalar_prefetch=1,
-            grid=(TILES,),
-            in_specs=[tile, *sub_specs(), *sub_specs(), pack, pack, HBM],
-            out_specs=pl.BlockSpec((TILE, 1024), lambda i, at: (i, 0)),
-            scratch_shapes=[pltpu.VMEM((3 * ROWS, 1024), BF), pltpu.SemaphoreType.DMA((24,))],
-        ),
-        out_shape=jax.ShapeDtypeStruct((VOC, 1024), F32),
-        compiler_params=params(),
-        cost_estimate=SMALL,
-        name="embed_a",
-    )(at, tgt, ep0, ep0, ep1, ep1, em0, em0, em1, em1, pack_p, pack_m, feats)
-
-
-def embed_b_body(at, acc, ea0, ea1, eb0, eb1, pack_d, feats, out, q, sem):
-    i = pl.program_id(0)
-
-    @pl.when(i == 0)
-    def _():
-        copies = quarter_copies(at, feats, (2,), q, sem)
-        for copy in copies:
-            copy.start()
-        for copy in copies:
-            copy.wait()
-
-    g = token_grad(pick(i, ea0, ea1, eb0, eb1), pack_d, pack_d[pl.ds(i, 1), :], i * TILE)
-    out[...] = (acc[...] + dot_nn(g, q[...])).astype(BF)
-
-
-def embed_b_call(at, acc, ea, eb, pack_d, feats):
-    tile = pl.BlockSpec((TILE, 1024), lambda i, at: (i, 0))
-    return pl.pallas_call(
-        embed_b_body,
-        grid_spec=pltpu.PrefetchScalarGridSpec(
-            num_scalar_prefetch=1,
-            grid=(TILES,),
-            in_specs=[
-                tile,
-                *sub_specs(),
-                pl.BlockSpec((8, ROWS), lambda i, at: (0, 0)),
-                HBM,
-            ],
-            out_specs=tile,
-            scratch_shapes=[pltpu.VMEM((ROWS, 1024), BF), pltpu.SemaphoreType.DMA((8,))],
+            grid=(CUT // TILE,),
+            in_specs=[pl.BlockSpec((TILE, ROWS), lambda i, at: (i + first, 0)), tile, tile, tile, pack, pack, pack, HBM]
+            + [HBM] * len(more),
+            out_specs=pl.BlockSpec((TILE, 1024), lambda i, at: (i + first, 0)),
+            scratch_shapes=[pltpu.VMEM((4 * ROWS, 1024), BF), pltpu.SemaphoreType.DMA((32,))],
         ),
         out_shape=jax.ShapeDtypeStruct((VOC, 1024), BF),
-        compiler_params=params(),
-        cost_estimate=SMALL,
-        name="embed_b",
-    )(at, acc, ea, ea, eb, eb, pack_d, feats)
+        input_output_aliases={9: 0} if more else {},
+        compiler_params=params(),
+        cost_estimate=SMALL,
+        name=name,
+    )(at, tgt, ep, em, ed, *packs, feats, *more)
 
 
 def local(comp_hidden, embed, mix, targets, weight):
@@ -429,7 +381,7 @@
     mine, other = jnp.where(c == 0, low, high), jnp.where(c == 0, high, low)
     got = sibling(other)
     block = jnp.where(c == 0, jnp.concatenate([mine, got], axis=1), jnp.concatenate([got, mine], axis=1))
-    pieces = gather_pieces(block)
+    pieces, turned = gather_pieces(block, turned)
     pieces = pieces + [sibling(p) for p in pieces]
 
     e0, e1, st, loc, turned = logits_call(at, pieces, tid, embed, turned)
@@ -439,17 +391,16 @@
     s = merge_call(loc, *(shift(loc, "x", d) for d in (1, 2, 3)))
     s = merge_call(s, *(shift(s, "z", d) for d in (1, 2, 3)))
     pack, grad_mix, e1 = finish_call(s, sibling(s), st, tid, mix, weight.reshape(1, 128), ep0, em0, e1)
-    ep1, em1 = shift(e1, "y", 1), shift(e1, "y", 3)
+    packs = [shift(pack, "y", d) for d in (1, 3, 2)]
+    em1, ed0 = shift(e1, "y", 3), shift(ep0, "y", 1)
     keep, send0, send1, tgt = hidden_call(at, e0, e1, pack, embed)
-    send0, send1, pack, ep1, em1 = gate(send0, send1, pack, ep1, em1)
-    recv0, recv1, pack_p, pack_m, pack_d, ep0, em1 = gate(
-        sibling(send0), sibling(send1), *(shift(pack, "y", d) for d in (1, 3, 2)), ep0, em1
-    )
-    diag = shift(ep0, "y", 1), shift(em1, "y", 3)
-
-    acc = embed_a_call(at, tgt, ep0, ep1, em0, em1, pack_p, pack_m, feats)
-    grad_hidden, acc = scatter(keep, (recv0, recv1), c, acc)
-    grad_embed = embed_b_call(at, acc, *diag, pack_d, feats)
+    send0, send1, e1, em1, ed0, *packs = gate(send0, send1, e1, em1, ed0, *packs)
+    ep1, ed1 = shift(e1, "y", 1), shift(em1, "y", 3)
+    recv = sibling(send0), sibling(send1)
+
+    grad_embed = embed_call(at, 0, tgt, ep0, em0, ed0, packs, feats, None, "embed_a")
+    grad_hidden, grad_embed = scatter(keep, recv, c, grad_embed)
+    grad_embed = embed_call(at, CUT, tgt, ep1, em1, ed1, packs, feats, grad_embed, "embed_b")
     return grad_hidden.reshape(4, 128, 128), grad_embed, grad_mix
 
 

time: 192 us -> 183 us (0.953)
  starting transfers between devices: 58.6 us -> 43.4 us
  waiting for transfers between devices: 36.8 us -> 49.4 us
  Pallas kernels: 63.3 us -> 59.9 us
  local copies, waits for them, and re-layouts: 8.72 us -> 6.5 us
    ppermute x15, starting transfers between devices: 35.2 us -> 17.1 us  [shift(): return lax.ppermute(a, axis, [((i + d) % 4, i) for i in range(4)])]
    ppermute x15, waiting for transfers between devices: 14.5 us -> 21.2 us  [shift(): return lax.ppermute(a, axis, [((i + d) % 4, i) for i in range(4)])]
    ppermute x12, starting transfers between devices: 20.7 us -> 24 us  [cross(): return lax.ppermute(a, ('x', 'z', 'c'), pairs)]
    ppermute x9, waiting for transfers between devices: 2.65 us -> 5.87 us  [sibling(): return lax.ppermute(a, 'c', [(0, 1), (1, 0)])]
    pallas_call x2, Pallas kernels: 24.1 us -> 20.9 us  [embed_call(): pl.pallas_call(functools.partial(embed_body, base), grid_spec=pltpu.Prefe...]
    ppermute x12, waiting for transfers between devices: 19.6 us -> 22.3 us  [cross(): return lax.ppermute(a, ('x', 'z', 'c'), pairs)]
    unnamed x56 -> x62, local copies, waits for them, and re-layouts: 8.04 us -> 5.94 us
  transfers between devices with their start and end apart: 38 -> 38, of which waited for: 20 -> 24; matrix products, arithmetic and copies ran while one was open for 3% -> 3% of each run, Pallas kernels for 24% -> 23%
where the time goes in v4:
time: 183 us; the launch traced here: 181 us
  Pallas kernels  59.9 us (33%)
  waiting for transfers between devices  49.4 us (27%)
  starting transfers between devices  43.4 us (24%)
  between operations  14.4 us (8%)
  other arithmetic  7.73 us (4%)
  local copies, waits for them, and re-layouts  6.5 us (4%)
    ppermute x12, starting transfers between devices, cross(): return lax.ppermute(a, ('x', 'z', 'c'), pairs)  24 us
    ppermute x12, waiting for transfers between devices, cross(): return lax.ppermute(a, ('x', 'z', 'c'), pairs)  22.3 us
    ppermute x15, waiting for transfers between devices, shift(): return lax.ppermute(a, axis, [((i + d) % 4, i) for i in range(4)])  21.2 us
    pallas_call x2, Pallas kernels, embed_call(): pl.pallas_call(functools.partial(embed_body, base), grid_spec=pltpu.Prefe...  20.9 us
    pallas_call x1, Pallas kernels, logits_call(): pl.pallas_call(logits_body, grid_spec=pltpu.PrefetchScalarGridSpec(num_sc...  17.9 us
    ppermute x15, starting transfers between devices, shift(): return lax.ppermute(a, axis, [((i + d) % 4, i) for i in range(4)])  17.1 us
    pallas_call x1, Pallas kernels, hidden_call(): pl.pallas_call(hidden_body, grid_spec=pltpu.PrefetchScalarGridSpec(num_sc...  16.9 us
    unnamed x62, local copies, waits for them, and re-layouts  5.94 us
  transfers between devices with their start and end apart: 38, of which 24 were waited for; matrix products, arithmetic and copies ran while one was open for 3% of the time, Pallas kernels for 23%

profile of v4, /device:TPU:0, one launch (start us, length us, event | category | flops | bytes accessed | tf_op | source)
XLA Modules:
  0.0 181.3 jit_solution(1122604646274194910)
XLA Ops:
  7.2 0.9 broadcast_select_fusion.1
  8.2 1.6 collective-permute-start.4
  9.8 6.2 %collective-permute-start.1 = (bf16[256,256]{1,0:T(8,128)(2,1)S(1)}, bf16[256,256]{1,0:T(8,128)(2,1)S(1)}, u32[]{:S(2)}, u32[]{:S(2)}) collective-permute-start(bf16[256,256]{1,0:T(8,128)(2,1)S(1)} %maximum_select_fusion.2), channel_id=1, source_target_pairs={{32,0},{12,4},{40,8},{20,12},{48,16},{28,20},{56,24},{4,28},{64,32... | collective-permute-start | bytes 393224 | tf_op jit(solution)/shard_map/ppermute | solution.py:36
  16.0 0.6 collective-permute-start.2
  16.6 1.3 collective-permute-start.3
  18.0 0.7 collective-permute-done.1.refs_0_
  18.7 3.8 %collective-permute-done.2.refs_1_ = bf16[256,256]{1,0:T(8,128)(2,1)S(1)} collective-permute-done((bf16[256,256]{1,0:T(8,128)(2,1)S(1)}, bf16[256,256]{1,0:T(8,128)(2,1)S(1)}, u32[]{:S(2)}, u32[]{:S(2)}) %collective-permute-start.2) | collective-permute-done | bytes 131104 | tf_op jit(solution)/shard_map/ppermute | solution.py:36
  22.5 3.1 %collective-permute-done.3.refs_2_ = bf16[256,256]{1,0:T(8,128)(2,1)S(1)} collective-permute-done((bf16[256,256]{1,0:T(8,128)(2,1)S(1)}, bf16[256,256]{1,0:T(8,128)(2,1)S(1)}, u32[]{:S(2)}, u32[]{:S(2)}) %collective-permute-start.3) | collective-permute-done | bytes 131104 | tf_op jit(solution)/shard_map/ppermute | solution.py:36
  25.6 0.6 copy-done.20
  26.2 1.1 pad_maximum_fusion.refs_0_
  27.3 4.0 %collective-permute-start.6 = (bf16[4,256,256]{2,1,0:T(8,128)(2,1)S(1)}, bf16[4,256,256]{2,1,0:T(8,128)(2,1)S(1)}, u32[]{:S(2)}, u32[]{:S(2)}) collective-permute-start(bf16[4,256,256]{2,1,0:T(8,128)(2,1)S(1)} %pad_maximum_fusion.refs_0_), channel_id=1, source_target_pairs={{16,0},{68,4},{24,8},{76,12},{0,16},{84,20},{8,24},{92,28},{48,32}... | collective-permute-start | bytes 1572872 | tf_op jit(solution)/shard_map/ppermute | solution.py:36
  31.3 1.0 collective-permute-start.7
  32.3 2.2 %collective-permute-start.5 = (bf16[4,256,256]{2,1,0:T(8,128)(2,1)S(1)}, bf16[4,256,256]{2,1,0:T(8,128)(2,1)S(1)}, u32[]{:S(2)}, u32[]{:S(2)}) collective-permute-start(bf16[4,256,256]{2,1,0:T(8,128)(2,1)S(1)} %pad_maximum_fusion.refs_0_), channel_id=1, source_target_pairs={{8,0},{36,4},{16,8},{44,12},{24,16},{52,20},{0,24},{60,28},{40,32}... | collective-permute-start | bytes 1572872 | tf_op jit(solution)/shard_map/ppermute | solution.py:36
  34.5 4.0 %collective-permute-done.6.refs_2_ = bf16[4,256,256]{2,1,0:T(8,128)(2,1)S(1)} collective-permute-done((bf16[4,256,256]{2,1,0:T(8,128)(2,1)S(1)}, bf16[4,256,256]{2,1,0:T(8,128)(2,1)S(1)}, u32[]{:S(2)}, u32[]{:S(2)}) %collective-permute-start.6) | collective-permute-done | bytes 524320 | tf_op jit(solution)/shard_map/ppermute | solution.py:36
  38.6 5.5 %collective-permute-done.7.refs_3_ = bf16[4,256,256]{2,1,0:T(8,128)(2,1)S(1)} collective-permute-done((bf16[4,256,256]{2,1,0:T(8,128)(2,1)S(1)}, bf16[4,256,256]{2,1,0:T(8,128)(2,1)S(1)}, u32[]{:S(2)}, u32[]{:S(2)}) %collective-permute-start.7) | collective-permute-done | bytes 524320 | tf_op jit(solution)/shard_map/ppermute | solution.py:36
  44.1 1.0 collective-permute-done.5.refs_1_
  45.1 0.7 pad_add_fusion.at
  45.9 0.7 broadcast_subtract_fusion
  46.6 0.6 collective-permute-done.9.refs_5_
  47.2 0.5 tile.2
  47.7 17.9 %logits.1 = (bf16[1024,512]{1,0:T(8,128)(2,1)}, bf16[1024,512]{1,0:T(8,128)(2,1)}, f32[8,512]{1,0:T(8,128)}, f32[8,512]{1,0:T(8,128)}, bf16[512,128]{1,0:T(8,128)(2,1)}) custom-call(s32[4]{0:T(128)} %pad_add_fusion.at, bf16[4,256,256]{2,1,0:T(8,128)(2,1)} %copy-done.7, bf16[4,256,256]{2,1,0:T(8,128)(2,1)} %copy-done.15, ...), custom_call_target="tpu_custom_call", output_to_operand_aliasing={{4}: (11, {})} | custom-call | flops 1000 | bytes 1000 | tf_op jit(solution)/shard_map/logits/pallas_call | solution.py:142
  65.6 2.1 %collective-permute-start.19 = (bf16[1024,512]{1,0:T(8,128)(2,1)}, bf16[1024,512]{1,0:T(8,128)(2,1)S(1)}, u32[]{:S(2)}, u32[]{:S(2)}) collective-permute-start(bf16[1024,512]{1,0:T(8,128)(2,1)} %get-tuple-element.35.e0), channel_id=1, source_target_pairs={{1,0},{2,1},{3,2},{0,3},{5,4},{6,5},{7,6},{4,7},{9,8},{10,9},{11,1... | collective-permute-start | bytes 3145736 | tf_op jit(solution)/shard_map/ppermute | solution.py:21
  67.7 1.7 collective-permute-start.12
  69.5 0.9 collective-permute-start.14
  70.3 1.3 collective-permute-done.12.refs_1_
  71.7 3.2 %collective-permute-done.13.refs_2_ = f32[8,512]{1,0:T(8,128)S(1)} collective-permute-done((f32[8,512]{1,0:T(8,128)}, f32[8,512]{1,0:T(8,128)S(1)}, u32[]{:S(2)}, u32[]{:S(2)}) %collective-permute-start.13) | collective-permute-done | bytes 16416 | tf_op jit(solution)/shard_map/ppermute | solution.py:21
  74.9 0.6 copy-done.27
  75.5 0.6 copy-done.29
  76.1 1.4 merge.2.refs_0_
  77.5 2.6 %collective-permute-start.15 = (f32[8,512]{1,0:T(8,128)}, f32[8,512]{1,0:T(8,128)S(1)}, u32[]{:S(2)}, u32[]{:S(2)}) collective-permute-start(f32[8,512]{1,0:T(8,128)} %merge.2.refs_0_), channel_id=1, source_target_pairs={{8,0},{16,8},{24,16},{0,24},{9,1},{17,9},{25,17},{1,25},{10,2},{18... | collective-permute-start | bytes 49160 | tf_op jit(solution)/shard_map/ppermute | solution.py:21
  80.2 1.2 collective-permute-start.16
  81.8 3.9 %collective-permute-done.16.refs_2_ = f32[8,512]{1,0:T(8,128)S(1)} collective-permute-done((f32[8,512]{1,0:T(8,128)}, f32[8,512]{1,0:T(8,128)S(1)}, u32[]{:S(2)}, u32[]{:S(2)}) %collective-permute-start.16) | collective-permute-done | bytes 16416 | tf_op jit(solution)/shard_map/ppermute | solution.py:21
  85.8 0.9 collective-permute-done.17.refs_3_
  86.7 0.6 copy-done.30
  87.3 1.4 merge.3.a
  88.7 1.4 collective-permute-done.18.b
  90.1 1.0 collective-permute-done.19.ep0.ep
  91.1 2.9 %collective-permute-done.20.em0.em = bf16[1024,512]{1,0:T(8,128)(2,1)S(1)} collective-permute-done((bf16[1024,512]{1,0:T(8,128)(2,1)}, bf16[1024,512]{1,0:T(8,128)(2,1)S(1)}, u32[]{:S(2)}, u32[]{:S(2)}) %collective-permute-start.20) | collective-permute-done | bytes 1048608 | tf_op jit(solution)/shard_map/ppermute | solution.py:21
  94.1 1.0 copy-done.6
  95.1 1.4 finish.1
  96.5 3.2 %collective-permute-start.22 = (bf16[1024,512]{1,0:T(8,128)(2,1)}, bf16[1024,512]{1,0:T(8,128)(2,1)S(1)}, u32[]{:S(2)}, u32[]{:S(2)}) collective-permute-start(bf16[1024,512]{1,0:T(8,128)(2,1)} %copy-done.5), channel_id=1, source_target_pairs={{1,0},{2,1},{3,2},{0,3},{5,4},{6,5},{7,6},{4,7},{9,8},{10,9},{11,1... | collective-permute-start | bytes 3145736 | tf_op jit(solution)/shard_map/ppermute | solution.py:21
  99.8 2.0 %collective-permute-start.24 = (f32[8,512]{1,0:T(8,128)}, f32[8,512]{1,0:T(8,128)S(1)}, u32[]{:S(2)}, u32[]{:S(2)}) collective-permute-start(f32[8,512]{1,0:T(8,128)} %get-tuple-element.40.pack), channel_id=1, source_target_pairs={{3,0},{0,1},{1,2},{2,3},{7,4},{4,5},{5,6},{6,7},{11,8},{8,9},{9,10... | collective-permute-start | bytes 49160 | tf_op jit(solution)/shard_map/ppermute | solution.py:21
  101.8 16.9 %hidden.1 = (f32[4,4,256,256]{3,2,1,0:T(8,128)}, bf16[2,4,256,256]{3,2,1,0:T(8,128)(2,1)}, bf16[2,4,256,256]{3,2,1,0:T(8,128)(2,1)}, bf16[2048,512]{1,0:T(8,128)(2,1)}) custom-call(s32[4]{0:T(128)} %pad_add_fusion.at, bf16[1024,512]{1,0:T(8,128)(2,1)} %get-tuple-element.35.e0, bf16[1024,512]{1,0:T(8,128)(2,1)} %get-tuple-element.39.e1.refs_2_, ...), custom_call_target="tpu_custom_call" | custom-call | flops 1000 | bytes 1000 | tf_op jit(solution)/shard_map/hidden/pallas_call | solution.py:279
  118.7 3.3 %collective-permute-done.23.refs_5_ = f32[8,512]{1,0:T(8,128)S(1)} collective-permute-done((f32[8,512]{1,0:T(8,128)}, f32[8,512]{1,0:T(8,128)S(1)}, u32[]{:S(2)}, u32[]{:S(2)}) %collective-permute-start.23) | collective-permute-done | bytes 16416 | tf_op jit(solution)/shard_map/ppermute | solution.py:21
  122.0 0.7 collective-permute-done.24.refs_6_
  122.8 0.5 copy-done.22
  124.1 0.5 collective-permute-start.28
  124.6 2.4 %collective-permute-done.26 = bf16[2,4,256,256]{3,2,1,0:T(8,128)(2,1)S(1)} collective-permute-done((bf16[2,4,256,256]{3,2,1,0:T(8,128)(2,1)}, bf16[2,4,256,256]{3,2,1,0:T(8,128)(2,1)S(1)}, u32[]{:S(2)}, u32[]{:S(2)}) %collective-permute-start.26) | collective-permute-done | bytes 1048608 | tf_op jit(solution)/shard_map/ppermute | solution.py:25
  126.9 1.5 collective-permute-done.28
  128.4 1.4 fusion.4
  129.9 3.1 %collective-permute-start.29 = (bf16[4,256,256]{2,1,0:T(8,128)(2,1)}, bf16[4,256,256]{2,1,0:T(8,128)(2,1)S(1)}, u32[]{:S(2)}, u32[]{:S(2)}) collective-permute-start(bf16[4,256,256]{2,1,0:T(8,128)(2,1)} %get-tuple-element.62), channel_id=1, source_target_pairs={{64,0},{20,4},{72,8},{28,12},{80,16},{4,20},{88,24},{12,28},{96,32... | collective-permute-start | bytes 1572872 | tf_op jit(solution)/shard_map/ppermute | solution.py:36
  133.1 3.0 %collective-permute-start.35 = (bf16[1024,512]{1,0:T(8,128)(2,1)S(1)}, bf16[1024,512]{1,0:T(8,128)(2,1)}, u32[]{:S(2)}, u32[]{:S(2)}) collective-permute-start(bf16[1024,512]{1,0:T(8,128)(2,1)S(1)} %copy-done), channel_id=1, source_target_pairs={{1,0},{2,1},{3,2},{0,3},{5,4},{6,5},{7,6},{4,7},{9,8},{10,9},{11,1... | collective-permute-start | bytes 3145736 | tf_op jit(solution)/shard_map/ppermute | solution.py:21
  136.1 10.5 %embed_a.1.refs_3_ = bf16[2048,1024]{1,0:T(8,128)(2,1)} custom-call(s32[4]{0:T(128)} %pad_add_fusion.at, bf16[2048,512]{1,0:T(8,128)(2,1)} %get-tuple-element.46.tgt, bf16[1024,512]{1,0:T(8,128)(2,1)} %copy-done.5, bf16[1024,512]{1,0:T(8,128)(2,1)} %copy-done.6, bf16[1024,512]{1,0:T(8,128)(2,1)} %get-tuple-element.47.ed, f32[8,512]{1,0:T(8,128)} %get-tuple-element.48.pack_p, ...), custom_call_target="tpu_custom_call" | custom-call | flops 1000 | bytes 1000 | tf_op jit(solution)/shard_map/embed_a/pallas_call | solution.py:353
  147.7 0.6 copy-done.12
  148.2 2.0 %fusion.8 = (bf16[4,256,256]{2,1,0:T(8,128)(2,1)S(1)}, f32[4,256,256]{2,1,0:T(8,128)S(1)}) fusion(bf16[4,256,256]{2,1,0:T(8,128)(2,1)} %get-tuple-element.54, bf16[4,256,256]{2,1,0:T(8,128)(2,1)} %get-tuple-element.53, bf16[4,256,256]{2,1,0:T(8,128)(2,1)} %get-tuple-element.52, bf16[2,4,256,256]{3,2,1,0:T(8,128)(2,1)S(1)} %copy-done.12, ...), kind=kLoop, calls=%fused_computation.26 | loop fusion | flops 2359296 | bytes 4718592 | tf_op jit(solution)/shard_map/convert.2
  150.3 1.8 %collective-permute-start.31 = (bf16[256,256]{1,0:T(8,128)(2,1)S(1)}, bf16[256,256]{1,0:T(8,128)(2,1)S(1)}, u32[]{:S(2)}, u32[]{:S(2)}) collective-permute-start(bf16[256,256]{1,0:T(8,128)(2,1)S(1)} %get-tuple-element.64), channel_id=1, source_target_pairs={{24,0},{100,4},{0,8},{108,12},{8,16},{116,20},{16,24},{124,28},{56... | collective-permute-start | bytes 393224 | tf_op jit(solution)/shard_map/ppermute | solution.py:36
  152.1 2.3 %collective-permute-start.32 = (bf16[256,256]{1,0:T(8,128)(2,1)S(1)}, bf16[256,256]{1,0:T(8,128)(2,1)S(1)}, u32[]{:S(2)}, u32[]{:S(2)}) collective-permute-start(bf16[256,256]{1,0:T(8,128)(2,1)S(1)} %get-tuple-element.66), channel_id=1, source_target_pairs={{16,0},{68,4},{24,8},{76,12},{0,16},{84,20},{8,24},{92,28},{48,32}... | collective-permute-start | bytes 393224 | tf_op jit(solution)/shard_map/ppermute | solution.py:36
  154.4 1.3 collective-permute-start.33
  155.7 0.8 collective-permute-done.31
  156.5 2.2 %collective-permute-done.32 = bf16[256,256]{1,0:T(8,128)(2,1)S(1)} collective-permute-done((bf16[256,256]{1,0:T(8,128)(2,1)S(1)}, bf16[256,256]{1,0:T(8,128)(2,1)S(1)}, u32[]{:S(2)}, u32[]{:S(2)}) %collective-permute-start.32) | collective-permute-done | bytes 131104 | tf_op jit(solution)/shard_map/ppermute | solution.py:36
  158.8 0.6 collective-permute-done.33
  159.6 3.7 %collective-permute-done.36.ed = bf16[1024,512]{1,0:T(8,128)(2,1)} collective-permute-done((bf16[1024,512]{1,0:T(8,128)(2,1)S(1)}, bf16[1024,512]{1,0:T(8,128)(2,1)}, u32[]{:S(2)}, u32[]{:S(2)}) %collective-permute-start.36) | collective-permute-done | bytes 1048608 | tf_op jit(solution)/shard_map/ppermute | solution.py:21
  163.3 10.5 %embed_b.1 = bf16[2048,1024]{1,0:T(8,128)(2,1)} custom-call(s32[4]{0:T(128)} %pad_add_fusion.at, bf16[2048,512]{1,0:T(8,128)(2,1)} %get-tuple-element.46.tgt, bf16[1024,512]{1,0:T(8,128)(2,1)} %collective-permute-done.35.ep, bf16[1024,512]{1,0:T(8,128)(2,1)} %get-tuple-element.56.em, ...), custom_call_target="tpu_custom_call", output_to_operand_aliasing={{}: (9, {})} | custom-call | flops 1000 | bytes 1000 | tf_op jit(solution)/shard_map/embed_b/pallas_call | solution.py:353
  173.7 0.7 maximum_select_fusion
  (98 shorter events, 3.0 us)
Async XLA Ops:
  7.2 128.9 %all-gather.3.cloned.1.call-start = ((), (), s32[]{:S(2)}) async-start(), calls=%async_computation | async-start | bytes 4325376 | tf_op jit(solution)/shard_map/all_gather | solution.py:388
  8.1 1.7 collective-permute-start
  8.2 9.8 %collective-permute-start.4 = (bf16[512,128]{1,0:T(8,128)(2,1)}, bf16[512,128]{1,0:T(8,128)(2,1)S(1)}, u32[]{:S(2)}, u32[]{:S(2)}) collective-permute-start(bf16[512,128]{1,0:T(8,128)(2,1)} %bitcast.52), channel_id=1, source_target_pairs={{0,0},{1,32},{2,64},{3,96},{32,1},{33,33},{34,65},{35,97},{64,2},{... | collective-permute-start | bytes 393224 | tf_op jit(solution)/shard_map/ppermute | solution.py:378
  9.8 8.9 %collective-permute-start.1 = (bf16[256,256]{1,0:T(8,128)(2,1)S(1)}, bf16[256,256]{1,0:T(8,128)(2,1)S(1)}, u32[]{:S(2)}, u32[]{:S(2)}) collective-permute-start(bf16[256,256]{1,0:T(8,128)(2,1)S(1)} %maximum_select_fusion.2), channel_id=1, source_target_pairs={{32,0},{12,4},{40,8},{20,12},{48,16},{28,20},{56,24},{4,28},{64,32... | collective-permute-start | bytes 393224 | tf_op jit(solution)/shard_map/ppermute | solution.py:36
  16.0 6.5 %collective-permute-start.2 = (bf16[256,256]{1,0:T(8,128)(2,1)S(1)}, bf16[256,256]{1,0:T(8,128)(2,1)S(1)}, u32[]{:S(2)}, u32[]{:S(2)}) collective-permute-start(bf16[256,256]{1,0:T(8,128)(2,1)S(1)} %maximum_select_fusion.2), channel_id=1, source_target_pairs={{64,0},{20,4},{72,8},{28,12},{80,16},{4,20},{88,24},{12,28},{96,32... | collective-permute-start | bytes 393224 | tf_op jit(solution)/shard_map/ppermute | solution.py:36
  16.6 9.0 %collective-permute-start.3 = (bf16[256,256]{1,0:T(8,128)(2,1)S(1)}, bf16[256,256]{1,0:T(8,128)(2,1)S(1)}, u32[]{:S(2)}, u32[]{:S(2)}) collective-permute-start(bf16[256,256]{1,0:T(8,128)(2,1)S(1)} %maximum_select_fusion.2), channel_id=1, source_target_pairs={{96,0},{28,4},{104,8},{4,12},{112,16},{12,20},{120,24},{20,28},{0,... | collective-permute-start | bytes 393224 | tf_op jit(solution)/shard_map/ppermute | solution.py:36
  18.0 7.6 %copy-start.10 = (bf16[512,128]{1,0:T(8,128)(2,1)}, bf16[512,128]{1,0:T(8,128)(2,1)S(1)}, u32[]{:S(2)}) copy-start(bf16[512,128]{1,0:T(8,128)(2,1)S(1)} %collective-permute-done.4.refs_3_) | copy-start | bytes 393220
  18.7 6.9 %copy-start.18 = (bf16[256,256]{1,0:T(8,128)(2,1)}, bf16[256,256]{1,0:T(8,128)(2,1)S(1)}, u32[]{:S(2)}) copy-start(bf16[256,256]{1,0:T(8,128)(2,1)S(1)} %collective-permute-done.1.refs_0_) | copy-start | bytes 393220
  22.5 3.1 %copy-start.19 = (bf16[256,256]{1,0:T(8,128)(2,1)}, bf16[256,256]{1,0:T(8,128)(2,1)S(1)}, u32[]{:S(2)}) copy-start(bf16[256,256]{1,0:T(8,128)(2,1)S(1)} %collective-permute-done.2.refs_1_) | copy-start | bytes 393220
  25.6 0.7 copy-start.20
  27.3 20.4 %copy-start.7 = (bf16[4,256,256]{2,1,0:T(8,128)(2,1)}, bf16[4,256,256]{2,1,0:T(8,128)(2,1)S(1)}, u32[]{:S(2)}) copy-start(bf16[4,256,256]{2,1,0:T(8,128)(2,1)S(1)} %pad_maximum_fusion.refs_0_) | copy-start | bytes 1572868
  27.3 11.2 %collective-permute-start.6 = (bf16[4,256,256]{2,1,0:T(8,128)(2,1)S(1)}, bf16[4,256,256]{2,1,0:T(8,128)(2,1)S(1)}, u32[]{:S(2)}, u32[]{:S(2)}) collective-permute-start(bf16[4,256,256]{2,1,0:T(8,128)(2,1)S(1)} %pad_maximum_fusion.refs_0_), channel_id=1, source_target_pairs={{16,0},{68,4},{24,8},{76,12},{0,16},{84,20},{8,24},{92,28},{48,32}... | collective-permute-start | bytes 1572872 | tf_op jit(solution)/shard_map/ppermute | solution.py:36
  31.3 12.8 %collective-permute-start.7 = (bf16[4,256,256]{2,1,0:T(8,128)(2,1)S(1)}, bf16[4,256,256]{2,1,0:T(8,128)(2,1)S(1)}, u32[]{:S(2)}, u32[]{:S(2)}) collective-permute-start(bf16[4,256,256]{2,1,0:T(8,128)(2,1)S(1)} %pad_maximum_fusion.refs_0_), channel_id=1, source_target_pairs={{24,0},{100,4},{0,8},{108,12},{8,16},{116,20},{16,24},{124,28},{56... | collective-permute-start | bytes 1572872 | tf_op jit(solution)/shard_map/ppermute | solution.py:36
  32.3 12.8 %collective-permute-start.5 = (bf16[4,256,256]{2,1,0:T(8,128)(2,1)S(1)}, bf16[4,256,256]{2,1,0:T(8,128)(2,1)S(1)}, u32[]{:S(2)}, u32[]{:S(2)}) collective-permute-start(bf16[4,256,256]{2,1,0:T(8,128)(2,1)S(1)} %pad_maximum_fusion.refs_0_), channel_id=1, source_target_pairs={{8,0},{36,4},{16,8},{44,12},{24,16},{52,20},{0,24},{60,28},{40,32}... | collective-permute-start | bytes 1572872 | tf_op jit(solution)/shard_map/ppermute | solution.py:36
  34.5 12.0 %collective-permute-start.8 = (bf16[4,256,256]{2,1,0:T(8,128)(2,1)S(1)}, bf16[4,256,256]{2,1,0:T(8,128)(2,1)S(1)}, u32[]{:S(2)}, u32[]{:S(2)}) collective-permute-start(bf16[4,256,256]{2,1,0:T(8,128)(2,1)S(1)} %pad_maximum_fusion.refs_0_), channel_id=1, source_target_pairs={{0,4},{4,0},{1,5},{5,1},{2,6},{6,2},{3,7},{7,3},{8,12},{12,8},{9,1... | collective-permute-start | bytes 1572872 | tf_op jit(solution)/shard_map/ppermute | solution.py:25
  38.6 9.1 %copy-start.13 = (bf16[4,256,256]{2,1,0:T(8,128)(2,1)}, bf16[4,256,256]{2,1,0:T(8,128)(2,1)S(1)}, u32[]{:S(2)}) copy-start(bf16[4,256,256]{2,1,0:T(8,128)(2,1)S(1)} %collective-permute-done.6.refs_2_) | copy-start | bytes 1572868
  38.6 8.0 %collective-permute-start.10 = (bf16[4,256,256]{2,1,0:T(8,128)(2,1)S(1)}, bf16[4,256,256]{2,1,0:T(8,128)(2,1)S(1)}, u32[]{:S(2)}, u32[]{:S(2)}) collective-permute-start(bf16[4,256,256]{2,1,0:T(8,128)(2,1)S(1)} %collective-permute-done.6.refs_2_), channel_id=1, source_target_pairs={{0,4},{4,0},{1,5},{5,1},{2,6},{6,2},{3,7},{7,3},{8,12},{12,8},{9,1... | collective-permute-start | bytes 1572872 | tf_op jit(solution)/shard_map/ppermute | solution.py:25
  44.1 3.6 %copy-start.14 = (bf16[4,256,256]{2,1,0:T(8,128)(2,1)}, bf16[4,256,256]{2,1,0:T(8,128)(2,1)S(1)}, u32[]{:S(2)}) copy-start(bf16[4,256,256]{2,1,0:T(8,128)(2,1)S(1)} %collective-permute-done.7.refs_3_) | copy-start | bytes 1572868
  44.1 2.5 %collective-permute-start.11 = (bf16[4,256,256]{2,1,0:T(8,128)(2,1)S(1)}, bf16[4,256,256]{2,1,0:T(8,128)(2,1)}, u32[]{:S(2)}, u32[]{:S(2)}) collective-permute-start(bf16[4,256,256]{2,1,0:T(8,128)(2,1)S(1)} %collective-permute-done.7.refs_3_), channel_id=1, source_target_pairs={{0,4},{4,0},{1,5},{5,1},{2,6},{6,2},{3,7},{7,3},{8,12},{12,8},{9,1... | collective-permute-start | bytes 1572872 | tf_op jit(solution)/shard_map/ppermute | solution.py:25
  45.1 2.6 %copy-start.15 = (bf16[4,256,256]{2,1,0:T(8,128)(2,1)}, bf16[4,256,256]{2,1,0:T(8,128)(2,1)S(1)}, u32[]{:S(2)}) copy-start(bf16[4,256,256]{2,1,0:T(8,128)(2,1)S(1)} %collective-permute-done.5.refs_1_) | copy-start | bytes 1572868
  45.1 2.0 %collective-permute-start.9 = (bf16[4,256,256]{2,1,0:T(8,128)(2,1)S(1)}, bf16[4,256,256]{2,1,0:T(8,128)(2,1)}, u32[]{:S(2)}, u32[]{:S(2)}) collective-permute-start(bf16[4,256,256]{2,1,0:T(8,128)(2,1)S(1)} %collective-permute-done.5.refs_1_), channel_id=1, source_target_pairs={{0,4},{4,0},{1,5},{5,1},{2,6},{6,2},{3,7},{7,3},{8,12},{12,8},{9,1... | collective-permute-start | bytes 1572872 | tf_op jit(solution)/shard_map/ppermute | solution.py:25
  46.5 1.2 copy-start.16
  46.5 1.2 copy-start.17
  65.6 25.5 %collective-permute-start.19 = (bf16[1024,512]{1,0:T(8,128)(2,1)}, bf16[1024,512]{1,0:T(8,128)(2,1)S(1)}, u32[]{:S(2)}, u32[]{:S(2)}) collective-permute-start(bf16[1024,512]{1,0:T(8,128)(2,1)} %get-tuple-element.35.e0), channel_id=1, source_target_pairs={{1,0},{2,1},{3,2},{0,3},{5,4},{6,5},{7,6},{4,7},{9,8},{10,9},{11,1... | collective-permute-start | bytes 3145736 | tf_op jit(solution)/shard_map/ppermute | solution.py:21
  67.7 26.3 %collective-permute-start.20 = (bf16[1024,512]{1,0:T(8,128)(2,1)}, bf16[1024,512]{1,0:T(8,128)(2,1)S(1)}, u32[]{:S(2)}, u32[]{:S(2)}) collective-permute-start(bf16[1024,512]{1,0:T(8,128)(2,1)} %get-tuple-element.35.e0), channel_id=1, source_target_pairs={{3,0},{0,1},{1,2},{2,3},{7,4},{4,5},{5,6},{6,7},{11,8},{8,9},{9,10... | collective-permute-start | bytes 3145736 | tf_op jit(solution)/shard_map/ppermute | solution.py:21
  67.7 3.9 %collective-permute-start.12 = (f32[8,512]{1,0:T(8,128)}, f32[8,512]{1,0:T(8,128)S(1)}, u32[]{:S(2)}, u32[]{:S(2)}) collective-permute-start(f32[8,512]{1,0:T(8,128)} %get-tuple-element.36.refs_0_), channel_id=1, source_target_pairs={{32,0},{64,32},{96,64},{0,96},{33,1},{65,33},{97,65},{1,97},{34,2}... | collective-permute-start | bytes 49160 | tf_op jit(solution)/shard_map/ppermute | solution.py:21
  69.5 5.5 %collective-permute-start.13 = (f32[8,512]{1,0:T(8,128)}, f32[8,512]{1,0:T(8,128)S(1)}, u32[]{:S(2)}, u32[]{:S(2)}) collective-permute-start(f32[8,512]{1,0:T(8,128)} %get-tuple-element.36.refs_0_), channel_id=1, source_target_pairs={{64,0},{96,32},{0,64},{32,96},{65,1},{97,33},{1,65},{33,97},{66,2}... | collective-permute-start | bytes 49160 | tf_op jit(solution)/shard_map/ppermute | solution.py:21
  69.5 5.5 %collective-permute-start.14 = (f32[8,512]{1,0:T(8,128)}, f32[8,512]{1,0:T(8,128)S(1)}, u32[]{:S(2)}, u32[]{:S(2)}) collective-permute-start(f32[8,512]{1,0:T(8,128)} %get-tuple-element.36.refs_0_), channel_id=1, source_target_pairs={{96,0},{0,32},{32,64},{64,96},{97,1},{1,33},{33,65},{65,97},{98,2}... | collective-permute-start | bytes 49160 | tf_op jit(solution)/shard_map/ppermute | solution.py:21
  71.7 3.3 %copy-start.25 = (f32[8,512]{1,0:T(8,128)}, f32[8,512]{1,0:T(8,128)S(1)}, u32[]{:S(2)}) copy-start(f32[8,512]{1,0:T(8,128)S(1)} %collective-permute-done.12.refs_1_) | copy-start | bytes 49156
  77.5 4.3 %collective-permute-start.15 = (f32[8,512]{1,0:T(8,128)}, f32[8,512]{1,0:T(8,128)S(1)}, u32[]{:S(2)}, u32[]{:S(2)}) collective-permute-start(f32[8,512]{1,0:T(8,128)} %merge.2.refs_0_), channel_id=1, source_target_pairs={{8,0},{16,8},{24,16},{0,24},{9,1},{17,9},{25,17},{1,25},{10,2},{18... | collective-permute-start | bytes 49160 | tf_op jit(solution)/shard_map/ppermute | solution.py:21
  80.2 5.6 %collective-permute-start.16 = (f32[8,512]{1,0:T(8,128)}, f32[8,512]{1,0:T(8,128)S(1)}, u32[]{:S(2)}, u32[]{:S(2)}) collective-permute-start(f32[8,512]{1,0:T(8,128)} %merge.2.refs_0_), channel_id=1, source_target_pairs={{16,0},{24,8},{0,16},{8,24},{17,1},{25,9},{1,17},{9,25},{18,2},{26... | collective-permute-start | bytes 49160 | tf_op jit(solution)/shard_map/ppermute | solution.py:21
  81.4 5.3 %collective-permute-start.17 = (f32[8,512]{1,0:T(8,128)}, f32[8,512]{1,0:T(8,128)S(1)}, u32[]{:S(2)}, u32[]{:S(2)}) collective-permute-start(f32[8,512]{1,0:T(8,128)} %merge.2.refs_0_), channel_id=1, source_target_pairs={{24,0},{0,8},{8,16},{16,24},{25,1},{1,9},{9,17},{17,25},{26,2},{2,... | collective-permute-start | bytes 49160 | tf_op jit(solution)/shard_map/ppermute | solution.py:21
  81.8 4.9 %copy-start.26 = (f32[8,512]{1,0:T(8,128)}, f32[8,512]{1,0:T(8,128)S(1)}, u32[]{:S(2)}) copy-start(f32[8,512]{1,0:T(8,128)S(1)} %collective-permute-done.15.refs_1_) | copy-start | bytes 49156
  85.8 0.9 copy-start.28
  88.7 1.4 collective-permute-start.18
  90.1 4.0 %copy-start.24 = (f32[8,512]{1,0:T(8,128)}, f32[8,512]{1,0:T(8,128)S(1)}, u32[]{:S(2)}) copy-start(f32[8,512]{1,0:T(8,128)S(1)} %collective-permute-done.18.b) | copy-start | bytes 49156
  91.1 2.9 %copy-start.5 = (bf16[1024,512]{1,0:T(8,128)(2,1)}, bf16[1024,512]{1,0:T(8,128)(2,1)S(1)}, u32[]{:S(2)}) copy-start(bf16[1024,512]{1,0:T(8,128)(2,1)S(1)} %collective-permute-done.19.ep0.ep) | copy-start | bytes 3145732
  94.1 1.0 copy-start.6
  96.5 26.2 %collective-permute-start.21 = (bf16[1024,512]{1,0:T(8,128)(2,1)}, bf16[1024,512]{1,0:T(8,128)(2,1)S(1)}, u32[]{:S(2)}, u32[]{:S(2)}) collective-permute-start(bf16[1024,512]{1,0:T(8,128)(2,1)} %get-tuple-element.39.e1.refs_2_), channel_id=1, source_target_pairs={{3,0},{0,1},{1,2},{2,3},{7,4},{4,5},{5,6},{6,7},{11,8},{8,9},{9,10... | collective-permute-start | bytes 3145736 | tf_op jit(solution)/shard_map/ppermute | solution.py:21
  96.5 26.2 %collective-permute-start.22 = (bf16[1024,512]{1,0:T(8,128)(2,1)}, bf16[1024,512]{1,0:T(8,128)(2,1)S(1)}, u32[]{:S(2)}, u32[]{:S(2)}) collective-permute-start(bf16[1024,512]{1,0:T(8,128)(2,1)} %copy-done.5), channel_id=1, source_target_pairs={{1,0},{2,1},{3,2},{0,3},{5,4},{6,5},{7,6},{4,7},{9,8},{10,9},{11,1... | collective-permute-start | bytes 3145736 | tf_op jit(solution)/shard_map/ppermute | solution.py:21
  99.8 22.3 %collective-permute-start.23 = (f32[8,512]{1,0:T(8,128)}, f32[8,512]{1,0:T(8,128)S(1)}, u32[]{:S(2)}, u32[]{:S(2)}) collective-permute-start(f32[8,512]{1,0:T(8,128)} %get-tuple-element.40.pack), channel_id=1, source_target_pairs={{1,0},{2,1},{3,2},{0,3},{5,4},{6,5},{7,6},{4,7},{9,8},{10,9},{11,1... | collective-permute-start | bytes 49160 | tf_op jit(solution)/shard_map/ppermute | solution.py:21
  99.8 22.9 %collective-permute-start.24 = (f32[8,512]{1,0:T(8,128)}, f32[8,512]{1,0:T(8,128)S(1)}, u32[]{:S(2)}, u32[]{:S(2)}) collective-permute-start(f32[8,512]{1,0:T(8,128)} %get-tuple-element.40.pack), channel_id=1, source_target_pairs={{3,0},{0,1},{1,2},{2,3},{7,4},{4,5},{5,6},{6,7},{11,8},{8,9},{9,10... | collective-permute-start | bytes 49160 | tf_op jit(solution)/shard_map/ppermute | solution.py:21
  101.8 21.0 %collective-permute-start.25 = (f32[8,512]{1,0:T(8,128)}, f32[8,512]{1,0:T(8,128)S(1)}, u32[]{:S(2)}, u32[]{:S(2)}) collective-permute-start(f32[8,512]{1,0:T(8,128)} %get-tuple-element.40.pack), channel_id=1, source_target_pairs={{2,0},{3,1},{0,2},{1,3},{6,4},{7,5},{4,6},{5,7},{10,8},{11,9},{8,1... | collective-permute-start | bytes 49160 | tf_op jit(solution)/shard_map/ppermute | solution.py:21
  118.7 9.8 %copy-start.3 = (f32[4,4,256,256]{3,2,1,0:T(8,128)S(1)}, f32[4,4,256,256]{3,2,1,0:T(8,128)}, u32[]{:S(2)}) copy-start(f32[4,4,256,256]{3,2,1,0:T(8,128)} %get-tuple-element.41) | copy-start | bytes 12582916
  122.0 0.8 copy-start.21
  122.7 1.0 copy-start.1
  122.8 1.3 copy-start.4
  124.1 9.0 %copy-start = (bf16[1024,512]{1,0:T(8,128)(2,1)S(1)}, bf16[1024,512]{1,0:T(8,128)(2,1)}, u32[]{:S(2)}) copy-start(bf16[1024,512]{1,0:T(8,128)(2,1)} %get-tuple-element.55) | copy-start | bytes 3145732
  124.1 12.0 %copy-start.2 = (bf16[1024,512]{1,0:T(8,128)(2,1)S(1)}, bf16[1024,512]{1,0:T(8,128)(2,1)}, u32[]{:S(2)}) copy-start(bf16[1024,512]{1,0:T(8,128)(2,1)} %get-tuple-element.56.em) | copy-start | bytes 3145732
  124.1 2.9 %collective-permute-start.26 = (bf16[2,4,256,256]{3,2,1,0:T(8,128)(2,1)}, bf16[2,4,256,256]{3,2,1,0:T(8,128)(2,1)S(1)}, u32[]{:S(2)}, u32[]{:S(2)}) collective-permute-start(bf16[2,4,256,256]{3,2,1,0:T(8,128)(2,1)} %get-tuple-element.44), channel_id=1, source_target_pairs={{0,4},{4,0},{1,5},{5,1},{2,6},{6,2},{3,7},{7,3},{8,12},{12,8},{9,1... | collective-permute-start | bytes 3145736 | tf_op jit(solution)/shard_map/ppermute | solution.py:25
  124.1 4.4 %collective-permute-start.28 = (bf16[2,4,256,256]{3,2,1,0:T(8,128)(2,1)}, bf16[2,4,256,256]{3,2,1,0:T(8,128)(2,1)S(1)}, u32[]{:S(2)}, u32[]{:S(2)}) collective-permute-start(bf16[2,4,256,256]{3,2,1,0:T(8,128)(2,1)} %get-tuple-element.45), channel_id=1, source_target_pairs={{0,4},{4,0},{1,5},{5,1},{2,6},{6,2},{3,7},{7,3},{8,12},{12,8},{9,1... | collective-permute-start | bytes 3145736 | tf_op jit(solution)/shard_map/ppermute | solution.py:25
  126.9 9.1 %copy-start.11 = (bf16[2,4,256,256]{3,2,1,0:T(8,128)(2,1)}, bf16[2,4,256,256]{3,2,1,0:T(8,128)(2,1)S(1)}, u32[]{:S(2)}) copy-start(bf16[2,4,256,256]{3,2,1,0:T(8,128)(2,1)S(1)} %collective-permute-done.26) | copy-start | bytes 3145732
  129.9 16.7 %collective-permute-start.27 = (bf16[4,256,256]{2,1,0:T(8,128)(2,1)}, bf16[4,256,256]{2,1,0:T(8,128)(2,1)S(1)}, u32[]{:S(2)}, u32[]{:S(2)}) collective-permute-start(bf16[4,256,256]{2,1,0:T(8,128)(2,1)} %get-tuple-element.63), channel_id=1, source_target_pairs={{96,0},{28,4},{104,8},{4,12},{112,16},{12,20},{120,24},{20,28},{0,... | collective-permute-start | bytes 1572872 | tf_op jit(solution)/shard_map/ppermute | solution.py:36
  129.9 16.8 %collective-permute-start.29 = (bf16[4,256,256]{2,1,0:T(8,128)(2,1)}, bf16[4,256,256]{2,1,0:T(8,128)(2,1)S(1)}, u32[]{:S(2)}, u32[]{:S(2)}) collective-permute-start(bf16[4,256,256]{2,1,0:T(8,128)(2,1)} %get-tuple-element.62), channel_id=1, source_target_pairs={{64,0},{20,4},{72,8},{28,12},{80,16},{4,20},{88,24},{12,28},{96,32... | collective-permute-start | bytes 1572872 | tf_op jit(solution)/shard_map/ppermute | solution.py:36
  133.0 14.1 %collective-permute-start.30 = (bf16[4,256,256]{2,1,0:T(8,128)(2,1)}, bf16[4,256,256]{2,1,0:T(8,128)(2,1)}, u32[]{:S(2)}, u32[]{:S(2)}) collective-permute-start(bf16[4,256,256]{2,1,0:T(8,128)(2,1)} %get-tuple-element.61), channel_id=1, source_target_pairs={{32,0},{12,4},{40,8},{20,12},{48,16},{28,20},{56,24},{4,28},{64,32... | collective-permute-start | bytes 1572872 | tf_op jit(solution)/shard_map/ppermute | solution.py:36
  133.1 26.5 %collective-permute-start.35 = (bf16[1024,512]{1,0:T(8,128)(2,1)S(1)}, bf16[1024,512]{1,0:T(8,128)(2,1)}, u32[]{:S(2)}, u32[]{:S(2)}) collective-permute-start(bf16[1024,512]{1,0:T(8,128)(2,1)S(1)} %copy-done), channel_id=1, source_target_pairs={{1,0},{2,1},{3,2},{0,3},{5,4},{6,5},{7,6},{4,7},{9,8},{10,9},{11,1... | collective-permute-start | bytes 3145736 | tf_op jit(solution)/shard_map/ppermute | solution.py:21
  136.1 27.2 %collective-permute-start.36 = (bf16[1024,512]{1,0:T(8,128)(2,1)S(1)}, bf16[1024,512]{1,0:T(8,128)(2,1)}, u32[]{:S(2)}, u32[]{:S(2)}) collective-permute-start(bf16[1024,512]{1,0:T(8,128)(2,1)S(1)} %copy-done.2), channel_id=1, source_target_pairs={{3,0},{0,1},{1,2},{2,3},{7,4},{4,5},{5,6},{6,7},{11,8},{8,9},{9,10... | collective-permute-start | bytes 3145736 | tf_op jit(solution)/shard_map/ppermute | solution.py:21
  146.6 1.6 copy-start.12
  146.6 0.8 copy-start.8
  146.6 1.0 copy-start.9
  150.3 6.2 %collective-permute-start.31 = (bf16[256,256]{1,0:T(8,128)(2,1)S(1)}, bf16[256,256]{1,0:T(8,128)(2,1)S(1)}, u32[]{:S(2)}, u32[]{:S(2)}) collective-permute-start(bf16[256,256]{1,0:T(8,128)(2,1)S(1)} %get-tuple-element.64), channel_id=1, source_target_pairs={{24,0},{100,4},{0,8},{108,12},{8,16},{116,20},{16,24},{124,28},{56... | collective-permute-start | bytes 393224 | tf_op jit(solution)/shard_map/ppermute | solution.py:36
  152.1 6.6 %collective-permute-start.32 = (bf16[256,256]{1,0:T(8,128)(2,1)S(1)}, bf16[256,256]{1,0:T(8,128)(2,1)S(1)}, u32[]{:S(2)}, u32[]{:S(2)}) collective-permute-start(bf16[256,256]{1,0:T(8,128)(2,1)S(1)} %get-tuple-element.66), channel_id=1, source_target_pairs={{16,0},{68,4},{24,8},{76,12},{0,16},{84,20},{8,24},{92,28},{48,32}... | collective-permute-start | bytes 393224 | tf_op jit(solution)/shard_map/ppermute | solution.py:36
  154.4 5.0 %collective-permute-start.33 = (bf16[256,256]{1,0:T(8,128)(2,1)S(1)}, bf16[256,256]{1,0:T(8,128)(2,1)S(1)}, u32[]{:S(2)}, u32[]{:S(2)}) collective-permute-start(bf16[256,256]{1,0:T(8,128)(2,1)S(1)} %get-tuple-element.65), channel_id=1, source_target_pairs={{8,0},{36,4},{16,8},{44,12},{24,16},{52,20},{0,24},{60,28},{40,32}... | collective-permute-start | bytes 393224 | tf_op jit(solution)/shard_map/ppermute | solution.py:36
  159.5 14.2 %collective-permute-start.34 = (f32[256,128]{1,0:T(8,128)S(1)}, f32[256,128]{1,0:T(8,128)S(1)}, u32[]{:S(2)}, u32[]{:S(2)}) collective-permute-start(f32[256,128]{1,0:T(8,128)S(1)} %get-tuple-element.68), channel_id=1, source_target_pairs={{0,4},{4,0},{1,5},{5,1},{2,6},{6,2},{3,7},{7,3},{8,12},{12,8},{9,1... | collective-permute-start | bytes 393224 | tf_op jit(solution)/shard_map/ppermute | solution.py:25
  (5 other events, 3.0 us)
Sparse Core Ops, SparseCore 0:
  65.8 44.9 all-gather.2

commit v5 on v4

--- a/solution.py
+++ b/solution.py
@@ -74,15 +74,14 @@
 SUB = 256
 
 
-def gather_pieces(block, other):
-    *ring, other = gate(*(cross(block, 0, d) for d in (1, 2, 3)), other)
-    s = jnp.stack([block, *ring])
-    return [s] + [cross(s, 1, d) for d in (1, 2, 3)], other
+def gather_pieces(block):
+    s = jnp.stack([block] + [cross(block, 0, d) for d in (1, 2, 3)])
+    return [s] + [cross(s, 1, d) for d in (1, 2, 3)]
 
 
 def logits_body(at, *refs):
     pieces, refs = refs[:8], refs[8:]
-    tid, emb, _, e0_out, e1_out, st_out, loc_out, _, full, sem = refs
+    tid, emb, e0_out, e1_out, st_out, loc_out, full, sem = refs
     step = pl.program_id(0)
     x, z, c = at[0], at[1], at[2]
 
@@ -137,7 +136,7 @@
         loc_out[pl.ds(2, 1), :] = loc_out[pl.ds(2, 1), :] + hit
 
 
-def logits_call(at, pieces, tid, emb, later):
+def logits_call(at, pieces, tid, emb):
     whole = pl.BlockSpec((8, ROWS), lambda i, at: (0, 0))
     return pl.pallas_call(
         logits_body,
@@ -145,13 +144,12 @@
             num_scalar_prefetch=1,
             grid=(TILES,),
             in_specs=[HBM] * 8
-            + [pl.BlockSpec((1, ROWS), lambda i, at: (0, 0)), pl.BlockSpec((TILE, WIDTH), lambda i, at: (i, 0)), HBM],
+            + [pl.BlockSpec((1, ROWS), lambda i, at: (0, 0)), pl.BlockSpec((TILE, WIDTH), lambda i, at: (i, 0))],
             out_specs=[
                 pl.BlockSpec((CUT, ROWS), lambda i, at: (0, 0)),
                 pl.BlockSpec((VOC - CUT, ROWS), lambda i, at: (0, 0)),
                 whole,
                 whole,
-                HBM,
             ],
             scratch_shapes=[pltpu.VMEM((ROWS, WIDTH), BF), pltpu.SemaphoreType.DMA((32,))],
         ),
@@ -160,13 +158,11 @@
             jax.ShapeDtypeStruct((VOC - CUT, ROWS), BF),
             jax.ShapeDtypeStruct((8, ROWS), F32),
             jax.ShapeDtypeStruct((8, ROWS), F32),
-            jax.ShapeDtypeStruct(later.shape, later.dtype),
         ],
-        input_output_aliases={11: 4},
         compiler_params=params(),
         cost_estimate=SMALL,
         name="logits",
-    )(at, *pieces, tid, emb, later)
+    )(at, *pieces, tid, emb)
 
 
 def merge(parts):
@@ -186,8 +182,12 @@
 
 
 def merge_call(*parts):
+    stat = pl.BlockSpec((8, ROWS), lambda i: (0, 0))
     return pl.pallas_call(
         merge_body,
+        grid=(1,),
+        in_specs=[stat] * len(parts),
+        out_specs=stat,
         out_shape=jax.ShapeDtypeStruct((8, ROWS), F32),
         compiler_params=params(),
         cost_estimate=SMALL,
@@ -222,10 +222,15 @@
 
 
 def finish_call(a, b, st, tid, mix, weight, *awaited):
+    stat = pl.BlockSpec((8, ROWS), lambda i: (0, 0))
+    part = pl.BlockSpec((4, 128), lambda i: (0, 0))
     return pl.pallas_call(
         finish_body,
-        in_specs=[pl.BlockSpec(memory_space=pltpu.VMEM)] * 6 + [HBM] * 3,
-        out_specs=[pl.BlockSpec(memory_space=pltpu.VMEM)] * 2 + [HBM],
+        grid=(1,),
+        in_specs=[stat] * 3
+        + [pl.BlockSpec((1, ROWS), lambda i: (0, 0)), part, pl.BlockSpec((1, 128), lambda i: (0, 0))]
+        + [HBM] * 3,
+        out_specs=[stat, part, HBM],
         out_shape=[
             jax.ShapeDtypeStruct((8, ROWS), F32),
             jax.ShapeDtypeStruct((4, 128), F32),
@@ -306,17 +311,18 @@
     return sum(x.astype(F32) for x in xs)
 
 
-def scatter(keep, recv, c, acc):
+def scatter(keep, recv, c, first, second):
     b = [add(keep[d], recv[d // 2][d % 2]) for d in range(4)]
     u = [cross(b[d].astype(BF), 0, 4 - d) for d in (1, 2, 3)]
-    *u, acc = gate(*u, acc)
+    *u, work = gate(*u, first())
     t = add(b[0], *u)
     u = [cross(t[d].astype(BF), 1, 4 - d) for d in (1, 2, 3)]
+    *u, work = gate(*u, second(work))
     f = add(t[0], *u)
     low, high = f[:, :128], f[:, 128:]
     mine, other = jnp.where(c == 0, low, high), jnp.where(c == 0, high, low)
     got = sibling(other)
-    return jnp.where(c == 0, jnp.concatenate([mine, got]), jnp.concatenate([got, mine])), acc
+    return jnp.where(c == 0, jnp.concatenate([mine, got]), jnp.concatenate([got, mine])), work
 
 
 def embed_body(base, at, tgt, ep, em, ed, pack_p, pack_m, pack_d, feats, *refs):
@@ -381,10 +387,11 @@
     mine, other = jnp.where(c == 0, low, high), jnp.where(c == 0, high, low)
     got = sibling(other)
     block = jnp.where(c == 0, jnp.concatenate([mine, got], axis=1), jnp.concatenate([got, mine], axis=1))
-    pieces, turned = gather_pieces(block, turned)
+    pieces = gather_pieces(block)
     pieces = pieces + [sibling(p) for p in pieces]
 
-    e0, e1, st, loc, turned = logits_call(at, pieces, tid, embed, turned)
+    e0, e1, st, loc = logits_call(at, pieces, tid, embed)
+    loc, turned = gate(loc, turned)
     feats = lax.all_gather(turned, ("x", "z", "c")).reshape(4, 4, 2, ROWS, 128)
     ep0, em0 = shift(e0, "y", 1), shift(e0, "y", 3)
 
@@ -398,9 +405,13 @@
     ep1, ed1 = shift(e1, "y", 1), shift(em1, "y", 3)
     recv = sibling(send0), sibling(send1)
 
-    grad_embed = embed_call(at, 0, tgt, ep0, em0, ed0, packs, feats, None, "embed_a")
-    grad_hidden, grad_embed = scatter(keep, recv, c, grad_embed)
-    grad_embed = embed_call(at, CUT, tgt, ep1, em1, ed1, packs, feats, grad_embed, "embed_b")
+    grad_hidden, grad_embed = scatter(
+        keep,
+        recv,
+        c,
+        lambda: embed_call(at, 0, tgt, ep0, em0, ed0, packs, feats, None, "embed_a"),
+        lambda made: embed_call(at, CUT, tgt, ep1, em1, ed1, packs, feats, made, "embed_b"),
+    )
     return grad_hidden.reshape(4, 128, 128), grad_embed, grad_mix
 
 

time: 183 us -> 183 us (level)
  waiting for transfers between devices: 49.4 us -> 46.8 us
  local copies, waits for them, and re-layouts: 6.5 us -> 8.46 us
    ppermute x12, waiting for transfers between devices: 22.3 us -> 16.9 us  [cross(): return lax.ppermute(a, ('x', 'z', 'c'), pairs)]
    ppermute x15, starting transfers between devices: 17.1 us -> 21.8 us  [shift(): return lax.ppermute(a, axis, [((i + d) % 4, i) for i in range(4)])]
    ppermute x12, starting transfers between devices: 24 us -> 20.7 us  [cross(): return lax.ppermute(a, ('x', 'z', 'c'), pairs)]
    ppermute x9, waiting for transfers between devices: 5.87 us -> 7.83 us  [sibling(): return lax.ppermute(a, 'c', [(0, 1), (1, 0)])]
  transfers between devices with their start and end apart: 38 -> 38, of which waited for: 24 -> 21; matrix products, arithmetic and copies ran while one was open for 3% -> 3% of each run, Pallas kernels for 23% -> 33%
where the time goes in v5:
time: 183 us; the launch traced here: 182 us
  Pallas kernels  59.9 us (33%)
  waiting for transfers between devices  46.8 us (26%)
  starting transfers between devices  44.8 us (24%)
  between operations  14.4 us (8%)
  local copies, waits for them, and re-layouts  8.46 us (5%)
  other arithmetic  7.47 us (4%)
    ppermute x15, waiting for transfers between devices, shift(): return lax.ppermute(a, axis, [((i + d) % 4, i) for i in range(4)])  22 us
    ppermute x15, starting transfers between devices, shift(): return lax.ppermute(a, axis, [((i + d) % 4, i) for i in range(4)])  21.8 us
    pallas_call x2, Pallas kernels, embed_call(): pl.pallas_call(functools.partial(embed_body, base), grid_spec=pltpu.Prefe...  21 us
    ppermute x12, starting transfers between devices, cross(): return lax.ppermute(a, ('x', 'z', 'c'), pairs)  20.7 us
    pallas_call x1, Pallas kernels, logits_call(): pl.pallas_call(logits_body, grid_spec=pltpu.PrefetchScalarGridSpec(num_sc...  17.9 us
    ppermute x12, waiting for transfers between devices, cross(): return lax.ppermute(a, ('x', 'z', 'c'), pairs)  16.9 us
    pallas_call x1, Pallas kernels, hidden_call(): pl.pallas_call(hidden_body, grid_spec=pltpu.PrefetchScalarGridSpec(num_sc...  16.9 us
    ppermute x9, waiting for transfers between devices, sibling(): return lax.ppermute(a, 'c', [(0, 1), (1, 0)])  7.83 us
  transfers between devices with their start and end apart: 38, of which 21 were waited for; matrix products, arithmetic and copies ran while one was open for 3% of the time, Pallas kernels for 33%

profile of v5, /device:TPU:0, one launch (start us, length us, event | category | flops | bytes accessed | tf_op | source)
XLA Modules:
  0.0 181.7 jit_solution(11477237197821197989)
XLA Ops:
  7.2 0.9 broadcast_select_fusion.1
  8.2 1.2 collective-permute-done
  9.5 1.6 collective-permute-start.3
  11.1 1.7 collective-permute-start.1
  12.8 1.9 %collective-permute-start.2 = (bf16[256,256]{1,0:T(8,128)(2,1)S(1)}, bf16[256,256]{1,0:T(8,128)(2,1)S(1)}, u32[]{:S(2)}, u32[]{:S(2)}) collective-permute-start(bf16[256,256]{1,0:T(8,128)(2,1)S(1)} %maximum_select_fusion.2), channel_id=1, source_target_pairs={{64,0},{20,4},{72,8},{28,12},{80,16},{4,20},{88,24},{12,28},{96,32... | collective-permute-start | bytes 393224 | tf_op jit(solution)/shard_map/ppermute | solution.py:36
  14.7 1.0 collective-permute-done.3
  16.1 3.2 %collective-permute-done.2 = bf16[256,256]{1,0:T(8,128)(2,1)S(1)} collective-permute-done((bf16[256,256]{1,0:T(8,128)(2,1)S(1)}, bf16[256,256]{1,0:T(8,128)(2,1)S(1)}, u32[]{:S(2)}, u32[]{:S(2)}) %collective-permute-start.2) | collective-permute-done | bytes 131104 | tf_op jit(solution)/shard_map/ppermute | solution.py:36
  19.3 2.1 %collective-permute-start.6 = (bf16[4,256,256]{2,1,0:T(8,128)(2,1)S(1)}, bf16[4,256,256]{2,1,0:T(8,128)(2,1)S(1)}, u32[]{:S(2)}, u32[]{:S(2)}) collective-permute-start(bf16[4,256,256]{2,1,0:T(8,128)(2,1)S(1)} %pad_maximum_fusion.refs_0_), channel_id=1, source_target_pairs={{24,0},{100,4},{0,8},{108,12},{8,16},{116,20},{16,24},{124,28},{56... | collective-permute-start | bytes 1572872 | tf_op jit(solution)/shard_map/ppermute | solution.py:36
  21.4 2.2 %collective-permute-start.4 = (bf16[4,256,256]{2,1,0:T(8,128)(2,1)S(1)}, bf16[4,256,256]{2,1,0:T(8,128)(2,1)S(1)}, u32[]{:S(2)}, u32[]{:S(2)}) collective-permute-start(bf16[4,256,256]{2,1,0:T(8,128)(2,1)S(1)} %pad_maximum_fusion.refs_0_), channel_id=1, source_target_pairs={{8,0},{36,4},{16,8},{44,12},{24,16},{52,20},{0,24},{60,28},{40,32}... | collective-permute-start | bytes 1572872 | tf_op jit(solution)/shard_map/ppermute | solution.py:36
  23.6 1.8 collective-permute-start.5
  25.4 5.3 %collective-permute-done.6.refs_3_ = bf16[4,256,256]{2,1,0:T(8,128)(2,1)S(1)} collective-permute-done((bf16[4,256,256]{2,1,0:T(8,128)(2,1)S(1)}, bf16[4,256,256]{2,1,0:T(8,128)(2,1)S(1)}, u32[]{:S(2)}, u32[]{:S(2)}) %collective-permute-start.6) | collective-permute-done | bytes 524320 | tf_op jit(solution)/shard_map/ppermute | solution.py:36
  30.7 5.3 %collective-permute-done.4.refs_1_ = bf16[4,256,256]{2,1,0:T(8,128)(2,1)S(1)} collective-permute-done((bf16[4,256,256]{2,1,0:T(8,128)(2,1)S(1)}, bf16[4,256,256]{2,1,0:T(8,128)(2,1)S(1)}, u32[]{:S(2)}, u32[]{:S(2)}) %collective-permute-start.4) | collective-permute-done | bytes 524320 | tf_op jit(solution)/shard_map/ppermute | solution.py:36
  36.0 1.8 collective-permute-done.5.refs_2_
  37.8 1.6 collective-permute-start.11
  39.3 0.7 broadcast_subtract_fusion
  40.0 0.6 pad_add_fusion.at
  40.6 0.7 tile.2
  41.5 17.9 %logits.1 = (bf16[1024,512]{1,0:T(8,128)(2,1)}, bf16[1024,512]{1,0:T(8,128)(2,1)}, f32[8,512]{1,0:T(8,128)}, f32[8,512]{1,0:T(8,128)}) custom-call(s32[4]{0:T(128)} %pad_add_fusion.at, bf16[4,256,256]{2,1,0:T(8,128)(2,1)} %copy-done.7, bf16[4,256,256]{2,1,0:T(8,128)(2,1)} %copy-done.13, bf16[4,256,256]{2,1,0:T(8,128)(2,1)} %copy-done.14, ...), custom_call_target="tpu_custom_call" | custom-call | flops 1000 | bytes 1000 | tf_op jit(solution)/shard_map/logits/pallas_call | solution.py:141
  59.4 0.6 copy-done.20
  60.1 4.7 %collective-permute-start.19 = (bf16[1024,512]{1,0:T(8,128)(2,1)}, bf16[1024,512]{1,0:T(8,128)(2,1)S(1)}, u32[]{:S(2)}, u32[]{:S(2)}) collective-permute-start(bf16[1024,512]{1,0:T(8,128)(2,1)} %get-tuple-element.32.e0), channel_id=1, source_target_pairs={{1,0},{2,1},{3,2},{0,3},{5,4},{6,5},{7,6},{4,7},{9,8},{10,9},{11,1... | collective-permute-start | bytes 3145736 | tf_op jit(solution)/shard_map/ppermute | solution.py:21
  64.7 3.5 %collective-permute-start.12 = (f32[8,512]{1,0:T(8,128)}, f32[8,512]{1,0:T(8,128)S(1)}, u32[]{:S(2)}, u32[]{:S(2)}) collective-permute-start(f32[8,512]{1,0:T(8,128)} %get-tuple-element.34.refs_0_), channel_id=1, source_target_pairs={{32,0},{64,32},{96,64},{0,96},{33,1},{65,33},{97,65},{1,97},{34,2}... | collective-permute-start | bytes 49160 | tf_op jit(solution)/shard_map/ppermute | solution.py:21
  68.7 1.4 collective-permute-start.14
  70.1 3.6 %collective-permute-done.13.refs_2_ = f32[8,512]{1,0:T(8,128)S(1)} collective-permute-done((f32[8,512]{1,0:T(8,128)}, f32[8,512]{1,0:T(8,128)S(1)}, u32[]{:S(2)}, u32[]{:S(2)}) %collective-permute-start.13) | collective-permute-done | bytes 16416 | tf_op jit(solution)/shard_map/ppermute | solution.py:21
  74.3 0.6 copy-done.29
  74.9 1.4 merge.2.refs_0_
  76.3 2.4 %collective-permute-start.15 = (f32[8,512]{1,0:T(8,128)}, f32[8,512]{1,0:T(8,128)S(1)}, u32[]{:S(2)}, u32[]{:S(2)}) collective-permute-start(f32[8,512]{1,0:T(8,128)} %merge.2.refs_0_), channel_id=1, source_target_pairs={{8,0},{16,8},{24,16},{0,24},{9,1},{17,9},{25,17},{1,25},{10,2},{18... | collective-permute-start | bytes 49160 | tf_op jit(solution)/shard_map/ppermute | solution.py:21
  78.7 1.1 collective-permute-start.16
  79.8 0.5 collective-permute-done.15.refs_1_
  80.3 3.9 %collective-permute-done.16.refs_2_ = f32[8,512]{1,0:T(8,128)S(1)} collective-permute-done((f32[8,512]{1,0:T(8,128)}, f32[8,512]{1,0:T(8,128)S(1)}, u32[]{:S(2)}, u32[]{:S(2)}) %collective-permute-start.16) | collective-permute-done | bytes 16416 | tf_op jit(solution)/shard_map/ppermute | solution.py:21
  84.2 0.8 collective-permute-done.17.refs_3_
  85.0 0.6 copy-done.30
  85.6 1.4 merge.3.a
  87.0 1.4 collective-permute-done.18.b
  88.4 2.8 %collective-permute-done.20.em0.em = bf16[1024,512]{1,0:T(8,128)(2,1)S(1)} collective-permute-done((bf16[1024,512]{1,0:T(8,128)(2,1)}, bf16[1024,512]{1,0:T(8,128)(2,1)S(1)}, u32[]{:S(2)}, u32[]{:S(2)}) %collective-permute-start.20) | collective-permute-done | bytes 1048608 | tf_op jit(solution)/shard_map/ppermute | solution.py:21
  91.2 1.0 copy-done.6
  92.2 1.4 finish.1
  93.6 3.2 %collective-permute-start.22 = (bf16[1024,512]{1,0:T(8,128)(2,1)}, bf16[1024,512]{1,0:T(8,128)(2,1)S(1)}, u32[]{:S(2)}, u32[]{:S(2)}) collective-permute-start(bf16[1024,512]{1,0:T(8,128)(2,1)} %copy-done.5), channel_id=1, source_target_pairs={{1,0},{2,1},{3,2},{0,3},{5,4},{6,5},{7,6},{4,7},{9,8},{10,9},{11,1... | collective-permute-start | bytes 3145736 | tf_op jit(solution)/shard_map/ppermute | solution.py:21
  96.9 2.0 %collective-permute-start.24 = (f32[8,512]{1,0:T(8,128)}, f32[8,512]{1,0:T(8,128)S(1)}, u32[]{:S(2)}, u32[]{:S(2)}) collective-permute-start(f32[8,512]{1,0:T(8,128)} %get-tuple-element.38.pack), channel_id=1, source_target_pairs={{3,0},{0,1},{1,2},{2,3},{7,4},{4,5},{5,6},{6,7},{11,8},{8,9},{9,10... | collective-permute-start | bytes 49160 | tf_op jit(solution)/shard_map/ppermute | solution.py:21
  98.9 16.9 %hidden.1 = (f32[4,4,256,256]{3,2,1,0:T(8,128)}, bf16[2,4,256,256]{3,2,1,0:T(8,128)(2,1)}, bf16[2,4,256,256]{3,2,1,0:T(8,128)(2,1)}, bf16[2048,512]{1,0:T(8,128)(2,1)}) custom-call(s32[4]{0:T(128)} %pad_add_fusion.at, bf16[1024,512]{1,0:T(8,128)(2,1)} %get-tuple-element.32.e0, bf16[1024,512]{1,0:T(8,128)(2,1)} %get-tuple-element.37.e1.refs_2_, ...), custom_call_target="tpu_custom_call" | custom-call | flops 1000 | bytes 1000 | tf_op jit(solution)/shard_map/hidden/pallas_call | solution.py:284
  115.8 3.4 %collective-permute-done.23.refs_5_ = f32[8,512]{1,0:T(8,128)S(1)} collective-permute-done((f32[8,512]{1,0:T(8,128)}, f32[8,512]{1,0:T(8,128)S(1)}, u32[]{:S(2)}, u32[]{:S(2)}) %collective-permute-start.23) | collective-permute-done | bytes 16416 | tf_op jit(solution)/shard_map/ppermute | solution.py:21
  119.2 0.7 collective-permute-done.24.refs_6_
  120.0 0.5 copy-done.22
  121.8 2.4 %collective-permute-done.26 = bf16[2,4,256,256]{3,2,1,0:T(8,128)(2,1)S(1)} collective-permute-done((bf16[2,4,256,256]{3,2,1,0:T(8,128)(2,1)}, bf16[2,4,256,256]{3,2,1,0:T(8,128)(2,1)S(1)}, u32[]{:S(2)}, u32[]{:S(2)}) %collective-permute-start.26) | collective-permute-done | bytes 1048608 | tf_op jit(solution)/shard_map/ppermute | solution.py:25
  124.2 1.5 collective-permute-done.28
  125.7 1.4 fusion.4
  127.1 1.9 %collective-permute-start.27 = (bf16[4,256,256]{2,1,0:T(8,128)(2,1)}, bf16[4,256,256]{2,1,0:T(8,128)(2,1)S(1)}, u32[]{:S(2)}, u32[]{:S(2)}) collective-permute-start(bf16[4,256,256]{2,1,0:T(8,128)(2,1)} %get-tuple-element.65), channel_id=1, source_target_pairs={{96,0},{28,4},{104,8},{4,12},{112,16},{12,20},{120,24},{20,28},{0,... | collective-permute-start | bytes 1572872 | tf_op jit(solution)/shard_map/ppermute | solution.py:36
  128.9 1.7 collective-permute-start.29
  130.6 1.7 collective-permute-start.30
  132.3 3.0 %collective-permute-start.34 = (bf16[1024,512]{1,0:T(8,128)(2,1)S(1)}, bf16[1024,512]{1,0:T(8,128)(2,1)}, u32[]{:S(2)}, u32[]{:S(2)}) collective-permute-start(bf16[1024,512]{1,0:T(8,128)(2,1)S(1)} %copy-done), channel_id=1, source_target_pairs={{1,0},{2,1},{3,2},{0,3},{5,4},{6,5},{7,6},{4,7},{9,8},{10,9},{11,1... | collective-permute-start | bytes 3145736 | tf_op jit(solution)/shard_map/ppermute | solution.py:21
  135.3 10.5 %embed_a.1.refs_3_ = bf16[2048,1024]{1,0:T(8,128)(2,1)} custom-call(s32[4]{0:T(128)} %pad_add_fusion.at, bf16[2048,512]{1,0:T(8,128)(2,1)} %get-tuple-element.44.tgt, bf16[1024,512]{1,0:T(8,128)(2,1)} %copy-done.5, bf16[1024,512]{1,0:T(8,128)(2,1)} %copy-done.6, bf16[1024,512]{1,0:T(8,128)(2,1)} %get-tuple-element.45.ed, f32[8,512]{1,0:T(8,128)} %get-tuple-element.46.pack_p, ...), custom_call_target="tpu_custom_call" | custom-call | flops 1000 | bytes 1000 | tf_op jit(solution)/shard_map/embed_a/pallas_call | solution.py:359
  145.8 0.8 copy-done.8
  146.8 0.6 copy-done.11
  147.4 2.0 %fusion.8 = (bf16[4,256,256]{2,1,0:T(8,128)(2,1)S(1)}, f32[4,256,256]{2,1,0:T(8,128)S(1)}) fusion(bf16[4,256,256]{2,1,0:T(8,128)(2,1)} %get-tuple-element.52, bf16[4,256,256]{2,1,0:T(8,128)(2,1)} %get-tuple-element.51, bf16[4,256,256]{2,1,0:T(8,128)(2,1)} %get-tuple-element.50, bf16[2,4,256,256]{3,2,1,0:T(8,128)(2,1)S(1)} %copy-done.11, ...), kind=kLoop, calls=%fused_computation.26 | loop fusion | flops 2359296 | bytes 4718592 | tf_op jit(solution)/shard_map/convert.2
  149.4 1.5 collective-permute-start.31
  150.9 1.5 collective-permute-start.32
  152.4 1.2 collective-permute-start.33
  153.7 2.6 %collective-permute-done.34.ep = bf16[1024,512]{1,0:T(8,128)(2,1)} collective-permute-done((bf16[1024,512]{1,0:T(8,128)(2,1)S(1)}, bf16[1024,512]{1,0:T(8,128)(2,1)}, u32[]{:S(2)}, u32[]{:S(2)}) %collective-permute-start.34) | collective-permute-done | bytes 1048608 | tf_op jit(solution)/shard_map/ppermute | solution.py:21
  156.2 3.5 %collective-permute-done.35.ed = bf16[1024,512]{1,0:T(8,128)(2,1)} collective-permute-done((bf16[1024,512]{1,0:T(8,128)(2,1)S(1)}, bf16[1024,512]{1,0:T(8,128)(2,1)}, u32[]{:S(2)}, u32[]{:S(2)}) %collective-permute-start.35) | collective-permute-done | bytes 1048608 | tf_op jit(solution)/shard_map/ppermute | solution.py:21
  159.8 10.5 %embed_b.1.refs_3_ = bf16[2048,1024]{1,0:T(8,128)(2,1)} custom-call(s32[4]{0:T(128)} %pad_add_fusion.at, bf16[2048,512]{1,0:T(8,128)(2,1)} %get-tuple-element.44.tgt, bf16[1024,512]{1,0:T(8,128)(2,1)} %collective-permute-done.34.ep, bf16[1024,512]{1,0:T(8,128)(2,1)} %get-tuple-element.54.em, ...), custom_call_target="tpu_custom_call", output_to_operand_aliasing={{}: (9, {})} | custom-call | flops 1000 | bytes 1000 | tf_op jit(solution)/shard_map/embed_b/pallas_call | solution.py:359
  170.3 0.6 copy-done.17
  171.0 0.6 copy-done.19
  171.6 1.1 fusion.7
  172.8 1.3 collective-permute-done.36
  174.2 0.7 maximum_select_fusion
  (99 shorter events, 3.8 us)
Async XLA Ops:
  7.2 128.1 %all-gather.3.cloned.1.call-start = ((), (), s32[]{:S(2)}) async-start(), calls=%async_computation | async-start | bytes 4325376 | tf_op jit(solution)/shard_map/all_gather | solution.py:395
  8.1 1.3 collective-permute-start
  9.5 6.2 %collective-permute-start.3 = (bf16[256,256]{1,0:T(8,128)(2,1)S(1)}, bf16[256,256]{1,0:T(8,128)(2,1)S(1)}, u32[]{:S(2)}, u32[]{:S(2)}) collective-permute-start(bf16[256,256]{1,0:T(8,128)(2,1)S(1)} %maximum_select_fusion.2), channel_id=1, source_target_pairs={{96,0},{28,4},{104,8},{4,12},{112,16},{12,20},{120,24},{20,28},{0,... | collective-permute-start | bytes 393224 | tf_op jit(solution)/shard_map/ppermute | solution.py:36
  11.1 5.0 %collective-permute-start.1 = (bf16[256,256]{1,0:T(8,128)(2,1)S(1)}, bf16[256,256]{1,0:T(8,128)(2,1)S(1)}, u32[]{:S(2)}, u32[]{:S(2)}) collective-permute-start(bf16[256,256]{1,0:T(8,128)(2,1)S(1)} %maximum_select_fusion.2), channel_id=1, source_target_pairs={{32,0},{12,4},{40,8},{20,12},{48,16},{28,20},{56,24},{4,28},{64,32... | collective-permute-start | bytes 393224 | tf_op jit(solution)/shard_map/ppermute | solution.py:36
  12.8 6.5 %collective-permute-start.2 = (bf16[256,256]{1,0:T(8,128)(2,1)S(1)}, bf16[256,256]{1,0:T(8,128)(2,1)S(1)}, u32[]{:S(2)}, u32[]{:S(2)}) collective-permute-start(bf16[256,256]{1,0:T(8,128)(2,1)S(1)} %maximum_select_fusion.2), channel_id=1, source_target_pairs={{64,0},{20,4},{72,8},{28,12},{80,16},{4,20},{88,24},{12,28},{96,32... | collective-permute-start | bytes 393224 | tf_op jit(solution)/shard_map/ppermute | solution.py:36
  19.3 21.9 %copy-start.7 = (bf16[4,256,256]{2,1,0:T(8,128)(2,1)}, bf16[4,256,256]{2,1,0:T(8,128)(2,1)S(1)}, u32[]{:S(2)}) copy-start(bf16[4,256,256]{2,1,0:T(8,128)(2,1)S(1)} %pad_maximum_fusion.refs_0_) | copy-start | bytes 1572868
  19.3 11.3 %collective-permute-start.6 = (bf16[4,256,256]{2,1,0:T(8,128)(2,1)S(1)}, bf16[4,256,256]{2,1,0:T(8,128)(2,1)S(1)}, u32[]{:S(2)}, u32[]{:S(2)}) collective-permute-start(bf16[4,256,256]{2,1,0:T(8,128)(2,1)S(1)} %pad_maximum_fusion.refs_0_), channel_id=1, source_target_pairs={{24,0},{100,4},{0,8},{108,12},{8,16},{116,20},{16,24},{124,28},{56... | collective-permute-start | bytes 1572872 | tf_op jit(solution)/shard_map/ppermute | solution.py:36
  21.4 14.6 %collective-permute-start.4 = (bf16[4,256,256]{2,1,0:T(8,128)(2,1)S(1)}, bf16[4,256,256]{2,1,0:T(8,128)(2,1)S(1)}, u32[]{:S(2)}, u32[]{:S(2)}) collective-permute-start(bf16[4,256,256]{2,1,0:T(8,128)(2,1)S(1)} %pad_maximum_fusion.refs_0_), channel_id=1, source_target_pairs={{8,0},{36,4},{16,8},{44,12},{24,16},{52,20},{0,24},{60,28},{40,32}... | collective-permute-start | bytes 1572872 | tf_op jit(solution)/shard_map/ppermute | solution.py:36
  23.6 14.2 %collective-permute-start.5 = (bf16[4,256,256]{2,1,0:T(8,128)(2,1)S(1)}, bf16[4,256,256]{2,1,0:T(8,128)(2,1)S(1)}, u32[]{:S(2)}, u32[]{:S(2)}) collective-permute-start(bf16[4,256,256]{2,1,0:T(8,128)(2,1)S(1)} %pad_maximum_fusion.refs_0_), channel_id=1, source_target_pairs={{16,0},{68,4},{24,8},{76,12},{0,16},{84,20},{8,24},{92,28},{48,32}... | collective-permute-start | bytes 1572872 | tf_op jit(solution)/shard_map/ppermute | solution.py:36
  25.4 15.1 %collective-permute-start.7 = (bf16[4,256,256]{2,1,0:T(8,128)(2,1)S(1)}, bf16[4,256,256]{2,1,0:T(8,128)(2,1)S(1)}, u32[]{:S(2)}, u32[]{:S(2)}) collective-permute-start(bf16[4,256,256]{2,1,0:T(8,128)(2,1)S(1)} %pad_maximum_fusion.refs_0_), channel_id=1, source_target_pairs={{0,4},{4,0},{1,5},{5,1},{2,6},{6,2},{3,7},{7,3},{8,12},{12,8},{9,1... | collective-permute-start | bytes 1572872 | tf_op jit(solution)/shard_map/ppermute | solution.py:25
  30.7 10.6 %copy-start.12 = (bf16[4,256,256]{2,1,0:T(8,128)(2,1)}, bf16[4,256,256]{2,1,0:T(8,128)(2,1)S(1)}, u32[]{:S(2)}) copy-start(bf16[4,256,256]{2,1,0:T(8,128)(2,1)S(1)} %collective-permute-done.6.refs_3_) | copy-start | bytes 1572868
  30.7 9.9 %collective-permute-start.10 = (bf16[4,256,256]{2,1,0:T(8,128)(2,1)S(1)}, bf16[4,256,256]{2,1,0:T(8,128)(2,1)S(1)}, u32[]{:S(2)}, u32[]{:S(2)}) collective-permute-start(bf16[4,256,256]{2,1,0:T(8,128)(2,1)S(1)} %collective-permute-done.6.refs_3_), channel_id=1, source_target_pairs={{0,4},{4,0},{1,5},{5,1},{2,6},{6,2},{3,7},{7,3},{8,12},{12,8},{9,1... | collective-permute-start | bytes 1572872 | tf_op jit(solution)/shard_map/ppermute | solution.py:25
  36.0 5.3 %copy-start.13 = (bf16[4,256,256]{2,1,0:T(8,128)(2,1)}, bf16[4,256,256]{2,1,0:T(8,128)(2,1)S(1)}, u32[]{:S(2)}) copy-start(bf16[4,256,256]{2,1,0:T(8,128)(2,1)S(1)} %collective-permute-done.4.refs_1_) | copy-start | bytes 1572868
  36.0 4.6 %collective-permute-start.8 = (bf16[4,256,256]{2,1,0:T(8,128)(2,1)S(1)}, bf16[4,256,256]{2,1,0:T(8,128)(2,1)}, u32[]{:S(2)}, u32[]{:S(2)}) collective-permute-start(bf16[4,256,256]{2,1,0:T(8,128)(2,1)S(1)} %collective-permute-done.4.refs_1_), channel_id=1, source_target_pairs={{0,4},{4,0},{1,5},{5,1},{2,6},{6,2},{3,7},{7,3},{8,12},{12,8},{9,1... | collective-permute-start | bytes 1572872 | tf_op jit(solution)/shard_map/ppermute | solution.py:25
  37.8 3.5 %copy-start.14 = (bf16[4,256,256]{2,1,0:T(8,128)(2,1)}, bf16[4,256,256]{2,1,0:T(8,128)(2,1)S(1)}, u32[]{:S(2)}) copy-start(bf16[4,256,256]{2,1,0:T(8,128)(2,1)S(1)} %collective-permute-done.5.refs_2_) | copy-start | bytes 1572868
  37.8 2.8 %collective-permute-start.9 = (bf16[4,256,256]{2,1,0:T(8,128)(2,1)S(1)}, bf16[4,256,256]{2,1,0:T(8,128)(2,1)}, u32[]{:S(2)}, u32[]{:S(2)}) collective-permute-start(bf16[4,256,256]{2,1,0:T(8,128)(2,1)S(1)} %collective-permute-done.5.refs_2_), channel_id=1, source_target_pairs={{0,4},{4,0},{1,5},{5,1},{2,6},{6,2},{3,7},{7,3},{8,12},{12,8},{9,1... | collective-permute-start | bytes 1572872 | tf_op jit(solution)/shard_map/ppermute | solution.py:25
  37.8 21.6 %collective-permute-start.11 = (bf16[512,128]{1,0:T(8,128)(2,1)}, bf16[512,128]{1,0:T(8,128)(2,1)S(1)}, u32[]{:S(2)}, u32[]{:S(2)}) collective-permute-start(bf16[512,128]{1,0:T(8,128)(2,1)} %bitcast.49), channel_id=1, source_target_pairs={{0,0},{1,32},{2,64},{3,96},{32,1},{33,33},{34,65},{35,97},{64,2},{... | collective-permute-start | bytes 393224 | tf_op jit(solution)/shard_map/ppermute | solution.py:384
  40.5 0.8 copy-start.15
  40.5 1.0 copy-start.16
  59.4 0.7 copy-start.20
  60.1 28.3 %collective-permute-start.19 = (bf16[1024,512]{1,0:T(8,128)(2,1)}, bf16[1024,512]{1,0:T(8,128)(2,1)S(1)}, u32[]{:S(2)}, u32[]{:S(2)}) collective-permute-start(bf16[1024,512]{1,0:T(8,128)(2,1)} %get-tuple-element.32.e0), channel_id=1, source_target_pairs={{1,0},{2,1},{3,2},{0,3},{5,4},{6,5},{7,6},{4,7},{9,8},{10,9},{11,1... | collective-permute-start | bytes 3145736 | tf_op jit(solution)/shard_map/ppermute | solution.py:21
  64.7 26.4 %collective-permute-start.20 = (bf16[1024,512]{1,0:T(8,128)(2,1)}, bf16[1024,512]{1,0:T(8,128)(2,1)S(1)}, u32[]{:S(2)}, u32[]{:S(2)}) collective-permute-start(bf16[1024,512]{1,0:T(8,128)(2,1)} %get-tuple-element.32.e0), channel_id=1, source_target_pairs={{3,0},{0,1},{1,2},{2,3},{7,4},{4,5},{5,6},{6,7},{11,8},{8,9},{9,10... | collective-permute-start | bytes 3145736 | tf_op jit(solution)/shard_map/ppermute | solution.py:21
  64.7 5.4 %collective-permute-start.12 = (f32[8,512]{1,0:T(8,128)}, f32[8,512]{1,0:T(8,128)S(1)}, u32[]{:S(2)}, u32[]{:S(2)}) collective-permute-start(f32[8,512]{1,0:T(8,128)} %get-tuple-element.34.refs_0_), channel_id=1, source_target_pairs={{32,0},{64,32},{96,64},{0,96},{33,1},{65,33},{97,65},{1,97},{34,2}... | collective-permute-start | bytes 49160 | tf_op jit(solution)/shard_map/ppermute | solution.py:21
  68.2 5.5 %collective-permute-start.13 = (f32[8,512]{1,0:T(8,128)}, f32[8,512]{1,0:T(8,128)S(1)}, u32[]{:S(2)}, u32[]{:S(2)}) collective-permute-start(f32[8,512]{1,0:T(8,128)} %get-tuple-element.34.refs_0_), channel_id=1, source_target_pairs={{64,0},{96,32},{0,64},{32,96},{65,1},{97,33},{1,65},{33,97},{66,2}... | collective-permute-start | bytes 49160 | tf_op jit(solution)/shard_map/ppermute | solution.py:21
  68.7 5.2 %collective-permute-start.14 = (f32[8,512]{1,0:T(8,128)}, f32[8,512]{1,0:T(8,128)S(1)}, u32[]{:S(2)}, u32[]{:S(2)}) collective-permute-start(f32[8,512]{1,0:T(8,128)} %get-tuple-element.34.refs_0_), channel_id=1, source_target_pairs={{96,0},{0,32},{32,64},{64,96},{97,1},{1,33},{33,65},{65,97},{98,2}... | collective-permute-start | bytes 49160 | tf_op jit(solution)/shard_map/ppermute | solution.py:21
  70.1 3.7 %copy-start.25 = (f32[8,512]{1,0:T(8,128)}, f32[8,512]{1,0:T(8,128)S(1)}, u32[]{:S(2)}) copy-start(f32[8,512]{1,0:T(8,128)S(1)} %collective-permute-done.12.refs_1_) | copy-start | bytes 49156
  76.3 4.0 %collective-permute-start.15 = (f32[8,512]{1,0:T(8,128)}, f32[8,512]{1,0:T(8,128)S(1)}, u32[]{:S(2)}, u32[]{:S(2)}) collective-permute-start(f32[8,512]{1,0:T(8,128)} %merge.2.refs_0_), channel_id=1, source_target_pairs={{8,0},{16,8},{24,16},{0,24},{9,1},{17,9},{25,17},{1,25},{10,2},{18... | collective-permute-start | bytes 49160 | tf_op jit(solution)/shard_map/ppermute | solution.py:21
  78.7 5.5 %collective-permute-start.16 = (f32[8,512]{1,0:T(8,128)}, f32[8,512]{1,0:T(8,128)S(1)}, u32[]{:S(2)}, u32[]{:S(2)}) collective-permute-start(f32[8,512]{1,0:T(8,128)} %merge.2.refs_0_), channel_id=1, source_target_pairs={{16,0},{24,8},{0,16},{8,24},{17,1},{25,9},{1,17},{9,25},{18,2},{26... | collective-permute-start | bytes 49160 | tf_op jit(solution)/shard_map/ppermute | solution.py:21
  79.8 5.2 %collective-permute-start.17 = (f32[8,512]{1,0:T(8,128)}, f32[8,512]{1,0:T(8,128)S(1)}, u32[]{:S(2)}, u32[]{:S(2)}) collective-permute-start(f32[8,512]{1,0:T(8,128)} %merge.2.refs_0_), channel_id=1, source_target_pairs={{24,0},{0,8},{8,16},{16,24},{25,1},{1,9},{9,17},{17,25},{26,2},{2,... | collective-permute-start | bytes 49160 | tf_op jit(solution)/shard_map/ppermute | solution.py:21
  80.3 4.6 %copy-start.26 = (f32[8,512]{1,0:T(8,128)}, f32[8,512]{1,0:T(8,128)S(1)}, u32[]{:S(2)}) copy-start(f32[8,512]{1,0:T(8,128)S(1)} %collective-permute-done.15.refs_1_) | copy-start | bytes 49156
  84.2 0.8 copy-start.28
  87.0 1.4 collective-permute-start.18
  88.4 2.8 %copy-start.24 = (f32[8,512]{1,0:T(8,128)}, f32[8,512]{1,0:T(8,128)S(1)}, u32[]{:S(2)}) copy-start(f32[8,512]{1,0:T(8,128)S(1)} %collective-permute-done.18.b) | copy-start | bytes 49156
  88.4 2.8 %copy-start.5 = (bf16[1024,512]{1,0:T(8,128)(2,1)}, bf16[1024,512]{1,0:T(8,128)(2,1)S(1)}, u32[]{:S(2)}) copy-start(bf16[1024,512]{1,0:T(8,128)(2,1)S(1)} %collective-permute-done.19.ep0.ep) | copy-start | bytes 3145732
  91.2 1.0 copy-start.6
  93.6 26.3 %collective-permute-start.21 = (bf16[1024,512]{1,0:T(8,128)(2,1)}, bf16[1024,512]{1,0:T(8,128)(2,1)S(1)}, u32[]{:S(2)}, u32[]{:S(2)}) collective-permute-start(bf16[1024,512]{1,0:T(8,128)(2,1)} %get-tuple-element.37.e1.refs_2_), channel_id=1, source_target_pairs={{3,0},{0,1},{1,2},{2,3},{7,4},{4,5},{5,6},{6,7},{11,8},{8,9},{9,10... | collective-permute-start | bytes 3145736 | tf_op jit(solution)/shard_map/ppermute | solution.py:21
  93.6 26.4 %collective-permute-start.22 = (bf16[1024,512]{1,0:T(8,128)(2,1)}, bf16[1024,512]{1,0:T(8,128)(2,1)S(1)}, u32[]{:S(2)}, u32[]{:S(2)}) collective-permute-start(bf16[1024,512]{1,0:T(8,128)(2,1)} %copy-done.5), channel_id=1, source_target_pairs={{1,0},{2,1},{3,2},{0,3},{5,4},{6,5},{7,6},{4,7},{9,8},{10,9},{11,1... | collective-permute-start | bytes 3145736 | tf_op jit(solution)/shard_map/ppermute | solution.py:21
  96.9 22.4 %collective-permute-start.23 = (f32[8,512]{1,0:T(8,128)}, f32[8,512]{1,0:T(8,128)S(1)}, u32[]{:S(2)}, u32[]{:S(2)}) collective-permute-start(f32[8,512]{1,0:T(8,128)} %get-tuple-element.38.pack), channel_id=1, source_target_pairs={{1,0},{2,1},{3,2},{0,3},{5,4},{6,5},{7,6},{4,7},{9,8},{10,9},{11,1... | collective-permute-start | bytes 49160 | tf_op jit(solution)/shard_map/ppermute | solution.py:21
  96.9 23.1 %collective-permute-start.24 = (f32[8,512]{1,0:T(8,128)}, f32[8,512]{1,0:T(8,128)S(1)}, u32[]{:S(2)}, u32[]{:S(2)}) collective-permute-start(f32[8,512]{1,0:T(8,128)} %get-tuple-element.38.pack), channel_id=1, source_target_pairs={{3,0},{0,1},{1,2},{2,3},{7,4},{4,5},{5,6},{6,7},{11,8},{8,9},{9,10... | collective-permute-start | bytes 49160 | tf_op jit(solution)/shard_map/ppermute | solution.py:21
  98.9 21.1 %collective-permute-start.25 = (f32[8,512]{1,0:T(8,128)}, f32[8,512]{1,0:T(8,128)S(1)}, u32[]{:S(2)}, u32[]{:S(2)}) collective-permute-start(f32[8,512]{1,0:T(8,128)} %get-tuple-element.38.pack), channel_id=1, source_target_pairs={{2,0},{3,1},{0,2},{1,3},{6,4},{7,5},{4,6},{5,7},{10,8},{11,9},{8,1... | collective-permute-start | bytes 49160 | tf_op jit(solution)/shard_map/ppermute | solution.py:21
  115.8 9.9 %copy-start.3 = (f32[4,4,256,256]{3,2,1,0:T(8,128)S(1)}, f32[4,4,256,256]{3,2,1,0:T(8,128)}, u32[]{:S(2)}) copy-start(f32[4,4,256,256]{3,2,1,0:T(8,128)} %get-tuple-element.39) | copy-start | bytes 12582916
  119.2 0.8 copy-start.21
  120.0 1.0 copy-start.1
  120.0 1.3 copy-start.4
  121.3 11.0 %copy-start = (bf16[1024,512]{1,0:T(8,128)(2,1)S(1)}, bf16[1024,512]{1,0:T(8,128)(2,1)}, u32[]{:S(2)}) copy-start(bf16[1024,512]{1,0:T(8,128)(2,1)} %get-tuple-element.53) | copy-start | bytes 3145732
  121.3 14.0 %copy-start.2 = (bf16[1024,512]{1,0:T(8,128)(2,1)S(1)}, bf16[1024,512]{1,0:T(8,128)(2,1)}, u32[]{:S(2)}) copy-start(bf16[1024,512]{1,0:T(8,128)(2,1)} %get-tuple-element.54.em) | copy-start | bytes 3145732
  121.3 2.9 %collective-permute-start.26 = (bf16[2,4,256,256]{3,2,1,0:T(8,128)(2,1)}, bf16[2,4,256,256]{3,2,1,0:T(8,128)(2,1)S(1)}, u32[]{:S(2)}, u32[]{:S(2)}) collective-permute-start(bf16[2,4,256,256]{3,2,1,0:T(8,128)(2,1)} %get-tuple-element.42), channel_id=1, source_target_pairs={{0,4},{4,0},{1,5},{5,1},{2,6},{6,2},{3,7},{7,3},{8,12},{12,8},{9,1... | collective-permute-start | bytes 3145736 | tf_op jit(solution)/shard_map/ppermute | solution.py:25
  121.3 4.4 %collective-permute-start.28 = (bf16[2,4,256,256]{3,2,1,0:T(8,128)(2,1)}, bf16[2,4,256,256]{3,2,1,0:T(8,128)(2,1)S(1)}, u32[]{:S(2)}, u32[]{:S(2)}) collective-permute-start(bf16[2,4,256,256]{3,2,1,0:T(8,128)(2,1)} %get-tuple-element.43), channel_id=1, source_target_pairs={{0,4},{4,0},{1,5},{5,1},{2,6},{6,2},{3,7},{7,3},{8,12},{12,8},{9,1... | collective-permute-start | bytes 3145736 | tf_op jit(solution)/shard_map/ppermute | solution.py:25
  124.2 11.1 %copy-start.10 = (bf16[2,4,256,256]{3,2,1,0:T(8,128)(2,1)}, bf16[2,4,256,256]{3,2,1,0:T(8,128)(2,1)S(1)}, u32[]{:S(2)}) copy-start(bf16[2,4,256,256]{3,2,1,0:T(8,128)(2,1)S(1)} %collective-permute-done.26) | copy-start | bytes 3145732
  127.1 18.7 %collective-permute-start.27 = (bf16[4,256,256]{2,1,0:T(8,128)(2,1)}, bf16[4,256,256]{2,1,0:T(8,128)(2,1)S(1)}, u32[]{:S(2)}, u32[]{:S(2)}) collective-permute-start(bf16[4,256,256]{2,1,0:T(8,128)(2,1)} %get-tuple-element.65), channel_id=1, source_target_pairs={{96,0},{28,4},{104,8},{4,12},{112,16},{12,20},{120,24},{20,28},{0,... | collective-permute-start | bytes 1572872 | tf_op jit(solution)/shard_map/ppermute | solution.py:36
  128.9 16.9 %collective-permute-start.29 = (bf16[4,256,256]{2,1,0:T(8,128)(2,1)}, bf16[4,256,256]{2,1,0:T(8,128)(2,1)S(1)}, u32[]{:S(2)}, u32[]{:S(2)}) collective-permute-start(bf16[4,256,256]{2,1,0:T(8,128)(2,1)} %get-tuple-element.64), channel_id=1, source_target_pairs={{64,0},{20,4},{72,8},{28,12},{80,16},{4,20},{88,24},{12,28},{96,32... | collective-permute-start | bytes 1572872 | tf_op jit(solution)/shard_map/ppermute | solution.py:36
  130.6 15.2 %collective-permute-start.30 = (bf16[4,256,256]{2,1,0:T(8,128)(2,1)}, bf16[4,256,256]{2,1,0:T(8,128)(2,1)}, u32[]{:S(2)}, u32[]{:S(2)}) collective-permute-start(bf16[4,256,256]{2,1,0:T(8,128)(2,1)} %get-tuple-element.63), channel_id=1, source_target_pairs={{32,0},{12,4},{40,8},{20,12},{48,16},{28,20},{56,24},{4,28},{64,32... | collective-permute-start | bytes 1572872 | tf_op jit(solution)/shard_map/ppermute | solution.py:36
  132.3 24.0 %collective-permute-start.34 = (bf16[1024,512]{1,0:T(8,128)(2,1)S(1)}, bf16[1024,512]{1,0:T(8,128)(2,1)}, u32[]{:S(2)}, u32[]{:S(2)}) collective-permute-start(bf16[1024,512]{1,0:T(8,128)(2,1)S(1)} %copy-done), channel_id=1, source_target_pairs={{1,0},{2,1},{3,2},{0,3},{5,4},{6,5},{7,6},{4,7},{9,8},{10,9},{11,1... | collective-permute-start | bytes 3145736 | tf_op jit(solution)/shard_map/ppermute | solution.py:21
  135.3 24.5 %collective-permute-start.35 = (bf16[1024,512]{1,0:T(8,128)(2,1)S(1)}, bf16[1024,512]{1,0:T(8,128)(2,1)}, u32[]{:S(2)}, u32[]{:S(2)}) collective-permute-start(bf16[1024,512]{1,0:T(8,128)(2,1)S(1)} %copy-done.2), channel_id=1, source_target_pairs={{3,0},{0,1},{1,2},{2,3},{7,4},{4,5},{5,6},{6,7},{11,8},{8,9},{9,10... | collective-permute-start | bytes 3145736 | tf_op jit(solution)/shard_map/ppermute | solution.py:21
  145.8 1.6 copy-start.11
  145.8 0.8 copy-start.8
  145.8 1.0 copy-start.9
  149.4 20.8 %collective-permute-start.31 = (bf16[256,256]{1,0:T(8,128)(2,1)S(1)}, bf16[256,256]{1,0:T(8,128)(2,1)S(1)}, u32[]{:S(2)}, u32[]{:S(2)}) collective-permute-start(bf16[256,256]{1,0:T(8,128)(2,1)S(1)} %get-tuple-element.68), channel_id=1, source_target_pairs={{24,0},{100,4},{0,8},{108,12},{8,16},{116,20},{16,24},{124,28},{56... | collective-permute-start | bytes 393224 | tf_op jit(solution)/shard_map/ppermute | solution.py:36
  150.9 19.4 %collective-permute-start.32 = (bf16[256,256]{1,0:T(8,128)(2,1)S(1)}, bf16[256,256]{1,0:T(8,128)(2,1)S(1)}, u32[]{:S(2)}, u32[]{:S(2)}) collective-permute-start(bf16[256,256]{1,0:T(8,128)(2,1)S(1)} %get-tuple-element.67), channel_id=1, source_target_pairs={{16,0},{68,4},{24,8},{76,12},{0,16},{84,20},{8,24},{92,28},{48,32}... | collective-permute-start | bytes 393224 | tf_op jit(solution)/shard_map/ppermute | solution.py:36
  152.4 17.9 %collective-permute-start.33 = (bf16[256,256]{1,0:T(8,128)(2,1)S(1)}, bf16[256,256]{1,0:T(8,128)(2,1)S(1)}, u32[]{:S(2)}, u32[]{:S(2)}) collective-permute-start(bf16[256,256]{1,0:T(8,128)(2,1)S(1)} %get-tuple-element.66), channel_id=1, source_target_pairs={{8,0},{36,4},{16,8},{44,12},{24,16},{52,20},{0,24},{60,28},{40,32}... | collective-permute-start | bytes 393224 | tf_op jit(solution)/shard_map/ppermute | solution.py:36
  170.3 0.7 copy-start.17
  170.3 0.7 copy-start.18
  171.0 0.6 copy-start.19
  172.7 1.4 collective-permute-start.36
  (5 other events, 3.0 us)
Sparse Core Ops, SparseCore 0:
  60.2 47.9 all-gather.2

commit v6 on v5

--- a/solution.py
+++ b/solution.py
@@ -81,13 +81,12 @@
 
 def logits_body(at, *refs):
     pieces, refs = refs[:8], refs[8:]
-    tid, emb, e0_out, e1_out, st_out, loc_out, full, sem = refs
+    tid, emb, e0_out, e1_out, st_out, loc_out, full = refs
     step = pl.program_id(0)
     x, z, c = at[0], at[1], at[2]
 
     @pl.when(step == 0)
     def _():
-        copies = []
         for n in range(8):
             core = c if n < 4 else 1 - c
             row = pl.multiple_of(core * HALF, HALF)
@@ -95,11 +94,7 @@
                 dx = jnp.where(core == 0, b, n % 4)
                 dz = jnp.where(core == 0, n % 4, b)
                 col = pl.multiple_of((((x + dx) & 3) * 4 + ((z + dz) & 3)) * 256, 256)
-                copies.append((pieces[n].at[b], full.at[pl.ds(row, HALF), pl.ds(col, 256)], sem.at[len(copies)]))
-        for copy in copies:
-            pltpu.make_async_copy(*copy).start()
-        for copy in copies:
-            pltpu.make_async_copy(*copy).wait()
+                full[pl.ds(row, HALF), pl.ds(col, 256)] = pieces[n][b]
         st_out[...] = jnp.zeros((8, ROWS), F32)
         loc_out[...] = jnp.zeros((8, ROWS), F32)
 
@@ -143,7 +138,7 @@
         grid_spec=pltpu.PrefetchScalarGridSpec(
             num_scalar_prefetch=1,
             grid=(TILES,),
-            in_specs=[HBM] * 8
+            in_specs=[pl.BlockSpec((4, HALF, 256), lambda i, at: (0, 0, 0))] * 8
             + [pl.BlockSpec((1, ROWS), lambda i, at: (0, 0)), pl.BlockSpec((TILE, WIDTH), lambda i, at: (i, 0))],
             out_specs=[
                 pl.BlockSpec((CUT, ROWS), lambda i, at: (0, 0)),
@@ -151,7 +146,7 @@
                 whole,
                 whole,
             ],
-            scratch_shapes=[pltpu.VMEM((ROWS, WIDTH), BF), pltpu.SemaphoreType.DMA((32,))],
+            scratch_shapes=[pltpu.VMEM((ROWS, WIDTH), BF)],
         ),
         out_shape=[
             jax.ShapeDtypeStruct((CUT, ROWS), BF),
@@ -172,27 +167,8 @@
     return top, total, hit
 
 
-def merge_body(*refs):
-    top, total, hit = merge([r[...] for r in refs[:-1]])
-    out = refs[-1]
-    out[...] = jnp.zeros((8, ROWS), F32)
-    out[pl.ds(0, 1), :] = top
-    out[pl.ds(1, 1), :] = total
-    out[pl.ds(2, 1), :] = hit
-
-
 def merge_call(*parts):
-    stat = pl.BlockSpec((8, ROWS), lambda i: (0, 0))
-    return pl.pallas_call(
-        merge_body,
-        grid=(1,),
-        in_specs=[stat] * len(parts),
-        out_specs=stat,
-        out_shape=jax.ShapeDtypeStruct((8, ROWS), F32),
-        compiler_params=params(),
-        cost_estimate=SMALL,
-        name="merge",
-    )(*parts)
+    return jnp.concatenate([*merge(parts), jnp.zeros((5, ROWS), F32)])
 
 
 def finish_body(a, b, st, tid, mix, weight, ep0, em0, e1, pack, grad_mix, e1_out):
@@ -311,13 +287,14 @@
     return sum(x.astype(F32) for x in xs)
 
 
-def scatter(keep, recv, c, first, second):
+def scatter(keep, recv, c, first, second, others):
     b = [add(keep[d], recv[d // 2][d % 2]) for d in range(4)]
     u = [cross(b[d].astype(BF), 0, 4 - d) for d in (1, 2, 3)]
-    *u, work = gate(*u, first())
+    u1, u2, u3, work, *others = gate(*u, first(), *others)
+    u = [u1, u2, u3]
     t = add(b[0], *u)
     u = [cross(t[d].astype(BF), 1, 4 - d) for d in (1, 2, 3)]
-    *u, work = gate(*u, second(work))
+    *u, work = gate(*u, second(work, *others))
     f = add(t[0], *u)
     low, high = f[:, :128], f[:, 128:]
     mine, other = jnp.where(c == 0, low, high), jnp.where(c == 0, high, low)
@@ -325,53 +302,40 @@
     return jnp.where(c == 0, jnp.concatenate([mine, got]), jnp.concatenate([got, mine])), work
 
 
-def embed_body(base, at, tgt, ep, em, ed, pack_p, pack_m, pack_d, feats, *refs):
-    out, q, sem = refs[-3:]
+def embed_body(base, at, tgt, ep, em, ed, pack_p, pack_m, pack_d, *refs):
+    feats, out = refs[:4], refs[-1]
     i = pl.program_id(0)
-
-    def copies(n, d):
-        group = (at[3] + d) & 3
-        for k in range(8):
-            dst = q.at[pl.ds(n * ROWS, ROWS), pl.ds(k * 128, 128)]
-            yield pltpu.make_async_copy(feats.at[group, k // 2, k % 2], dst, sem.at[n * 8 + k])
-
-    @pl.when(i == 0)
-    def _():
-        for n, d in enumerate((0, 1, 3, 2)):
-            for copy in copies(n, d):
-                copy.start()
-        for n, d in enumerate((0, 1, 3, 2)):
-            for copy in copies(n, d):
-                copy.wait()
 
     parts = [tgt[...]]
     tile = base // TILE + i
     for e, pack in ((ep, pack_p), (em, pack_m), (ed, pack_d)):
         parts.append(token_grad(e[...], pack, pack[pl.ds(tile, 1), :], tile * TILE))
-    out[...] = dot_nn(jnp.concatenate(parts, axis=1), q[...]).astype(BF)
+    q = [jnp.concatenate([f[0, k // 2, k % 2] for k in range(8)], axis=1) for f in feats]
+    out[...] = dot_nn(jnp.concatenate(parts, axis=1), jnp.concatenate(q, axis=0)).astype(BF)
 
 
 def embed_call(at, base, tgt, ep, em, ed, packs, feats, into, name):
     first = base // TILE
     tile = pl.BlockSpec((TILE, ROWS), lambda i, at: (i, 0))
     pack = pl.BlockSpec((8, ROWS), lambda i, at: (0, 0))
+    feat = lambda d: pl.BlockSpec((1, 4, 2, ROWS, 128), lambda i, at: ((at[3] + d) & 3, 0, 0, 0, 0))
     more = [] if into is None else [into]
     return pl.pallas_call(
         functools.partial(embed_body, base),
         grid_spec=pltpu.PrefetchScalarGridSpec(
             num_scalar_prefetch=1,
             grid=(CUT // TILE,),
-            in_specs=[pl.BlockSpec((TILE, ROWS), lambda i, at: (i + first, 0)), tile, tile, tile, pack, pack, pack, HBM]
+            in_specs=[pl.BlockSpec((TILE, ROWS), lambda i, at: (i + first, 0)), tile, tile, tile, pack, pack, pack]
+            + [feat(d) for d in (0, 1, 3, 2)]
             + [HBM] * len(more),
             out_specs=pl.BlockSpec((TILE, 1024), lambda i, at: (i + first, 0)),
-            scratch_shapes=[pltpu.VMEM((4 * ROWS, 1024), BF), pltpu.SemaphoreType.DMA((32,))],
         ),
         out_shape=jax.ShapeDtypeStruct((VOC, 1024), BF),
-        input_output_aliases={9: 0} if more else {},
+        input_output_aliases={12: 0} if more else {},
         compiler_params=params(),
         cost_estimate=SMALL,
         name=name,
-    )(at, tgt, ep, em, ed, *packs, feats, *more)
+    )(at, tgt, ep, em, ed, *packs, *[feats] * 4, *more)
 
 
 def local(comp_hidden, embed, mix, targets, weight):
@@ -410,7 +374,8 @@
         recv,
         c,
         lambda: embed_call(at, 0, tgt, ep0, em0, ed0, packs, feats, None, "embed_a"),
-        lambda made: embed_call(at, CUT, tgt, ep1, em1, ed1, packs, feats, made, "embed_b"),
+        lambda made, ep1, ed1: embed_call(at, CUT, tgt, ep1, em1, ed1, packs, feats, made, "embed_b"),
+        (ep1, ed1),
     )
     return grad_hidden.reshape(4, 128, 128), grad_embed, grad_mix
 

time: 183 us -> 179 us (0.978)
  waiting for transfers between devices: 46.8 us -> 39.7 us
  starting transfers between devices: 44.8 us -> 51.6 us
  Pallas kernels: 59.9 us -> 54 us
  other arithmetic: 7.47 us -> 10.5 us
    ppermute x15, starting transfers between devices: 21.8 us -> 27.3 us  [shift(): return lax.ppermute(a, axis, [((i + d) % 4, i) for i in range(4)])]
    ppermute x9, waiting for transfers between devices: 7.83 us -> 4.96 us  [sibling(): return lax.ppermute(a, 'c', [(0, 1), (1, 0)])]
    pallas_call x2 -> x0, Pallas kernels: 2.79 us -> none  [merge_call(): pl.pallas_call(merge_body, grid=(1,), in_specs=[stat] * len(parts), out_s...]
    ppermute x15, waiting for transfers between devices: 22 us -> 19.5 us  [shift(): return lax.ppermute(a, axis, [((i + d) % 4, i) for i in range(4)])]
    pallas_call x2, Pallas kernels: 21 us -> 18.8 us  [embed_call(): pl.pallas_call(functools.partial(embed_body, base), grid_spec=pltpu.Prefe...]
    convert_element_type x1, other arithmetic: 1.41 us -> 3.29 us  [scatter(): u = [cross(b[d].astype(BF), 0, 4 - d) for d in (1, 2, 3)]]
    unnamed x62 -> x50, local copies, waits for them, and re-layouts: 7.77 us -> 6.35 us
  transfers between devices with their start and end apart: 38 -> 38, of which waited for: 21 -> 18; matrix products, arithmetic and copies ran while one was open for 3% -> 4% of each run, Pallas kernels for 33% -> 30%
where the time goes in v6:
time: 179 us; the launch traced here: 177 us
  Pallas kernels  54 us (30%)
  starting transfers between devices  51.6 us (29%)
  waiting for transfers between devices  39.7 us (22%)
  between operations  14.3 us (8%)
  other arithmetic  10.5 us (6%)
  local copies, waits for them, and re-layouts  7.12 us (4%)
    ppermute x15, starting transfers between devices, shift(): return lax.ppermute(a, axis, [((i + d) % 4, i) for i in range(4)])  27.3 us
    ppermute x12, starting transfers between devices, cross(): return lax.ppermute(a, ('x', 'z', 'c'), pairs)  21.6 us
    ppermute x15, waiting for transfers between devices, shift(): return lax.ppermute(a, axis, [((i + d) % 4, i) for i in range(4)])  19.5 us
    pallas_call x2, Pallas kernels, embed_call(): pl.pallas_call(functools.partial(embed_body, base), grid_spec=pltpu.Prefe...  18.8 us
    pallas_call x1, Pallas kernels, hidden_call(): pl.pallas_call(hidden_body, grid_spec=pltpu.PrefetchScalarGridSpec(num_sc...  16.9 us
    pallas_call x1, Pallas kernels, logits_call(): pl.pallas_call(logits_body, grid_spec=pltpu.PrefetchScalarGridSpec(num_sc...  16.9 us
    ppermute x12, waiting for transfers between devices, cross(): return lax.ppermute(a, ('x', 'z', 'c'), pairs)  15.3 us
    unnamed x50, local copies, waits for them, and re-layouts  6.35 us
  transfers between devices with their start and end apart: 38, of which 18 were waited for; matrix products, arithmetic and copies ran while one was open for 4% of the time, Pallas kernels for 30%

profile of v6, /device:TPU:0, one launch (start us, length us, event | category | flops | bytes accessed | tf_op | source)
XLA Modules:
  0.0 177.3 jit_solution(5400088850351605647)
XLA Ops:
  7.2 0.9 broadcast_select_fusion.1
  8.2 1.2 collective-permute-done
  9.5 1.6 collective-permute-start.3
  11.1 2.7 %collective-permute-start.2 = (bf16[256,256]{1,0:T(8,128)(2,1)S(1)}, bf16[256,256]{1,0:T(8,128)(2,1)S(1)}, u32[]{:S(2)}, u32[]{:S(2)}) collective-permute-start(bf16[256,256]{1,0:T(8,128)(2,1)S(1)} %maximum_select_fusion.2), channel_id=1, source_target_pairs={{64,0},{20,4},{72,8},{28,12},{80,16},{4,20},{88,24},{12,28},{96,32... | collective-permute-start | bytes 393224 | tf_op jit(solution)/shard_map/ppermute | solution.py:36
  13.9 1.4 collective-permute-start.1
  15.7 2.5 %collective-permute-done.2 = bf16[256,256]{1,0:T(8,128)(2,1)S(1)} collective-permute-done((bf16[256,256]{1,0:T(8,128)(2,1)S(1)}, bf16[256,256]{1,0:T(8,128)(2,1)S(1)}, u32[]{:S(2)}, u32[]{:S(2)}) %collective-permute-start.2) | collective-permute-done | bytes 131104 | tf_op jit(solution)/shard_map/ppermute | solution.py:36
  18.2 0.6 collective-permute-done.1
  18.9 2.0 %collective-permute-start.6 = (bf16[4,256,256]{2,1,0:T(8,128)(2,1)S(1)}, bf16[4,256,256]{2,1,0:T(8,128)(2,1)S(1)}, u32[]{:S(2)}, u32[]{:S(2)}) collective-permute-start(bf16[4,256,256]{2,1,0:T(8,128)(2,1)S(1)} %pad_maximum_fusion.refs_0_), channel_id=1, source_target_pairs={{24,0},{100,4},{0,8},{108,12},{8,16},{116,20},{16,24},{124,28},{56... | collective-permute-start | bytes 1572872 | tf_op jit(solution)/shard_map/ppermute | solution.py:36
  20.9 3.6 %collective-permute-start.5 = (bf16[4,256,256]{2,1,0:T(8,128)(2,1)S(1)}, bf16[4,256,256]{2,1,0:T(8,128)(2,1)S(1)}, u32[]{:S(2)}, u32[]{:S(2)}) collective-permute-start(bf16[4,256,256]{2,1,0:T(8,128)(2,1)S(1)} %pad_maximum_fusion.refs_0_), channel_id=1, source_target_pairs={{16,0},{68,4},{24,8},{76,12},{0,16},{84,20},{8,24},{92,28},{48,32}... | collective-permute-start | bytes 1572872 | tf_op jit(solution)/shard_map/ppermute | solution.py:36
  24.5 1.0 collective-permute-start.4
  25.5 4.7 %collective-permute-done.6.refs_3_ = bf16[4,256,256]{2,1,0:T(8,128)(2,1)S(1)} collective-permute-done((bf16[4,256,256]{2,1,0:T(8,128)(2,1)S(1)}, bf16[4,256,256]{2,1,0:T(8,128)(2,1)S(1)}, u32[]{:S(2)}, u32[]{:S(2)}) %collective-permute-start.6) | collective-permute-done | bytes 524320 | tf_op jit(solution)/shard_map/ppermute | solution.py:36
  30.2 7.1 %collective-permute-done.5.refs_2_ = bf16[4,256,256]{2,1,0:T(8,128)(2,1)S(1)} collective-permute-done((bf16[4,256,256]{2,1,0:T(8,128)(2,1)S(1)}, bf16[4,256,256]{2,1,0:T(8,128)(2,1)S(1)}, u32[]{:S(2)}, u32[]{:S(2)}) %collective-permute-start.5) | collective-permute-done | bytes 524320 | tf_op jit(solution)/shard_map/ppermute | solution.py:36
  37.8 1.6 collective-permute-start.11
  39.3 0.7 broadcast_subtract_fusion
  40.0 0.7 pad_add_fusion.at
  40.7 0.7 tile.2
  41.6 16.9 %logits.1 = (bf16[1024,512]{1,0:T(8,128)(2,1)}, bf16[1024,512]{1,0:T(8,128)(2,1)}, f32[8,512]{1,0:T(8,128)}, f32[8,512]{1,0:T(8,128)}) custom-call(s32[4]{0:T(128)} %pad_add_fusion.at, bf16[4,256,256]{2,1,0:T(8,128)(2,1)} %copy-done.6, bf16[4,256,256]{2,1,0:T(8,128)(2,1)} %copy-done.13, bf16[4,256,256]{2,1,0:T(8,128)(2,1)} %copy-done.12, ...), custom_call_target="tpu_custom_call" | custom-call | flops 1000 | bytes 1000 | tf_op jit(solution)/shard_map/logits/pallas_call | solution.py:136
  58.5 0.6 copy-done.19
  59.2 3.2 %collective-permute-start.20 = (bf16[1024,512]{1,0:T(8,128)(2,1)}, bf16[1024,512]{1,0:T(8,128)(2,1)S(1)}, u32[]{:S(2)}, u32[]{:S(2)}) collective-permute-start(bf16[1024,512]{1,0:T(8,128)(2,1)} %get-tuple-element.34.e0), channel_id=1, source_target_pairs={{3,0},{0,1},{1,2},{2,3},{7,4},{4,5},{5,6},{6,7},{11,8},{8,9},{9,10... | collective-permute-start | bytes 3145736 | tf_op jit(solution)/shard_map/ppermute | solution.py:21
  62.3 2.7 %collective-permute-start.19 = (bf16[1024,512]{1,0:T(8,128)(2,1)}, bf16[1024,512]{1,0:T(8,128)(2,1)S(1)}, u32[]{:S(2)}, u32[]{:S(2)}) collective-permute-start(bf16[1024,512]{1,0:T(8,128)(2,1)} %get-tuple-element.34.e0), channel_id=1, source_target_pairs={{1,0},{2,1},{3,2},{0,3},{5,4},{6,5},{7,6},{4,7},{9,8},{10,9},{11,1... | collective-permute-start | bytes 3145736 | tf_op jit(solution)/shard_map/ppermute | solution.py:21
  65.0 1.9 %collective-permute-start.14 = (f32[8,512]{1,0:T(8,128)}, f32[8,512]{1,0:T(8,128)S(1)}, u32[]{:S(2)}, u32[]{:S(2)}) collective-permute-start(f32[8,512]{1,0:T(8,128)} %get-tuple-element.36), channel_id=1, source_target_pairs={{96,0},{0,32},{32,64},{64,96},{97,1},{1,33},{33,65},{65,97},{98,2}... | collective-permute-start | bytes 49160 | tf_op jit(solution)/shard_map/ppermute | solution.py:21
  66.9 3.1 %collective-permute-start.13 = (f32[8,512]{1,0:T(8,128)}, f32[8,512]{1,0:T(8,128)S(1)}, u32[]{:S(2)}, u32[]{:S(2)}) collective-permute-start(f32[8,512]{1,0:T(8,128)} %get-tuple-element.36), channel_id=1, source_target_pairs={{64,0},{96,32},{0,64},{32,96},{65,1},{97,33},{1,65},{33,97},{66,2}... | collective-permute-start | bytes 49160 | tf_op jit(solution)/shard_map/ppermute | solution.py:21
  70.0 1.6 collective-permute-start.12
  71.7 0.6 collective-permute-done.13
  72.3 1.9 %collective-permute-done.12 = f32[8,512]{1,0:T(8,128)S(1)} collective-permute-done((f32[8,512]{1,0:T(8,128)}, f32[8,512]{1,0:T(8,128)S(1)}, u32[]{:S(2)}, u32[]{:S(2)}) %collective-permute-start.12) | collective-permute-done | bytes 16416 | tf_op jit(solution)/shard_map/ppermute | solution.py:21
  74.2 0.9 fusion.11
  75.1 0.8 collective-permute-start.17
  75.9 2.1 %collective-permute-start.16 = (f32[8,512]{1,0:T(8,128)S(1)}, f32[8,512]{1,0:T(8,128)S(1)}, u32[]{:S(2)}, u32[]{:S(2)}) collective-permute-start(f32[8,512]{1,0:T(8,128)S(1)} %maximum_maximum_fusion), channel_id=1, source_target_pairs={{16,0},{24,8},{0,16},{8,24},{17,1},{25,9},{1,17},{9,25},{18,2},{26... | collective-permute-start | bytes 49160 | tf_op jit(solution)/shard_map/ppermute | solution.py:21
  78.0 1.5 collective-permute-start.15
  79.5 0.5 collective-permute-done.17
  80.1 1.1 collective-permute-done.16
  81.1 0.6 collective-permute-done.15
  81.9 1.2 collective-permute-done.18.b
  83.1 5.2 %collective-permute-done.20.em0.em = bf16[1024,512]{1,0:T(8,128)(2,1)S(1)} collective-permute-done((bf16[1024,512]{1,0:T(8,128)(2,1)}, bf16[1024,512]{1,0:T(8,128)(2,1)S(1)}, u32[]{:S(2)}, u32[]{:S(2)}) %collective-permute-start.20) | collective-permute-done | bytes 1048608 | tf_op jit(solution)/shard_map/ppermute | solution.py:21
  88.3 1.0 copy-done.4
  89.7 1.4 finish.1
  91.2 0.9 collective-permute-start.21
  92.1 2.3 %collective-permute-start.22 = (bf16[1024,512]{1,0:T(8,128)(2,1)}, bf16[1024,512]{1,0:T(8,128)(2,1)S(1)}, u32[]{:S(2)}, u32[]{:S(2)}) collective-permute-start(bf16[1024,512]{1,0:T(8,128)(2,1)} %copy-done.5), channel_id=1, source_target_pairs={{1,0},{2,1},{3,2},{0,3},{5,4},{6,5},{7,6},{4,7},{9,8},{10,9},{11,1... | collective-permute-start | bytes 3145736 | tf_op jit(solution)/shard_map/ppermute | solution.py:21
  94.4 1.3 collective-permute-start.25
  95.7 1.0 collective-permute-start.24
  96.6 2.3 %collective-permute-start.23 = (f32[8,512]{1,0:T(8,128)}, f32[8,512]{1,0:T(8,128)S(1)}, u32[]{:S(2)}, u32[]{:S(2)}) collective-permute-start(f32[8,512]{1,0:T(8,128)} %get-tuple-element.40.pack), channel_id=1, source_target_pairs={{1,0},{2,1},{3,2},{0,3},{5,4},{6,5},{7,6},{4,7},{9,8},{10,9},{11,1... | collective-permute-start | bytes 49160 | tf_op jit(solution)/shard_map/ppermute | solution.py:21
  98.9 16.9 %hidden.1 = (f32[4,4,256,256]{3,2,1,0:T(8,128)}, bf16[2,4,256,256]{3,2,1,0:T(8,128)(2,1)}, bf16[2,4,256,256]{3,2,1,0:T(8,128)(2,1)}, bf16[2048,512]{1,0:T(8,128)(2,1)}) custom-call(s32[4]{0:T(128)} %pad_add_fusion.at, bf16[1024,512]{1,0:T(8,128)(2,1)} %get-tuple-element.34.e0, bf16[1024,512]{1,0:T(8,128)(2,1)} %get-tuple-element.39.e1.refs_2_, ...), custom_call_target="tpu_custom_call" | custom-call | flops 1000 | bytes 1000 | tf_op jit(solution)/shard_map/hidden/pallas_call | solution.py:260
  115.8 2.1 %collective-permute-done.25.refs_7_ = f32[8,512]{1,0:T(8,128)S(1)} collective-permute-done((f32[8,512]{1,0:T(8,128)}, f32[8,512]{1,0:T(8,128)S(1)}, u32[]{:S(2)}, u32[]{:S(2)}) %collective-permute-start.25) | collective-permute-done | bytes 16416 | tf_op jit(solution)/shard_map/ppermute | solution.py:21
  118.0 0.5 copy-done.20
  119.3 0.5 collective-permute-start.28
  119.8 2.6 %collective-permute-start.31 = (bf16[1024,512]{1,0:T(8,128)(2,1)}, bf16[1024,512]{1,0:T(8,128)(2,1)S(1)}, u32[]{:S(2)}, u32[]{:S(2)}) collective-permute-start(bf16[1024,512]{1,0:T(8,128)(2,1)} %get-tuple-element.52), channel_id=1, source_target_pairs={{1,0},{2,1},{3,2},{0,3},{5,4},{6,5},{7,6},{4,7},{9,8},{10,9},{11,1... | collective-permute-start | bytes 3145736 | tf_op jit(solution)/shard_map/ppermute | solution.py:21
  122.5 1.2 collective-permute-done.28
  123.7 3.3 %fusion.4 = (bf16[4,256,256]{2,1,0:T(8,128)(2,1)}, bf16[4,256,256]{2,1,0:T(8,128)(2,1)}, bf16[4,256,256]{2,1,0:T(8,128)(2,1)}) fusion(f32[4,4,256,256]{3,2,1,0:T(8,128)} %get-tuple-element.41, bf16[2,4,256,256]{3,2,1,0:T(8,128)(2,1)S(1)} %collective-permute-done.28, bf16[2,4,256,256]{3,2,1,0:T(8,128)(2,1)S(1)} %collective-permute-done.26), kind=kLoop, calls=%fused_computation.8 | loop fusion | flops 2359296 | bytes 6291456 | tf_op jit(solution)/shard_map/convert_element_type | solution.py:292
  127.0 2.9 %collective-permute-start.30 = (bf16[4,256,256]{2,1,0:T(8,128)(2,1)}, bf16[4,256,256]{2,1,0:T(8,128)(2,1)S(1)}, u32[]{:S(2)}, u32[]{:S(2)}) collective-permute-start(bf16[4,256,256]{2,1,0:T(8,128)(2,1)} %get-tuple-element.71), channel_id=1, source_target_pairs={{32,0},{12,4},{40,8},{20,12},{48,16},{28,20},{56,24},{4,28},{64,32... | collective-permute-start | bytes 1572872 | tf_op jit(solution)/shard_map/ppermute | solution.py:36
  129.9 1.0 collective-permute-start.29
  130.9 0.9 collective-permute-start.27
  131.8 9.4 %embed_a.1.refs_3_ = bf16[2048,1024]{1,0:T(8,128)(2,1)} custom-call(s32[4]{0:T(128)} %pad_add_fusion.at, bf16[2048,512]{1,0:T(8,128)(2,1)} %get-tuple-element.46.tgt, bf16[1024,512]{1,0:T(8,128)(2,1)} %copy-done.5, bf16[1024,512]{1,0:T(8,128)(2,1)} %copy-done.4, bf16[1024,512]{1,0:T(8,128)(2,1)} %get-tuple-element.47.ed, f32[8,512]{1,0:T(8,128)} %get-tuple-element.48.pack_p, ...), custom_call_target="tpu_custom_call" | custom-call | flops 1000 | bytes 1000 | tf_op jit(solution)/shard_map/embed_a/pallas_call | solution.py:323
  141.2 4.2 %collective-permute-done.31.refs_4_ = bf16[1024,512]{1,0:T(8,128)(2,1)S(1)} collective-permute-done((bf16[1024,512]{1,0:T(8,128)(2,1)}, bf16[1024,512]{1,0:T(8,128)(2,1)S(1)}, u32[]{:S(2)}, u32[]{:S(2)}) %collective-permute-start.31) | collective-permute-done | bytes 1048608 | tf_op jit(solution)/shard_map/ppermute | solution.py:21
  145.4 3.3 %collective-permute-done.32.refs_5_ = bf16[1024,512]{1,0:T(8,128)(2,1)S(1)} collective-permute-done((bf16[1024,512]{1,0:T(8,128)(2,1)}, bf16[1024,512]{1,0:T(8,128)(2,1)S(1)}, u32[]{:S(2)}, u32[]{:S(2)}) %collective-permute-start.32) | collective-permute-done | bytes 1048608 | tf_op jit(solution)/shard_map/ppermute | solution.py:21
  148.7 1.0 copy-done.1
  150.0 2.0 %fusion.14 = (bf16[4,256,256]{2,1,0:T(8,128)(2,1)S(1)}, f32[4,256,256]{2,1,0:T(8,128)S(1)}) fusion(bf16[4,256,256]{2,1,0:T(8,128)(2,1)} %get-tuple-element.56, bf16[4,256,256]{2,1,0:T(8,128)(2,1)} %get-tuple-element.55, bf16[4,256,256]{2,1,0:T(8,128)(2,1)} %get-tuple-element.54, bf16[2,4,256,256]{3,2,1,0:T(8,128)(2,1)S(1)} %copy-done.10, ...), kind=kLoop, calls=%fused_computation.48 | loop fusion | flops 2359296 | bytes 4718592 | tf_op jit(solution)/shard_map/convert.2
  152.1 2.6 %collective-permute-start.35 = (bf16[256,256]{1,0:T(8,128)(2,1)S(1)}, bf16[256,256]{1,0:T(8,128)(2,1)S(1)}, u32[]{:S(2)}, u32[]{:S(2)}) collective-permute-start(bf16[256,256]{1,0:T(8,128)(2,1)S(1)} %get-tuple-element.74), channel_id=1, source_target_pairs={{8,0},{36,4},{16,8},{44,12},{24,16},{52,20},{0,24},{60,28},{40,32}... | collective-permute-start | bytes 393224 | tf_op jit(solution)/shard_map/ppermute | solution.py:36
  154.6 1.4 collective-permute-start.34
  156.4 9.4 %embed_b.1.refs_3_ = bf16[2048,1024]{1,0:T(8,128)(2,1)} custom-call(s32[4]{0:T(128)} %pad_add_fusion.at, bf16[2048,512]{1,0:T(8,128)(2,1)} %get-tuple-element.46.tgt, bf16[1024,512]{1,0:T(8,128)(2,1)} %get-tuple-element.57.ep, bf16[1024,512]{1,0:T(8,128)(2,1)} %get-tuple-element.53.em, ...), custom_call_target="tpu_custom_call", output_to_operand_aliasing={{}: (12, {})} | custom-call | flops 1000 | bytes 1000 | tf_op jit(solution)/shard_map/embed_b/pallas_call | solution.py:323
  165.9 0.6 copy-done.16
  166.5 0.7 copy-done.18
  167.2 1.1 fusion.7
  168.4 1.3 collective-permute-done.36
  169.7 0.7 maximum_select_fusion
  (91 shorter events, 3.9 us)
Async XLA Ops:
  7.2 124.6 %all-gather.3.cloned.1.call-start = ((), (), s32[]{:S(2)}) async-start(), calls=%async_computation | async-start | bytes 4325376 | tf_op jit(solution)/shard_map/all_gather | solution.py:359
  8.1 1.3 collective-permute-start
  9.5 6.2 %collective-permute-start.3 = (bf16[256,256]{1,0:T(8,128)(2,1)S(1)}, bf16[256,256]{1,0:T(8,128)(2,1)S(1)}, u32[]{:S(2)}, u32[]{:S(2)}) collective-permute-start(bf16[256,256]{1,0:T(8,128)(2,1)S(1)} %maximum_select_fusion.2), channel_id=1, source_target_pairs={{96,0},{28,4},{104,8},{4,12},{112,16},{12,20},{120,24},{20,28},{0,... | collective-permute-start | bytes 393224 | tf_op jit(solution)/shard_map/ppermute | solution.py:36
  11.1 7.1 %collective-permute-start.2 = (bf16[256,256]{1,0:T(8,128)(2,1)S(1)}, bf16[256,256]{1,0:T(8,128)(2,1)S(1)}, u32[]{:S(2)}, u32[]{:S(2)}) collective-permute-start(bf16[256,256]{1,0:T(8,128)(2,1)S(1)} %maximum_select_fusion.2), channel_id=1, source_target_pairs={{64,0},{20,4},{72,8},{28,12},{80,16},{4,20},{88,24},{12,28},{96,32... | collective-permute-start | bytes 393224 | tf_op jit(solution)/shard_map/ppermute | solution.py:36
  13.9 5.0 %collective-permute-start.1 = (bf16[256,256]{1,0:T(8,128)(2,1)S(1)}, bf16[256,256]{1,0:T(8,128)(2,1)S(1)}, u32[]{:S(2)}, u32[]{:S(2)}) collective-permute-start(bf16[256,256]{1,0:T(8,128)(2,1)S(1)} %maximum_select_fusion.2), channel_id=1, source_target_pairs={{32,0},{12,4},{40,8},{20,12},{48,16},{28,20},{56,24},{4,28},{64,32... | collective-permute-start | bytes 393224 | tf_op jit(solution)/shard_map/ppermute | solution.py:36
  18.9 22.4 %copy-start.6 = (bf16[4,256,256]{2,1,0:T(8,128)(2,1)}, bf16[4,256,256]{2,1,0:T(8,128)(2,1)S(1)}, u32[]{:S(2)}) copy-start(bf16[4,256,256]{2,1,0:T(8,128)(2,1)S(1)} %pad_maximum_fusion.refs_0_) | copy-start | bytes 1572868
  18.9 11.3 %collective-permute-start.6 = (bf16[4,256,256]{2,1,0:T(8,128)(2,1)S(1)}, bf16[4,256,256]{2,1,0:T(8,128)(2,1)S(1)}, u32[]{:S(2)}, u32[]{:S(2)}) collective-permute-start(bf16[4,256,256]{2,1,0:T(8,128)(2,1)S(1)} %pad_maximum_fusion.refs_0_), channel_id=1, source_target_pairs={{24,0},{100,4},{0,8},{108,12},{8,16},{116,20},{16,24},{124,28},{56... | collective-permute-start | bytes 1572872 | tf_op jit(solution)/shard_map/ppermute | solution.py:36
  20.9 16.4 %collective-permute-start.5 = (bf16[4,256,256]{2,1,0:T(8,128)(2,1)S(1)}, bf16[4,256,256]{2,1,0:T(8,128)(2,1)S(1)}, u32[]{:S(2)}, u32[]{:S(2)}) collective-permute-start(bf16[4,256,256]{2,1,0:T(8,128)(2,1)S(1)} %pad_maximum_fusion.refs_0_), channel_id=1, source_target_pairs={{16,0},{68,4},{24,8},{76,12},{0,16},{84,20},{8,24},{92,28},{48,32}... | collective-permute-start | bytes 1572872 | tf_op jit(solution)/shard_map/ppermute | solution.py:36
  24.5 12.8 %collective-permute-start.4 = (bf16[4,256,256]{2,1,0:T(8,128)(2,1)S(1)}, bf16[4,256,256]{2,1,0:T(8,128)(2,1)S(1)}, u32[]{:S(2)}, u32[]{:S(2)}) collective-permute-start(bf16[4,256,256]{2,1,0:T(8,128)(2,1)S(1)} %pad_maximum_fusion.refs_0_), channel_id=1, source_target_pairs={{8,0},{36,4},{16,8},{44,12},{24,16},{52,20},{0,24},{60,28},{40,32}... | collective-permute-start | bytes 1572872 | tf_op jit(solution)/shard_map/ppermute | solution.py:36
  25.5 15.1 %collective-permute-start.7 = (bf16[4,256,256]{2,1,0:T(8,128)(2,1)S(1)}, bf16[4,256,256]{2,1,0:T(8,128)(2,1)S(1)}, u32[]{:S(2)}, u32[]{:S(2)}) collective-permute-start(bf16[4,256,256]{2,1,0:T(8,128)(2,1)S(1)} %pad_maximum_fusion.refs_0_), channel_id=1, source_target_pairs={{0,4},{4,0},{1,5},{5,1},{2,6},{6,2},{3,7},{7,3},{8,12},{12,8},{9,1... | collective-permute-start | bytes 1572872 | tf_op jit(solution)/shard_map/ppermute | solution.py:25
  30.2 11.2 %copy-start.11 = (bf16[4,256,256]{2,1,0:T(8,128)(2,1)}, bf16[4,256,256]{2,1,0:T(8,128)(2,1)S(1)}, u32[]{:S(2)}) copy-start(bf16[4,256,256]{2,1,0:T(8,128)(2,1)S(1)} %collective-permute-done.6.refs_3_) | copy-start | bytes 1572868
  30.2 10.5 %collective-permute-start.10 = (bf16[4,256,256]{2,1,0:T(8,128)(2,1)S(1)}, bf16[4,256,256]{2,1,0:T(8,128)(2,1)S(1)}, u32[]{:S(2)}, u32[]{:S(2)}) collective-permute-start(bf16[4,256,256]{2,1,0:T(8,128)(2,1)S(1)} %collective-permute-done.6.refs_3_), channel_id=1, source_target_pairs={{0,4},{4,0},{1,5},{5,1},{2,6},{6,2},{3,7},{7,3},{8,12},{12,8},{9,1... | collective-permute-start | bytes 1572872 | tf_op jit(solution)/shard_map/ppermute | solution.py:25
  37.2 4.1 %copy-start.12 = (bf16[4,256,256]{2,1,0:T(8,128)(2,1)}, bf16[4,256,256]{2,1,0:T(8,128)(2,1)S(1)}, u32[]{:S(2)}) copy-start(bf16[4,256,256]{2,1,0:T(8,128)(2,1)S(1)} %collective-permute-done.5.refs_2_) | copy-start | bytes 1572868
  37.2 3.4 %collective-permute-start.9 = (bf16[4,256,256]{2,1,0:T(8,128)(2,1)S(1)}, bf16[4,256,256]{2,1,0:T(8,128)(2,1)}, u32[]{:S(2)}, u32[]{:S(2)}) collective-permute-start(bf16[4,256,256]{2,1,0:T(8,128)(2,1)S(1)} %collective-permute-done.5.refs_2_), channel_id=1, source_target_pairs={{0,4},{4,0},{1,5},{5,1},{2,6},{6,2},{3,7},{7,3},{8,12},{12,8},{9,1... | collective-permute-start | bytes 1572872 | tf_op jit(solution)/shard_map/ppermute | solution.py:25
  37.3 4.1 %copy-start.13 = (bf16[4,256,256]{2,1,0:T(8,128)(2,1)}, bf16[4,256,256]{2,1,0:T(8,128)(2,1)S(1)}, u32[]{:S(2)}) copy-start(bf16[4,256,256]{2,1,0:T(8,128)(2,1)S(1)} %collective-permute-done.4.refs_1_) | copy-start | bytes 1572868
  37.3 3.4 %collective-permute-start.8 = (bf16[4,256,256]{2,1,0:T(8,128)(2,1)S(1)}, bf16[4,256,256]{2,1,0:T(8,128)(2,1)}, u32[]{:S(2)}, u32[]{:S(2)}) collective-permute-start(bf16[4,256,256]{2,1,0:T(8,128)(2,1)S(1)} %collective-permute-done.4.refs_1_), channel_id=1, source_target_pairs={{0,4},{4,0},{1,5},{5,1},{2,6},{6,2},{3,7},{7,3},{8,12},{12,8},{9,1... | collective-permute-start | bytes 1572872 | tf_op jit(solution)/shard_map/ppermute | solution.py:25
  37.8 20.7 %collective-permute-start.11 = (bf16[512,128]{1,0:T(8,128)(2,1)}, bf16[512,128]{1,0:T(8,128)(2,1)S(1)}, u32[]{:S(2)}, u32[]{:S(2)}) collective-permute-start(bf16[512,128]{1,0:T(8,128)(2,1)} %bitcast.55), channel_id=1, source_target_pairs={{0,0},{1,32},{2,64},{3,96},{32,1},{33,33},{34,65},{35,97},{64,2},{... | collective-permute-start | bytes 393224 | tf_op jit(solution)/shard_map/ppermute | solution.py:348
  40.6 0.8 copy-start.14
  40.6 1.0 copy-start.15
  58.5 0.7 copy-start.19
  59.2 29.1 %collective-permute-start.20 = (bf16[1024,512]{1,0:T(8,128)(2,1)}, bf16[1024,512]{1,0:T(8,128)(2,1)S(1)}, u32[]{:S(2)}, u32[]{:S(2)}) collective-permute-start(bf16[1024,512]{1,0:T(8,128)(2,1)} %get-tuple-element.34.e0), channel_id=1, source_target_pairs={{3,0},{0,1},{1,2},{2,3},{7,4},{4,5},{5,6},{6,7},{11,8},{8,9},{9,10... | collective-permute-start | bytes 3145736 | tf_op jit(solution)/shard_map/ppermute | solution.py:21
  62.3 25.9 %collective-permute-start.19 = (bf16[1024,512]{1,0:T(8,128)(2,1)}, bf16[1024,512]{1,0:T(8,128)(2,1)S(1)}, u32[]{:S(2)}, u32[]{:S(2)}) collective-permute-start(bf16[1024,512]{1,0:T(8,128)(2,1)} %get-tuple-element.34.e0), channel_id=1, source_target_pairs={{1,0},{2,1},{3,2},{0,3},{5,4},{6,5},{7,6},{4,7},{9,8},{10,9},{11,1... | collective-permute-start | bytes 3145736 | tf_op jit(solution)/shard_map/ppermute | solution.py:21
  65.0 6.7 %collective-permute-start.14 = (f32[8,512]{1,0:T(8,128)}, f32[8,512]{1,0:T(8,128)S(1)}, u32[]{:S(2)}, u32[]{:S(2)}) collective-permute-start(f32[8,512]{1,0:T(8,128)} %get-tuple-element.36), channel_id=1, source_target_pairs={{96,0},{0,32},{32,64},{64,96},{97,1},{1,33},{33,65},{65,97},{98,2}... | collective-permute-start | bytes 49160 | tf_op jit(solution)/shard_map/ppermute | solution.py:21
  66.9 5.5 %collective-permute-start.13 = (f32[8,512]{1,0:T(8,128)}, f32[8,512]{1,0:T(8,128)S(1)}, u32[]{:S(2)}, u32[]{:S(2)}) collective-permute-start(f32[8,512]{1,0:T(8,128)} %get-tuple-element.36), channel_id=1, source_target_pairs={{64,0},{96,32},{0,64},{32,96},{65,1},{97,33},{1,65},{33,97},{66,2}... | collective-permute-start | bytes 49160 | tf_op jit(solution)/shard_map/ppermute | solution.py:21
  70.0 4.2 %collective-permute-start.12 = (f32[8,512]{1,0:T(8,128)}, f32[8,512]{1,0:T(8,128)S(1)}, u32[]{:S(2)}, u32[]{:S(2)}) collective-permute-start(f32[8,512]{1,0:T(8,128)} %get-tuple-element.36), channel_id=1, source_target_pairs={{32,0},{64,32},{96,64},{0,96},{33,1},{65,33},{97,65},{1,97},{34,2}... | collective-permute-start | bytes 49160 | tf_op jit(solution)/shard_map/ppermute | solution.py:21
  75.1 5.0 %collective-permute-start.17 = (f32[8,512]{1,0:T(8,128)S(1)}, f32[8,512]{1,0:T(8,128)S(1)}, u32[]{:S(2)}, u32[]{:S(2)}) collective-permute-start(f32[8,512]{1,0:T(8,128)S(1)} %maximum_maximum_fusion), channel_id=1, source_target_pairs={{24,0},{0,8},{8,16},{16,24},{25,1},{1,9},{9,17},{17,25},{26,2},{2,... | collective-permute-start | bytes 49160 | tf_op jit(solution)/shard_map/ppermute | solution.py:21
  75.9 5.2 %collective-permute-start.16 = (f32[8,512]{1,0:T(8,128)S(1)}, f32[8,512]{1,0:T(8,128)S(1)}, u32[]{:S(2)}, u32[]{:S(2)}) collective-permute-start(f32[8,512]{1,0:T(8,128)S(1)} %maximum_maximum_fusion), channel_id=1, source_target_pairs={{16,0},{24,8},{0,16},{8,24},{17,1},{25,9},{1,17},{9,25},{18,2},{26... | collective-permute-start | bytes 49160 | tf_op jit(solution)/shard_map/ppermute | solution.py:21
  78.0 3.7 %collective-permute-start.15 = (f32[8,512]{1,0:T(8,128)S(1)}, f32[8,512]{1,0:T(8,128)S(1)}, u32[]{:S(2)}, u32[]{:S(2)}) collective-permute-start(f32[8,512]{1,0:T(8,128)S(1)} %maximum_maximum_fusion), channel_id=1, source_target_pairs={{8,0},{16,8},{24,16},{0,24},{9,1},{17,9},{25,17},{1,25},{10,2},{18... | collective-permute-start | bytes 49160 | tf_op jit(solution)/shard_map/ppermute | solution.py:21
  81.9 6.4 %copy-start.23 = (f32[8,512]{1,0:T(8,128)}, f32[8,512]{1,0:T(8,128)S(1)}, u32[]{:S(2)}) copy-start(f32[8,512]{1,0:T(8,128)S(1)} %maximum_maximum_fusion.1.a) | copy-start | bytes 49156
  81.9 1.2 collective-permute-start.18
  83.1 5.2 %copy-start.24 = (f32[8,512]{1,0:T(8,128)}, f32[8,512]{1,0:T(8,128)S(1)}, u32[]{:S(2)}) copy-start(f32[8,512]{1,0:T(8,128)S(1)} %collective-permute-done.18.b) | copy-start | bytes 49156
  88.3 1.1 copy-start.4
  88.3 1.4 copy-start.5
  91.2 26.8 %collective-permute-start.21 = (bf16[1024,512]{1,0:T(8,128)(2,1)}, bf16[1024,512]{1,0:T(8,128)(2,1)S(1)}, u32[]{:S(2)}, u32[]{:S(2)}) collective-permute-start(bf16[1024,512]{1,0:T(8,128)(2,1)} %get-tuple-element.39.e1.refs_2_), channel_id=1, source_target_pairs={{3,0},{0,1},{1,2},{2,3},{7,4},{4,5},{5,6},{6,7},{11,8},{8,9},{9,10... | collective-permute-start | bytes 3145736 | tf_op jit(solution)/shard_map/ppermute | solution.py:21
  92.1 25.9 %collective-permute-start.22 = (bf16[1024,512]{1,0:T(8,128)(2,1)}, bf16[1024,512]{1,0:T(8,128)(2,1)S(1)}, u32[]{:S(2)}, u32[]{:S(2)}) collective-permute-start(bf16[1024,512]{1,0:T(8,128)(2,1)} %copy-done.5), channel_id=1, source_target_pairs={{1,0},{2,1},{3,2},{0,3},{5,4},{6,5},{7,6},{4,7},{9,8},{10,9},{11,1... | collective-permute-start | bytes 3145736 | tf_op jit(solution)/shard_map/ppermute | solution.py:21
  94.4 23.5 %collective-permute-start.25 = (f32[8,512]{1,0:T(8,128)}, f32[8,512]{1,0:T(8,128)S(1)}, u32[]{:S(2)}, u32[]{:S(2)}) collective-permute-start(f32[8,512]{1,0:T(8,128)} %get-tuple-element.40.pack), channel_id=1, source_target_pairs={{2,0},{3,1},{0,2},{1,3},{6,4},{7,5},{4,6},{5,7},{10,8},{11,9},{8,1... | collective-permute-start | bytes 49160 | tf_op jit(solution)/shard_map/ppermute | solution.py:21
  95.7 22.3 %collective-permute-start.24 = (f32[8,512]{1,0:T(8,128)}, f32[8,512]{1,0:T(8,128)S(1)}, u32[]{:S(2)}, u32[]{:S(2)}) collective-permute-start(f32[8,512]{1,0:T(8,128)} %get-tuple-element.40.pack), channel_id=1, source_target_pairs={{3,0},{0,1},{1,2},{2,3},{7,4},{4,5},{5,6},{6,7},{11,8},{8,9},{9,10... | collective-permute-start | bytes 49160 | tf_op jit(solution)/shard_map/ppermute | solution.py:21
  96.6 21.3 %collective-permute-start.23 = (f32[8,512]{1,0:T(8,128)}, f32[8,512]{1,0:T(8,128)S(1)}, u32[]{:S(2)}, u32[]{:S(2)}) collective-permute-start(f32[8,512]{1,0:T(8,128)} %get-tuple-element.40.pack), channel_id=1, source_target_pairs={{1,0},{2,1},{3,2},{0,3},{5,4},{6,5},{7,6},{4,7},{9,8},{10,9},{11,1... | collective-permute-start | bytes 49160 | tf_op jit(solution)/shard_map/ppermute | solution.py:21
  117.9 0.6 copy-start.20
  117.9 0.6 copy-start.21
  117.9 0.6 copy-start.22
  118.0 1.0 copy-start.2
  118.0 1.3 copy-start.3
  119.3 3.2 %collective-permute-start.26 = (bf16[2,4,256,256]{3,2,1,0:T(8,128)(2,1)}, bf16[2,4,256,256]{3,2,1,0:T(8,128)(2,1)S(1)}, u32[]{:S(2)}, u32[]{:S(2)}) collective-permute-start(bf16[2,4,256,256]{3,2,1,0:T(8,128)(2,1)} %get-tuple-element.44), channel_id=1, source_target_pairs={{0,4},{4,0},{1,5},{5,1},{2,6},{6,2},{3,7},{7,3},{8,12},{12,8},{9,1... | collective-permute-start | bytes 3145736 | tf_op jit(solution)/shard_map/ppermute | solution.py:25
  119.3 4.4 %collective-permute-start.28 = (bf16[2,4,256,256]{3,2,1,0:T(8,128)(2,1)}, bf16[2,4,256,256]{3,2,1,0:T(8,128)(2,1)S(1)}, u32[]{:S(2)}, u32[]{:S(2)}) collective-permute-start(bf16[2,4,256,256]{3,2,1,0:T(8,128)(2,1)} %get-tuple-element.45), channel_id=1, source_target_pairs={{0,4},{4,0},{1,5},{5,1},{2,6},{6,2},{3,7},{7,3},{8,12},{12,8},{9,1... | collective-permute-start | bytes 3145736 | tf_op jit(solution)/shard_map/ppermute | solution.py:25
  119.8 25.5 %collective-permute-start.31 = (bf16[1024,512]{1,0:T(8,128)(2,1)}, bf16[1024,512]{1,0:T(8,128)(2,1)S(1)}, u32[]{:S(2)}, u32[]{:S(2)}) collective-permute-start(bf16[1024,512]{1,0:T(8,128)(2,1)} %get-tuple-element.52), channel_id=1, source_target_pairs={{1,0},{2,1},{3,2},{0,3},{5,4},{6,5},{7,6},{4,7},{9,8},{10,9},{11,1... | collective-permute-start | bytes 3145736 | tf_op jit(solution)/shard_map/ppermute | solution.py:21
  122.5 26.2 %collective-permute-start.32 = (bf16[1024,512]{1,0:T(8,128)(2,1)}, bf16[1024,512]{1,0:T(8,128)(2,1)S(1)}, u32[]{:S(2)}, u32[]{:S(2)}) collective-permute-start(bf16[1024,512]{1,0:T(8,128)(2,1)} %get-tuple-element.53.em), channel_id=1, source_target_pairs={{3,0},{0,1},{1,2},{2,3},{7,4},{4,5},{5,6},{6,7},{11,8},{8,9},{9,10... | collective-permute-start | bytes 3145736 | tf_op jit(solution)/shard_map/ppermute | solution.py:21
  122.5 7.4 %copy-start.9 = (bf16[2,4,256,256]{3,2,1,0:T(8,128)(2,1)}, bf16[2,4,256,256]{3,2,1,0:T(8,128)(2,1)S(1)}, u32[]{:S(2)}) copy-start(bf16[2,4,256,256]{3,2,1,0:T(8,128)(2,1)S(1)} %collective-permute-done.26) | copy-start | bytes 3145732
  127.0 21.7 %collective-permute-start.30 = (bf16[4,256,256]{2,1,0:T(8,128)(2,1)}, bf16[4,256,256]{2,1,0:T(8,128)(2,1)S(1)}, u32[]{:S(2)}, u32[]{:S(2)}) collective-permute-start(bf16[4,256,256]{2,1,0:T(8,128)(2,1)} %get-tuple-element.71), channel_id=1, source_target_pairs={{32,0},{12,4},{40,8},{20,12},{48,16},{28,20},{56,24},{4,28},{64,32... | collective-permute-start | bytes 1572872 | tf_op jit(solution)/shard_map/ppermute | solution.py:36
  129.9 18.8 %collective-permute-start.29 = (bf16[4,256,256]{2,1,0:T(8,128)(2,1)}, bf16[4,256,256]{2,1,0:T(8,128)(2,1)S(1)}, u32[]{:S(2)}, u32[]{:S(2)}) collective-permute-start(bf16[4,256,256]{2,1,0:T(8,128)(2,1)} %get-tuple-element.72), channel_id=1, source_target_pairs={{64,0},{20,4},{72,8},{28,12},{80,16},{4,20},{88,24},{12,28},{96,32... | collective-permute-start | bytes 1572872 | tf_op jit(solution)/shard_map/ppermute | solution.py:36
  130.9 17.8 %collective-permute-start.27 = (bf16[4,256,256]{2,1,0:T(8,128)(2,1)}, bf16[4,256,256]{2,1,0:T(8,128)(2,1)}, u32[]{:S(2)}, u32[]{:S(2)}) collective-permute-start(bf16[4,256,256]{2,1,0:T(8,128)(2,1)} %get-tuple-element.73), channel_id=1, source_target_pairs={{96,0},{28,4},{104,8},{4,12},{112,16},{12,20},{120,24},{20,28},{0,... | collective-permute-start | bytes 1572872 | tf_op jit(solution)/shard_map/ppermute | solution.py:36
  141.2 8.8 %copy-start.10 = (bf16[2,4,256,256]{3,2,1,0:T(8,128)(2,1)S(1)}, bf16[2,4,256,256]{3,2,1,0:T(8,128)(2,1)}, u32[]{:S(2)}) copy-start(bf16[2,4,256,256]{3,2,1,0:T(8,128)(2,1)} %copy-done.9) | copy-start | bytes 3145732
  145.4 3.3 %copy-start = (bf16[1024,512]{1,0:T(8,128)(2,1)}, bf16[1024,512]{1,0:T(8,128)(2,1)S(1)}, u32[]{:S(2)}) copy-start(bf16[1024,512]{1,0:T(8,128)(2,1)S(1)} %collective-permute-done.31.refs_4_) | copy-start | bytes 3145732
  148.7 1.1 copy-start.1
  148.7 1.2 copy-start.7
  148.7 1.3 copy-start.8
  152.1 13.8 %collective-permute-start.35 = (bf16[256,256]{1,0:T(8,128)(2,1)S(1)}, bf16[256,256]{1,0:T(8,128)(2,1)S(1)}, u32[]{:S(2)}, u32[]{:S(2)}) collective-permute-start(bf16[256,256]{1,0:T(8,128)(2,1)S(1)} %get-tuple-element.74), channel_id=1, source_target_pairs={{8,0},{36,4},{16,8},{44,12},{24,16},{52,20},{0,24},{60,28},{40,32}... | collective-permute-start | bytes 393224 | tf_op jit(solution)/shard_map/ppermute | solution.py:36
  154.6 11.2 %collective-permute-start.34 = (bf16[256,256]{1,0:T(8,128)(2,1)S(1)}, bf16[256,256]{1,0:T(8,128)(2,1)S(1)}, u32[]{:S(2)}, u32[]{:S(2)}) collective-permute-start(bf16[256,256]{1,0:T(8,128)(2,1)S(1)} %get-tuple-element.75), channel_id=1, source_target_pairs={{16,0},{68,4},{24,8},{76,12},{0,16},{84,20},{8,24},{92,28},{48,32}... | collective-permute-start | bytes 393224 | tf_op jit(solution)/shard_map/ppermute | solution.py:36
  156.1 9.8 %collective-permute-start.33 = (bf16[256,256]{1,0:T(8,128)(2,1)S(1)}, bf16[256,256]{1,0:T(8,128)(2,1)S(1)}, u32[]{:S(2)}, u32[]{:S(2)}) collective-permute-start(bf16[256,256]{1,0:T(8,128)(2,1)S(1)} %get-tuple-element.76), channel_id=1, source_target_pairs={{24,0},{100,4},{0,8},{108,12},{8,16},{116,20},{16,24},{124,28},{56... | collective-permute-start | bytes 393224 | tf_op jit(solution)/shard_map/ppermute | solution.py:36
  165.8 0.7 copy-start.16
  165.8 0.7 copy-start.17
  166.5 0.7 copy-start.18
  168.3 1.4 collective-permute-start.36
Sparse Core Ops, SparseCore 0:
  59.3 48.3 all-gather.2

commit v7 on v6

--- a/solution.py
+++ b/solution.py
@@ -74,14 +74,16 @@
 SUB = 256
 
 
-def gather_pieces(block):
+def gather_pieces(block, *others):
     s = jnp.stack([block] + [cross(block, 0, d) for d in (1, 2, 3)])
-    return [s] + [cross(s, 1, d) for d in (1, 2, 3)]
-
-
-def logits_body(at, *refs):
+    far = [cross(s, 1, d) for d in (1, 2, 3)]
+    far[2], *others = gate(far[2], *others)
+    return [s] + far, others
+
+
+def logits_body(v0, at, *refs):
     pieces, refs = refs[:8], refs[8:]
-    tid, emb, e0_out, e1_out, st_out, loc_out, full = refs
+    tid, emb, before, e_out, st_out, loc_out, full = refs
     step = pl.program_id(0)
     x, z, c = at[0], at[1], at[2]
 
@@ -96,68 +98,54 @@
                 col = pl.multiple_of((((x + dx) & 3) * 4 + ((z + dz) & 3)) * 256, 256)
                 full[pl.ds(row, HALF), pl.ds(col, 256)] = pieces[n][b]
         st_out[...] = jnp.zeros((8, ROWS), F32)
-        loc_out[...] = jnp.zeros((8, ROWS), F32)
+        loc_out[...] = before[...]
 
     logits = dot_nt(emb[...], full[...])
     top = jnp.max(logits, axis=0, keepdims=True)
-    ids = lax.broadcasted_iota(jnp.int32, logits.shape, 0) + step * TILE
+    ids = lax.broadcasted_iota(jnp.int32, logits.shape, 0) + (v0 + step * TILE)
     hit = jnp.sum(jnp.where(ids == tid[...], logits, 0.0), axis=0, keepdims=True)
     e = jnp.exp(logits - top)
     total = jnp.sum(e, axis=0, keepdims=True)
-    e = e.astype(BF)
-
-    for s in range(TILES):
+    e_out[...] = e.astype(BF)
+    for s in range(CUT // TILE):
 
         @pl.when(step == s)
         def _():
             st_out[pl.ds(s, 1), :] = top
-            for k in (0, 1):
-                row = s * TILE + k * SUB
-                ref, row = (e0_out, row) if row < CUT else (e1_out, row - CUT)
-                ref[pl.ds(row, SUB), :] = e[k * SUB : (k + 1) * SUB]
-
-    @pl.when(step == 0)
-    def _():
-        loc_out[pl.ds(0, 1), :] = top
-        loc_out[pl.ds(1, 1), :] = total
-        loc_out[pl.ds(2, 1), :] = hit
-
-    @pl.when(step > 0)
-    def _():
-        old = loc_out[pl.ds(0, 1), :]
-        new = jnp.maximum(old, top)
-        loc_out[pl.ds(1, 1), :] = loc_out[pl.ds(1, 1), :] * jnp.exp(old - new) + total * jnp.exp(top - new)
-        loc_out[pl.ds(0, 1), :] = new
-        loc_out[pl.ds(2, 1), :] = loc_out[pl.ds(2, 1), :] + hit
-
-
-def logits_call(at, pieces, tid, emb):
-    whole = pl.BlockSpec((8, ROWS), lambda i, at: (0, 0))
-    return pl.pallas_call(
-        logits_body,
+
+    old = loc_out[pl.ds(0, 1), :]
+    new = jnp.maximum(old, top)
+    loc_out[pl.ds(1, 1), :] = loc_out[pl.ds(1, 1), :] * jnp.exp(old - new) + total * jnp.exp(top - new)
+    loc_out[pl.ds(0, 1), :] = new
+    loc_out[pl.ds(2, 1), :] = loc_out[pl.ds(2, 1), :] + hit
+
+
+def logits_call(at, pieces, tid, emb, v0, before, name):
+    first = v0 // TILE
+    stat = pl.BlockSpec((8, ROWS), lambda i, at: (0, 0))
+    return pl.pallas_call(
+        functools.partial(logits_body, v0),
         grid_spec=pltpu.PrefetchScalarGridSpec(
             num_scalar_prefetch=1,
-            grid=(TILES,),
+            grid=(CUT // TILE,),
             in_specs=[pl.BlockSpec((4, HALF, 256), lambda i, at: (0, 0, 0))] * 8
-            + [pl.BlockSpec((1, ROWS), lambda i, at: (0, 0)), pl.BlockSpec((TILE, WIDTH), lambda i, at: (i, 0))],
-            out_specs=[
-                pl.BlockSpec((CUT, ROWS), lambda i, at: (0, 0)),
-                pl.BlockSpec((VOC - CUT, ROWS), lambda i, at: (0, 0)),
-                whole,
-                whole,
+            + [
+                pl.BlockSpec((1, ROWS), lambda i, at: (0, 0)),
+                pl.BlockSpec((TILE, WIDTH), lambda i, at: (i + first, 0)),
+                stat,
             ],
+            out_specs=[pl.BlockSpec((TILE, ROWS), lambda i, at: (i, 0)), stat, stat],
             scratch_shapes=[pltpu.VMEM((ROWS, WIDTH), BF)],
         ),
         out_shape=[
             jax.ShapeDtypeStruct((CUT, ROWS), BF),
-            jax.ShapeDtypeStruct((VOC - CUT, ROWS), BF),
             jax.ShapeDtypeStruct((8, ROWS), F32),
             jax.ShapeDtypeStruct((8, ROWS), F32),
         ],
         compiler_params=params(),
         cost_estimate=SMALL,
-        name="logits",
-    )(at, *pieces, tid, emb)
+        name=name,
+    )(at, *pieces, tid, emb, before)
 
 
 def merge(parts):
@@ -171,7 +159,7 @@
     return jnp.concatenate([*merge(parts), jnp.zeros((5, ROWS), F32)])
 
 
-def finish_body(a, b, st, tid, mix, weight, ep0, em0, e1, pack, grad_mix, e1_out):
+def finish_body(a, b, st0, st1, tid, mix, weight, ep0, em0, e1, pack, grad_mix, e1_out):
     top, total, hit = merge([a[...], b[...]])
     lse = top + jnp.log(total)
     gap = hit - lse
@@ -191,19 +179,21 @@
         scaled.append(w * resp)
     d = jnp.concatenate(scaled, axis=1)
     pack[...] = jnp.zeros((8, ROWS), F32)
-    pack[pl.ds(0, TILES), :] = jnp.exp(st[pl.ds(0, TILES), :] - lse) * d
+    n = CUT // TILE
+    pack[pl.ds(0, n), :] = jnp.exp(st0[pl.ds(0, n), :] - lse) * d
+    pack[pl.ds(n, n), :] = jnp.exp(st1[pl.ds(0, n), :] - lse) * d
     pack[pl.ds(4, 1), :] = d
     pack[pl.ds(5, 1), :] = lse
     pack[pl.ds(6, 1), :] = tid[...].astype(F32)
 
 
-def finish_call(a, b, st, tid, mix, weight, *awaited):
+def finish_call(a, b, st0, st1, tid, mix, weight, *awaited):
     stat = pl.BlockSpec((8, ROWS), lambda i: (0, 0))
     part = pl.BlockSpec((4, 128), lambda i: (0, 0))
     return pl.pallas_call(
         finish_body,
         grid=(1,),
-        in_specs=[stat] * 3
+        in_specs=[stat] * 4
         + [pl.BlockSpec((1, ROWS), lambda i: (0, 0)), part, pl.BlockSpec((1, 128), lambda i: (0, 0))]
         + [HBM] * 3,
         out_specs=[stat, part, HBM],
@@ -212,11 +202,11 @@
             jax.ShapeDtypeStruct((4, 128), F32),
             jax.ShapeDtypeStruct((VOC - CUT, ROWS), BF),
         ],
-        input_output_aliases={8: 2},
+        input_output_aliases={9: 2},
         compiler_params=params(),
         cost_estimate=SMALL,
         name="finish",
-    )(a, b, st, tid, mix, weight, *awaited)
+    )(a, b, st0, st1, tid, mix, weight, *awaited)
 
 
 def token_grad(e, pack, scale, base):
@@ -242,7 +232,7 @@
     for k in range(4):
         cols = slice(k * 256, (k + 1) * 256)
         a, b = r[:HALF, cols], r[HALF:, cols]
-        keep[0, k] = jnp.where(first, a, b)
+        keep[0, k] = jnp.where(first, a, b).astype(BF)
         (send0, send1)[k // 2][k % 2, 0] = jnp.where(first, b, a).astype(BF)
 
 
@@ -273,7 +263,7 @@
             scratch_shapes=[pltpu.VMEM((ROWS, VOC), BF)],
         ),
         out_shape=[
-            jax.ShapeDtypeStruct((4, 4, HALF, 256), F32),
+            jax.ShapeDtypeStruct((4, 4, HALF, 256), BF),
         ]
         + [jax.ShapeDtypeStruct((2, 4, HALF, 256), BF)] * 2
         + [jax.ShapeDtypeStruct((VOC, ROWS), BF)],
@@ -351,17 +341,18 @@
     mine, other = jnp.where(c == 0, low, high), jnp.where(c == 0, high, low)
     got = sibling(other)
     block = jnp.where(c == 0, jnp.concatenate([mine, got], axis=1), jnp.concatenate([got, mine], axis=1))
-    pieces = gather_pieces(block)
+    pieces, (turned, at, tid) = gather_pieces(block, turned, at, tid)
     pieces = pieces + [sibling(p) for p in pieces]
 
-    e0, e1, st, loc = logits_call(at, pieces, tid, embed)
-    loc, turned = gate(loc, turned)
+    none = jnp.zeros((8, ROWS), F32).at[0].set(-3e38)
+    e0, st0, loc = logits_call(at, pieces, tid, embed, 0, none, "logits_a")
+    e1, st1, loc = logits_call(at, pieces, tid, embed, CUT, loc, "logits_b")
     feats = lax.all_gather(turned, ("x", "z", "c")).reshape(4, 4, 2, ROWS, 128)
     ep0, em0 = shift(e0, "y", 1), shift(e0, "y", 3)
 
     s = merge_call(loc, *(shift(loc, "x", d) for d in (1, 2, 3)))
     s = merge_call(s, *(shift(s, "z", d) for d in (1, 2, 3)))
-    pack, grad_mix, e1 = finish_call(s, sibling(s), st, tid, mix, weight.reshape(1, 128), ep0, em0, e1)
+    pack, grad_mix, e1 = finish_call(s, sibling(s), st0, st1, tid, mix, weight.reshape(1, 128), ep0, em0, e1)
     packs = [shift(pack, "y", d) for d in (1, 3, 2)]
     em1, ed0 = shift(e1, "y", 3), shift(ep0, "y", 1)
     keep, send0, send1, tgt = hidden_call(at, e0, e1, pack, embed)

time: 179 us -> 189 us (1.056)
  Pallas kernels: 54 us -> 58.5 us
  starting transfers between devices: 51.6 us -> 55.7 us
  waiting for transfers between devices: 39.7 us -> 43.4 us
  other arithmetic: 10.5 us -> 8.42 us
    ppermute x9, starting transfers between devices: 1.23 us -> 7.79 us  [sibling(): return lax.ppermute(a, 'c', [(0, 1), (1, 0)])]
    pallas_call x2 -> x3, Pallas kernels: 18.3 us -> 23.3 us  [the longest x2 21.8 us: logits_call(): pl.pallas_call(functools.partial(logits_body, v0), grid_spec=pltpu.Prefet...]
    ppermute x12, starting transfers between devices: 21.6 us -> 18.7 us  [cross(): return lax.ppermute(a, ('x', 'z', 'c'), pairs)]
    ppermute x12, waiting for transfers between devices: 15.3 us -> 17.9 us  [cross(): return lax.ppermute(a, ('x', 'z', 'c'), pairs)]
    ppermute x9, waiting for transfers between devices: 4.96 us -> 7.12 us  [sibling(): return lax.ppermute(a, 'c', [(0, 1), (1, 0)])]
    convert_element_type x1, other arithmetic: 3.29 us -> 1.38 us  [scatter(): u = [cross(b[d].astype(BF), 0, 4 - d) for d in (1, 2, 3)]]
    unnamed x50 -> x56, local copies, waits for them, and re-layouts: 6.35 us -> 6.34 us
  transfers between devices with their start and end apart: 38 -> 38, of which waited for: 18 -> 20; matrix products, arithmetic and copies ran while one was open for 4% -> 2% of each run, Pallas kernels for 30% -> 31%
where the time goes in v7:
time: 189 us; the launch traced here: 187 us
  Pallas kernels  58.5 us (31%)
  starting transfers between devices  55.7 us (29%)
  waiting for transfers between devices  43.4 us (23%)
  between operations  14.3 us (8%)
  other arithmetic  8.42 us (4%)
  local copies, waits for them, and re-layouts  7 us (4%)
    ppermute x15, starting transfers between devices, shift(): return lax.ppermute(a, axis, [((i + d) % 4, i) for i in range(4)])  27.6 us
    pallas_call x2, Pallas kernels, logits_call(): pl.pallas_call(functools.partial(logits_body, v0), grid_spec=pltpu.Prefet...  21.8 us
    pallas_call x2, Pallas kernels, embed_call(): pl.pallas_call(functools.partial(embed_body, base), grid_spec=pltpu.Prefe...  18.8 us
    ppermute x12, starting transfers between devices, cross(): return lax.ppermute(a, ('x', 'z', 'c'), pairs)  18.7 us
    ppermute x15, waiting for transfers between devices, shift(): return lax.ppermute(a, axis, [((i + d) % 4, i) for i in range(4)])  18.3 us
    ppermute x12, waiting for transfers between devices, cross(): return lax.ppermute(a, ('x', 'z', 'c'), pairs)  17.9 us
    pallas_call x1, Pallas kernels, hidden_call(): pl.pallas_call(hidden_body, grid_spec=pltpu.PrefetchScalarGridSpec(num_sc...  16.4 us
    ppermute x9, starting transfers between devices, sibling(): return lax.ppermute(a, 'c', [(0, 1), (1, 0)])  7.79 us
  transfers between devices with their start and end apart: 38, of which 20 were waited for; matrix products, arithmetic and copies ran while one was open for 2% of the time, Pallas kernels for 31%

profile of v7, /device:TPU:0, one launch (start us, length us, event | category | flops | bytes accessed | tf_op | source)
XLA Modules:
  0.0 187.2 jit_solution(655705992409009124)
XLA Ops:
  7.2 0.9 broadcast_select_fusion.1
  8.2 1.2 collective-permute-done
  9.5 1.6 collective-permute-start.3
  11.1 2.7 %collective-permute-start.2 = (bf16[256,256]{1,0:T(8,128)(2,1)S(1)}, bf16[256,256]{1,0:T(8,128)(2,1)S(1)}, u32[]{:S(2)}, u32[]{:S(2)}) collective-permute-start(bf16[256,256]{1,0:T(8,128)(2,1)S(1)} %maximum_select_fusion.2), channel_id=1, source_target_pairs={{64,0},{20,4},{72,8},{28,12},{80,16},{4,20},{88,24},{12,28},{96,32... | collective-permute-start | bytes 393224 | tf_op jit(solution)/shard_map/ppermute | solution.py:36
  13.9 1.4 collective-permute-start.1
  15.7 2.5 %collective-permute-done.2 = bf16[256,256]{1,0:T(8,128)(2,1)S(1)} collective-permute-done((bf16[256,256]{1,0:T(8,128)(2,1)S(1)}, bf16[256,256]{1,0:T(8,128)(2,1)S(1)}, u32[]{:S(2)}, u32[]{:S(2)}) %collective-permute-start.2) | collective-permute-done | bytes 131104 | tf_op jit(solution)/shard_map/ppermute | solution.py:36
  18.2 0.6 collective-permute-done.1
  18.9 2.0 %collective-permute-start.4 = (bf16[4,256,256]{2,1,0:T(8,128)(2,1)S(1)}, bf16[4,256,256]{2,1,0:T(8,128)(2,1)S(1)}, u32[]{:S(2)}, u32[]{:S(2)}) collective-permute-start(bf16[4,256,256]{2,1,0:T(8,128)(2,1)S(1)} %pad_maximum_fusion.refs_0_), channel_id=1, source_target_pairs={{24,0},{100,4},{0,8},{108,12},{8,16},{116,20},{16,24},{124,28},{56... | collective-permute-start | bytes 1572872 | tf_op jit(solution)/shard_map/ppermute | solution.py:36
  20.9 1.6 collective-permute-start.5
  22.4 0.7 broadcast_subtract_fusion
  23.1 0.6 pad_add_fusion.refs_2_
  23.8 6.4 %collective-permute-done.4.refs_0_ = bf16[4,256,256]{2,1,0:T(8,128)(2,1)S(1)} collective-permute-done((bf16[4,256,256]{2,1,0:T(8,128)(2,1)S(1)}, bf16[4,256,256]{2,1,0:T(8,128)(2,1)S(1)}, u32[]{:S(2)}, u32[]{:S(2)}) %collective-permute-start.4) | collective-permute-done | bytes 524320 | tf_op jit(solution)/shard_map/ppermute | solution.py:36
  30.2 0.6 tile.2
  31.0 1.9 %collective-permute-start.7 = (bf16[4,256,256]{2,1,0:T(8,128)(2,1)S(1)}, bf16[4,256,256]{2,1,0:T(8,128)(2,1)S(1)}, u32[]{:S(2)}, u32[]{:S(2)}) collective-permute-start(bf16[4,256,256]{2,1,0:T(8,128)(2,1)S(1)} %pad_maximum_fusion.refs_0_), channel_id=1, source_target_pairs={{16,0},{68,4},{24,8},{76,12},{0,16},{84,20},{8,24},{92,28},{48,32}... | collective-permute-start | bytes 1572872 | tf_op jit(solution)/shard_map/ppermute | solution.py:36
  32.9 0.7 collective-permute-start.6
  33.7 3.9 %collective-permute-start.8 = (bf16[4,256,256]{2,1,0:T(8,128)(2,1)S(1)}, bf16[4,256,256]{2,1,0:T(8,128)(2,1)S(1)}, u32[]{:S(2)}, u32[]{:S(2)}) collective-permute-start(bf16[4,256,256]{2,1,0:T(8,128)(2,1)S(1)} %pad_maximum_fusion.refs_0_), channel_id=1, source_target_pairs={{0,4},{4,0},{1,5},{5,1},{2,6},{6,2},{3,7},{7,3},{8,12},{12,8},{9,1... | collective-permute-start | bytes 1572872 | tf_op jit(solution)/shard_map/ppermute | solution.py:25
  37.6 4.2 %collective-permute-done.7.refs_2_ = bf16[4,256,256]{2,1,0:T(8,128)(2,1)S(1)} collective-permute-done((bf16[4,256,256]{2,1,0:T(8,128)(2,1)S(1)}, bf16[4,256,256]{2,1,0:T(8,128)(2,1)S(1)}, u32[]{:S(2)}, u32[]{:S(2)}) %collective-permute-start.7) | collective-permute-done | bytes 524320 | tf_op jit(solution)/shard_map/ppermute | solution.py:36
  41.8 1.7 collective-permute-start.10
  43.5 3.7 %collective-permute-done.6.refs_1_ = bf16[4,256,256]{2,1,0:T(8,128)(2,1)S(1)} collective-permute-done((bf16[4,256,256]{2,1,0:T(8,128)(2,1)S(1)}, bf16[4,256,256]{2,1,0:T(8,128)(2,1)S(1)}, u32[]{:S(2)}, u32[]{:S(2)}) %collective-permute-start.6) | collective-permute-done | bytes 524320 | tf_op jit(solution)/shard_map/ppermute | solution.py:36
  47.3 1.2 collective-permute-start.9
  48.5 2.2 %collective-permute-done.9.refs_5_ = bf16[4,256,256]{2,1,0:T(8,128)(2,1)S(1)} collective-permute-done((bf16[4,256,256]{2,1,0:T(8,128)(2,1)S(1)}, bf16[4,256,256]{2,1,0:T(8,128)(2,1)S(1)}, u32[]{:S(2)}, u32[]{:S(2)}) %collective-permute-start.9) | collective-permute-done | bytes 524320 | tf_op jit(solution)/shard_map/ppermute | solution.py:25
  51.0 0.5 copy-done.12
  51.8 10.9 %logits_a.1 = (bf16[1024,512]{1,0:T(8,128)(2,1)}, f32[8,512]{1,0:T(8,128)}, f32[8,512]{1,0:T(8,128)}) custom-call(s32[4]{0:T(128)} %get-tuple-element.50.at, bf16[4,256,256]{2,1,0:T(8,128)(2,1)} %copy-done, bf16[4,256,256]{2,1,0:T(8,128)(2,1)} %copy-done.9, bf16[4,256,256]{2,1,0:T(8,128)(2,1)} %copy-done.8, bf16[4,256,256]{2,1,0:T(8,128)(2,1)} %get-tuple-element.51.refs_3_, ...), custom_call_target="tpu_custom_call" | custom-call | flops 1000 | bytes 1000 | tf_op jit(solution)/shard_map/logits_a/pallas_call | solution.py:126
  62.7 0.9 collective-permute-start.20
  63.6 6.0 %collective-permute-start.19 = (bf16[1024,512]{1,0:T(8,128)(2,1)}, bf16[1024,512]{1,0:T(8,128)(2,1)S(1)}, u32[]{:S(2)}, u32[]{:S(2)}) collective-permute-start(bf16[1024,512]{1,0:T(8,128)(2,1)} %get-tuple-element.53.e0), channel_id=1, source_target_pairs={{1,0},{2,1},{3,2},{0,3},{5,4},{6,5},{7,6},{4,7},{9,8},{10,9},{11,1... | collective-permute-start | bytes 3145736 | tf_op jit(solution)/shard_map/ppermute | solution.py:21
  69.6 11.0 %logits_b.1 = (bf16[1024,512]{1,0:T(8,128)(2,1)}, f32[8,512]{1,0:T(8,128)}, f32[8,512]{1,0:T(8,128)}) custom-call(s32[4]{0:T(128)} %get-tuple-element.50.at, bf16[4,256,256]{2,1,0:T(8,128)(2,1)} %copy-done, bf16[4,256,256]{2,1,0:T(8,128)(2,1)} %copy-done.9, bf16[4,256,256]{2,1,0:T(8,128)(2,1)} %copy-done.8, bf16[4,256,256]{2,1,0:T(8,128)(2,1)} %get-tuple-element.51.refs_3_, ...), custom_call_target="tpu_custom_call" | custom-call | flops 1000 | bytes 1000 | tf_op jit(solution)/shard_map/logits_b/pallas_call | solution.py:126
  80.6 1.4 collective-permute-start.14
  82.0 2.2 %collective-permute-start.13 = (f32[8,512]{1,0:T(8,128)}, f32[8,512]{1,0:T(8,128)S(1)}, u32[]{:S(2)}, u32[]{:S(2)}) collective-permute-start(f32[8,512]{1,0:T(8,128)} %get-tuple-element.55), channel_id=1, source_target_pairs={{64,0},{96,32},{0,64},{32,96},{65,1},{97,33},{1,65},{33,97},{66,2}... | collective-permute-start | bytes 49160 | tf_op jit(solution)/shard_map/ppermute | solution.py:21
  84.2 2.0 %collective-permute-start.12 = (f32[8,512]{1,0:T(8,128)}, f32[8,512]{1,0:T(8,128)S(1)}, u32[]{:S(2)}, u32[]{:S(2)}) collective-permute-start(f32[8,512]{1,0:T(8,128)} %get-tuple-element.55), channel_id=1, source_target_pairs={{32,0},{64,32},{96,64},{0,96},{33,1},{65,33},{97,65},{1,97},{34,2}... | collective-permute-start | bytes 49160 | tf_op jit(solution)/shard_map/ppermute | solution.py:21
  86.3 1.1 collective-permute-done.13
  87.4 0.7 collective-permute-done.12
  88.1 0.9 fusion.11
  89.1 1.8 collective-permute-start.17
  90.9 1.9 %collective-permute-start.16 = (f32[8,512]{1,0:T(8,128)S(1)}, f32[8,512]{1,0:T(8,128)S(1)}, u32[]{:S(2)}, u32[]{:S(2)}) collective-permute-start(f32[8,512]{1,0:T(8,128)S(1)} %maximum_maximum_fusion), channel_id=1, source_target_pairs={{16,0},{24,8},{0,16},{8,24},{17,1},{25,9},{1,17},{9,25},{18,2},{26... | collective-permute-start | bytes 49160 | tf_op jit(solution)/shard_map/ppermute | solution.py:21
  92.8 1.7 collective-permute-start.15
  94.5 1.6 collective-permute-done.16
  96.9 1.2 collective-permute-done.18.b
  98.1 0.6 copy-done.27
  99.4 1.4 finish.1
  100.8 0.7 collective-permute-start.21
  101.6 2.5 %collective-permute-start.22 = (bf16[1024,512]{1,0:T(8,128)(2,1)}, bf16[1024,512]{1,0:T(8,128)(2,1)S(1)}, u32[]{:S(2)}, u32[]{:S(2)}) collective-permute-start(bf16[1024,512]{1,0:T(8,128)(2,1)} %copy-done.7), channel_id=1, source_target_pairs={{1,0},{2,1},{3,2},{0,3},{5,4},{6,5},{7,6},{4,7},{9,8},{10,9},{11,1... | collective-permute-start | bytes 3145736 | tf_op jit(solution)/shard_map/ppermute | solution.py:21
  104.3 0.9 collective-permute-start.24
  105.1 2.4 %collective-permute-start.23 = (f32[8,512]{1,0:T(8,128)}, f32[8,512]{1,0:T(8,128)S(1)}, u32[]{:S(2)}, u32[]{:S(2)}) collective-permute-start(f32[8,512]{1,0:T(8,128)} %get-tuple-element.60.pack), channel_id=1, source_target_pairs={{1,0},{2,1},{3,2},{0,3},{5,4},{6,5},{7,6},{4,7},{9,8},{10,9},{11,1... | collective-permute-start | bytes 49160 | tf_op jit(solution)/shard_map/ppermute | solution.py:21
  107.5 16.4 %hidden.1 = (bf16[4,4,256,256]{3,2,1,0:T(8,128)(2,1)}, bf16[2,4,256,256]{3,2,1,0:T(8,128)(2,1)}, bf16[2,4,256,256]{3,2,1,0:T(8,128)(2,1)}, bf16[2048,512]{1,0:T(8,128)(2,1)}) custom-call(s32[4]{0:T(128)} %get-tuple-element.50.at, bf16[1024,512]{1,0:T(8,128)(2,1)} %get-tuple-element.53.e0, bf16[1024,512]{1,0:T(8,128)(2,1)} %get-tuple-element.59.e1.refs_2_, ...), custom_call_target="tpu_custom_call" | custom-call | flops 1000 | bytes 1000 | tf_op jit(solution)/shard_map/hidden/pallas_call | solution.py:250
  123.9 3.9 %collective-permute-done.25.refs_7_ = f32[8,512]{1,0:T(8,128)S(1)} collective-permute-done((f32[8,512]{1,0:T(8,128)}, f32[8,512]{1,0:T(8,128)S(1)}, u32[]{:S(2)}, u32[]{:S(2)}) %collective-permute-start.25) | collective-permute-done | bytes 16416 | tf_op jit(solution)/shard_map/ppermute | solution.py:21
  129.5 0.5 collective-permute-start.28
  130.0 2.9 %collective-permute-start.31 = (bf16[1024,512]{1,0:T(8,128)(2,1)}, bf16[1024,512]{1,0:T(8,128)(2,1)S(1)}, u32[]{:S(2)}, u32[]{:S(2)}) collective-permute-start(bf16[1024,512]{1,0:T(8,128)(2,1)} %get-tuple-element.72), channel_id=1, source_target_pairs={{1,0},{2,1},{3,2},{0,3},{5,4},{6,5},{7,6},{4,7},{9,8},{10,9},{11,1... | collective-permute-start | bytes 3145736 | tf_op jit(solution)/shard_map/ppermute | solution.py:21
  133.0 0.9 collective-permute-done.28
  133.9 1.4 fusion.4
  135.3 3.5 %collective-permute-start.30 = (bf16[4,256,256]{2,1,0:T(8,128)(2,1)}, bf16[4,256,256]{2,1,0:T(8,128)(2,1)S(1)}, u32[]{:S(2)}, u32[]{:S(2)}) collective-permute-start(bf16[4,256,256]{2,1,0:T(8,128)(2,1)} %get-tuple-element.91), channel_id=1, source_target_pairs={{32,0},{12,4},{40,8},{20,12},{48,16},{28,20},{56,24},{4,28},{64,32... | collective-permute-start | bytes 1572872 | tf_op jit(solution)/shard_map/ppermute | solution.py:36
  138.8 0.9 collective-permute-start.27
  139.6 9.4 %embed_a.1.refs_3_ = bf16[2048,1024]{1,0:T(8,128)(2,1)} custom-call(s32[4]{0:T(128)} %get-tuple-element.50.at, bf16[2048,512]{1,0:T(8,128)(2,1)} %get-tuple-element.66.tgt, bf16[1024,512]{1,0:T(8,128)(2,1)} %copy-done.7, bf16[1024,512]{1,0:T(8,128)(2,1)} %copy-done.6, bf16[1024,512]{1,0:T(8,128)(2,1)} %get-tuple-element.67.ed, ...), custom_call_target="tpu_custom_call" | custom-call | flops 1000 | bytes 1000 | tf_op jit(solution)/shard_map/embed_a/pallas_call | solution.py:313
  149.0 6.8 %collective-permute-done.31.refs_4_ = bf16[1024,512]{1,0:T(8,128)(2,1)S(1)} collective-permute-done((bf16[1024,512]{1,0:T(8,128)(2,1)}, bf16[1024,512]{1,0:T(8,128)(2,1)S(1)}, u32[]{:S(2)}, u32[]{:S(2)}) %collective-permute-start.31) | collective-permute-done | bytes 1048608 | tf_op jit(solution)/shard_map/ppermute | solution.py:21
  155.9 3.3 %collective-permute-done.32.refs_5_ = bf16[1024,512]{1,0:T(8,128)(2,1)S(1)} collective-permute-done((bf16[1024,512]{1,0:T(8,128)(2,1)}, bf16[1024,512]{1,0:T(8,128)(2,1)S(1)}, u32[]{:S(2)}, u32[]{:S(2)}) %collective-permute-start.32) | collective-permute-done | bytes 1048608 | tf_op jit(solution)/shard_map/ppermute | solution.py:21
  159.2 0.9 copy-done.3
  160.6 1.8 fusion.14
  162.4 3.0 %collective-permute-start.35 = (bf16[256,256]{1,0:T(8,128)(2,1)S(1)}, bf16[256,256]{1,0:T(8,128)(2,1)S(1)}, u32[]{:S(2)}, u32[]{:S(2)}) collective-permute-start(bf16[256,256]{1,0:T(8,128)(2,1)S(1)} %get-tuple-element.94), channel_id=1, source_target_pairs={{8,0},{36,4},{16,8},{44,12},{24,16},{52,20},{0,24},{60,28},{40,32}... | collective-permute-start | bytes 393224 | tf_op jit(solution)/shard_map/ppermute | solution.py:36
  165.4 0.9 collective-permute-start.33
  166.3 9.4 %embed_b.1.refs_3_ = bf16[2048,1024]{1,0:T(8,128)(2,1)} custom-call(s32[4]{0:T(128)} %get-tuple-element.50.at, bf16[2048,512]{1,0:T(8,128)(2,1)} %get-tuple-element.66.tgt, bf16[1024,512]{1,0:T(8,128)(2,1)} %get-tuple-element.77.ep, bf16[1024,512]{1,0:T(8,128)(2,1)} %get-tuple-element.73.em, ...), custom_call_target="tpu_custom_call", output_to_operand_aliasing={{}: (12, {})} | custom-call | flops 1000 | bytes 1000 | tf_op jit(solution)/shard_map/embed_b/pallas_call | solution.py:313
  175.8 0.6 copy-done.19
  176.5 0.7 copy-done.21
  177.1 1.1 fusion.7
  178.3 1.3 collective-permute-done.36
  179.7 0.7 maximum_select_fusion
  (98 shorter events, 5.7 us)
Async XLA Ops:
  7.2 132.5 %all-gather.3.cloned.1.call-start = ((), (), s32[]{:S(2)}) async-start(), calls=%async_computation | async-start | bytes 4325376 | tf_op jit(solution)/shard_map/all_gather | solution.py:350
  8.1 1.3 collective-permute-start
  9.5 6.2 %collective-permute-start.3 = (bf16[256,256]{1,0:T(8,128)(2,1)S(1)}, bf16[256,256]{1,0:T(8,128)(2,1)S(1)}, u32[]{:S(2)}, u32[]{:S(2)}) collective-permute-start(bf16[256,256]{1,0:T(8,128)(2,1)S(1)} %maximum_select_fusion.2), channel_id=1, source_target_pairs={{96,0},{28,4},{104,8},{4,12},{112,16},{12,20},{120,24},{20,28},{0,... | collective-permute-start | bytes 393224 | tf_op jit(solution)/shard_map/ppermute | solution.py:36
  11.1 7.1 %collective-permute-start.2 = (bf16[256,256]{1,0:T(8,128)(2,1)S(1)}, bf16[256,256]{1,0:T(8,128)(2,1)S(1)}, u32[]{:S(2)}, u32[]{:S(2)}) collective-permute-start(bf16[256,256]{1,0:T(8,128)(2,1)S(1)} %maximum_select_fusion.2), channel_id=1, source_target_pairs={{64,0},{20,4},{72,8},{28,12},{80,16},{4,20},{88,24},{12,28},{96,32... | collective-permute-start | bytes 393224 | tf_op jit(solution)/shard_map/ppermute | solution.py:36
  13.9 5.0 %collective-permute-start.1 = (bf16[256,256]{1,0:T(8,128)(2,1)S(1)}, bf16[256,256]{1,0:T(8,128)(2,1)S(1)}, u32[]{:S(2)}, u32[]{:S(2)}) collective-permute-start(bf16[256,256]{1,0:T(8,128)(2,1)S(1)} %maximum_select_fusion.2), channel_id=1, source_target_pairs={{32,0},{12,4},{40,8},{20,12},{48,16},{28,20},{56,24},{4,28},{64,32... | collective-permute-start | bytes 393224 | tf_op jit(solution)/shard_map/ppermute | solution.py:36
  18.9 32.1 %copy-start = (bf16[4,256,256]{2,1,0:T(8,128)(2,1)}, bf16[4,256,256]{2,1,0:T(8,128)(2,1)S(1)}, u32[]{:S(2)}) copy-start(bf16[4,256,256]{2,1,0:T(8,128)(2,1)S(1)} %pad_maximum_fusion.refs_0_) | copy-start | bytes 1572868
  18.9 11.3 %collective-permute-start.4 = (bf16[4,256,256]{2,1,0:T(8,128)(2,1)S(1)}, bf16[4,256,256]{2,1,0:T(8,128)(2,1)S(1)}, u32[]{:S(2)}, u32[]{:S(2)}) collective-permute-start(bf16[4,256,256]{2,1,0:T(8,128)(2,1)S(1)} %pad_maximum_fusion.refs_0_), channel_id=1, source_target_pairs={{24,0},{100,4},{0,8},{108,12},{8,16},{116,20},{16,24},{124,28},{56... | collective-permute-start | bytes 1572872 | tf_op jit(solution)/shard_map/ppermute | solution.py:36
  20.9 2.9 %collective-permute-start.5 = (bf16[512,128]{1,0:T(8,128)(2,1)}, bf16[512,128]{1,0:T(8,128)(2,1)S(1)}, u32[]{:S(2)}, u32[]{:S(2)}) collective-permute-start(bf16[512,128]{1,0:T(8,128)(2,1)} %bitcast.55), channel_id=1, source_target_pairs={{0,0},{1,32},{2,64},{3,96},{32,1},{33,33},{34,65},{35,97},{64,2},{... | collective-permute-start | bytes 393224 | tf_op jit(solution)/shard_map/ppermute | solution.py:338
  23.8 7.0 %copy-start.22 = (bf16[512,128]{1,0:T(8,128)(2,1)}, bf16[512,128]{1,0:T(8,128)(2,1)S(1)}, u32[]{:S(2)}) copy-start(bf16[512,128]{1,0:T(8,128)(2,1)S(1)} %collective-permute-done.5.refs_1_) | copy-start | bytes 393220
  30.2 0.8 copy-start.1
  31.0 10.8 %collective-permute-start.7 = (bf16[4,256,256]{2,1,0:T(8,128)(2,1)S(1)}, bf16[4,256,256]{2,1,0:T(8,128)(2,1)S(1)}, u32[]{:S(2)}, u32[]{:S(2)}) collective-permute-start(bf16[4,256,256]{2,1,0:T(8,128)(2,1)S(1)} %pad_maximum_fusion.refs_0_), channel_id=1, source_target_pairs={{16,0},{68,4},{24,8},{76,12},{0,16},{84,20},{8,24},{92,28},{48,32}... | collective-permute-start | bytes 1572872 | tf_op jit(solution)/shard_map/ppermute | solution.py:36
  32.9 14.3 %collective-permute-start.6 = (bf16[4,256,256]{2,1,0:T(8,128)(2,1)S(1)}, bf16[4,256,256]{2,1,0:T(8,128)(2,1)S(1)}, u32[]{:S(2)}, u32[]{:S(2)}) collective-permute-start(bf16[4,256,256]{2,1,0:T(8,128)(2,1)S(1)} %pad_maximum_fusion.refs_0_), channel_id=1, source_target_pairs={{8,0},{36,4},{16,8},{44,12},{24,16},{52,20},{0,24},{60,28},{40,32}... | collective-permute-start | bytes 1572872 | tf_op jit(solution)/shard_map/ppermute | solution.py:36
  33.7 14.8 %collective-permute-start.8 = (bf16[4,256,256]{2,1,0:T(8,128)(2,1)S(1)}, bf16[4,256,256]{2,1,0:T(8,128)(2,1)S(1)}, u32[]{:S(2)}, u32[]{:S(2)}) collective-permute-start(bf16[4,256,256]{2,1,0:T(8,128)(2,1)S(1)} %pad_maximum_fusion.refs_0_), channel_id=1, source_target_pairs={{0,4},{4,0},{1,5},{5,1},{2,6},{6,2},{3,7},{7,3},{8,12},{12,8},{9,1... | collective-permute-start | bytes 1572872 | tf_op jit(solution)/shard_map/ppermute | solution.py:25
  41.8 9.2 %copy-start.8 = (bf16[4,256,256]{2,1,0:T(8,128)(2,1)}, bf16[4,256,256]{2,1,0:T(8,128)(2,1)S(1)}, u32[]{:S(2)}) copy-start(bf16[4,256,256]{2,1,0:T(8,128)(2,1)S(1)} %collective-permute-done.7.refs_2_) | copy-start | bytes 1572868
  41.8 6.7 %collective-permute-start.10 = (bf16[4,256,256]{2,1,0:T(8,128)(2,1)S(1)}, bf16[4,256,256]{2,1,0:T(8,128)(2,1)S(1)}, u32[]{:S(2)}, u32[]{:S(2)}) collective-permute-start(bf16[4,256,256]{2,1,0:T(8,128)(2,1)S(1)} %collective-permute-done.7.refs_2_), channel_id=1, source_target_pairs={{0,4},{4,0},{1,5},{5,1},{2,6},{6,2},{3,7},{7,3},{8,12},{12,8},{9,1... | collective-permute-start | bytes 1572872 | tf_op jit(solution)/shard_map/ppermute | solution.py:25
  47.3 3.8 %copy-start.9 = (bf16[4,256,256]{2,1,0:T(8,128)(2,1)}, bf16[4,256,256]{2,1,0:T(8,128)(2,1)S(1)}, u32[]{:S(2)}) copy-start(bf16[4,256,256]{2,1,0:T(8,128)(2,1)S(1)} %collective-permute-done.6.refs_1_) | copy-start | bytes 1572868
  47.3 3.5 %collective-permute-start.9 = (bf16[4,256,256]{2,1,0:T(8,128)(2,1)S(1)}, bf16[4,256,256]{2,1,0:T(8,128)(2,1)S(1)}, u32[]{:S(2)}, u32[]{:S(2)}) collective-permute-start(bf16[4,256,256]{2,1,0:T(8,128)(2,1)S(1)} %collective-permute-done.6.refs_1_), channel_id=1, source_target_pairs={{0,4},{4,0},{1,5},{5,1},{2,6},{6,2},{3,7},{7,3},{8,12},{12,8},{9,1... | collective-permute-start | bytes 1572872 | tf_op jit(solution)/shard_map/ppermute | solution.py:25
  48.5 2.5 %collective-permute-start.11 = (bf16[4,256,256]{2,1,0:T(8,128)(2,1)}, bf16[4,256,256]{2,1,0:T(8,128)(2,1)S(1)}, u32[]{:S(2)}, u32[]{:S(2)}) collective-permute-start(bf16[4,256,256]{2,1,0:T(8,128)(2,1)} %get-tuple-element.51.refs_3_), channel_id=1, source_target_pairs={{0,4},{4,0},{1,5},{5,1},{2,6},{6,2},{3,7},{7,3},{8,12},{12,8},{9,1... | collective-permute-start | bytes 1572872 | tf_op jit(solution)/shard_map/ppermute | solution.py:25
  48.5 2.5 %copy-start.10 = (bf16[4,256,256]{2,1,0:T(8,128)(2,1)}, bf16[4,256,256]{2,1,0:T(8,128)(2,1)S(1)}, u32[]{:S(2)}) copy-start(bf16[4,256,256]{2,1,0:T(8,128)(2,1)S(1)} %collective-permute-done.8.refs_4_) | copy-start | bytes 1572868
  48.5 2.5 %copy-start.11 = (bf16[4,256,256]{2,1,0:T(8,128)(2,1)}, bf16[4,256,256]{2,1,0:T(8,128)(2,1)S(1)}, u32[]{:S(2)}) copy-start(bf16[4,256,256]{2,1,0:T(8,128)(2,1)S(1)} %collective-permute-done.10.refs_6_) | copy-start | bytes 1572868
  50.8 0.8 copy-start.12
  51.0 0.8 copy-start.13
  62.7 35.4 %collective-permute-start.20 = (bf16[1024,512]{1,0:T(8,128)(2,1)}, bf16[1024,512]{1,0:T(8,128)(2,1)S(1)}, u32[]{:S(2)}, u32[]{:S(2)}) collective-permute-start(bf16[1024,512]{1,0:T(8,128)(2,1)} %get-tuple-element.53.e0), channel_id=1, source_target_pairs={{3,0},{0,1},{1,2},{2,3},{7,4},{4,5},{5,6},{6,7},{11,8},{8,9},{9,10... | collective-permute-start | bytes 3145736 | tf_op jit(solution)/shard_map/ppermute | solution.py:21
  63.6 34.5 %collective-permute-start.19 = (bf16[1024,512]{1,0:T(8,128)(2,1)}, bf16[1024,512]{1,0:T(8,128)(2,1)S(1)}, u32[]{:S(2)}, u32[]{:S(2)}) collective-permute-start(bf16[1024,512]{1,0:T(8,128)(2,1)} %get-tuple-element.53.e0), channel_id=1, source_target_pairs={{1,0},{2,1},{3,2},{0,3},{5,4},{6,5},{7,6},{4,7},{9,8},{10,9},{11,1... | collective-permute-start | bytes 3145736 | tf_op jit(solution)/shard_map/ppermute | solution.py:21
  80.6 5.7 %collective-permute-start.14 = (f32[8,512]{1,0:T(8,128)}, f32[8,512]{1,0:T(8,128)S(1)}, u32[]{:S(2)}, u32[]{:S(2)}) collective-permute-start(f32[8,512]{1,0:T(8,128)} %get-tuple-element.55), channel_id=1, source_target_pairs={{96,0},{0,32},{32,64},{64,96},{97,1},{1,33},{33,65},{65,97},{98,2}... | collective-permute-start | bytes 49160 | tf_op jit(solution)/shard_map/ppermute | solution.py:21
  82.0 5.5 %collective-permute-start.13 = (f32[8,512]{1,0:T(8,128)}, f32[8,512]{1,0:T(8,128)S(1)}, u32[]{:S(2)}, u32[]{:S(2)}) collective-permute-start(f32[8,512]{1,0:T(8,128)} %get-tuple-element.55), channel_id=1, source_target_pairs={{64,0},{96,32},{0,64},{32,96},{65,1},{97,33},{1,65},{33,97},{66,2}... | collective-permute-start | bytes 49160 | tf_op jit(solution)/shard_map/ppermute | solution.py:21
  84.2 3.9 %collective-permute-start.12 = (f32[8,512]{1,0:T(8,128)}, f32[8,512]{1,0:T(8,128)S(1)}, u32[]{:S(2)}, u32[]{:S(2)}) collective-permute-start(f32[8,512]{1,0:T(8,128)} %get-tuple-element.55), channel_id=1, source_target_pairs={{32,0},{64,32},{96,64},{0,96},{33,1},{65,33},{97,65},{1,97},{34,2}... | collective-permute-start | bytes 49160 | tf_op jit(solution)/shard_map/ppermute | solution.py:21
  89.1 5.4 %collective-permute-start.17 = (f32[8,512]{1,0:T(8,128)S(1)}, f32[8,512]{1,0:T(8,128)S(1)}, u32[]{:S(2)}, u32[]{:S(2)}) collective-permute-start(f32[8,512]{1,0:T(8,128)S(1)} %maximum_maximum_fusion), channel_id=1, source_target_pairs={{24,0},{0,8},{8,16},{16,24},{25,1},{1,9},{9,17},{17,25},{26,2},{2,... | collective-permute-start | bytes 49160 | tf_op jit(solution)/shard_map/ppermute | solution.py:21
  90.9 5.2 %collective-permute-start.16 = (f32[8,512]{1,0:T(8,128)S(1)}, f32[8,512]{1,0:T(8,128)S(1)}, u32[]{:S(2)}, u32[]{:S(2)}) collective-permute-start(f32[8,512]{1,0:T(8,128)S(1)} %maximum_maximum_fusion), channel_id=1, source_target_pairs={{16,0},{24,8},{0,16},{8,24},{17,1},{25,9},{1,17},{9,25},{18,2},{26... | collective-permute-start | bytes 49160 | tf_op jit(solution)/shard_map/ppermute | solution.py:21
  92.8 3.7 %collective-permute-start.15 = (f32[8,512]{1,0:T(8,128)S(1)}, f32[8,512]{1,0:T(8,128)S(1)}, u32[]{:S(2)}, u32[]{:S(2)}) collective-permute-start(f32[8,512]{1,0:T(8,128)S(1)} %maximum_maximum_fusion), channel_id=1, source_target_pairs={{8,0},{16,8},{24,16},{0,24},{9,1},{17,9},{25,17},{1,25},{10,2},{18... | collective-permute-start | bytes 49160 | tf_op jit(solution)/shard_map/ppermute | solution.py:21
  96.7 1.4 copy-start.26
  96.7 1.4 collective-permute-start.18
  98.1 1.0 copy-start.6
  98.1 1.3 copy-start.7
  100.8 27.4 %collective-permute-start.21 = (bf16[1024,512]{1,0:T(8,128)(2,1)}, bf16[1024,512]{1,0:T(8,128)(2,1)S(1)}, u32[]{:S(2)}, u32[]{:S(2)}) collective-permute-start(bf16[1024,512]{1,0:T(8,128)(2,1)} %get-tuple-element.59.e1.refs_2_), channel_id=1, source_target_pairs={{3,0},{0,1},{1,2},{2,3},{7,4},{4,5},{5,6},{6,7},{11,8},{8,9},{9,10... | collective-permute-start | bytes 3145736 | tf_op jit(solution)/shard_map/ppermute | solution.py:21
  101.6 26.7 %collective-permute-start.22 = (bf16[1024,512]{1,0:T(8,128)(2,1)}, bf16[1024,512]{1,0:T(8,128)(2,1)S(1)}, u32[]{:S(2)}, u32[]{:S(2)}) collective-permute-start(bf16[1024,512]{1,0:T(8,128)(2,1)} %copy-done.7), channel_id=1, source_target_pairs={{1,0},{2,1},{3,2},{0,3},{5,4},{6,5},{7,6},{4,7},{9,8},{10,9},{11,1... | collective-permute-start | bytes 3145736 | tf_op jit(solution)/shard_map/ppermute | solution.py:21
  104.1 23.7 %collective-permute-start.25 = (f32[8,512]{1,0:T(8,128)}, f32[8,512]{1,0:T(8,128)S(1)}, u32[]{:S(2)}, u32[]{:S(2)}) collective-permute-start(f32[8,512]{1,0:T(8,128)} %get-tuple-element.60.pack), channel_id=1, source_target_pairs={{2,0},{3,1},{0,2},{1,3},{6,4},{7,5},{4,6},{5,7},{10,8},{11,9},{8,1... | collective-permute-start | bytes 49160 | tf_op jit(solution)/shard_map/ppermute | solution.py:21
  104.3 23.9 %collective-permute-start.24 = (f32[8,512]{1,0:T(8,128)}, f32[8,512]{1,0:T(8,128)S(1)}, u32[]{:S(2)}, u32[]{:S(2)}) collective-permute-start(f32[8,512]{1,0:T(8,128)} %get-tuple-element.60.pack), channel_id=1, source_target_pairs={{3,0},{0,1},{1,2},{2,3},{7,4},{4,5},{5,6},{6,7},{11,8},{8,9},{9,10... | collective-permute-start | bytes 49160 | tf_op jit(solution)/shard_map/ppermute | solution.py:21
  105.1 23.1 %collective-permute-start.23 = (f32[8,512]{1,0:T(8,128)}, f32[8,512]{1,0:T(8,128)S(1)}, u32[]{:S(2)}, u32[]{:S(2)}) collective-permute-start(f32[8,512]{1,0:T(8,128)} %get-tuple-element.60.pack), channel_id=1, source_target_pairs={{1,0},{2,1},{3,2},{0,3},{5,4},{6,5},{7,6},{4,7},{9,8},{10,9},{11,1... | collective-permute-start | bytes 49160 | tf_op jit(solution)/shard_map/ppermute | solution.py:21
  123.9 10.0 %copy-start.14 = (bf16[4,4,256,256]{3,2,1,0:T(8,128)(2,1)S(1)}, bf16[4,4,256,256]{3,2,1,0:T(8,128)(2,1)}, u32[]{:S(2)}) copy-start(bf16[4,4,256,256]{3,2,1,0:T(8,128)(2,1)} %get-tuple-element.61) | copy-start | bytes 6291460
  128.2 0.6 copy-start.24
  128.2 0.6 copy-start.25
  128.2 1.0 copy-start.4
  128.2 1.3 copy-start.5
  129.5 3.5 %collective-permute-start.26 = (bf16[2,4,256,256]{3,2,1,0:T(8,128)(2,1)}, bf16[2,4,256,256]{3,2,1,0:T(8,128)(2,1)S(1)}, u32[]{:S(2)}, u32[]{:S(2)}) collective-permute-start(bf16[2,4,256,256]{3,2,1,0:T(8,128)(2,1)} %get-tuple-element.64), channel_id=1, source_target_pairs={{0,4},{4,0},{1,5},{5,1},{2,6},{6,2},{3,7},{7,3},{8,12},{12,8},{9,1... | collective-permute-start | bytes 3145736 | tf_op jit(solution)/shard_map/ppermute | solution.py:25
  129.5 4.4 %collective-permute-start.28 = (bf16[2,4,256,256]{3,2,1,0:T(8,128)(2,1)}, bf16[2,4,256,256]{3,2,1,0:T(8,128)(2,1)S(1)}, u32[]{:S(2)}, u32[]{:S(2)}) collective-permute-start(bf16[2,4,256,256]{3,2,1,0:T(8,128)(2,1)} %get-tuple-element.65), channel_id=1, source_target_pairs={{0,4},{4,0},{1,5},{5,1},{2,6},{6,2},{3,7},{7,3},{8,12},{12,8},{9,1... | collective-permute-start | bytes 3145736 | tf_op jit(solution)/shard_map/ppermute | solution.py:25
  130.0 25.9 %collective-permute-start.31 = (bf16[1024,512]{1,0:T(8,128)(2,1)}, bf16[1024,512]{1,0:T(8,128)(2,1)S(1)}, u32[]{:S(2)}, u32[]{:S(2)}) collective-permute-start(bf16[1024,512]{1,0:T(8,128)(2,1)} %get-tuple-element.72), channel_id=1, source_target_pairs={{1,0},{2,1},{3,2},{0,3},{5,4},{6,5},{7,6},{4,7},{9,8},{10,9},{11,1... | collective-permute-start | bytes 3145736 | tf_op jit(solution)/shard_map/ppermute | solution.py:21
  133.0 26.2 %collective-permute-start.32 = (bf16[1024,512]{1,0:T(8,128)(2,1)}, bf16[1024,512]{1,0:T(8,128)(2,1)S(1)}, u32[]{:S(2)}, u32[]{:S(2)}) collective-permute-start(bf16[1024,512]{1,0:T(8,128)(2,1)} %get-tuple-element.73.em), channel_id=1, source_target_pairs={{3,0},{0,1},{1,2},{2,3},{7,4},{4,5},{5,6},{6,7},{11,8},{8,9},{9,10... | collective-permute-start | bytes 3145736 | tf_op jit(solution)/shard_map/ppermute | solution.py:21
  133.0 5.8 %copy-start.17 = (bf16[2,4,256,256]{3,2,1,0:T(8,128)(2,1)}, bf16[2,4,256,256]{3,2,1,0:T(8,128)(2,1)S(1)}, u32[]{:S(2)}) copy-start(bf16[2,4,256,256]{3,2,1,0:T(8,128)(2,1)S(1)} %collective-permute-done.26) | copy-start | bytes 3145732
  135.3 23.9 %collective-permute-start.30 = (bf16[4,256,256]{2,1,0:T(8,128)(2,1)}, bf16[4,256,256]{2,1,0:T(8,128)(2,1)S(1)}, u32[]{:S(2)}, u32[]{:S(2)}) collective-permute-start(bf16[4,256,256]{2,1,0:T(8,128)(2,1)} %get-tuple-element.91), channel_id=1, source_target_pairs={{32,0},{12,4},{40,8},{20,12},{48,16},{28,20},{56,24},{4,28},{64,32... | collective-permute-start | bytes 1572872 | tf_op jit(solution)/shard_map/ppermute | solution.py:36
  138.8 20.4 %collective-permute-start.29 = (bf16[4,256,256]{2,1,0:T(8,128)(2,1)}, bf16[4,256,256]{2,1,0:T(8,128)(2,1)S(1)}, u32[]{:S(2)}, u32[]{:S(2)}) collective-permute-start(bf16[4,256,256]{2,1,0:T(8,128)(2,1)} %get-tuple-element.92), channel_id=1, source_target_pairs={{64,0},{20,4},{72,8},{28,12},{80,16},{4,20},{88,24},{12,28},{96,32... | collective-permute-start | bytes 1572872 | tf_op jit(solution)/shard_map/ppermute | solution.py:36
  138.8 20.4 %collective-permute-start.27 = (bf16[4,256,256]{2,1,0:T(8,128)(2,1)}, bf16[4,256,256]{2,1,0:T(8,128)(2,1)}, u32[]{:S(2)}, u32[]{:S(2)}) collective-permute-start(bf16[4,256,256]{2,1,0:T(8,128)(2,1)} %get-tuple-element.93), channel_id=1, source_target_pairs={{96,0},{28,4},{104,8},{4,12},{112,16},{12,20},{120,24},{20,28},{0,... | collective-permute-start | bytes 1572872 | tf_op jit(solution)/shard_map/ppermute | solution.py:36
  149.0 11.5 %copy-start.18 = (bf16[2,4,256,256]{3,2,1,0:T(8,128)(2,1)S(1)}, bf16[2,4,256,256]{3,2,1,0:T(8,128)(2,1)}, u32[]{:S(2)}) copy-start(bf16[2,4,256,256]{3,2,1,0:T(8,128)(2,1)} %copy-done.17) | copy-start | bytes 3145732
  155.9 3.3 %copy-start.2 = (bf16[1024,512]{1,0:T(8,128)(2,1)}, bf16[1024,512]{1,0:T(8,128)(2,1)S(1)}, u32[]{:S(2)}) copy-start(bf16[1024,512]{1,0:T(8,128)(2,1)S(1)} %collective-permute-done.31.refs_4_) | copy-start | bytes 3145732
  159.2 1.0 copy-start.3
  159.2 1.2 copy-start.15
  159.2 1.3 copy-start.16
  162.4 13.3 %collective-permute-start.35 = (bf16[256,256]{1,0:T(8,128)(2,1)S(1)}, bf16[256,256]{1,0:T(8,128)(2,1)S(1)}, u32[]{:S(2)}, u32[]{:S(2)}) collective-permute-start(bf16[256,256]{1,0:T(8,128)(2,1)S(1)} %get-tuple-element.94), channel_id=1, source_target_pairs={{8,0},{36,4},{16,8},{44,12},{24,16},{52,20},{0,24},{60,28},{40,32}... | collective-permute-start | bytes 393224 | tf_op jit(solution)/shard_map/ppermute | solution.py:36
  165.4 10.4 %collective-permute-start.34 = (bf16[256,256]{1,0:T(8,128)(2,1)S(1)}, bf16[256,256]{1,0:T(8,128)(2,1)S(1)}, u32[]{:S(2)}, u32[]{:S(2)}) collective-permute-start(bf16[256,256]{1,0:T(8,128)(2,1)S(1)} %get-tuple-element.95), channel_id=1, source_target_pairs={{16,0},{68,4},{24,8},{76,12},{0,16},{84,20},{8,24},{92,28},{48,32}... | collective-permute-start | bytes 393224 | tf_op jit(solution)/shard_map/ppermute | solution.py:36
  165.4 10.4 %collective-permute-start.33 = (bf16[256,256]{1,0:T(8,128)(2,1)S(1)}, bf16[256,256]{1,0:T(8,128)(2,1)S(1)}, u32[]{:S(2)}, u32[]{:S(2)}) collective-permute-start(bf16[256,256]{1,0:T(8,128)(2,1)S(1)} %get-tuple-element.96), channel_id=1, source_target_pairs={{24,0},{100,4},{0,8},{108,12},{8,16},{116,20},{16,24},{124,28},{56... | collective-permute-start | bytes 393224 | tf_op jit(solution)/shard_map/ppermute | solution.py:36
  175.7 0.6 copy-start.19
  175.8 0.7 copy-start.20
  176.5 0.7 copy-start.21
  178.2 1.4 collective-permute-start.36
  (2 other events, 1.2 us)
Sparse Core Ops, SparseCore 0:
  31.1 48.9 all-gather.2

commit v8 on v6

--- a/solution.py
+++ b/solution.py
@@ -74,9 +74,12 @@
 SUB = 256
 
 
-def gather_pieces(block):
-    s = jnp.stack([block] + [cross(block, 0, d) for d in (1, 2, 3)])
-    return [s] + [cross(s, 1, d) for d in (1, 2, 3)]
+def gather_pieces(block, *early):
+    near = [cross(block, 0, d) for d in (1, 2, 3)]
+    near[2], *early = gate(near[2], *early)
+    s = jnp.stack([block, *near])
+    far = [cross(s, 1, d) for d in (1, 2, 3)]
+    return [s] + far, *early
 
 
 def logits_body(at, *refs):
@@ -171,7 +174,7 @@
     return jnp.concatenate([*merge(parts), jnp.zeros((5, ROWS), F32)])
 
 
-def finish_body(a, b, st, tid, mix, weight, ep0, em0, e1, pack, grad_mix, e1_out):
+def finish_body(a, b, st, tid, mix, weight, pack, grad_mix):
     top, total, hit = merge([a[...], b[...]])
     lse = top + jnp.log(total)
     gap = hit - lse
@@ -197,26 +200,23 @@
     pack[pl.ds(6, 1), :] = tid[...].astype(F32)
 
 
-def finish_call(a, b, st, tid, mix, weight, *awaited):
+def finish_call(a, b, st, tid, mix, weight):
     stat = pl.BlockSpec((8, ROWS), lambda i: (0, 0))
     part = pl.BlockSpec((4, 128), lambda i: (0, 0))
     return pl.pallas_call(
         finish_body,
         grid=(1,),
         in_specs=[stat] * 3
-        + [pl.BlockSpec((1, ROWS), lambda i: (0, 0)), part, pl.BlockSpec((1, 128), lambda i: (0, 0))]
-        + [HBM] * 3,
-        out_specs=[stat, part, HBM],
+        + [pl.BlockSpec((1, ROWS), lambda i: (0, 0)), part, pl.BlockSpec((1, 128), lambda i: (0, 0))],
+        out_specs=[stat, part],
         out_shape=[
             jax.ShapeDtypeStruct((8, ROWS), F32),
             jax.ShapeDtypeStruct((4, 128), F32),
-            jax.ShapeDtypeStruct((VOC - CUT, ROWS), BF),
         ],
-        input_output_aliases={8: 2},
         compiler_params=params(),
         cost_estimate=SMALL,
         name="finish",
-    )(a, b, st, tid, mix, weight, *awaited)
+    )(a, b, st, tid, mix, weight)
 
 
 def token_grad(e, pack, scale, base):
@@ -242,7 +242,7 @@
     for k in range(4):
         cols = slice(k * 256, (k + 1) * 256)
         a, b = r[:HALF, cols], r[HALF:, cols]
-        keep[0, k] = jnp.where(first, a, b)
+        keep[0, k] = jnp.where(first, a, b).astype(BF)
         (send0, send1)[k // 2][k % 2, 0] = jnp.where(first, b, a).astype(BF)
 
 
@@ -273,7 +273,7 @@
             scratch_shapes=[pltpu.VMEM((ROWS, VOC), BF)],
         ),
         out_shape=[
-            jax.ShapeDtypeStruct((4, 4, HALF, 256), F32),
+            jax.ShapeDtypeStruct((4, 4, HALF, 256), BF),
         ]
         + [jax.ShapeDtypeStruct((2, 4, HALF, 256), BF)] * 2
         + [jax.ShapeDtypeStruct((VOC, ROWS), BF)],
@@ -291,8 +291,7 @@
     b = [add(keep[d], recv[d // 2][d % 2]) for d in range(4)]
     u = [cross(b[d].astype(BF), 0, 4 - d) for d in (1, 2, 3)]
     u1, u2, u3, work, *others = gate(*u, first(), *others)
-    u = [u1, u2, u3]
-    t = add(b[0], *u)
+    t = add(b[0], u1, u2, u3)
     u = [cross(t[d].astype(BF), 1, 4 - d) for d in (1, 2, 3)]
     *u, work = gate(*u, second(work, *others))
     f = add(t[0], *u)
@@ -351,7 +350,7 @@
     mine, other = jnp.where(c == 0, low, high), jnp.where(c == 0, high, low)
     got = sibling(other)
     block = jnp.where(c == 0, jnp.concatenate([mine, got], axis=1), jnp.concatenate([got, mine], axis=1))
-    pieces = gather_pieces(block)
+    pieces, at, tid = gather_pieces(block, at, tid)
     pieces = pieces + [sibling(p) for p in pieces]
 
     e0, e1, st, loc = logits_call(at, pieces, tid, embed)
@@ -361,11 +360,12 @@
 
     s = merge_call(loc, *(shift(loc, "x", d) for d in (1, 2, 3)))
     s = merge_call(s, *(shift(s, "z", d) for d in (1, 2, 3)))
-    pack, grad_mix, e1 = finish_call(s, sibling(s), st, tid, mix, weight.reshape(1, 128), ep0, em0, e1)
+    pack, grad_mix = finish_call(s, sibling(s), st, tid, mix, weight.reshape(1, 128))
     packs = [shift(pack, "y", d) for d in (1, 3, 2)]
+    pack, e1, ep0, em0, *packs = gate(pack, e1, ep0, em0, *packs)
     em1, ed0 = shift(e1, "y", 3), shift(ep0, "y", 1)
     keep, send0, send1, tgt = hidden_call(at, e0, e1, pack, embed)
-    send0, send1, e1, em1, ed0, *packs = gate(send0, send1, e1, em1, ed0, *packs)
+    send0, send1, e1, em1, ed0 = gate(send0, send1, e1, em1, ed0)
     ep1, ed1 = shift(e1, "y", 1), shift(em1, "y", 3)
     recv = sibling(send0), sibling(send1)
 

time: 179 us -> 179 us (level)
  waiting for transfers between devices: 39.7 us -> 45.2 us
  starting transfers between devices: 51.6 us -> 47.3 us
    ppermute x15, waiting for transfers between devices: 19.5 us -> 23.3 us  [shift(): return lax.ppermute(a, axis, [((i + d) % 4, i) for i in range(4)])]
    ppermute x12, starting transfers between devices: 21.6 us -> 19.2 us  [cross(): return lax.ppermute(a, ('x', 'z', 'c'), pairs)]
    ppermute x15, starting transfers between devices: 27.3 us -> 25.3 us  [shift(): return lax.ppermute(a, axis, [((i + d) % 4, i) for i in range(4)])]
    convert_element_type x1, other arithmetic: 3.29 us -> 1.39 us  [scatter(): u = [cross(b[d].astype(BF), 0, 4 - d) for d in (1, 2, 3)]]
    unnamed x50 -> x58, local copies, waits for them, and re-layouts: 6.35 us -> 7.28 us
  transfers between devices with their start and end apart: 38 -> 38, of which waited for: 18 -> 19; matrix products, arithmetic and copies ran while one was open for 4% -> 3% of each run, Pallas kernels for 30% -> 30%
where the time goes in v8:
time: 179 us; the launch traced here: 178 us
  Pallas kernels  53.9 us (30%)
  starting transfers between devices  47.3 us (26%)
  waiting for transfers between devices  45.2 us (25%)
  between operations  14.4 us (8%)
  other arithmetic  9.34 us (5%)
  local copies, waits for them, and re-layouts  7.99 us (4%)
    ppermute x15, starting transfers between devices, shift(): return lax.ppermute(a, axis, [((i + d) % 4, i) for i in range(4)])  25.3 us
    ppermute x15, waiting for transfers between devices, shift(): return lax.ppermute(a, axis, [((i + d) % 4, i) for i in range(4)])  23.3 us
    ppermute x12, starting transfers between devices, cross(): return lax.ppermute(a, ('x', 'z', 'c'), pairs)  19.2 us
    pallas_call x2, Pallas kernels, embed_call(): pl.pallas_call(functools.partial(embed_body, base), grid_spec=pltpu.Prefe...  18.8 us
    pallas_call x1, Pallas kernels, logits_call(): pl.pallas_call(logits_body, grid_spec=pltpu.PrefetchScalarGridSpec(num_sc...  16.9 us
    pallas_call x1, Pallas kernels, hidden_call(): pl.pallas_call(hidden_body, grid_spec=pltpu.PrefetchScalarGridSpec(num_sc...  16.8 us
    ppermute x12, waiting for transfers between devices, cross(): return lax.ppermute(a, ('x', 'z', 'c'), pairs)  16.4 us
    unnamed x58, local copies, waits for them, and re-layouts  7.28 us
  transfers between devices with their start and end apart: 38, of which 19 were waited for; matrix products, arithmetic and copies ran while one was open for 3% of the time, Pallas kernels for 30%

profile of v8, /device:TPU:0, one launch (start us, length us, event | category | flops | bytes accessed | tf_op | source)
XLA Modules:
  0.0 178.0 jit_solution(1765084474718599338)
XLA Ops:
  7.2 0.9 broadcast_select_fusion.1
  8.2 0.7 broadcast_subtract_fusion
  8.9 0.6 collective-permute-done
  9.5 3.2 %collective-permute-start.3 = (bf16[256,256]{1,0:T(8,128)(2,1)S(1)}, bf16[256,256]{1,0:T(8,128)(2,1)S(1)}, u32[]{:S(2)}, u32[]{:S(2)}) collective-permute-start(bf16[256,256]{1,0:T(8,128)(2,1)S(1)} %maximum_select_fusion.1), channel_id=1, source_target_pairs={{64,0},{20,4},{72,8},{28,12},{80,16},{4,20},{88,24},{12,28},{96,32... | collective-permute-start | bytes 393224 | tf_op jit(solution)/shard_map/ppermute | solution.py:36
  12.7 1.1 collective-permute-start.2
  13.8 0.9 collective-permute-start.1
  14.7 0.7 pad_add_fusion.refs_1_
  15.4 4.6 %collective-permute-done.1.refs_0_ = bf16[256,256]{1,0:T(8,128)(2,1)S(1)} collective-permute-done((bf16[256,256]{1,0:T(8,128)(2,1)S(1)}, bf16[256,256]{1,0:T(8,128)(2,1)S(1)}, u32[]{:S(2)}, u32[]{:S(2)}) %collective-permute-start.1) | collective-permute-done | bytes 131104 | tf_op jit(solution)/shard_map/ppermute | solution.py:36
  20.0 0.6 tile.2
  20.7 1.0 pad_maximum_fusion.refs_0_
  21.6 2.0 %collective-permute-start.6 = (bf16[4,256,256]{2,1,0:T(8,128)(2,1)S(1)}, bf16[4,256,256]{2,1,0:T(8,128)(2,1)S(1)}, u32[]{:S(2)}, u32[]{:S(2)}) collective-permute-start(bf16[4,256,256]{2,1,0:T(8,128)(2,1)S(1)} %pad_maximum_fusion.refs_0_), channel_id=1, source_target_pairs={{24,0},{100,4},{0,8},{108,12},{8,16},{116,20},{16,24},{124,28},{56... | collective-permute-start | bytes 1572872 | tf_op jit(solution)/shard_map/ppermute | solution.py:36
  23.6 3.6 %collective-permute-start.5 = (bf16[4,256,256]{2,1,0:T(8,128)(2,1)S(1)}, bf16[4,256,256]{2,1,0:T(8,128)(2,1)S(1)}, u32[]{:S(2)}, u32[]{:S(2)}) collective-permute-start(bf16[4,256,256]{2,1,0:T(8,128)(2,1)S(1)} %pad_maximum_fusion.refs_0_), channel_id=1, source_target_pairs={{16,0},{68,4},{24,8},{76,12},{0,16},{84,20},{8,24},{92,28},{48,32}... | collective-permute-start | bytes 1572872 | tf_op jit(solution)/shard_map/ppermute | solution.py:36
  27.2 1.0 collective-permute-start.4
  28.2 4.7 %collective-permute-done.6.refs_3_ = bf16[4,256,256]{2,1,0:T(8,128)(2,1)S(1)} collective-permute-done((bf16[4,256,256]{2,1,0:T(8,128)(2,1)S(1)}, bf16[4,256,256]{2,1,0:T(8,128)(2,1)S(1)}, u32[]{:S(2)}, u32[]{:S(2)}) %collective-permute-start.6) | collective-permute-done | bytes 524320 | tf_op jit(solution)/shard_map/ppermute | solution.py:36
  32.9 7.1 %collective-permute-done.5.refs_2_ = bf16[4,256,256]{2,1,0:T(8,128)(2,1)S(1)} collective-permute-done((bf16[4,256,256]{2,1,0:T(8,128)(2,1)S(1)}, bf16[4,256,256]{2,1,0:T(8,128)(2,1)S(1)}, u32[]{:S(2)}, u32[]{:S(2)}) %collective-permute-start.5) | collective-permute-done | bytes 524320 | tf_op jit(solution)/shard_map/ppermute | solution.py:36
  40.0 0.5 collective-permute-start.8
  40.5 1.6 collective-permute-start.11
  42.1 0.5 collective-permute-done.8.refs_5_
  43.4 16.9 %logits.1 = (bf16[1024,512]{1,0:T(8,128)(2,1)}, bf16[1024,512]{1,0:T(8,128)(2,1)}, f32[8,512]{1,0:T(8,128)}, f32[8,512]{1,0:T(8,128)}) custom-call(s32[4]{0:T(128)} %get-tuple-element.40.at, bf16[4,256,256]{2,1,0:T(8,128)(2,1)} %copy-done.6, bf16[4,256,256]{2,1,0:T(8,128)(2,1)} %copy-done.14, bf16[4,256,256]{2,1,0:T(8,128)(2,1)} %copy-done.13, ...), custom_call_target="tpu_custom_call" | custom-call | flops 1000 | bytes 1000 | tf_op jit(solution)/shard_map/logits/pallas_call | solution.py:139
  60.3 0.6 copy-done.22
  61.0 2.0 %collective-permute-start.20 = (bf16[1024,512]{1,0:T(8,128)(2,1)}, bf16[1024,512]{1,0:T(8,128)(2,1)S(1)}, u32[]{:S(2)}, u32[]{:S(2)}) collective-permute-start(bf16[1024,512]{1,0:T(8,128)(2,1)} %get-tuple-element.43.e0), channel_id=1, source_target_pairs={{3,0},{0,1},{1,2},{2,3},{7,4},{4,5},{5,6},{6,7},{11,8},{8,9},{9,10... | collective-permute-start | bytes 3145736 | tf_op jit(solution)/shard_map/ppermute | solution.py:21
  63.0 1.5 collective-permute-start.19
  64.5 3.2 %collective-permute-start.14 = (f32[8,512]{1,0:T(8,128)}, f32[8,512]{1,0:T(8,128)S(1)}, u32[]{:S(2)}, u32[]{:S(2)}) collective-permute-start(f32[8,512]{1,0:T(8,128)} %get-tuple-element.45), channel_id=1, source_target_pairs={{96,0},{0,32},{32,64},{64,96},{97,1},{1,33},{33,65},{65,97},{98,2}... | collective-permute-start | bytes 49160 | tf_op jit(solution)/shard_map/ppermute | solution.py:21
  67.7 4.1 %collective-permute-start.13 = (f32[8,512]{1,0:T(8,128)}, f32[8,512]{1,0:T(8,128)S(1)}, u32[]{:S(2)}, u32[]{:S(2)}) collective-permute-start(f32[8,512]{1,0:T(8,128)} %get-tuple-element.45), channel_id=1, source_target_pairs={{64,0},{96,32},{0,64},{32,96},{65,1},{97,33},{1,65},{33,97},{66,2}... | collective-permute-start | bytes 49160 | tf_op jit(solution)/shard_map/ppermute | solution.py:21
  71.8 1.6 collective-permute-start.12
  73.9 1.9 %collective-permute-done.12 = f32[8,512]{1,0:T(8,128)S(1)} collective-permute-done((f32[8,512]{1,0:T(8,128)}, f32[8,512]{1,0:T(8,128)S(1)}, u32[]{:S(2)}, u32[]{:S(2)}) %collective-permute-start.12) | collective-permute-done | bytes 16416 | tf_op jit(solution)/shard_map/ppermute | solution.py:21
  75.8 0.9 fusion.11
  76.7 1.4 collective-permute-start.17
  78.1 1.7 collective-permute-start.16
  79.8 1.5 collective-permute-start.15
  81.3 0.5 collective-permute-done.17
  81.8 1.6 collective-permute-done.16
  83.8 1.2 collective-permute-done.18.b
  85.0 0.6 copy-done.28
  85.6 1.4 finish.1
  87.0 0.8 collective-permute-start.22
  87.8 2.5 %collective-permute-start.21 = (f32[8,512]{1,0:T(8,128)}, f32[8,512]{1,0:T(8,128)S(1)}, u32[]{:S(2)}, u32[]{:S(2)}) collective-permute-start(f32[8,512]{1,0:T(8,128)} %get-tuple-element.47.refs_0_), channel_id=1, source_target_pairs={{1,0},{2,1},{3,2},{0,3},{5,4},{6,5},{7,6},{4,7},{9,8},{10,9},{11,1... | collective-permute-start | bytes 49160 | tf_op jit(solution)/shard_map/ppermute | solution.py:21
  90.2 2.2 %collective-permute-done.23.refs_6_ = f32[8,512]{1,0:T(8,128)S(1)} collective-permute-done((f32[8,512]{1,0:T(8,128)}, f32[8,512]{1,0:T(8,128)S(1)}, u32[]{:S(2)}, u32[]{:S(2)}) %collective-permute-start.23) | collective-permute-done | bytes 16416 | tf_op jit(solution)/shard_map/ppermute | solution.py:21
  92.5 0.5 copy-done.24
  93.9 2.9 %collective-permute-start.25 = (bf16[1024,512]{1,0:T(8,128)(2,1)}, bf16[1024,512]{1,0:T(8,128)(2,1)S(1)}, u32[]{:S(2)}, u32[]{:S(2)}) collective-permute-start(bf16[1024,512]{1,0:T(8,128)(2,1)} %get-tuple-element.54.ep), channel_id=1, source_target_pairs={{1,0},{2,1},{3,2},{0,3},{5,4},{6,5},{7,6},{4,7},{9,8},{10,9},{11,1... | collective-permute-start | bytes 3145736 | tf_op jit(solution)/shard_map/ppermute | solution.py:21
  96.8 16.8 %hidden.1 = (bf16[4,4,256,256]{3,2,1,0:T(8,128)(2,1)}, bf16[2,4,256,256]{3,2,1,0:T(8,128)(2,1)}, bf16[2,4,256,256]{3,2,1,0:T(8,128)(2,1)}, bf16[2048,512]{1,0:T(8,128)(2,1)}) custom-call(s32[4]{0:T(128)} %get-tuple-element.40.at, bf16[1024,512]{1,0:T(8,128)(2,1)} %get-tuple-element.43.e0, bf16[1024,512]{1,0:T(8,128)(2,1)} %get-tuple-element.49.e1.refs_2_, ...), custom_call_target="tpu_custom_call" | custom-call | flops 1000 | bytes 1000 | tf_op jit(solution)/shard_map/hidden/pallas_call | solution.py:260
  113.6 4.9 %collective-permute-done.25.refs_4_ = bf16[1024,512]{1,0:T(8,128)(2,1)S(1)} collective-permute-done((bf16[1024,512]{1,0:T(8,128)(2,1)}, bf16[1024,512]{1,0:T(8,128)(2,1)S(1)}, u32[]{:S(2)}, u32[]{:S(2)}) %collective-permute-start.25) | collective-permute-done | bytes 1048608 | tf_op jit(solution)/shard_map/ppermute | solution.py:21
  118.5 3.3 %collective-permute-done.24.refs_3_ = bf16[1024,512]{1,0:T(8,128)(2,1)S(1)} collective-permute-done((bf16[1024,512]{1,0:T(8,128)(2,1)}, bf16[1024,512]{1,0:T(8,128)(2,1)S(1)}, u32[]{:S(2)}, u32[]{:S(2)}) %collective-permute-start.24) | collective-permute-done | bytes 1048608 | tf_op jit(solution)/shard_map/ppermute | solution.py:21
  121.8 1.0 copy-done.5
  122.8 0.5 collective-permute-start.28
  123.3 0.6 collective-permute-start.31
  123.9 1.4 collective-permute-start.32
  125.7 1.5 collective-permute-done.28
  127.2 1.4 fusion.4
  128.5 2.9 %collective-permute-start.30 = (bf16[4,256,256]{2,1,0:T(8,128)(2,1)}, bf16[4,256,256]{2,1,0:T(8,128)(2,1)S(1)}, u32[]{:S(2)}, u32[]{:S(2)}) collective-permute-start(bf16[4,256,256]{2,1,0:T(8,128)(2,1)} %get-tuple-element.83), channel_id=1, source_target_pairs={{32,0},{12,4},{40,8},{20,12},{48,16},{28,20},{56,24},{4,28},{64,32... | collective-permute-start | bytes 1572872 | tf_op jit(solution)/shard_map/ppermute | solution.py:36
  131.4 0.9 collective-permute-start.27
  132.3 9.4 %embed_a.1.refs_3_ = bf16[2048,1024]{1,0:T(8,128)(2,1)} custom-call(s32[4]{0:T(128)} %get-tuple-element.40.at, bf16[2048,512]{1,0:T(8,128)(2,1)} %get-tuple-element.57.tgt, bf16[1024,512]{1,0:T(8,128)(2,1)} %get-tuple-element.54.ep, bf16[1024,512]{1,0:T(8,128)(2,1)} %get-tuple-element.58.em, bf16[1024,512]{1,0:T(8,128)(2,1)} %get-tuple-element.59.ed, ...), custom_call_target="tpu_custom_call" | custom-call | flops 1000 | bytes 1000 | tf_op jit(solution)/shard_map/embed_a/pallas_call | solution.py:322
  141.7 6.9 %collective-permute-done.31.refs_4_ = bf16[1024,512]{1,0:T(8,128)(2,1)S(1)} collective-permute-done((bf16[1024,512]{1,0:T(8,128)(2,1)}, bf16[1024,512]{1,0:T(8,128)(2,1)S(1)}, u32[]{:S(2)}, u32[]{:S(2)}) %collective-permute-start.31) | collective-permute-done | bytes 1048608 | tf_op jit(solution)/shard_map/ppermute | solution.py:21
  148.6 1.5 collective-permute-done.32.refs_5_
  150.2 1.0 copy-done.3
  151.6 1.8 %fusion.14 = (bf16[4,256,256]{2,1,0:T(8,128)(2,1)S(1)}, f32[4,256,256]{2,1,0:T(8,128)S(1)}) fusion(bf16[4,256,256]{2,1,0:T(8,128)(2,1)} %get-tuple-element.68, bf16[4,256,256]{2,1,0:T(8,128)(2,1)} %get-tuple-element.67, bf16[4,256,256]{2,1,0:T(8,128)(2,1)} %get-tuple-element.66, bf16[2,4,256,256]{3,2,1,0:T(8,128)(2,1)S(1)} %copy-done.11, ...), kind=kLoop, calls=%fused_computation.48 | loop fusion | flops 2621440 | bytes 4194304 | tf_op jit(solution)/shard_map/convert.2
  153.4 2.7 %collective-permute-start.35 = (bf16[256,256]{1,0:T(8,128)(2,1)S(1)}, bf16[256,256]{1,0:T(8,128)(2,1)S(1)}, u32[]{:S(2)}, u32[]{:S(2)}) collective-permute-start(bf16[256,256]{1,0:T(8,128)(2,1)S(1)} %get-tuple-element.86), channel_id=1, source_target_pairs={{8,0},{36,4},{16,8},{44,12},{24,16},{52,20},{0,24},{60,28},{40,32}... | collective-permute-start | bytes 393224 | tf_op jit(solution)/shard_map/ppermute | solution.py:36
  156.5 0.6 collective-permute-start.33
  157.1 9.4 %embed_b.1.refs_3_ = bf16[2048,1024]{1,0:T(8,128)(2,1)} custom-call(s32[4]{0:T(128)} %get-tuple-element.40.at, bf16[2048,512]{1,0:T(8,128)(2,1)} %get-tuple-element.57.tgt, bf16[1024,512]{1,0:T(8,128)(2,1)} %get-tuple-element.69.ep, bf16[1024,512]{1,0:T(8,128)(2,1)} %get-tuple-element.65.em, ...), custom_call_target="tpu_custom_call", output_to_operand_aliasing={{}: (12, {})} | custom-call | flops 1000 | bytes 1000 | tf_op jit(solution)/shard_map/embed_b/pallas_call | solution.py:322
  166.6 0.6 copy-done.19
  167.2 0.7 copy-done.21
  167.9 1.1 fusion.7
  169.1 1.3 collective-permute-done.36
  170.4 0.7 maximum_select_fusion
  (101 shorter events, 4.3 us)
Async XLA Ops:
  7.2 125.1 %all-gather.3.cloned.1.call-start = ((), (), s32[]{:S(2)}) async-start(), calls=%async_computation | async-start | bytes 4325376 | tf_op jit(solution)/shard_map/all_gather | solution.py:358
  8.1 1.3 collective-permute-start
  9.5 11.2 %collective-permute-start.3 = (bf16[256,256]{1,0:T(8,128)(2,1)S(1)}, bf16[256,256]{1,0:T(8,128)(2,1)S(1)}, u32[]{:S(2)}, u32[]{:S(2)}) collective-permute-start(bf16[256,256]{1,0:T(8,128)(2,1)S(1)} %maximum_select_fusion.1), channel_id=1, source_target_pairs={{64,0},{20,4},{72,8},{28,12},{80,16},{4,20},{88,24},{12,28},{96,32... | collective-permute-start | bytes 393224 | tf_op jit(solution)/shard_map/ppermute | solution.py:36
  12.7 8.0 %collective-permute-start.2 = (bf16[256,256]{1,0:T(8,128)(2,1)S(1)}, bf16[256,256]{1,0:T(8,128)(2,1)S(1)}, u32[]{:S(2)}, u32[]{:S(2)}) collective-permute-start(bf16[256,256]{1,0:T(8,128)(2,1)S(1)} %maximum_select_fusion.1), channel_id=1, source_target_pairs={{32,0},{12,4},{40,8},{20,12},{48,16},{28,20},{56,24},{4,28},{64,32... | collective-permute-start | bytes 393224 | tf_op jit(solution)/shard_map/ppermute | solution.py:36
  13.8 6.2 %collective-permute-start.1 = (bf16[256,256]{1,0:T(8,128)(2,1)S(1)}, bf16[256,256]{1,0:T(8,128)(2,1)S(1)}, u32[]{:S(2)}, u32[]{:S(2)}) collective-permute-start(bf16[256,256]{1,0:T(8,128)(2,1)S(1)} %maximum_select_fusion.1), channel_id=1, source_target_pairs={{96,0},{28,4},{104,8},{4,12},{112,16},{12,20},{120,24},{20,28},{0,... | collective-permute-start | bytes 393224 | tf_op jit(solution)/shard_map/ppermute | solution.py:36
  20.0 0.7 copy-start.23
  21.6 21.0 %copy-start.6 = (bf16[4,256,256]{2,1,0:T(8,128)(2,1)}, bf16[4,256,256]{2,1,0:T(8,128)(2,1)S(1)}, u32[]{:S(2)}) copy-start(bf16[4,256,256]{2,1,0:T(8,128)(2,1)S(1)} %pad_maximum_fusion.refs_0_) | copy-start | bytes 1572868
  21.6 11.3 %collective-permute-start.6 = (bf16[4,256,256]{2,1,0:T(8,128)(2,1)S(1)}, bf16[4,256,256]{2,1,0:T(8,128)(2,1)S(1)}, u32[]{:S(2)}, u32[]{:S(2)}) collective-permute-start(bf16[4,256,256]{2,1,0:T(8,128)(2,1)S(1)} %pad_maximum_fusion.refs_0_), channel_id=1, source_target_pairs={{24,0},{100,4},{0,8},{108,12},{8,16},{116,20},{16,24},{124,28},{56... | collective-permute-start | bytes 1572872 | tf_op jit(solution)/shard_map/ppermute | solution.py:36
  23.6 16.4 %collective-permute-start.5 = (bf16[4,256,256]{2,1,0:T(8,128)(2,1)S(1)}, bf16[4,256,256]{2,1,0:T(8,128)(2,1)S(1)}, u32[]{:S(2)}, u32[]{:S(2)}) collective-permute-start(bf16[4,256,256]{2,1,0:T(8,128)(2,1)S(1)} %pad_maximum_fusion.refs_0_), channel_id=1, source_target_pairs={{16,0},{68,4},{24,8},{76,12},{0,16},{84,20},{8,24},{92,28},{48,32}... | collective-permute-start | bytes 1572872 | tf_op jit(solution)/shard_map/ppermute | solution.py:36
  27.2 12.8 %collective-permute-start.4 = (bf16[4,256,256]{2,1,0:T(8,128)(2,1)S(1)}, bf16[4,256,256]{2,1,0:T(8,128)(2,1)S(1)}, u32[]{:S(2)}, u32[]{:S(2)}) collective-permute-start(bf16[4,256,256]{2,1,0:T(8,128)(2,1)S(1)} %pad_maximum_fusion.refs_0_), channel_id=1, source_target_pairs={{8,0},{36,4},{16,8},{44,12},{24,16},{52,20},{0,24},{60,28},{40,32}... | collective-permute-start | bytes 1572872 | tf_op jit(solution)/shard_map/ppermute | solution.py:36
  28.2 13.8 %collective-permute-start.7 = (bf16[4,256,256]{2,1,0:T(8,128)(2,1)S(1)}, bf16[4,256,256]{2,1,0:T(8,128)(2,1)S(1)}, u32[]{:S(2)}, u32[]{:S(2)}) collective-permute-start(bf16[4,256,256]{2,1,0:T(8,128)(2,1)S(1)} %pad_maximum_fusion.refs_0_), channel_id=1, source_target_pairs={{0,4},{4,0},{1,5},{5,1},{2,6},{6,2},{3,7},{7,3},{8,12},{12,8},{9,1... | collective-permute-start | bytes 1572872 | tf_op jit(solution)/shard_map/ppermute | solution.py:25
  32.9 9.7 %copy-start.12 = (bf16[4,256,256]{2,1,0:T(8,128)(2,1)}, bf16[4,256,256]{2,1,0:T(8,128)(2,1)S(1)}, u32[]{:S(2)}) copy-start(bf16[4,256,256]{2,1,0:T(8,128)(2,1)S(1)} %collective-permute-done.6.refs_3_) | copy-start | bytes 1572868
  32.9 9.2 %collective-permute-start.10 = (bf16[4,256,256]{2,1,0:T(8,128)(2,1)S(1)}, bf16[4,256,256]{2,1,0:T(8,128)(2,1)S(1)}, u32[]{:S(2)}, u32[]{:S(2)}) collective-permute-start(bf16[4,256,256]{2,1,0:T(8,128)(2,1)S(1)} %collective-permute-done.6.refs_3_), channel_id=1, source_target_pairs={{0,4},{4,0},{1,5},{5,1},{2,6},{6,2},{3,7},{7,3},{8,12},{12,8},{9,1... | collective-permute-start | bytes 1572872 | tf_op jit(solution)/shard_map/ppermute | solution.py:25
  40.0 2.7 %copy-start.13 = (bf16[4,256,256]{2,1,0:T(8,128)(2,1)}, bf16[4,256,256]{2,1,0:T(8,128)(2,1)S(1)}, u32[]{:S(2)}) copy-start(bf16[4,256,256]{2,1,0:T(8,128)(2,1)S(1)} %collective-permute-done.5.refs_2_) | copy-start | bytes 1572868
  40.0 2.1 %collective-permute-start.9 = (bf16[4,256,256]{2,1,0:T(8,128)(2,1)S(1)}, bf16[4,256,256]{2,1,0:T(8,128)(2,1)S(1)}, u32[]{:S(2)}, u32[]{:S(2)}) collective-permute-start(bf16[4,256,256]{2,1,0:T(8,128)(2,1)S(1)} %collective-permute-done.5.refs_2_), channel_id=1, source_target_pairs={{0,4},{4,0},{1,5},{5,1},{2,6},{6,2},{3,7},{7,3},{8,12},{12,8},{9,1... | collective-permute-start | bytes 1572872 | tf_op jit(solution)/shard_map/ppermute | solution.py:25
  40.0 2.7 %copy-start.14 = (bf16[4,256,256]{2,1,0:T(8,128)(2,1)}, bf16[4,256,256]{2,1,0:T(8,128)(2,1)S(1)}, u32[]{:S(2)}) copy-start(bf16[4,256,256]{2,1,0:T(8,128)(2,1)S(1)} %collective-permute-done.4.refs_1_) | copy-start | bytes 1572868
  40.0 2.6 %collective-permute-start.8 = (bf16[4,256,256]{2,1,0:T(8,128)(2,1)S(1)}, bf16[4,256,256]{2,1,0:T(8,128)(2,1)S(1)}, u32[]{:S(2)}, u32[]{:S(2)}) collective-permute-start(bf16[4,256,256]{2,1,0:T(8,128)(2,1)S(1)} %collective-permute-done.4.refs_1_), channel_id=1, source_target_pairs={{0,4},{4,0},{1,5},{5,1},{2,6},{6,2},{3,7},{7,3},{8,12},{12,8},{9,1... | collective-permute-start | bytes 1572872 | tf_op jit(solution)/shard_map/ppermute | solution.py:25
  40.5 19.8 %collective-permute-start.11 = (bf16[512,128]{1,0:T(8,128)(2,1)}, bf16[512,128]{1,0:T(8,128)(2,1)S(1)}, u32[]{:S(2)}, u32[]{:S(2)}) collective-permute-start(bf16[512,128]{1,0:T(8,128)(2,1)} %bitcast.56), channel_id=1, source_target_pairs={{0,0},{1,32},{2,64},{3,96},{32,1},{33,33},{34,65},{35,97},{64,2},{... | collective-permute-start | bytes 393224 | tf_op jit(solution)/shard_map/ppermute | solution.py:347
  42.1 0.8 copy-start.15
  42.1 1.0 copy-start.16
  42.1 1.1 copy-start.17
  42.6 0.8 copy-start.18
  60.3 0.7 copy-start.22
  61.0 31.5 %collective-permute-start.20 = (bf16[1024,512]{1,0:T(8,128)(2,1)}, bf16[1024,512]{1,0:T(8,128)(2,1)S(1)}, u32[]{:S(2)}, u32[]{:S(2)}) collective-permute-start(bf16[1024,512]{1,0:T(8,128)(2,1)} %get-tuple-element.43.e0), channel_id=1, source_target_pairs={{3,0},{0,1},{1,2},{2,3},{7,4},{4,5},{5,6},{6,7},{11,8},{8,9},{9,10... | collective-permute-start | bytes 3145736 | tf_op jit(solution)/shard_map/ppermute | solution.py:21
  63.0 29.5 %collective-permute-start.19 = (bf16[1024,512]{1,0:T(8,128)(2,1)}, bf16[1024,512]{1,0:T(8,128)(2,1)S(1)}, u32[]{:S(2)}, u32[]{:S(2)}) collective-permute-start(bf16[1024,512]{1,0:T(8,128)(2,1)} %get-tuple-element.43.e0), channel_id=1, source_target_pairs={{1,0},{2,1},{3,2},{0,3},{5,4},{6,5},{7,6},{4,7},{9,8},{10,9},{11,1... | collective-permute-start | bytes 3145736 | tf_op jit(solution)/shard_map/ppermute | solution.py:21
  64.5 9.0 %collective-permute-start.14 = (f32[8,512]{1,0:T(8,128)}, f32[8,512]{1,0:T(8,128)S(1)}, u32[]{:S(2)}, u32[]{:S(2)}) collective-permute-start(f32[8,512]{1,0:T(8,128)} %get-tuple-element.45), channel_id=1, source_target_pairs={{96,0},{0,32},{32,64},{64,96},{97,1},{1,33},{33,65},{65,97},{98,2}... | collective-permute-start | bytes 49160 | tf_op jit(solution)/shard_map/ppermute | solution.py:21
  67.7 6.2 %collective-permute-start.13 = (f32[8,512]{1,0:T(8,128)}, f32[8,512]{1,0:T(8,128)S(1)}, u32[]{:S(2)}, u32[]{:S(2)}) collective-permute-start(f32[8,512]{1,0:T(8,128)} %get-tuple-element.45), channel_id=1, source_target_pairs={{64,0},{96,32},{0,64},{32,96},{65,1},{97,33},{1,65},{33,97},{66,2}... | collective-permute-start | bytes 49160 | tf_op jit(solution)/shard_map/ppermute | solution.py:21
  71.8 4.0 %collective-permute-start.12 = (f32[8,512]{1,0:T(8,128)}, f32[8,512]{1,0:T(8,128)S(1)}, u32[]{:S(2)}, u32[]{:S(2)}) collective-permute-start(f32[8,512]{1,0:T(8,128)} %get-tuple-element.45), channel_id=1, source_target_pairs={{32,0},{64,32},{96,64},{0,96},{33,1},{65,33},{97,65},{1,97},{34,2}... | collective-permute-start | bytes 49160 | tf_op jit(solution)/shard_map/ppermute | solution.py:21
  76.7 5.1 %collective-permute-start.17 = (f32[8,512]{1,0:T(8,128)S(1)}, f32[8,512]{1,0:T(8,128)S(1)}, u32[]{:S(2)}, u32[]{:S(2)}) collective-permute-start(f32[8,512]{1,0:T(8,128)S(1)} %maximum_maximum_fusion), channel_id=1, source_target_pairs={{24,0},{0,8},{8,16},{16,24},{25,1},{1,9},{9,17},{17,25},{26,2},{2,... | collective-permute-start | bytes 49160 | tf_op jit(solution)/shard_map/ppermute | solution.py:21
  78.1 5.3 %collective-permute-start.16 = (f32[8,512]{1,0:T(8,128)S(1)}, f32[8,512]{1,0:T(8,128)S(1)}, u32[]{:S(2)}, u32[]{:S(2)}) collective-permute-start(f32[8,512]{1,0:T(8,128)S(1)} %maximum_maximum_fusion), channel_id=1, source_target_pairs={{16,0},{24,8},{0,16},{8,24},{17,1},{25,9},{1,17},{9,25},{18,2},{26... | collective-permute-start | bytes 49160 | tf_op jit(solution)/shard_map/ppermute | solution.py:21
  79.8 3.8 %collective-permute-start.15 = (f32[8,512]{1,0:T(8,128)S(1)}, f32[8,512]{1,0:T(8,128)S(1)}, u32[]{:S(2)}, u32[]{:S(2)}) collective-permute-start(f32[8,512]{1,0:T(8,128)S(1)} %maximum_maximum_fusion), channel_id=1, source_target_pairs={{8,0},{16,8},{24,16},{0,24},{9,1},{17,9},{25,17},{1,25},{10,2},{18... | collective-permute-start | bytes 49160 | tf_op jit(solution)/shard_map/ppermute | solution.py:21
  83.7 1.2 copy-start.27
  83.7 1.2 collective-permute-start.18
  87.0 5.5 %collective-permute-start.23 = (f32[8,512]{1,0:T(8,128)}, f32[8,512]{1,0:T(8,128)S(1)}, u32[]{:S(2)}, u32[]{:S(2)}) collective-permute-start(f32[8,512]{1,0:T(8,128)} %get-tuple-element.47.refs_0_), channel_id=1, source_target_pairs={{2,0},{3,1},{0,2},{1,3},{6,4},{7,5},{4,6},{5,7},{10,8},{11,9},{8,1... | collective-permute-start | bytes 49160 | tf_op jit(solution)/shard_map/ppermute | solution.py:21
  87.0 5.5 %collective-permute-start.22 = (f32[8,512]{1,0:T(8,128)}, f32[8,512]{1,0:T(8,128)S(1)}, u32[]{:S(2)}, u32[]{:S(2)}) collective-permute-start(f32[8,512]{1,0:T(8,128)} %get-tuple-element.47.refs_0_), channel_id=1, source_target_pairs={{3,0},{0,1},{1,2},{2,3},{7,4},{4,5},{5,6},{6,7},{11,8},{8,9},{9,10... | collective-permute-start | bytes 49160 | tf_op jit(solution)/shard_map/ppermute | solution.py:21
  87.8 4.7 %collective-permute-start.21 = (f32[8,512]{1,0:T(8,128)}, f32[8,512]{1,0:T(8,128)S(1)}, u32[]{:S(2)}, u32[]{:S(2)}) collective-permute-start(f32[8,512]{1,0:T(8,128)} %get-tuple-element.47.refs_0_), channel_id=1, source_target_pairs={{1,0},{2,1},{3,2},{0,3},{5,4},{6,5},{7,6},{4,7},{9,8},{10,9},{11,1... | collective-permute-start | bytes 49160 | tf_op jit(solution)/shard_map/ppermute | solution.py:21
  92.4 0.6 copy-start.26
  92.5 1.0 copy-start
  92.5 1.4 copy-start.1
  93.9 24.6 %collective-permute-start.25 = (bf16[1024,512]{1,0:T(8,128)(2,1)}, bf16[1024,512]{1,0:T(8,128)(2,1)S(1)}, u32[]{:S(2)}, u32[]{:S(2)}) collective-permute-start(bf16[1024,512]{1,0:T(8,128)(2,1)} %get-tuple-element.54.ep), channel_id=1, source_target_pairs={{1,0},{2,1},{3,2},{0,3},{5,4},{6,5},{7,6},{4,7},{9,8},{10,9},{11,1... | collective-permute-start | bytes 3145736 | tf_op jit(solution)/shard_map/ppermute | solution.py:21
  96.8 24.9 %collective-permute-start.24 = (bf16[1024,512]{1,0:T(8,128)(2,1)}, bf16[1024,512]{1,0:T(8,128)(2,1)S(1)}, u32[]{:S(2)}, u32[]{:S(2)}) collective-permute-start(bf16[1024,512]{1,0:T(8,128)(2,1)} %get-tuple-element.49.e1.refs_2_), channel_id=1, source_target_pairs={{3,0},{0,1},{1,2},{2,3},{7,4},{4,5},{5,6},{6,7},{11,8},{8,9},{9,10... | collective-permute-start | bytes 3145736 | tf_op jit(solution)/shard_map/ppermute | solution.py:21
  113.6 13.6 %copy-start.7 = (bf16[4,4,256,256]{3,2,1,0:T(8,128)(2,1)S(1)}, bf16[4,4,256,256]{3,2,1,0:T(8,128)(2,1)}, u32[]{:S(2)}) copy-start(bf16[4,4,256,256]{3,2,1,0:T(8,128)(2,1)} %get-tuple-element.51) | copy-start | bytes 6291460
  118.5 3.3 %copy-start.4 = (bf16[1024,512]{1,0:T(8,128)(2,1)}, bf16[1024,512]{1,0:T(8,128)(2,1)S(1)}, u32[]{:S(2)}) copy-start(bf16[1024,512]{1,0:T(8,128)(2,1)S(1)} %collective-permute-done.25.refs_4_) | copy-start | bytes 3145732
  121.8 1.0 copy-start.5
  122.8 2.9 %collective-permute-start.26 = (bf16[2,4,256,256]{3,2,1,0:T(8,128)(2,1)}, bf16[2,4,256,256]{3,2,1,0:T(8,128)(2,1)S(1)}, u32[]{:S(2)}, u32[]{:S(2)}) collective-permute-start(bf16[2,4,256,256]{3,2,1,0:T(8,128)(2,1)} %get-tuple-element.55), channel_id=1, source_target_pairs={{0,4},{4,0},{1,5},{5,1},{2,6},{6,2},{3,7},{7,3},{8,12},{12,8},{9,1... | collective-permute-start | bytes 3145736 | tf_op jit(solution)/shard_map/ppermute | solution.py:25
  122.8 4.4 %collective-permute-start.28 = (bf16[2,4,256,256]{3,2,1,0:T(8,128)(2,1)}, bf16[2,4,256,256]{3,2,1,0:T(8,128)(2,1)S(1)}, u32[]{:S(2)}, u32[]{:S(2)}) collective-permute-start(bf16[2,4,256,256]{3,2,1,0:T(8,128)(2,1)} %get-tuple-element.56), channel_id=1, source_target_pairs={{0,4},{4,0},{1,5},{5,1},{2,6},{6,2},{3,7},{7,3},{8,12},{12,8},{9,1... | collective-permute-start | bytes 3145736 | tf_op jit(solution)/shard_map/ppermute | solution.py:25
  123.3 25.3 %collective-permute-start.31 = (bf16[1024,512]{1,0:T(8,128)(2,1)}, bf16[1024,512]{1,0:T(8,128)(2,1)S(1)}, u32[]{:S(2)}, u32[]{:S(2)}) collective-permute-start(bf16[1024,512]{1,0:T(8,128)(2,1)} %get-tuple-element.64), channel_id=1, source_target_pairs={{1,0},{2,1},{3,2},{0,3},{5,4},{6,5},{7,6},{4,7},{9,8},{10,9},{11,1... | collective-permute-start | bytes 3145736 | tf_op jit(solution)/shard_map/ppermute | solution.py:21
  123.9 26.2 %collective-permute-start.32 = (bf16[1024,512]{1,0:T(8,128)(2,1)}, bf16[1024,512]{1,0:T(8,128)(2,1)S(1)}, u32[]{:S(2)}, u32[]{:S(2)}) collective-permute-start(bf16[1024,512]{1,0:T(8,128)(2,1)} %get-tuple-element.65.em), channel_id=1, source_target_pairs={{3,0},{0,1},{1,2},{2,3},{7,4},{4,5},{5,6},{6,7},{11,8},{8,9},{9,10... | collective-permute-start | bytes 3145736 | tf_op jit(solution)/shard_map/ppermute | solution.py:21
  125.7 5.8 %copy-start.10 = (bf16[2,4,256,256]{3,2,1,0:T(8,128)(2,1)}, bf16[2,4,256,256]{3,2,1,0:T(8,128)(2,1)S(1)}, u32[]{:S(2)}) copy-start(bf16[2,4,256,256]{3,2,1,0:T(8,128)(2,1)S(1)} %collective-permute-done.26) | copy-start | bytes 3145732
  128.5 21.6 %collective-permute-start.30 = (bf16[4,256,256]{2,1,0:T(8,128)(2,1)}, bf16[4,256,256]{2,1,0:T(8,128)(2,1)S(1)}, u32[]{:S(2)}, u32[]{:S(2)}) collective-permute-start(bf16[4,256,256]{2,1,0:T(8,128)(2,1)} %get-tuple-element.83), channel_id=1, source_target_pairs={{32,0},{12,4},{40,8},{20,12},{48,16},{28,20},{56,24},{4,28},{64,32... | collective-permute-start | bytes 1572872 | tf_op jit(solution)/shard_map/ppermute | solution.py:36
  131.4 18.7 %collective-permute-start.29 = (bf16[4,256,256]{2,1,0:T(8,128)(2,1)}, bf16[4,256,256]{2,1,0:T(8,128)(2,1)S(1)}, u32[]{:S(2)}, u32[]{:S(2)}) collective-permute-start(bf16[4,256,256]{2,1,0:T(8,128)(2,1)} %get-tuple-element.84), channel_id=1, source_target_pairs={{64,0},{20,4},{72,8},{28,12},{80,16},{4,20},{88,24},{12,28},{96,32... | collective-permute-start | bytes 1572872 | tf_op jit(solution)/shard_map/ppermute | solution.py:36
  131.4 18.7 %collective-permute-start.27 = (bf16[4,256,256]{2,1,0:T(8,128)(2,1)}, bf16[4,256,256]{2,1,0:T(8,128)(2,1)}, u32[]{:S(2)}, u32[]{:S(2)}) collective-permute-start(bf16[4,256,256]{2,1,0:T(8,128)(2,1)} %get-tuple-element.85), channel_id=1, source_target_pairs={{96,0},{28,4},{104,8},{4,12},{112,16},{12,20},{120,24},{20,28},{0,... | collective-permute-start | bytes 1572872 | tf_op jit(solution)/shard_map/ppermute | solution.py:36
  141.7 9.9 %copy-start.11 = (bf16[2,4,256,256]{3,2,1,0:T(8,128)(2,1)S(1)}, bf16[2,4,256,256]{3,2,1,0:T(8,128)(2,1)}, u32[]{:S(2)}) copy-start(bf16[2,4,256,256]{3,2,1,0:T(8,128)(2,1)} %copy-done.10) | copy-start | bytes 3145732
  148.6 1.6 copy-start.2
  150.1 1.0 copy-start.3
  150.1 1.2 copy-start.8
  150.1 1.4 copy-start.9
  153.4 13.1 %collective-permute-start.35 = (bf16[256,256]{1,0:T(8,128)(2,1)S(1)}, bf16[256,256]{1,0:T(8,128)(2,1)S(1)}, u32[]{:S(2)}, u32[]{:S(2)}) collective-permute-start(bf16[256,256]{1,0:T(8,128)(2,1)S(1)} %get-tuple-element.86), channel_id=1, source_target_pairs={{8,0},{36,4},{16,8},{44,12},{24,16},{52,20},{0,24},{60,28},{40,32}... | collective-permute-start | bytes 393224 | tf_op jit(solution)/shard_map/ppermute | solution.py:36
  156.2 10.4 %collective-permute-start.34 = (bf16[256,256]{1,0:T(8,128)(2,1)S(1)}, bf16[256,256]{1,0:T(8,128)(2,1)S(1)}, u32[]{:S(2)}, u32[]{:S(2)}) collective-permute-start(bf16[256,256]{1,0:T(8,128)(2,1)S(1)} %get-tuple-element.87), channel_id=1, source_target_pairs={{16,0},{68,4},{24,8},{76,12},{0,16},{84,20},{8,24},{92,28},{48,32}... | collective-permute-start | bytes 393224 | tf_op jit(solution)/shard_map/ppermute | solution.py:36
  156.5 10.1 %collective-permute-start.33 = (bf16[256,256]{1,0:T(8,128)(2,1)S(1)}, bf16[256,256]{1,0:T(8,128)(2,1)S(1)}, u32[]{:S(2)}, u32[]{:S(2)}) collective-permute-start(bf16[256,256]{1,0:T(8,128)(2,1)S(1)} %get-tuple-element.88), channel_id=1, source_target_pairs={{24,0},{100,4},{0,8},{108,12},{8,16},{116,20},{16,24},{124,28},{56... | collective-permute-start | bytes 393224 | tf_op jit(solution)/shard_map/ppermute | solution.py:36
  166.5 0.6 copy-start.19
  166.5 0.7 copy-start.20
  167.2 0.7 copy-start.21
  169.0 1.4 collective-permute-start.36
  (3 other events, 1.8 us)
Sparse Core Ops, SparseCore 0:
  61.1 47.5 all-gather.2

commit v9 on v8

--- a/solution.py
+++ b/solution.py
@@ -70,8 +70,8 @@
     )(*arrays)
 
 
+SUB = 256
 CUT = VOC // 2
-SUB = 256
 
 
 def gather_pieces(block, *early):
@@ -84,7 +84,7 @@
 
 def logits_body(at, *refs):
     pieces, refs = refs[:8], refs[8:]
-    tid, emb, e0_out, e1_out, st_out, loc_out, full = refs
+    tid, emb, e_out, st_out, loc_out, full = refs
     step = pl.program_id(0)
     x, z, c = at[0], at[1], at[2]
 
@@ -107,17 +107,12 @@
     hit = jnp.sum(jnp.where(ids == tid[...], logits, 0.0), axis=0, keepdims=True)
     e = jnp.exp(logits - top)
     total = jnp.sum(e, axis=0, keepdims=True)
-    e = e.astype(BF)
-
+    e_out[...] = e.astype(BF)
     for s in range(TILES):
 
         @pl.when(step == s)
         def _():
             st_out[pl.ds(s, 1), :] = top
-            for k in (0, 1):
-                row = s * TILE + k * SUB
-                ref, row = (e0_out, row) if row < CUT else (e1_out, row - CUT)
-                ref[pl.ds(row, SUB), :] = e[k * SUB : (k + 1) * SUB]
 
     @pl.when(step == 0)
     def _():
@@ -144,16 +139,14 @@
             in_specs=[pl.BlockSpec((4, HALF, 256), lambda i, at: (0, 0, 0))] * 8
             + [pl.BlockSpec((1, ROWS), lambda i, at: (0, 0)), pl.BlockSpec((TILE, WIDTH), lambda i, at: (i, 0))],
             out_specs=[
-                pl.BlockSpec((CUT, ROWS), lambda i, at: (0, 0)),
-                pl.BlockSpec((VOC - CUT, ROWS), lambda i, at: (0, 0)),
+                pl.BlockSpec((TILE, ROWS), lambda i, at: (i, 0)),
                 whole,
                 whole,
             ],
             scratch_shapes=[pltpu.VMEM((ROWS, WIDTH), BF)],
         ),
         out_shape=[
-            jax.ShapeDtypeStruct((CUT, ROWS), BF),
-            jax.ShapeDtypeStruct((VOC - CUT, ROWS), BF),
+            jax.ShapeDtypeStruct((VOC, ROWS), BF),
             jax.ShapeDtypeStruct((8, ROWS), F32),
             jax.ShapeDtypeStruct((8, ROWS), F32),
         ],
@@ -226,13 +219,12 @@
     return (g - jnp.where(ids == tid, pack[pl.ds(4, 1), :], 0.0)).astype(BF)
 
 
-def hidden_body(at, e0, e1, pack, w0, w1, w2, w3, keep, send0, send1, tgt_out, tg):
+def hidden_body(at, e, pack, w0, w1, w2, w3, keep, send0, send1, tgt_out, tg):
     @pl.when(pl.program_id(0) == 0)
     def _():
         for t in range(VOC // SUB):
             rows = pl.ds(t * SUB, SUB)
-            e = e0[rows, :] if t * SUB < CUT else e1[pl.ds(t * SUB - CUT, SUB), :]
-            g = token_grad(e, pack, pack[pl.ds(t * SUB // TILE, 1), :], t * SUB)
+            g = token_grad(e[rows, :], pack, pack[pl.ds(t * SUB // TILE, 1), :], t * SUB)
             tgt_out[rows, :] = g
             tg[:, rows] = g.T
 
@@ -246,7 +238,7 @@
         (send0, send1)[k // 2][k % 2, 0] = jnp.where(first, b, a).astype(BF)
 
 
-def hidden_call(at, e0, e1, pack, emb):
+def hidden_call(at, e, pack, emb):
     whole = lambda s: pl.BlockSpec(s, lambda i, at: (0,) * len(s))
 
     def weight(k):
@@ -262,7 +254,7 @@
         grid_spec=pltpu.PrefetchScalarGridSpec(
             num_scalar_prefetch=1,
             grid=(4,),
-            in_specs=[whole((CUT, ROWS)), whole((VOC - CUT, ROWS)), whole((8, ROWS))] + [weight(k) for k in range(4)],
+            in_specs=[whole((VOC, ROWS)), whole((8, ROWS))] + [weight(k) for k in range(4)],
             out_specs=[
                 pl.BlockSpec((1, 4, HALF, 256), lambda i, at: (i, 0, 0, 0)),
             ]
@@ -280,7 +272,7 @@
         compiler_params=params(),
         cost_estimate=SMALL,
         name="hidden",
-    )(at, e0, e1, pack, emb, emb, emb, emb)
+    )(at, e, pack, emb, emb, emb, emb)
 
 
 def add(*xs):
@@ -301,40 +293,69 @@
     return jnp.where(c == 0, jnp.concatenate([mine, got]), jnp.concatenate([got, mine])), work
 
 
-def embed_body(base, at, tgt, ep, em, ed, pack_p, pack_m, pack_d, *refs):
-    feats, out = refs[:4], refs[-1]
+def feature_spec(d):
+    return pl.BlockSpec((1, 4, 2, ROWS, 128), lambda i, at: ((at[3] + d) & 3, 0, 0, 0, 0))
+
+
+def columns(f):
+    return jnp.concatenate([f[0, k // 2, k % 2] for k in range(8)], axis=1)
+
+
+def embed_a_body(at, tgt, ep, em, pack_p, pack_m, f0, f1, f3, acc):
     i = pl.program_id(0)
-
     parts = [tgt[...]]
-    tile = base // TILE + i
-    for e, pack in ((ep, pack_p), (em, pack_m), (ed, pack_d)):
-        parts.append(token_grad(e[...], pack, pack[pl.ds(tile, 1), :], tile * TILE))
-    q = [jnp.concatenate([f[0, k // 2, k % 2] for k in range(8)], axis=1) for f in feats]
-    out[...] = dot_nn(jnp.concatenate(parts, axis=1), jnp.concatenate(q, axis=0)).astype(BF)
-
-
-def embed_call(at, base, tgt, ep, em, ed, packs, feats, into, name):
-    first = base // TILE
+    for e, pack in ((ep, pack_p), (em, pack_m)):
+        parts.append(token_grad(e[...], pack, pack[pl.ds(i, 1), :], i * TILE))
+    q = jnp.concatenate([columns(f) for f in (f0, f1, f3)], axis=0)
+    acc[...] = dot_nn(jnp.concatenate(parts, axis=1), q)
+
+
+def embed_a_call(at, tgt, ep, em, packs, feats):
     tile = pl.BlockSpec((TILE, ROWS), lambda i, at: (i, 0))
     pack = pl.BlockSpec((8, ROWS), lambda i, at: (0, 0))
-    feat = lambda d: pl.BlockSpec((1, 4, 2, ROWS, 128), lambda i, at: ((at[3] + d) & 3, 0, 0, 0, 0))
-    more = [] if into is None else [into]
-    return pl.pallas_call(
-        functools.partial(embed_body, base),
+    return pl.pallas_call(
+        embed_a_body,
         grid_spec=pltpu.PrefetchScalarGridSpec(
             num_scalar_prefetch=1,
-            grid=(CUT // TILE,),
-            in_specs=[pl.BlockSpec((TILE, ROWS), lambda i, at: (i + first, 0)), tile, tile, tile, pack, pack, pack]
-            + [feat(d) for d in (0, 1, 3, 2)]
-            + [HBM] * len(more),
-            out_specs=pl.BlockSpec((TILE, 1024), lambda i, at: (i + first, 0)),
+            grid=(TILES,),
+            in_specs=[tile, tile, tile, pack, pack] + [feature_spec(d) for d in (0, 1, 3)],
+            out_specs=pl.BlockSpec((TILE, 1024), lambda i, at: (i, 0)),
+        ),
+        out_shape=jax.ShapeDtypeStruct((VOC, 1024), F32),
+        compiler_params=params(),
+        cost_estimate=SMALL,
+        name="embed_a",
+    )(at, tgt, ep, em, *packs, feats, feats, feats)
+
+
+def embed_b_body(at, acc, low, high, pack, f2, out):
+    i = pl.program_id(0)
+    e = jnp.where(i < CUT // TILE, low[...], high[...])
+    g = token_grad(e, pack, pack[pl.ds(i, 1), :], i * TILE)
+    out[...] = (acc[...] + dot_nn(g, columns(f2))).astype(BF)
+
+
+def embed_b_call(at, acc, low, high, pack, feats):
+    n = CUT // TILE
+    return pl.pallas_call(
+        embed_b_body,
+        grid_spec=pltpu.PrefetchScalarGridSpec(
+            num_scalar_prefetch=1,
+            grid=(TILES,),
+            in_specs=[
+                pl.BlockSpec((TILE, 1024), lambda i, at: (i, 0)),
+                pl.BlockSpec((TILE, ROWS), lambda i, at: (jnp.minimum(i, n - 1), 0)),
+                pl.BlockSpec((TILE, ROWS), lambda i, at: (jnp.maximum(i - n, 0), 0)),
+                pl.BlockSpec((8, ROWS), lambda i, at: (0, 0)),
+                feature_spec(2),
+            ],
+            out_specs=pl.BlockSpec((TILE, 1024), lambda i, at: (i, 0)),
         ),
         out_shape=jax.ShapeDtypeStruct((VOC, 1024), BF),
-        input_output_aliases={12: 0} if more else {},
-        compiler_params=params(),
-        cost_estimate=SMALL,
-        name=name,
-    )(at, tgt, ep, em, ed, *packs, *[feats] * 4, *more)
+        compiler_params=params(),
+        cost_estimate=SMALL,
+        name="embed_b",
+    )(at, acc, low, high, pack, feats)
 
 
 def local(comp_hidden, embed, mix, targets, weight):
@@ -353,29 +374,27 @@
     pieces, at, tid = gather_pieces(block, at, tid)
     pieces = pieces + [sibling(p) for p in pieces]
 
-    e0, e1, st, loc = logits_call(at, pieces, tid, embed)
+    e, st, loc = logits_call(at, pieces, tid, embed)
     loc, turned = gate(loc, turned)
     feats = lax.all_gather(turned, ("x", "z", "c")).reshape(4, 4, 2, ROWS, 128)
-    ep0, em0 = shift(e0, "y", 1), shift(e0, "y", 3)
+    ep, em = shift(e, "y", 1), shift(e, "y", 3)
 
     s = merge_call(loc, *(shift(loc, "x", d) for d in (1, 2, 3)))
     s = merge_call(s, *(shift(s, "z", d) for d in (1, 2, 3)))
     pack, grad_mix = finish_call(s, sibling(s), st, tid, mix, weight.reshape(1, 128))
     packs = [shift(pack, "y", d) for d in (1, 3, 2)]
-    pack, e1, ep0, em0, *packs = gate(pack, e1, ep0, em0, *packs)
-    em1, ed0 = shift(e1, "y", 3), shift(ep0, "y", 1)
-    keep, send0, send1, tgt = hidden_call(at, e0, e1, pack, embed)
-    send0, send1, e1, em1, ed0 = gate(send0, send1, e1, em1, ed0)
-    ep1, ed1 = shift(e1, "y", 1), shift(em1, "y", 3)
+    keep, send0, send1, tgt = hidden_call(at, e, pack, embed)
+    send0, send1, ep, em, *packs = gate(send0, send1, ep, em, *packs)
+    low, high = shift(ep[:CUT], "y", 1), shift(em[CUT:], "y", 3)
     recv = sibling(send0), sibling(send1)
 
     grad_hidden, grad_embed = scatter(
         keep,
         recv,
         c,
-        lambda: embed_call(at, 0, tgt, ep0, em0, ed0, packs, feats, None, "embed_a"),
-        lambda made, ep1, ed1: embed_call(at, CUT, tgt, ep1, em1, ed1, packs, feats, made, "embed_b"),
-        (ep1, ed1),
+        lambda: embed_a_call(at, tgt, ep, em, packs[:2], feats),
+        lambda acc, low, high: embed_b_call(at, acc, low, high, packs[2], feats),
+        (low, high),
     )
     return grad_hidden.reshape(4, 128, 128), grad_embed, grad_mix
 

time: 179 us -> 174 us (0.972)
  waiting for transfers between devices: 45.2 us -> 32.6 us
  local copies, waits for them, and re-layouts: 7.99 us -> 11.3 us
    ppermute x15 -> x13, waiting for transfers between devices: 23.3 us -> 12.9 us  [shift(): return lax.ppermute(a, axis, [((i + d) % 4, i) for i in range(4)])]
    slice x0 -> x2, local copies, waits for them, and re-layouts: none -> 3.5 us  [local(): low, high = (shift(ep[:CUT], 'y', 1), shift(em[CUT:], 'y', 3))]
    ppermute x12, starting transfers between devices: 19.2 us -> 21.9 us  [cross(): return lax.ppermute(a, ('x', 'z', 'c'), pairs)]
    ppermute x9, waiting for transfers between devices: 5.46 us -> 3.29 us  [sibling(): return lax.ppermute(a, 'c', [(0, 1), (1, 0)])]
    pallas_call x2, Pallas kernels: 18.8 us -> 20.8 us  [the longest x1 12.2 us: embed_a_call(): pl.pallas_call(embed_a_body, grid_spec=pltpu.PrefetchScalarGridSpec(num_s...]
    ppermute x15 -> x13, starting transfers between devices: 25.3 us -> 23.5 us  [shift(): return lax.ppermute(a, axis, [((i + d) % 4, i) for i in range(4)])]
    unnamed x58 -> x56, local copies, waits for them, and re-layouts: 7.28 us -> 7.08 us
  transfers between devices with their start and end apart: 38 -> 36, of which waited for: 19 -> 14; matrix products, arithmetic and copies ran while one was open for 3% -> 5% of each run, Pallas kernels for 30% -> 32%
where the time goes in v9:
time: 174 us; the launch traced here: 172 us
  Pallas kernels  55.5 us (32%)
  starting transfers between devices  48.9 us (28%)
  waiting for transfers between devices  32.6 us (19%)
  between operations  14.4 us (8%)
  local copies, waits for them, and re-layouts  11.3 us (6%)
  other arithmetic  9.44 us (5%)
    ppermute x13, starting transfers between devices, shift(): return lax.ppermute(a, axis, [((i + d) % 4, i) for i in range(4)])  23.5 us
    ppermute x12, starting transfers between devices, cross(): return lax.ppermute(a, ('x', 'z', 'c'), pairs)  21.9 us
    pallas_call x1, Pallas kernels, hidden_call(): pl.pallas_call(hidden_body, grid_spec=pltpu.PrefetchScalarGridSpec(num_sc...  16.9 us
    ppermute x12, waiting for transfers between devices, cross(): return lax.ppermute(a, ('x', 'z', 'c'), pairs)  16.4 us
    pallas_call x1, Pallas kernels, logits_call(): pl.pallas_call(logits_body, grid_spec=pltpu.PrefetchScalarGridSpec(num_sc...  16.3 us
    ppermute x13, waiting for transfers between devices, shift(): return lax.ppermute(a, axis, [((i + d) % 4, i) for i in range(4)])  12.9 us
    pallas_call x1, Pallas kernels, embed_a_call(): pl.pallas_call(embed_a_body, grid_spec=pltpu.PrefetchScalarGridSpec(num_s...  12.2 us
    pallas_call x1, Pallas kernels, embed_b_call(): pl.pallas_call(embed_b_body, grid_spec=pltpu.PrefetchScalarGridSpec(num_s...  8.59 us
  transfers between devices with their start and end apart: 36, of which 14 were waited for; matrix products, arithmetic and copies ran while one was open for 5% of the time, Pallas kernels for 32%

profile of v9, /device:TPU:0, one launch (start us, length us, event | category | flops | bytes accessed | tf_op | source)
XLA Modules:
  0.0 172.1 jit_solution(14320678779798528918)
XLA Ops:
  7.2 0.9 broadcast_select_fusion.1
  8.2 0.7 broadcast_subtract_fusion
  8.9 0.6 collective-permute-done
  9.5 3.2 %collective-permute-start.3 = (bf16[256,256]{1,0:T(8,128)(2,1)S(1)}, bf16[256,256]{1,0:T(8,128)(2,1)S(1)}, u32[]{:S(2)}, u32[]{:S(2)}) collective-permute-start(bf16[256,256]{1,0:T(8,128)(2,1)S(1)} %maximum_select_fusion.1), channel_id=1, source_target_pairs={{64,0},{20,4},{72,8},{28,12},{80,16},{4,20},{88,24},{12,28},{96,32... | collective-permute-start | bytes 393224 | tf_op jit(solution)/shard_map/ppermute | solution.py:36
  12.7 1.1 collective-permute-start.2
  13.8 0.9 collective-permute-start.1
  14.7 0.6 pad_add_fusion.refs_1_
  15.4 4.6 %collective-permute-done.1.refs_0_ = bf16[256,256]{1,0:T(8,128)(2,1)S(1)} collective-permute-done((bf16[256,256]{1,0:T(8,128)(2,1)S(1)}, bf16[256,256]{1,0:T(8,128)(2,1)S(1)}, u32[]{:S(2)}, u32[]{:S(2)}) %collective-permute-start.1) | collective-permute-done | bytes 131104 | tf_op jit(solution)/shard_map/ppermute | solution.py:36
  20.0 0.6 tile.2
  20.7 1.0 pad_maximum_fusion.refs_0_
  21.6 2.0 %collective-permute-start.6 = (bf16[4,256,256]{2,1,0:T(8,128)(2,1)S(1)}, bf16[4,256,256]{2,1,0:T(8,128)(2,1)S(1)}, u32[]{:S(2)}, u32[]{:S(2)}) collective-permute-start(bf16[4,256,256]{2,1,0:T(8,128)(2,1)S(1)} %pad_maximum_fusion.refs_0_), channel_id=1, source_target_pairs={{24,0},{100,4},{0,8},{108,12},{8,16},{116,20},{16,24},{124,28},{56... | collective-permute-start | bytes 1572872 | tf_op jit(solution)/shard_map/ppermute | solution.py:36
  23.6 3.6 %collective-permute-start.5 = (bf16[4,256,256]{2,1,0:T(8,128)(2,1)S(1)}, bf16[4,256,256]{2,1,0:T(8,128)(2,1)S(1)}, u32[]{:S(2)}, u32[]{:S(2)}) collective-permute-start(bf16[4,256,256]{2,1,0:T(8,128)(2,1)S(1)} %pad_maximum_fusion.refs_0_), channel_id=1, source_target_pairs={{16,0},{68,4},{24,8},{76,12},{0,16},{84,20},{8,24},{92,28},{48,32}... | collective-permute-start | bytes 1572872 | tf_op jit(solution)/shard_map/ppermute | solution.py:36
  27.2 1.0 collective-permute-start.4
  28.2 4.7 %collective-permute-done.6.refs_3_ = bf16[4,256,256]{2,1,0:T(8,128)(2,1)S(1)} collective-permute-done((bf16[4,256,256]{2,1,0:T(8,128)(2,1)S(1)}, bf16[4,256,256]{2,1,0:T(8,128)(2,1)S(1)}, u32[]{:S(2)}, u32[]{:S(2)}) %collective-permute-start.6) | collective-permute-done | bytes 524320 | tf_op jit(solution)/shard_map/ppermute | solution.py:36
  32.9 7.1 %collective-permute-done.5.refs_2_ = bf16[4,256,256]{2,1,0:T(8,128)(2,1)S(1)} collective-permute-done((bf16[4,256,256]{2,1,0:T(8,128)(2,1)S(1)}, bf16[4,256,256]{2,1,0:T(8,128)(2,1)S(1)}, u32[]{:S(2)}, u32[]{:S(2)}) %collective-permute-start.5) | collective-permute-done | bytes 524320 | tf_op jit(solution)/shard_map/ppermute | solution.py:36
  40.0 0.5 collective-permute-start.8
  40.5 1.6 collective-permute-start.11
  42.1 0.5 collective-permute-done.8.refs_5_
  43.5 16.3 %logits.1 = (bf16[2048,512]{1,0:T(8,128)(2,1)}, f32[8,512]{1,0:T(8,128)}, f32[8,512]{1,0:T(8,128)}) custom-call(s32[4]{0:T(128)} %get-tuple-element.34.at, bf16[4,256,256]{2,1,0:T(8,128)(2,1)} %copy-done.5, bf16[4,256,256]{2,1,0:T(8,128)(2,1)} %copy-done.13, bf16[4,256,256]{2,1,0:T(8,128)(2,1)} %copy-done.12, bf16[4,256,256]{2,1,0:T(8,128)(2,1)} %copy-done.11, ...), custom_call_target="tpu_custom_call" | custom-call | flops 1000 | bytes 1000 | tf_op jit(solution)/shard_map/logits/pallas_call | solution.py:134
  59.8 0.6 copy-done.21
  60.5 2.0 %collective-permute-start.20 = (bf16[2048,512]{1,0:T(8,128)(2,1)}, bf16[2048,512]{1,0:T(8,128)(2,1)S(1)}, u32[]{:S(2)}, u32[]{:S(2)}) collective-permute-start(bf16[2048,512]{1,0:T(8,128)(2,1)} %get-tuple-element.37.e), channel_id=1, source_target_pairs={{3,0},{0,1},{1,2},{2,3},{7,4},{4,5},{5,6},{6,7},{11,8},{8,9},{9,10... | collective-permute-start | bytes 6291464 | tf_op jit(solution)/shard_map/ppermute | solution.py:21
  62.5 1.5 collective-permute-start.19
  64.0 3.2 %collective-permute-start.14 = (f32[8,512]{1,0:T(8,128)}, f32[8,512]{1,0:T(8,128)S(1)}, u32[]{:S(2)}, u32[]{:S(2)}) collective-permute-start(f32[8,512]{1,0:T(8,128)} %get-tuple-element.39), channel_id=1, source_target_pairs={{96,0},{0,32},{32,64},{64,96},{97,1},{1,33},{33,65},{65,97},{98,2}... | collective-permute-start | bytes 49160 | tf_op jit(solution)/shard_map/ppermute | solution.py:21
  67.1 4.1 %collective-permute-start.13 = (f32[8,512]{1,0:T(8,128)}, f32[8,512]{1,0:T(8,128)S(1)}, u32[]{:S(2)}, u32[]{:S(2)}) collective-permute-start(f32[8,512]{1,0:T(8,128)} %get-tuple-element.39), channel_id=1, source_target_pairs={{64,0},{96,32},{0,64},{32,96},{65,1},{97,33},{1,65},{33,97},{66,2}... | collective-permute-start | bytes 49160 | tf_op jit(solution)/shard_map/ppermute | solution.py:21
  71.3 1.6 collective-permute-start.12
  73.4 1.9 %collective-permute-done.12 = f32[8,512]{1,0:T(8,128)S(1)} collective-permute-done((f32[8,512]{1,0:T(8,128)}, f32[8,512]{1,0:T(8,128)S(1)}, u32[]{:S(2)}, u32[]{:S(2)}) %collective-permute-start.12) | collective-permute-done | bytes 16416 | tf_op jit(solution)/shard_map/ppermute | solution.py:21
  75.2 0.9 fusion.11
  76.2 1.4 collective-permute-start.17
  77.6 1.7 collective-permute-start.16
  79.3 1.5 collective-permute-start.15
  80.8 0.4 collective-permute-done.17
  81.3 1.6 collective-permute-done.16
  83.3 1.2 collective-permute-done.18.b
  84.4 0.6 copy-done.27
  85.0 1.4 finish.1
  86.5 0.8 collective-permute-start.22
  87.2 2.5 %collective-permute-start.21 = (f32[8,512]{1,0:T(8,128)}, f32[8,512]{1,0:T(8,128)S(1)}, u32[]{:S(2)}, u32[]{:S(2)}) collective-permute-start(f32[8,512]{1,0:T(8,128)} %get-tuple-element.41.pack), channel_id=1, source_target_pairs={{1,0},{2,1},{3,2},{0,3},{5,4},{6,5},{7,6},{4,7},{9,8},{10,9},{11,1... | collective-permute-start | bytes 49160 | tf_op jit(solution)/shard_map/ppermute | solution.py:21
  89.7 16.9 %hidden.1 = (bf16[4,4,256,256]{3,2,1,0:T(8,128)(2,1)}, bf16[2,4,256,256]{3,2,1,0:T(8,128)(2,1)}, bf16[2,4,256,256]{3,2,1,0:T(8,128)(2,1)}, bf16[2048,512]{1,0:T(8,128)(2,1)}) custom-call(s32[4]{0:T(128)} %get-tuple-element.34.at, bf16[2048,512]{1,0:T(8,128)(2,1)} %get-tuple-element.37.e, f32[8,512]{1,0:T(8,128)} %get-tuple-element.41.pack, ...), custom_call_target="tpu_custom_call" | custom-call | flops 1000 | bytes 1000 | tf_op jit(solution)/shard_map/hidden/pallas_call | solution.py:252
  106.6 5.1 %collective-permute-done.23.refs_6_ = f32[8,512]{1,0:T(8,128)S(1)} collective-permute-done((f32[8,512]{1,0:T(8,128)}, f32[8,512]{1,0:T(8,128)S(1)}, u32[]{:S(2)}, u32[]{:S(2)}) %collective-permute-start.23) | collective-permute-done | bytes 16416 | tf_op jit(solution)/shard_map/ppermute | solution.py:21
  111.8 0.5 copy-done.23
  112.3 0.7 copy-done
  113.1 0.7 copy-done.2
  113.8 0.5 collective-permute-start.26
  114.3 2.4 %slice.160 = bf16[1024,512]{1,0:T(8,128)(2,1)} slice(bf16[2048,512]{1,0:T(8,128)(2,1)} %get-tuple-element.48.ep), slice={[0:1024], [0:512]} | slice | bytes 2097152 | tf_op jit(solution)/shard_map/slice | solution.py:388
  116.7 1.1 slice.161
  117.8 1.1 collective-permute-start.30
  118.9 2.1 %collective-permute-start.29 = (bf16[1024,512]{1,0:T(8,128)(2,1)}, bf16[1024,512]{1,0:T(8,128)(2,1)S(1)}, u32[]{:S(2)}, u32[]{:S(2)}) collective-permute-start(bf16[1024,512]{1,0:T(8,128)(2,1)} %slice.160), channel_id=1, source_target_pairs={{1,0},{2,1},{3,2},{0,3},{5,4},{6,5},{7,6},{4,7},{9,8},{10,9},{11,1... | collective-permute-start | bytes 3145736 | tf_op jit(solution)/shard_map/ppermute | solution.py:21
  121.0 1.5 fusion.4
  122.5 4.3 %collective-permute-start.28 = (bf16[4,256,256]{2,1,0:T(8,128)(2,1)}, bf16[4,256,256]{2,1,0:T(8,128)(2,1)S(1)}, u32[]{:S(2)}, u32[]{:S(2)}) collective-permute-start(bf16[4,256,256]{2,1,0:T(8,128)(2,1)} %get-tuple-element.71), channel_id=1, source_target_pairs={{32,0},{12,4},{40,8},{20,12},{48,16},{28,20},{56,24},{4,28},{64,32... | collective-permute-start | bytes 1572872 | tf_op jit(solution)/shard_map/ppermute | solution.py:36
  126.8 0.5 collective-permute-start.27
  127.3 1.4 collective-permute-start.25
  128.7 12.2 %embed_a.1.refs_3_ = f32[2048,1024]{1,0:T(8,128)} custom-call(s32[4]{0:T(128)} %get-tuple-element.34.at, bf16[2048,512]{1,0:T(8,128)(2,1)} %get-tuple-element.47.tgt, bf16[2048,512]{1,0:T(8,128)(2,1)} %get-tuple-element.48.ep, bf16[2048,512]{1,0:T(8,128)(2,1)} %get-tuple-element.49.em, f32[8,512]{1,0:T(8,128)} %get-tuple-element.50.pack_p, ...), custom_call_target="tpu_custom_call" | custom-call | flops 1000 | bytes 1000 | tf_op jit(solution)/shard_map/embed_a/pallas_call | solution.py:316
  141.0 3.3 %collective-permute-done.30.refs_5_ = bf16[1024,512]{1,0:T(8,128)(2,1)S(1)} collective-permute-done((bf16[1024,512]{1,0:T(8,128)(2,1)}, bf16[1024,512]{1,0:T(8,128)(2,1)S(1)}, u32[]{:S(2)}, u32[]{:S(2)}) %collective-permute-start.30) | collective-permute-done | bytes 1048608 | tf_op jit(solution)/shard_map/ppermute | solution.py:21
  144.3 0.9 copy-done.3
  145.9 1.8 %fusion.14 = (bf16[4,256,256]{2,1,0:T(8,128)(2,1)S(1)}, f32[4,256,256]{2,1,0:T(8,128)S(1)}) fusion(bf16[4,256,256]{2,1,0:T(8,128)(2,1)} %get-tuple-element.55, bf16[4,256,256]{2,1,0:T(8,128)(2,1)} %get-tuple-element.54, bf16[4,256,256]{2,1,0:T(8,128)(2,1)} %get-tuple-element.53, bf16[2,4,256,256]{3,2,1,0:T(8,128)(2,1)S(1)} %copy-done.10, ...), kind=kLoop, calls=%fused_computation.48 | loop fusion | flops 2621440 | bytes 4194304 | tf_op jit(solution)/shard_map/convert.2
  147.8 2.1 %collective-permute-start.33 = (bf16[256,256]{1,0:T(8,128)(2,1)S(1)}, bf16[256,256]{1,0:T(8,128)(2,1)S(1)}, u32[]{:S(2)}, u32[]{:S(2)}) collective-permute-start(bf16[256,256]{1,0:T(8,128)(2,1)S(1)} %get-tuple-element.74), channel_id=1, source_target_pairs={{8,0},{36,4},{16,8},{44,12},{24,16},{52,20},{0,24},{60,28},{40,32}... | collective-permute-start | bytes 393224 | tf_op jit(solution)/shard_map/ppermute | solution.py:36
  149.9 1.4 collective-permute-start.32
  151.7 8.6 %embed_b.1.refs_3_ = bf16[2048,1024]{1,0:T(8,128)(2,1)} custom-call(s32[4]{0:T(128)} %get-tuple-element.34.at, f32[2048,1024]{1,0:T(8,128)} %get-tuple-element.56.acc, bf16[1024,512]{1,0:T(8,128)(2,1)} %get-tuple-element.57.low, bf16[1024,512]{1,0:T(8,128)(2,1)} %get-tuple-element.58.high, f32[8,512]{1,0:T(8,128)} %get-tuple-element.59.pack, ...), custom_call_target="tpu_custom_call" | custom-call | flops 1000 | bytes 1000 | tf_op jit(solution)/shard_map/embed_b/pallas_call | solution.py:340
  160.4 0.6 copy-done.18
  161.0 0.7 copy-done.20
  161.7 1.1 fusion.7
  162.8 0.7 collective-permute-start.34
  163.6 1.0 collective-permute-done.34
  164.5 0.7 maximum_select_fusion
  (96 shorter events, 3.2 us)
Async XLA Ops:
  7.2 121.6 %all-gather.3.cloned.1.call-start = ((), (), s32[]{:S(2)}) async-start(), calls=%async_computation | async-start | bytes 4325376 | tf_op jit(solution)/shard_map/all_gather | solution.py:379
  8.1 1.3 collective-permute-start
  9.5 11.2 %collective-permute-start.3 = (bf16[256,256]{1,0:T(8,128)(2,1)S(1)}, bf16[256,256]{1,0:T(8,128)(2,1)S(1)}, u32[]{:S(2)}, u32[]{:S(2)}) collective-permute-start(bf16[256,256]{1,0:T(8,128)(2,1)S(1)} %maximum_select_fusion.1), channel_id=1, source_target_pairs={{64,0},{20,4},{72,8},{28,12},{80,16},{4,20},{88,24},{12,28},{96,32... | collective-permute-start | bytes 393224 | tf_op jit(solution)/shard_map/ppermute | solution.py:36
  12.7 8.0 %collective-permute-start.2 = (bf16[256,256]{1,0:T(8,128)(2,1)S(1)}, bf16[256,256]{1,0:T(8,128)(2,1)S(1)}, u32[]{:S(2)}, u32[]{:S(2)}) collective-permute-start(bf16[256,256]{1,0:T(8,128)(2,1)S(1)} %maximum_select_fusion.1), channel_id=1, source_target_pairs={{32,0},{12,4},{40,8},{20,12},{48,16},{28,20},{56,24},{4,28},{64,32... | collective-permute-start | bytes 393224 | tf_op jit(solution)/shard_map/ppermute | solution.py:36
  13.8 6.2 %collective-permute-start.1 = (bf16[256,256]{1,0:T(8,128)(2,1)S(1)}, bf16[256,256]{1,0:T(8,128)(2,1)S(1)}, u32[]{:S(2)}, u32[]{:S(2)}) collective-permute-start(bf16[256,256]{1,0:T(8,128)(2,1)S(1)} %maximum_select_fusion.1), channel_id=1, source_target_pairs={{96,0},{28,4},{104,8},{4,12},{112,16},{12,20},{120,24},{20,28},{0,... | collective-permute-start | bytes 393224 | tf_op jit(solution)/shard_map/ppermute | solution.py:36
  20.0 0.7 copy-start.22
  21.6 21.0 %copy-start.5 = (bf16[4,256,256]{2,1,0:T(8,128)(2,1)}, bf16[4,256,256]{2,1,0:T(8,128)(2,1)S(1)}, u32[]{:S(2)}) copy-start(bf16[4,256,256]{2,1,0:T(8,128)(2,1)S(1)} %pad_maximum_fusion.refs_0_) | copy-start | bytes 1572868
  21.6 11.3 %collective-permute-start.6 = (bf16[4,256,256]{2,1,0:T(8,128)(2,1)S(1)}, bf16[4,256,256]{2,1,0:T(8,128)(2,1)S(1)}, u32[]{:S(2)}, u32[]{:S(2)}) collective-permute-start(bf16[4,256,256]{2,1,0:T(8,128)(2,1)S(1)} %pad_maximum_fusion.refs_0_), channel_id=1, source_target_pairs={{24,0},{100,4},{0,8},{108,12},{8,16},{116,20},{16,24},{124,28},{56... | collective-permute-start | bytes 1572872 | tf_op jit(solution)/shard_map/ppermute | solution.py:36
  23.6 16.4 %collective-permute-start.5 = (bf16[4,256,256]{2,1,0:T(8,128)(2,1)S(1)}, bf16[4,256,256]{2,1,0:T(8,128)(2,1)S(1)}, u32[]{:S(2)}, u32[]{:S(2)}) collective-permute-start(bf16[4,256,256]{2,1,0:T(8,128)(2,1)S(1)} %pad_maximum_fusion.refs_0_), channel_id=1, source_target_pairs={{16,0},{68,4},{24,8},{76,12},{0,16},{84,20},{8,24},{92,28},{48,32}... | collective-permute-start | bytes 1572872 | tf_op jit(solution)/shard_map/ppermute | solution.py:36
  27.2 12.8 %collective-permute-start.4 = (bf16[4,256,256]{2,1,0:T(8,128)(2,1)S(1)}, bf16[4,256,256]{2,1,0:T(8,128)(2,1)S(1)}, u32[]{:S(2)}, u32[]{:S(2)}) collective-permute-start(bf16[4,256,256]{2,1,0:T(8,128)(2,1)S(1)} %pad_maximum_fusion.refs_0_), channel_id=1, source_target_pairs={{8,0},{36,4},{16,8},{44,12},{24,16},{52,20},{0,24},{60,28},{40,32}... | collective-permute-start | bytes 1572872 | tf_op jit(solution)/shard_map/ppermute | solution.py:36
  28.2 13.8 %collective-permute-start.7 = (bf16[4,256,256]{2,1,0:T(8,128)(2,1)S(1)}, bf16[4,256,256]{2,1,0:T(8,128)(2,1)S(1)}, u32[]{:S(2)}, u32[]{:S(2)}) collective-permute-start(bf16[4,256,256]{2,1,0:T(8,128)(2,1)S(1)} %pad_maximum_fusion.refs_0_), channel_id=1, source_target_pairs={{0,4},{4,0},{1,5},{5,1},{2,6},{6,2},{3,7},{7,3},{8,12},{12,8},{9,1... | collective-permute-start | bytes 1572872 | tf_op jit(solution)/shard_map/ppermute | solution.py:25
  32.9 9.7 %copy-start.11 = (bf16[4,256,256]{2,1,0:T(8,128)(2,1)}, bf16[4,256,256]{2,1,0:T(8,128)(2,1)S(1)}, u32[]{:S(2)}) copy-start(bf16[4,256,256]{2,1,0:T(8,128)(2,1)S(1)} %collective-permute-done.6.refs_3_) | copy-start | bytes 1572868
  32.9 9.2 %collective-permute-start.10 = (bf16[4,256,256]{2,1,0:T(8,128)(2,1)S(1)}, bf16[4,256,256]{2,1,0:T(8,128)(2,1)S(1)}, u32[]{:S(2)}, u32[]{:S(2)}) collective-permute-start(bf16[4,256,256]{2,1,0:T(8,128)(2,1)S(1)} %collective-permute-done.6.refs_3_), channel_id=1, source_target_pairs={{0,4},{4,0},{1,5},{5,1},{2,6},{6,2},{3,7},{7,3},{8,12},{12,8},{9,1... | collective-permute-start | bytes 1572872 | tf_op jit(solution)/shard_map/ppermute | solution.py:25
  40.0 2.7 %copy-start.12 = (bf16[4,256,256]{2,1,0:T(8,128)(2,1)}, bf16[4,256,256]{2,1,0:T(8,128)(2,1)S(1)}, u32[]{:S(2)}) copy-start(bf16[4,256,256]{2,1,0:T(8,128)(2,1)S(1)} %collective-permute-done.5.refs_2_) | copy-start | bytes 1572868
  40.0 2.1 %collective-permute-start.9 = (bf16[4,256,256]{2,1,0:T(8,128)(2,1)S(1)}, bf16[4,256,256]{2,1,0:T(8,128)(2,1)S(1)}, u32[]{:S(2)}, u32[]{:S(2)}) collective-permute-start(bf16[4,256,256]{2,1,0:T(8,128)(2,1)S(1)} %collective-permute-done.5.refs_2_), channel_id=1, source_target_pairs={{0,4},{4,0},{1,5},{5,1},{2,6},{6,2},{3,7},{7,3},{8,12},{12,8},{9,1... | collective-permute-start | bytes 1572872 | tf_op jit(solution)/shard_map/ppermute | solution.py:25
  40.0 2.7 %copy-start.13 = (bf16[4,256,256]{2,1,0:T(8,128)(2,1)}, bf16[4,256,256]{2,1,0:T(8,128)(2,1)S(1)}, u32[]{:S(2)}) copy-start(bf16[4,256,256]{2,1,0:T(8,128)(2,1)S(1)} %collective-permute-done.4.refs_1_) | copy-start | bytes 1572868
  40.0 2.6 %collective-permute-start.8 = (bf16[4,256,256]{2,1,0:T(8,128)(2,1)S(1)}, bf16[4,256,256]{2,1,0:T(8,128)(2,1)S(1)}, u32[]{:S(2)}, u32[]{:S(2)}) collective-permute-start(bf16[4,256,256]{2,1,0:T(8,128)(2,1)S(1)} %collective-permute-done.4.refs_1_), channel_id=1, source_target_pairs={{0,4},{4,0},{1,5},{5,1},{2,6},{6,2},{3,7},{7,3},{8,12},{12,8},{9,1... | collective-permute-start | bytes 1572872 | tf_op jit(solution)/shard_map/ppermute | solution.py:25
  40.5 19.3 %collective-permute-start.11 = (bf16[512,128]{1,0:T(8,128)(2,1)}, bf16[512,128]{1,0:T(8,128)(2,1)S(1)}, u32[]{:S(2)}, u32[]{:S(2)}) collective-permute-start(bf16[512,128]{1,0:T(8,128)(2,1)} %bitcast.52), channel_id=1, source_target_pairs={{0,0},{1,32},{2,64},{3,96},{32,1},{33,33},{34,65},{35,97},{64,2},{... | collective-permute-start | bytes 393224 | tf_op jit(solution)/shard_map/ppermute | solution.py:368
  42.1 0.8 copy-start.14
  42.1 1.0 copy-start.15
  42.1 1.1 copy-start.16
  42.6 0.8 copy-start.17
  59.8 0.7 copy-start.21
  60.5 51.3 %collective-permute-start.20 = (bf16[2048,512]{1,0:T(8,128)(2,1)}, bf16[2048,512]{1,0:T(8,128)(2,1)S(1)}, u32[]{:S(2)}, u32[]{:S(2)}) collective-permute-start(bf16[2048,512]{1,0:T(8,128)(2,1)} %get-tuple-element.37.e), channel_id=1, source_target_pairs={{3,0},{0,1},{1,2},{2,3},{7,4},{4,5},{5,6},{6,7},{11,8},{8,9},{9,10... | collective-permute-start | bytes 6291464 | tf_op jit(solution)/shard_map/ppermute | solution.py:21
  62.5 49.3 %collective-permute-start.19 = (bf16[2048,512]{1,0:T(8,128)(2,1)}, bf16[2048,512]{1,0:T(8,128)(2,1)S(1)}, u32[]{:S(2)}, u32[]{:S(2)}) collective-permute-start(bf16[2048,512]{1,0:T(8,128)(2,1)} %get-tuple-element.37.e), channel_id=1, source_target_pairs={{1,0},{2,1},{3,2},{0,3},{5,4},{6,5},{7,6},{4,7},{9,8},{10,9},{11,1... | collective-permute-start | bytes 6291464 | tf_op jit(solution)/shard_map/ppermute | solution.py:21
  64.0 9.0 %collective-permute-start.14 = (f32[8,512]{1,0:T(8,128)}, f32[8,512]{1,0:T(8,128)S(1)}, u32[]{:S(2)}, u32[]{:S(2)}) collective-permute-start(f32[8,512]{1,0:T(8,128)} %get-tuple-element.39), channel_id=1, source_target_pairs={{96,0},{0,32},{32,64},{64,96},{97,1},{1,33},{33,65},{65,97},{98,2}... | collective-permute-start | bytes 49160 | tf_op jit(solution)/shard_map/ppermute | solution.py:21
  67.1 6.2 %collective-permute-start.13 = (f32[8,512]{1,0:T(8,128)}, f32[8,512]{1,0:T(8,128)S(1)}, u32[]{:S(2)}, u32[]{:S(2)}) collective-permute-start(f32[8,512]{1,0:T(8,128)} %get-tuple-element.39), channel_id=1, source_target_pairs={{64,0},{96,32},{0,64},{32,96},{65,1},{97,33},{1,65},{33,97},{66,2}... | collective-permute-start | bytes 49160 | tf_op jit(solution)/shard_map/ppermute | solution.py:21
  71.3 4.0 %collective-permute-start.12 = (f32[8,512]{1,0:T(8,128)}, f32[8,512]{1,0:T(8,128)S(1)}, u32[]{:S(2)}, u32[]{:S(2)}) collective-permute-start(f32[8,512]{1,0:T(8,128)} %get-tuple-element.39), channel_id=1, source_target_pairs={{32,0},{64,32},{96,64},{0,96},{33,1},{65,33},{97,65},{1,97},{34,2}... | collective-permute-start | bytes 49160 | tf_op jit(solution)/shard_map/ppermute | solution.py:21
  76.2 5.1 %collective-permute-start.17 = (f32[8,512]{1,0:T(8,128)S(1)}, f32[8,512]{1,0:T(8,128)S(1)}, u32[]{:S(2)}, u32[]{:S(2)}) collective-permute-start(f32[8,512]{1,0:T(8,128)S(1)} %maximum_maximum_fusion), channel_id=1, source_target_pairs={{24,0},{0,8},{8,16},{16,24},{25,1},{1,9},{9,17},{17,25},{26,2},{2,... | collective-permute-start | bytes 49160 | tf_op jit(solution)/shard_map/ppermute | solution.py:21
  77.6 5.3 %collective-permute-start.16 = (f32[8,512]{1,0:T(8,128)S(1)}, f32[8,512]{1,0:T(8,128)S(1)}, u32[]{:S(2)}, u32[]{:S(2)}) collective-permute-start(f32[8,512]{1,0:T(8,128)S(1)} %maximum_maximum_fusion), channel_id=1, source_target_pairs={{16,0},{24,8},{0,16},{8,24},{17,1},{25,9},{1,17},{9,25},{18,2},{26... | collective-permute-start | bytes 49160 | tf_op jit(solution)/shard_map/ppermute | solution.py:21
  79.3 3.8 %collective-permute-start.15 = (f32[8,512]{1,0:T(8,128)S(1)}, f32[8,512]{1,0:T(8,128)S(1)}, u32[]{:S(2)}, u32[]{:S(2)}) collective-permute-start(f32[8,512]{1,0:T(8,128)S(1)} %maximum_maximum_fusion), channel_id=1, source_target_pairs={{8,0},{16,8},{24,16},{0,24},{9,1},{17,9},{25,17},{1,25},{10,2},{18... | collective-permute-start | bytes 49160 | tf_op jit(solution)/shard_map/ppermute | solution.py:21
  83.2 1.2 copy-start.26
  83.2 1.2 collective-permute-start.18
  84.4 0.6 copy-start.27
  86.5 25.2 %collective-permute-start.23 = (f32[8,512]{1,0:T(8,128)}, f32[8,512]{1,0:T(8,128)S(1)}, u32[]{:S(2)}, u32[]{:S(2)}) collective-permute-start(f32[8,512]{1,0:T(8,128)} %get-tuple-element.41.pack), channel_id=1, source_target_pairs={{2,0},{3,1},{0,2},{1,3},{6,4},{7,5},{4,6},{5,7},{10,8},{11,9},{8,1... | collective-permute-start | bytes 49160 | tf_op jit(solution)/shard_map/ppermute | solution.py:21
  86.5 25.2 %collective-permute-start.22 = (f32[8,512]{1,0:T(8,128)}, f32[8,512]{1,0:T(8,128)S(1)}, u32[]{:S(2)}, u32[]{:S(2)}) collective-permute-start(f32[8,512]{1,0:T(8,128)} %get-tuple-element.41.pack), channel_id=1, source_target_pairs={{3,0},{0,1},{1,2},{2,3},{7,4},{4,5},{5,6},{6,7},{11,8},{8,9},{9,10... | collective-permute-start | bytes 49160 | tf_op jit(solution)/shard_map/ppermute | solution.py:21
  87.2 24.5 %collective-permute-start.21 = (f32[8,512]{1,0:T(8,128)}, f32[8,512]{1,0:T(8,128)S(1)}, u32[]{:S(2)}, u32[]{:S(2)}) collective-permute-start(f32[8,512]{1,0:T(8,128)} %get-tuple-element.41.pack), channel_id=1, source_target_pairs={{1,0},{2,1},{3,2},{0,3},{5,4},{6,5},{7,6},{4,7},{9,8},{10,9},{11,1... | collective-permute-start | bytes 49160 | tf_op jit(solution)/shard_map/ppermute | solution.py:21
  111.7 0.6 copy-start.23
  111.7 0.6 copy-start.24
  111.7 0.6 copy-start.25
  111.7 1.3 copy-start
  111.8 2.0 %copy-start.2 = (bf16[2048,512]{1,0:T(8,128)(2,1)}, bf16[2048,512]{1,0:T(8,128)(2,1)S(1)}, u32[]{:S(2)}) copy-start(bf16[2048,512]{1,0:T(8,128)(2,1)S(1)} %collective-permute-done.19.refs_2_) | copy-start | bytes 6291460
  113.7 2.9 %copy-start.1 = (bf16[2048,512]{1,0:T(8,128)(2,1)S(1)}, bf16[2048,512]{1,0:T(8,128)(2,1)}, u32[]{:S(2)}) copy-start(bf16[2048,512]{1,0:T(8,128)(2,1)} %get-tuple-element.49.em) | copy-start | bytes 6291460
  113.8 7.3 %collective-permute-start.24 = (bf16[2,4,256,256]{3,2,1,0:T(8,128)(2,1)}, bf16[2,4,256,256]{3,2,1,0:T(8,128)(2,1)S(1)}, u32[]{:S(2)}, u32[]{:S(2)}) collective-permute-start(bf16[2,4,256,256]{3,2,1,0:T(8,128)(2,1)} %get-tuple-element.45), channel_id=1, source_target_pairs={{0,4},{4,0},{1,5},{5,1},{2,6},{6,2},{3,7},{7,3},{8,12},{12,8},{9,1... | collective-permute-start | bytes 3145736 | tf_op jit(solution)/shard_map/ppermute | solution.py:25
  113.8 7.3 %collective-permute-start.26 = (bf16[2,4,256,256]{3,2,1,0:T(8,128)(2,1)}, bf16[2,4,256,256]{3,2,1,0:T(8,128)(2,1)S(1)}, u32[]{:S(2)}, u32[]{:S(2)}) collective-permute-start(bf16[2,4,256,256]{3,2,1,0:T(8,128)(2,1)} %get-tuple-element.46), channel_id=1, source_target_pairs={{0,4},{4,0},{1,5},{5,1},{2,6},{6,2},{3,7},{7,3},{8,12},{12,8},{9,1... | collective-permute-start | bytes 3145736 | tf_op jit(solution)/shard_map/ppermute | solution.py:25
  114.3 6.8 %copy-start.6 = (bf16[4,4,256,256]{3,2,1,0:T(8,128)(2,1)S(1)}, bf16[4,4,256,256]{3,2,1,0:T(8,128)(2,1)}, u32[]{:S(2)}) copy-start(bf16[4,4,256,256]{3,2,1,0:T(8,128)(2,1)} %get-tuple-element.42) | copy-start | bytes 6291460
  117.8 26.5 %collective-permute-start.30 = (bf16[1024,512]{1,0:T(8,128)(2,1)}, bf16[1024,512]{1,0:T(8,128)(2,1)S(1)}, u32[]{:S(2)}, u32[]{:S(2)}) collective-permute-start(bf16[1024,512]{1,0:T(8,128)(2,1)} %slice.161), channel_id=1, source_target_pairs={{3,0},{0,1},{1,2},{2,3},{7,4},{4,5},{5,6},{6,7},{11,8},{8,9},{9,10... | collective-permute-start | bytes 3145736 | tf_op jit(solution)/shard_map/ppermute | solution.py:21
  118.9 25.4 %collective-permute-start.29 = (bf16[1024,512]{1,0:T(8,128)(2,1)}, bf16[1024,512]{1,0:T(8,128)(2,1)S(1)}, u32[]{:S(2)}, u32[]{:S(2)}) collective-permute-start(bf16[1024,512]{1,0:T(8,128)(2,1)} %slice.160), channel_id=1, source_target_pairs={{1,0},{2,1},{3,2},{0,3},{5,4},{6,5},{7,6},{4,7},{9,8},{10,9},{11,1... | collective-permute-start | bytes 3145736 | tf_op jit(solution)/shard_map/ppermute | solution.py:21
  121.0 1.5 copy-start.9
  122.5 21.7 %collective-permute-start.28 = (bf16[4,256,256]{2,1,0:T(8,128)(2,1)}, bf16[4,256,256]{2,1,0:T(8,128)(2,1)S(1)}, u32[]{:S(2)}, u32[]{:S(2)}) collective-permute-start(bf16[4,256,256]{2,1,0:T(8,128)(2,1)} %get-tuple-element.71), channel_id=1, source_target_pairs={{32,0},{12,4},{40,8},{20,12},{48,16},{28,20},{56,24},{4,28},{64,32... | collective-permute-start | bytes 1572872 | tf_op jit(solution)/shard_map/ppermute | solution.py:36
  126.8 17.4 %collective-permute-start.27 = (bf16[4,256,256]{2,1,0:T(8,128)(2,1)}, bf16[4,256,256]{2,1,0:T(8,128)(2,1)S(1)}, u32[]{:S(2)}, u32[]{:S(2)}) collective-permute-start(bf16[4,256,256]{2,1,0:T(8,128)(2,1)} %get-tuple-element.72), channel_id=1, source_target_pairs={{64,0},{20,4},{72,8},{28,12},{80,16},{4,20},{88,24},{12,28},{96,32... | collective-permute-start | bytes 1572872 | tf_op jit(solution)/shard_map/ppermute | solution.py:36
  127.3 17.0 %collective-permute-start.25 = (bf16[4,256,256]{2,1,0:T(8,128)(2,1)}, bf16[4,256,256]{2,1,0:T(8,128)(2,1)}, u32[]{:S(2)}, u32[]{:S(2)}) collective-permute-start(bf16[4,256,256]{2,1,0:T(8,128)(2,1)} %get-tuple-element.73), channel_id=1, source_target_pairs={{96,0},{28,4},{104,8},{4,12},{112,16},{12,20},{120,24},{20,28},{0,... | collective-permute-start | bytes 1572872 | tf_op jit(solution)/shard_map/ppermute | solution.py:36
  141.0 4.9 %copy-start.10 = (bf16[2,4,256,256]{3,2,1,0:T(8,128)(2,1)S(1)}, bf16[2,4,256,256]{3,2,1,0:T(8,128)(2,1)}, u32[]{:S(2)}) copy-start(bf16[2,4,256,256]{3,2,1,0:T(8,128)(2,1)} %copy-done.9) | copy-start | bytes 3145732
  144.3 1.0 copy-start.3
  144.3 1.3 copy-start.4
  144.3 1.5 copy-start.7
  144.3 1.6 copy-start.8
  147.8 12.5 %collective-permute-start.33 = (bf16[256,256]{1,0:T(8,128)(2,1)S(1)}, bf16[256,256]{1,0:T(8,128)(2,1)S(1)}, u32[]{:S(2)}, u32[]{:S(2)}) collective-permute-start(bf16[256,256]{1,0:T(8,128)(2,1)S(1)} %get-tuple-element.74), channel_id=1, source_target_pairs={{8,0},{36,4},{16,8},{44,12},{24,16},{52,20},{0,24},{60,28},{40,32}... | collective-permute-start | bytes 393224 | tf_op jit(solution)/shard_map/ppermute | solution.py:36
  149.9 10.4 %collective-permute-start.32 = (bf16[256,256]{1,0:T(8,128)(2,1)S(1)}, bf16[256,256]{1,0:T(8,128)(2,1)S(1)}, u32[]{:S(2)}, u32[]{:S(2)}) collective-permute-start(bf16[256,256]{1,0:T(8,128)(2,1)S(1)} %get-tuple-element.75), channel_id=1, source_target_pairs={{16,0},{68,4},{24,8},{76,12},{0,16},{84,20},{8,24},{92,28},{48,32}... | collective-permute-start | bytes 393224 | tf_op jit(solution)/shard_map/ppermute | solution.py:36
  151.4 9.0 %collective-permute-start.31 = (bf16[256,256]{1,0:T(8,128)(2,1)S(1)}, bf16[256,256]{1,0:T(8,128)(2,1)S(1)}, u32[]{:S(2)}, u32[]{:S(2)}) collective-permute-start(bf16[256,256]{1,0:T(8,128)(2,1)S(1)} %get-tuple-element.76), channel_id=1, source_target_pairs={{24,0},{100,4},{0,8},{108,12},{8,16},{116,20},{16,24},{124,28},{56... | collective-permute-start | bytes 393224 | tf_op jit(solution)/shard_map/ppermute | solution.py:36
  160.3 0.7 copy-start.18
  160.3 0.7 copy-start.19
  161.0 0.7 copy-start.20
  162.8 1.7 %collective-permute-start.34 = (f32[256,128]{1,0:T(8,128)S(1)}, f32[256,128]{1,0:T(8,128)S(1)}, u32[]{:S(2)}, u32[]{:S(2)}) collective-permute-start(f32[256,128]{1,0:T(8,128)S(1)} %get-tuple-element.78), channel_id=1, source_target_pairs={{0,4},{4,0},{1,5},{5,1},{2,6},{6,2},{3,7},{7,3},{8,12},{12,8},{9,1... | collective-permute-start | bytes 393224 | tf_op jit(solution)/shard_map/ppermute | solution.py:25
Sparse Core Ops, SparseCore 0:
  60.6 47.5 all-gather.2

commit v10 on v9

--- a/solution.py
+++ b/solution.py
@@ -72,6 +72,37 @@
 
 SUB = 256
 CUT = VOC // 2
+
+
+def onward_body(*refs):
+    low, high, sem = refs[-3:]
+    ep, em = refs[0], refs[1]
+    copies = []
+    for k in range(4):
+        rows = pl.ds(k * SUB, SUB)
+        copies.append(pltpu.make_async_copy(ep.at[rows], low.at[rows], sem.at[2 * k]))
+        copies.append(pltpu.make_async_copy(em.at[pl.ds(CUT + k * SUB, SUB)], high.at[rows], sem.at[2 * k + 1]))
+    for copy in copies:
+        copy.start()
+    for copy in copies:
+        copy.wait()
+
+
+def onward(ep, em, *others):
+    arrays = (ep, em, *others)
+    n = len(arrays)
+    half = jax.ShapeDtypeStruct((CUT, ROWS), BF)
+    return pl.pallas_call(
+        onward_body,
+        in_specs=[HBM] * n,
+        out_specs=[HBM] * (n + 2),
+        out_shape=[jax.ShapeDtypeStruct(a.shape, a.dtype) for a in arrays] + [half, half],
+        input_output_aliases={i: i for i in range(n)},
+        scratch_shapes=[pltpu.SemaphoreType.DMA((8,))],
+        compiler_params=params(),
+        cost_estimate=SMALL,
+        name="onward",
+    )(*arrays)
 
 
 def gather_pieces(block, *early):
@@ -307,7 +338,7 @@
     for e, pack in ((ep, pack_p), (em, pack_m)):
         parts.append(token_grad(e[...], pack, pack[pl.ds(i, 1), :], i * TILE))
     q = jnp.concatenate([columns(f) for f in (f0, f1, f3)], axis=0)
-    acc[...] = dot_nn(jnp.concatenate(parts, axis=1), q)
+    acc[...] = dot_nn(jnp.concatenate(parts, axis=1), q).astype(BF)
 
 
 def embed_a_call(at, tgt, ep, em, packs, feats):
@@ -321,7 +352,7 @@
             in_specs=[tile, tile, tile, pack, pack] + [feature_spec(d) for d in (0, 1, 3)],
             out_specs=pl.BlockSpec((TILE, 1024), lambda i, at: (i, 0)),
         ),
-        out_shape=jax.ShapeDtypeStruct((VOC, 1024), F32),
+        out_shape=jax.ShapeDtypeStruct((VOC, 1024), BF),
         compiler_params=params(),
         cost_estimate=SMALL,
         name="embed_a",
@@ -332,7 +363,7 @@
     i = pl.program_id(0)
     e = jnp.where(i < CUT // TILE, low[...], high[...])
     g = token_grad(e, pack, pack[pl.ds(i, 1), :], i * TILE)
-    out[...] = (acc[...] + dot_nn(g, columns(f2))).astype(BF)
+    out[...] = (acc[...].astype(F32) + dot_nn(g, columns(f2))).astype(BF)
 
 
 def embed_b_call(at, acc, low, high, pack, feats):
@@ -384,8 +415,8 @@
     pack, grad_mix = finish_call(s, sibling(s), st, tid, mix, weight.reshape(1, 128))
     packs = [shift(pack, "y", d) for d in (1, 3, 2)]
     keep, send0, send1, tgt = hidden_call(at, e, pack, embed)
-    send0, send1, ep, em, *packs = gate(send0, send1, ep, em, *packs)
-    low, high = shift(ep[:CUT], "y", 1), shift(em[CUT:], "y", 3)
+    ep, em, send0, send1, *packs, low, high = onward(ep, em, send0, send1, *packs)
+    low, high = shift(low, "y", 1), shift(high, "y", 3)
     recv = sibling(send0), sibling(send1)
 
     grad_hidden, grad_embed = scatter(

time: 174 us -> 236 us (1.36)
  Pallas kernels: 55.5 us -> 119 us
  waiting for transfers between devices: 32.6 us -> 39.6 us
  starting transfers between devices: 48.9 us -> 43.3 us
  local copies, waits for them, and re-layouts: 11.3 us -> 7.62 us
    pallas_call x0 -> x1, Pallas kernels: none -> 64.7 us  [onward(): pl.pallas_call(onward_body, in_specs=[HBM] * n, out_specs=[HBM] * (n + 2)...]
    ppermute x13, waiting for transfers between devices: 12.9 us -> 19.7 us  [shift(): return lax.ppermute(a, axis, [((i + d) % 4, i) for i in range(4)])]
    slice x2 -> x0, local copies, waits for them, and re-layouts: 3.5 us -> none  [local(): low, high = (shift(ep[:CUT], 'y', 1), shift(em[CUT:], 'y', 3))]
    ppermute x13, starting transfers between devices: 23.5 us -> 20.2 us  [shift(): return lax.ppermute(a, axis, [((i + d) % 4, i) for i in range(4)])]
    unnamed x56 -> x52, local copies, waits for them, and re-layouts: 7.08 us -> 6.92 us
  transfers between devices with their start and end apart: 36 -> 36, of which waited for: 14 -> 20; matrix products, arithmetic and copies ran while one was open for 5% -> 2% of each run, Pallas kernels for 32% -> 51%
where the time goes in v10:
time: 236 us; the launch traced here: 234 us
  Pallas kernels  119 us (50%)
  starting transfers between devices  43.3 us (18%)
  waiting for transfers between devices  39.6 us (17%)
  between operations  14.4 us (6%)
  other arithmetic  10.7 us (5%)
  local copies, waits for them, and re-layouts  7.62 us (3%)
    pallas_call x1, Pallas kernels, onward(): pl.pallas_call(onward_body, in_specs=[HBM] * n, out_specs=[HBM] * (n + 2)...  64.7 us
    ppermute x12, starting transfers between devices, cross(): return lax.ppermute(a, ('x', 'z', 'c'), pairs)  20.7 us
    ppermute x13, starting transfers between devices, shift(): return lax.ppermute(a, axis, [((i + d) % 4, i) for i in range(4)])  20.2 us
    ppermute x13, waiting for transfers between devices, shift(): return lax.ppermute(a, axis, [((i + d) % 4, i) for i in range(4)])  19.7 us
    pallas_call x1, Pallas kernels, hidden_call(): pl.pallas_call(hidden_body, grid_spec=pltpu.PrefetchScalarGridSpec(num_sc...  16.7 us
    pallas_call x1, Pallas kernels, logits_call(): pl.pallas_call(logits_body, grid_spec=pltpu.PrefetchScalarGridSpec(num_sc...  16.3 us
    ppermute x12, waiting for transfers between devices, cross(): return lax.ppermute(a, ('x', 'z', 'c'), pairs)  14.6 us
    pallas_call x1, Pallas kernels, embed_a_call(): pl.pallas_call(embed_a_body, grid_spec=pltpu.PrefetchScalarGridSpec(num_s...  11.6 us
  transfers between devices with their start and end apart: 36, of which 20 were waited for; matrix products, arithmetic and copies ran while one was open for 2% of the time, Pallas kernels for 51%

profile of v10, /device:TPU:0, one launch (start us, length us, event | category | flops | bytes accessed | tf_op | source)
XLA Modules:
  0.0 234.1 jit_solution(14615824255867070143)
XLA Ops:
  7.2 0.9 broadcast_select_fusion.1
  8.2 0.7 broadcast_subtract_fusion
  8.9 0.6 collective-permute-done
  9.5 1.6 collective-permute-start.1
  11.1 2.7 %collective-permute-start.3 = (bf16[256,256]{1,0:T(8,128)(2,1)S(1)}, bf16[256,256]{1,0:T(8,128)(2,1)S(1)}, u32[]{:S(2)}, u32[]{:S(2)}) collective-permute-start(bf16[256,256]{1,0:T(8,128)(2,1)S(1)} %maximum_select_fusion.1), channel_id=1, source_target_pairs={{64,0},{20,4},{72,8},{28,12},{80,16},{4,20},{88,24},{12,28},{96,32... | collective-permute-start | bytes 393224 | tf_op jit(solution)/shard_map/ppermute | solution.py:36
  13.9 1.4 collective-permute-start.2
  15.3 0.6 pad_add_fusion.refs_1_
  15.9 0.6 tile.2
  16.6 1.6 collective-permute-done.3
  18.2 0.6 collective-permute-done.2
  18.8 1.0 pad_maximum_fusion.refs_0_
  19.8 2.0 collective-permute-start.6
  21.8 2.2 collective-permute-start.4
  24.0 1.8 collective-permute-start.5
  25.8 5.3 %collective-permute-done.6.refs_3_ = bf16[4,256,256]{2,1,0:T(8,128)(2,1)S(1)} collective-permute-done((bf16[4,256,256]{2,1,0:T(8,128)(2,1)S(1)}, bf16[4,256,256]{2,1,0:T(8,128)(2,1)S(1)}, u32[]{:S(2)}, u32[]{:S(2)}) %collective-permute-start.6) | collective-permute-done | bytes 524320 | tf_op jit(solution)/shard_map/ppermute | solution.py:36
  31.1 5.3 %collective-permute-done.4.refs_1_ = bf16[4,256,256]{2,1,0:T(8,128)(2,1)S(1)} collective-permute-done((bf16[4,256,256]{2,1,0:T(8,128)(2,1)S(1)}, bf16[4,256,256]{2,1,0:T(8,128)(2,1)S(1)}, u32[]{:S(2)}, u32[]{:S(2)}) %collective-permute-start.4) | collective-permute-done | bytes 524320 | tf_op jit(solution)/shard_map/ppermute | solution.py:36
  36.4 1.8 collective-permute-done.5.refs_2_
  38.2 1.6 collective-permute-start.11
  40.1 0.4 copy-done.12
  41.1 16.3 %logits.1 = (bf16[2048,512]{1,0:T(8,128)(2,1)}, f32[8,512]{1,0:T(8,128)}, f32[8,512]{1,0:T(8,128)}) custom-call(s32[4]{0:T(128)} %get-tuple-element.36.at, bf16[4,256,256]{2,1,0:T(8,128)(2,1)} %copy-done.4, bf16[4,256,256]{2,1,0:T(8,128)(2,1)} %copy-done.10, bf16[4,256,256]{2,1,0:T(8,128)(2,1)} %copy-done.11, bf16[4,256,256]{2,1,0:T(8,128)(2,1)} %copy-done.9, ...), custom_call_target="tpu_custom_call" | custom-call | flops 1000 | bytes 1000 | tf_op jit(solution)/shard_map/logits/pallas_call | solution.py:165
  57.4 0.6 copy-done.19
  58.1 5.7 %collective-permute-start.19 = (bf16[2048,512]{1,0:T(8,128)(2,1)}, bf16[2048,512]{1,0:T(8,128)(2,1)S(1)}, u32[]{:S(2)}, u32[]{:S(2)}) collective-permute-start(bf16[2048,512]{1,0:T(8,128)(2,1)} %get-tuple-element.39.e), channel_id=1, source_target_pairs={{1,0},{2,1},{3,2},{0,3},{5,4},{6,5},{7,6},{4,7},{9,8},{10,9},{11,1... | collective-permute-start | bytes 6291464 | tf_op jit(solution)/shard_map/ppermute | solution.py:21
  63.9 2.4 %collective-permute-start.12 = (f32[8,512]{1,0:T(8,128)}, f32[8,512]{1,0:T(8,128)S(1)}, u32[]{:S(2)}, u32[]{:S(2)}) collective-permute-start(f32[8,512]{1,0:T(8,128)} %get-tuple-element.41), channel_id=1, source_target_pairs={{32,0},{64,32},{96,64},{0,96},{33,1},{65,33},{97,65},{1,97},{34,2}... | collective-permute-start | bytes 49160 | tf_op jit(solution)/shard_map/ppermute | solution.py:21
  66.2 1.5 collective-permute-start.13
  68.2 3.5 %collective-permute-done.13 = f32[8,512]{1,0:T(8,128)S(1)} collective-permute-done((f32[8,512]{1,0:T(8,128)}, f32[8,512]{1,0:T(8,128)S(1)}, u32[]{:S(2)}, u32[]{:S(2)}) %collective-permute-start.13) | collective-permute-done | bytes 16416 | tf_op jit(solution)/shard_map/ppermute | solution.py:21
  71.7 1.3 collective-permute-done.14
  73.0 0.9 fusion.11
  73.9 2.4 %collective-permute-start.15 = (f32[8,512]{1,0:T(8,128)S(1)}, f32[8,512]{1,0:T(8,128)S(1)}, u32[]{:S(2)}, u32[]{:S(2)}) collective-permute-start(f32[8,512]{1,0:T(8,128)S(1)} %maximum_maximum_fusion), channel_id=1, source_target_pairs={{8,0},{16,8},{24,16},{0,24},{9,1},{17,9},{25,17},{1,25},{10,2},{18... | collective-permute-start | bytes 49160 | tf_op jit(solution)/shard_map/ppermute | solution.py:21
  76.3 1.1 collective-permute-start.16
  77.7 3.8 %collective-permute-done.16 = f32[8,512]{1,0:T(8,128)S(1)} collective-permute-done((f32[8,512]{1,0:T(8,128)S(1)}, f32[8,512]{1,0:T(8,128)S(1)}, u32[]{:S(2)}, u32[]{:S(2)}) %collective-permute-start.16) | collective-permute-done | bytes 16416 | tf_op jit(solution)/shard_map/ppermute | solution.py:21
  81.6 0.9 collective-permute-done.17
  82.6 1.2 collective-permute-done.18.b
  83.8 0.6 copy-done.25
  84.4 1.4 finish.1
  85.8 3.2 %collective-permute-start.21 = (f32[8,512]{1,0:T(8,128)}, f32[8,512]{1,0:T(8,128)S(1)}, u32[]{:S(2)}, u32[]{:S(2)}) collective-permute-start(f32[8,512]{1,0:T(8,128)} %get-tuple-element.43.pack), channel_id=1, source_target_pairs={{1,0},{2,1},{3,2},{0,3},{5,4},{6,5},{7,6},{4,7},{9,8},{10,9},{11,1... | collective-permute-start | bytes 49160 | tf_op jit(solution)/shard_map/ppermute | solution.py:21
  89.0 1.5 collective-permute-start.23
  90.5 16.7 %hidden.1 = (bf16[4,4,256,256]{3,2,1,0:T(8,128)(2,1)}, bf16[2,4,256,256]{3,2,1,0:T(8,128)(2,1)}, bf16[2,4,256,256]{3,2,1,0:T(8,128)(2,1)}, bf16[2048,512]{1,0:T(8,128)(2,1)}) custom-call(s32[4]{0:T(128)} %get-tuple-element.36.at, bf16[2048,512]{1,0:T(8,128)(2,1)} %get-tuple-element.39.e, f32[8,512]{1,0:T(8,128)} %get-tuple-element.43.pack, ...), custom_call_target="tpu_custom_call" | custom-call | flops 1000 | bytes 1000 | tf_op jit(solution)/shard_map/hidden/pallas_call | solution.py:283
  107.2 2.8 %collective-permute-done.21.refs_4_ = f32[8,512]{1,0:T(8,128)S(1)} collective-permute-done((f32[8,512]{1,0:T(8,128)}, f32[8,512]{1,0:T(8,128)S(1)}, u32[]{:S(2)}, u32[]{:S(2)}) %collective-permute-start.21) | collective-permute-done | bytes 16416 | tf_op jit(solution)/shard_map/ppermute | solution.py:21
  110.1 3.4 %collective-permute-done.22.refs_5_ = f32[8,512]{1,0:T(8,128)S(1)} collective-permute-done((f32[8,512]{1,0:T(8,128)}, f32[8,512]{1,0:T(8,128)S(1)}, u32[]{:S(2)}, u32[]{:S(2)}) %collective-permute-start.22) | collective-permute-done | bytes 16416 | tf_op jit(solution)/shard_map/ppermute | solution.py:21
  113.5 0.5 copy-done.22
  114.1 0.7 copy-done
  114.8 0.7 copy-done.1
  115.5 64.7 %onward.1 = (bf16[2048,512]{1,0:T(8,128)(2,1)}, bf16[2048,512]{1,0:T(8,128)(2,1)}, bf16[2,4,256,256]{3,2,1,0:T(8,128)(2,1)}, bf16[2,4,256,256]{3,2,1,0:T(8,128)(...) custom-call(bf16[2048,512]{1,0:T(8,128)(2,1)} %copy-done, ...), custom_call_target="tpu_custom_call", output_to_operand_aliasing={{0}: (0, {}), {1}: (1, {}), {2}: (2, {}), {3}: (3, {}), {4}... | custom-call | flops 1000 | bytes 1000 | tf_op jit(solution)/shard_map/onward/pallas_call | solution.py:95
  180.3 0.5 collective-permute-start.26
  181.1 1.7 collective-permute-start.30
  183.1 1.5 collective-permute-done.26
  184.6 2.8 %fusion.4 = (bf16[4,256,256]{2,1,0:T(8,128)(2,1)}, bf16[4,256,256]{2,1,0:T(8,128)(2,1)}, bf16[4,256,256]{2,1,0:T(8,128)(2,1)}) fusion(bf16[2,4,256,256]{3,2,1,0:T(8,128)(2,1)S(1)} %collective-permute-done.26, bf16[4,4,256,256]{3,2,1,0:T(8,128)(2,1)} %get-tuple-element.44, bf16[2,4,256,256]{3,2,1,0:T(8,128)(2,1)S(1)} %collective-permute-done.24), kind=kLoop, calls=%fused_computation.8 | loop fusion | flops 3145728 | bytes 4718592 | tf_op jit(solution)/shard_map/convert_element_type | solution.py:315
  187.4 1.9 collective-permute-start.25
  189.3 0.7 collective-permute-start.27
  190.0 2.1 collective-permute-start.28
  192.1 11.6 %embed_a.1.refs_3_ = bf16[2048,1024]{1,0:T(8,128)(2,1)} custom-call(s32[4]{0:T(128)} %get-tuple-element.36.at, bf16[2048,512]{1,0:T(8,128)(2,1)} %get-tuple-element.49.tgt, bf16[2048,512]{1,0:T(8,128)(2,1)} %get-tuple-element.50.ep, bf16[2048,512]{1,0:T(8,128)(2,1)} %get-tuple-element.51.em, f32[8,512]{1,0:T(8,128)} %get-tuple-element.52.pack_p, ...), custom_call_target="tpu_custom_call" | custom-call | flops 1000 | bytes 1000 | tf_op jit(solution)/shard_map/embed_a/pallas_call | solution.py:347
  203.7 2.5 %collective-permute-done.29.refs_4_ = bf16[1024,512]{1,0:T(8,128)(2,1)S(1)} collective-permute-done((bf16[1024,512]{1,0:T(8,128)(2,1)}, bf16[1024,512]{1,0:T(8,128)(2,1)S(1)}, u32[]{:S(2)}, u32[]{:S(2)}) %collective-permute-start.29) | collective-permute-done | bytes 1048608 | tf_op jit(solution)/shard_map/ppermute | solution.py:21
  206.2 1.2 collective-permute-done.30.refs_5_
  207.4 1.0 copy-done.3
  208.7 1.8 fusion.14
  210.6 1.5 collective-permute-start.31
  212.1 2.0 collective-permute-start.32
  214.1 0.8 collective-permute-start.33
  214.9 7.7 %embed_b.1.refs_3_ = bf16[2048,1024]{1,0:T(8,128)(2,1)} custom-call(s32[4]{0:T(128)} %get-tuple-element.36.at, bf16[2048,1024]{1,0:T(8,128)(2,1)} %get-tuple-element.60.acc, bf16[1024,512]{1,0:T(8,128)(2,1)} %get-tuple-element.61.low, bf16[1024,512]{1,0:T(8,128)(2,1)} %get-tuple-element.62.high, f32[8,512]{1,0:T(8,128)} %get-tuple-element.63.pack, ...), custom_call_target="tpu_custom_call" | custom-call | flops 1000 | bytes 1000 | tf_op jit(solution)/shard_map/embed_b/pallas_call | solution.py:371
  222.6 0.6 copy-done.16
  223.3 0.7 copy-done.18
  223.9 1.1 fusion.7
  225.2 1.3 collective-permute-done.34
  226.5 0.7 maximum_select_fusion
  (90 shorter events, 3.4 us)
Async XLA Ops:
  7.2 184.9 %all-gather.3.cloned.1.call-start = ((), (), s32[]{:S(2)}) async-start(), calls=%async_computation | async-start | bytes 4325376 | tf_op jit(solution)/shard_map/all_gather | solution.py:410
  8.1 1.3 collective-permute-start
  9.5 6.4 %collective-permute-start.1 = (bf16[256,256]{1,0:T(8,128)(2,1)S(1)}, bf16[256,256]{1,0:T(8,128)(2,1)S(1)}, u32[]{:S(2)}, u32[]{:S(2)}) collective-permute-start(bf16[256,256]{1,0:T(8,128)(2,1)S(1)} %maximum_select_fusion.1), channel_id=1, source_target_pairs={{96,0},{28,4},{104,8},{4,12},{112,16},{12,20},{120,24},{20,28},{0,... | collective-permute-start | bytes 393224 | tf_op jit(solution)/shard_map/ppermute | solution.py:36
  11.1 7.1 %collective-permute-start.3 = (bf16[256,256]{1,0:T(8,128)(2,1)S(1)}, bf16[256,256]{1,0:T(8,128)(2,1)S(1)}, u32[]{:S(2)}, u32[]{:S(2)}) collective-permute-start(bf16[256,256]{1,0:T(8,128)(2,1)S(1)} %maximum_select_fusion.1), channel_id=1, source_target_pairs={{64,0},{20,4},{72,8},{28,12},{80,16},{4,20},{88,24},{12,28},{96,32... | collective-permute-start | bytes 393224 | tf_op jit(solution)/shard_map/ppermute | solution.py:36
  13.9 5.0 %collective-permute-start.2 = (bf16[256,256]{1,0:T(8,128)(2,1)S(1)}, bf16[256,256]{1,0:T(8,128)(2,1)S(1)}, u32[]{:S(2)}, u32[]{:S(2)}) collective-permute-start(bf16[256,256]{1,0:T(8,128)(2,1)S(1)} %maximum_select_fusion.1), channel_id=1, source_target_pairs={{32,0},{12,4},{40,8},{20,12},{48,16},{28,20},{56,24},{4,28},{64,32... | collective-permute-start | bytes 393224 | tf_op jit(solution)/shard_map/ppermute | solution.py:36
  15.9 0.7 copy-start.20
  19.8 20.3 %copy-start.4 = (bf16[4,256,256]{2,1,0:T(8,128)(2,1)}, bf16[4,256,256]{2,1,0:T(8,128)(2,1)S(1)}, u32[]{:S(2)}) copy-start(bf16[4,256,256]{2,1,0:T(8,128)(2,1)S(1)} %pad_maximum_fusion.refs_0_) | copy-start | bytes 1572868
  19.8 11.3 %collective-permute-start.6 = (bf16[4,256,256]{2,1,0:T(8,128)(2,1)S(1)}, bf16[4,256,256]{2,1,0:T(8,128)(2,1)S(1)}, u32[]{:S(2)}, u32[]{:S(2)}) collective-permute-start(bf16[4,256,256]{2,1,0:T(8,128)(2,1)S(1)} %pad_maximum_fusion.refs_0_), channel_id=1, source_target_pairs={{24,0},{100,4},{0,8},{108,12},{8,16},{116,20},{16,24},{124,28},{56... | collective-permute-start | bytes 1572872 | tf_op jit(solution)/shard_map/ppermute | solution.py:36
  21.8 14.6 %collective-permute-start.4 = (bf16[4,256,256]{2,1,0:T(8,128)(2,1)S(1)}, bf16[4,256,256]{2,1,0:T(8,128)(2,1)S(1)}, u32[]{:S(2)}, u32[]{:S(2)}) collective-permute-start(bf16[4,256,256]{2,1,0:T(8,128)(2,1)S(1)} %pad_maximum_fusion.refs_0_), channel_id=1, source_target_pairs={{8,0},{36,4},{16,8},{44,12},{24,16},{52,20},{0,24},{60,28},{40,32}... | collective-permute-start | bytes 1572872 | tf_op jit(solution)/shard_map/ppermute | solution.py:36
  24.0 14.2 %collective-permute-start.5 = (bf16[4,256,256]{2,1,0:T(8,128)(2,1)S(1)}, bf16[4,256,256]{2,1,0:T(8,128)(2,1)S(1)}, u32[]{:S(2)}, u32[]{:S(2)}) collective-permute-start(bf16[4,256,256]{2,1,0:T(8,128)(2,1)S(1)} %pad_maximum_fusion.refs_0_), channel_id=1, source_target_pairs={{16,0},{68,4},{24,8},{76,12},{0,16},{84,20},{8,24},{92,28},{48,32}... | collective-permute-start | bytes 1572872 | tf_op jit(solution)/shard_map/ppermute | solution.py:36
  25.8 13.9 %collective-permute-start.7 = (bf16[4,256,256]{2,1,0:T(8,128)(2,1)S(1)}, bf16[4,256,256]{2,1,0:T(8,128)(2,1)S(1)}, u32[]{:S(2)}, u32[]{:S(2)}) collective-permute-start(bf16[4,256,256]{2,1,0:T(8,128)(2,1)S(1)} %pad_maximum_fusion.refs_0_), channel_id=1, source_target_pairs={{0,4},{4,0},{1,5},{5,1},{2,6},{6,2},{3,7},{7,3},{8,12},{12,8},{9,1... | collective-permute-start | bytes 1572872 | tf_op jit(solution)/shard_map/ppermute | solution.py:25
  31.1 9.0 %copy-start.9 = (bf16[4,256,256]{2,1,0:T(8,128)(2,1)}, bf16[4,256,256]{2,1,0:T(8,128)(2,1)S(1)}, u32[]{:S(2)}) copy-start(bf16[4,256,256]{2,1,0:T(8,128)(2,1)S(1)} %collective-permute-done.6.refs_3_) | copy-start | bytes 1572868
  31.1 8.6 %collective-permute-start.10 = (bf16[4,256,256]{2,1,0:T(8,128)(2,1)S(1)}, bf16[4,256,256]{2,1,0:T(8,128)(2,1)S(1)}, u32[]{:S(2)}, u32[]{:S(2)}) collective-permute-start(bf16[4,256,256]{2,1,0:T(8,128)(2,1)S(1)} %collective-permute-done.6.refs_3_), channel_id=1, source_target_pairs={{0,4},{4,0},{1,5},{5,1},{2,6},{6,2},{3,7},{7,3},{8,12},{12,8},{9,1... | collective-permute-start | bytes 1572872 | tf_op jit(solution)/shard_map/ppermute | solution.py:25
  36.3 3.7 %copy-start.10 = (bf16[4,256,256]{2,1,0:T(8,128)(2,1)}, bf16[4,256,256]{2,1,0:T(8,128)(2,1)S(1)}, u32[]{:S(2)}) copy-start(bf16[4,256,256]{2,1,0:T(8,128)(2,1)S(1)} %collective-permute-done.4.refs_1_) | copy-start | bytes 1572868
  36.3 3.4 %collective-permute-start.8 = (bf16[4,256,256]{2,1,0:T(8,128)(2,1)S(1)}, bf16[4,256,256]{2,1,0:T(8,128)(2,1)S(1)}, u32[]{:S(2)}, u32[]{:S(2)}) collective-permute-start(bf16[4,256,256]{2,1,0:T(8,128)(2,1)S(1)} %collective-permute-done.4.refs_1_), channel_id=1, source_target_pairs={{0,4},{4,0},{1,5},{5,1},{2,6},{6,2},{3,7},{7,3},{8,12},{12,8},{9,1... | collective-permute-start | bytes 1572872 | tf_op jit(solution)/shard_map/ppermute | solution.py:25
  38.1 1.9 copy-start.11
  38.2 1.9 collective-permute-start.9
  38.2 19.3 %collective-permute-start.11 = (bf16[512,128]{1,0:T(8,128)(2,1)}, bf16[512,128]{1,0:T(8,128)(2,1)S(1)}, u32[]{:S(2)}, u32[]{:S(2)}) collective-permute-start(bf16[512,128]{1,0:T(8,128)(2,1)} %bitcast.52), channel_id=1, source_target_pairs={{0,0},{1,32},{2,64},{3,96},{32,1},{33,33},{34,65},{35,97},{64,2},{... | collective-permute-start | bytes 393224 | tf_op jit(solution)/shard_map/ppermute | solution.py:399
  39.7 0.8 copy-start.12
  39.7 1.0 copy-start.13
  39.7 1.2 copy-start.14
  40.1 1.0 copy-start.15
  57.4 0.7 copy-start.19
  58.1 55.4 %collective-permute-start.19 = (bf16[2048,512]{1,0:T(8,128)(2,1)}, bf16[2048,512]{1,0:T(8,128)(2,1)S(1)}, u32[]{:S(2)}, u32[]{:S(2)}) collective-permute-start(bf16[2048,512]{1,0:T(8,128)(2,1)} %get-tuple-element.39.e), channel_id=1, source_target_pairs={{1,0},{2,1},{3,2},{0,3},{5,4},{6,5},{7,6},{4,7},{9,8},{10,9},{11,1... | collective-permute-start | bytes 6291464 | tf_op jit(solution)/shard_map/ppermute | solution.py:21
  63.8 49.6 %collective-permute-start.20 = (bf16[2048,512]{1,0:T(8,128)(2,1)}, bf16[2048,512]{1,0:T(8,128)(2,1)S(1)}, u32[]{:S(2)}, u32[]{:S(2)}) collective-permute-start(bf16[2048,512]{1,0:T(8,128)(2,1)} %get-tuple-element.39.e), channel_id=1, source_target_pairs={{3,0},{0,1},{1,2},{2,3},{7,4},{4,5},{5,6},{6,7},{11,8},{8,9},{9,10... | collective-permute-start | bytes 6291464 | tf_op jit(solution)/shard_map/ppermute | solution.py:21
  63.9 4.4 %collective-permute-start.12 = (f32[8,512]{1,0:T(8,128)}, f32[8,512]{1,0:T(8,128)S(1)}, u32[]{:S(2)}, u32[]{:S(2)}) collective-permute-start(f32[8,512]{1,0:T(8,128)} %get-tuple-element.41), channel_id=1, source_target_pairs={{32,0},{64,32},{96,64},{0,96},{33,1},{65,33},{97,65},{1,97},{34,2}... | collective-permute-start | bytes 49160 | tf_op jit(solution)/shard_map/ppermute | solution.py:21
  66.2 5.5 %collective-permute-start.13 = (f32[8,512]{1,0:T(8,128)}, f32[8,512]{1,0:T(8,128)S(1)}, u32[]{:S(2)}, u32[]{:S(2)}) collective-permute-start(f32[8,512]{1,0:T(8,128)} %get-tuple-element.41), channel_id=1, source_target_pairs={{64,0},{96,32},{0,64},{32,96},{65,1},{97,33},{1,65},{33,97},{66,2}... | collective-permute-start | bytes 49160 | tf_op jit(solution)/shard_map/ppermute | solution.py:21
  67.8 5.2 %collective-permute-start.14 = (f32[8,512]{1,0:T(8,128)}, f32[8,512]{1,0:T(8,128)S(1)}, u32[]{:S(2)}, u32[]{:S(2)}) collective-permute-start(f32[8,512]{1,0:T(8,128)} %get-tuple-element.41), channel_id=1, source_target_pairs={{96,0},{0,32},{32,64},{64,96},{97,1},{1,33},{33,65},{65,97},{98,2}... | collective-permute-start | bytes 49160 | tf_op jit(solution)/shard_map/ppermute | solution.py:21
  73.9 3.8 %collective-permute-start.15 = (f32[8,512]{1,0:T(8,128)S(1)}, f32[8,512]{1,0:T(8,128)S(1)}, u32[]{:S(2)}, u32[]{:S(2)}) collective-permute-start(f32[8,512]{1,0:T(8,128)S(1)} %maximum_maximum_fusion), channel_id=1, source_target_pairs={{8,0},{16,8},{24,16},{0,24},{9,1},{17,9},{25,17},{1,25},{10,2},{18... | collective-permute-start | bytes 49160 | tf_op jit(solution)/shard_map/ppermute | solution.py:21
  76.3 5.3 %collective-permute-start.16 = (f32[8,512]{1,0:T(8,128)S(1)}, f32[8,512]{1,0:T(8,128)S(1)}, u32[]{:S(2)}, u32[]{:S(2)}) collective-permute-start(f32[8,512]{1,0:T(8,128)S(1)} %maximum_maximum_fusion), channel_id=1, source_target_pairs={{16,0},{24,8},{0,16},{8,24},{17,1},{25,9},{1,17},{9,25},{18,2},{26... | collective-permute-start | bytes 49160 | tf_op jit(solution)/shard_map/ppermute | solution.py:21
  77.4 5.1 %collective-permute-start.17 = (f32[8,512]{1,0:T(8,128)S(1)}, f32[8,512]{1,0:T(8,128)S(1)}, u32[]{:S(2)}, u32[]{:S(2)}) collective-permute-start(f32[8,512]{1,0:T(8,128)S(1)} %maximum_maximum_fusion), channel_id=1, source_target_pairs={{24,0},{0,8},{8,16},{16,24},{25,1},{1,9},{9,17},{17,25},{26,2},{2,... | collective-permute-start | bytes 49160 | tf_op jit(solution)/shard_map/ppermute | solution.py:21
  82.6 1.2 copy-start.24
  82.6 1.2 collective-permute-start.18
  83.8 0.6 copy-start.25
  85.8 24.2 %collective-permute-start.21 = (f32[8,512]{1,0:T(8,128)}, f32[8,512]{1,0:T(8,128)S(1)}, u32[]{:S(2)}, u32[]{:S(2)}) collective-permute-start(f32[8,512]{1,0:T(8,128)} %get-tuple-element.43.pack), channel_id=1, source_target_pairs={{1,0},{2,1},{3,2},{0,3},{5,4},{6,5},{7,6},{4,7},{9,8},{10,9},{11,1... | collective-permute-start | bytes 49160 | tf_op jit(solution)/shard_map/ppermute | solution.py:21
  89.0 24.4 %collective-permute-start.22 = (f32[8,512]{1,0:T(8,128)}, f32[8,512]{1,0:T(8,128)S(1)}, u32[]{:S(2)}, u32[]{:S(2)}) collective-permute-start(f32[8,512]{1,0:T(8,128)} %get-tuple-element.43.pack), channel_id=1, source_target_pairs={{3,0},{0,1},{1,2},{2,3},{7,4},{4,5},{5,6},{6,7},{11,8},{8,9},{9,10... | collective-permute-start | bytes 49160 | tf_op jit(solution)/shard_map/ppermute | solution.py:21
  89.0 24.4 %collective-permute-start.23 = (f32[8,512]{1,0:T(8,128)}, f32[8,512]{1,0:T(8,128)S(1)}, u32[]{:S(2)}, u32[]{:S(2)}) collective-permute-start(f32[8,512]{1,0:T(8,128)} %get-tuple-element.43.pack), channel_id=1, source_target_pairs={{2,0},{3,1},{0,2},{1,3},{6,4},{7,5},{4,6},{5,7},{10,8},{11,9},{8,1... | collective-permute-start | bytes 49160 | tf_op jit(solution)/shard_map/ppermute | solution.py:21
  110.1 3.5 %copy-start.21 = (f32[8,512]{1,0:T(8,128)}, f32[8,512]{1,0:T(8,128)S(1)}, u32[]{:S(2)}) copy-start(f32[8,512]{1,0:T(8,128)S(1)} %collective-permute-done.21.refs_4_) | copy-start | bytes 49156
  113.5 0.6 copy-start.22
  113.5 0.6 copy-start.23
  113.5 1.3 copy-start
  113.5 2.0 copy-start.1
  180.2 3.0 %collective-permute-start.24 = (bf16[2,4,256,256]{3,2,1,0:T(8,128)(2,1)}, bf16[2,4,256,256]{3,2,1,0:T(8,128)(2,1)S(1)}, u32[]{:S(2)}, u32[]{:S(2)}) collective-permute-start(bf16[2,4,256,256]{3,2,1,0:T(8,128)(2,1)} %get-tuple-element.47), channel_id=1, source_target_pairs={{0,4},{4,0},{1,5},{5,1},{2,6},{6,2},{3,7},{7,3},{8,12},{12,8},{9,1... | collective-permute-start | bytes 3145736 | tf_op jit(solution)/shard_map/ppermute | solution.py:25
  180.3 4.4 %collective-permute-start.26 = (bf16[2,4,256,256]{3,2,1,0:T(8,128)(2,1)}, bf16[2,4,256,256]{3,2,1,0:T(8,128)(2,1)S(1)}, u32[]{:S(2)}, u32[]{:S(2)}) collective-permute-start(bf16[2,4,256,256]{3,2,1,0:T(8,128)(2,1)} %get-tuple-element.48), channel_id=1, source_target_pairs={{0,4},{4,0},{1,5},{5,1},{2,6},{6,2},{3,7},{7,3},{8,12},{12,8},{9,1... | collective-permute-start | bytes 3145736 | tf_op jit(solution)/shard_map/ppermute | solution.py:25
  180.8 25.4 %collective-permute-start.29 = (bf16[1024,512]{1,0:T(8,128)(2,1)}, bf16[1024,512]{1,0:T(8,128)(2,1)S(1)}, u32[]{:S(2)}, u32[]{:S(2)}) collective-permute-start(bf16[1024,512]{1,0:T(8,128)(2,1)} %get-tuple-element.55), channel_id=1, source_target_pairs={{1,0},{2,1},{3,2},{0,3},{5,4},{6,5},{7,6},{4,7},{9,8},{10,9},{11,1... | collective-permute-start | bytes 3145736 | tf_op jit(solution)/shard_map/ppermute | solution.py:21
  181.1 26.3 %collective-permute-start.30 = (bf16[1024,512]{1,0:T(8,128)(2,1)}, bf16[1024,512]{1,0:T(8,128)(2,1)S(1)}, u32[]{:S(2)}, u32[]{:S(2)}) collective-permute-start(bf16[1024,512]{1,0:T(8,128)(2,1)} %get-tuple-element.56), channel_id=1, source_target_pairs={{3,0},{0,1},{1,2},{2,3},{7,4},{4,5},{5,6},{6,7},{11,8},{8,9},{9,10... | collective-permute-start | bytes 3145736 | tf_op jit(solution)/shard_map/ppermute | solution.py:21
  183.1 4.3 %copy-start.7 = (bf16[2,4,256,256]{3,2,1,0:T(8,128)(2,1)}, bf16[2,4,256,256]{3,2,1,0:T(8,128)(2,1)S(1)}, u32[]{:S(2)}) copy-start(bf16[2,4,256,256]{3,2,1,0:T(8,128)(2,1)S(1)} %collective-permute-done.24) | copy-start | bytes 3145732
  187.4 19.9 %collective-permute-start.25 = (bf16[4,256,256]{2,1,0:T(8,128)(2,1)}, bf16[4,256,256]{2,1,0:T(8,128)(2,1)S(1)}, u32[]{:S(2)}, u32[]{:S(2)}) collective-permute-start(bf16[4,256,256]{2,1,0:T(8,128)(2,1)} %get-tuple-element.77), channel_id=1, source_target_pairs={{96,0},{28,4},{104,8},{4,12},{112,16},{12,20},{120,24},{20,28},{0,... | collective-permute-start | bytes 1572872 | tf_op jit(solution)/shard_map/ppermute | solution.py:36
  189.3 18.1 %collective-permute-start.27 = (bf16[4,256,256]{2,1,0:T(8,128)(2,1)}, bf16[4,256,256]{2,1,0:T(8,128)(2,1)S(1)}, u32[]{:S(2)}, u32[]{:S(2)}) collective-permute-start(bf16[4,256,256]{2,1,0:T(8,128)(2,1)} %get-tuple-element.76), channel_id=1, source_target_pairs={{64,0},{20,4},{72,8},{28,12},{80,16},{4,20},{88,24},{12,28},{96,32... | collective-permute-start | bytes 1572872 | tf_op jit(solution)/shard_map/ppermute | solution.py:36
  190.0 17.4 %collective-permute-start.28 = (bf16[4,256,256]{2,1,0:T(8,128)(2,1)}, bf16[4,256,256]{2,1,0:T(8,128)(2,1)}, u32[]{:S(2)}, u32[]{:S(2)}) collective-permute-start(bf16[4,256,256]{2,1,0:T(8,128)(2,1)} %get-tuple-element.75), channel_id=1, source_target_pairs={{32,0},{12,4},{40,8},{20,12},{48,16},{28,20},{56,24},{4,28},{64,32... | collective-permute-start | bytes 1572872 | tf_op jit(solution)/shard_map/ppermute | solution.py:36
  203.7 5.0 %copy-start.8 = (bf16[2,4,256,256]{3,2,1,0:T(8,128)(2,1)S(1)}, bf16[2,4,256,256]{3,2,1,0:T(8,128)(2,1)}, u32[]{:S(2)}) copy-start(bf16[2,4,256,256]{3,2,1,0:T(8,128)(2,1)} %copy-done.7) | copy-start | bytes 3145732
  206.2 1.3 copy-start.2
  207.4 1.1 copy-start.3
  207.4 1.1 copy-start.5
  207.4 1.3 copy-start.6
  210.6 12.0 %collective-permute-start.31 = (bf16[256,256]{1,0:T(8,128)(2,1)S(1)}, bf16[256,256]{1,0:T(8,128)(2,1)S(1)}, u32[]{:S(2)}, u32[]{:S(2)}) collective-permute-start(bf16[256,256]{1,0:T(8,128)(2,1)S(1)} %get-tuple-element.80), channel_id=1, source_target_pairs={{24,0},{100,4},{0,8},{108,12},{8,16},{116,20},{16,24},{124,28},{56... | collective-permute-start | bytes 393224 | tf_op jit(solution)/shard_map/ppermute | solution.py:36
  212.1 10.5 %collective-permute-start.32 = (bf16[256,256]{1,0:T(8,128)(2,1)S(1)}, bf16[256,256]{1,0:T(8,128)(2,1)S(1)}, u32[]{:S(2)}, u32[]{:S(2)}) collective-permute-start(bf16[256,256]{1,0:T(8,128)(2,1)S(1)} %get-tuple-element.79), channel_id=1, source_target_pairs={{16,0},{68,4},{24,8},{76,12},{0,16},{84,20},{8,24},{92,28},{48,32}... | collective-permute-start | bytes 393224 | tf_op jit(solution)/shard_map/ppermute | solution.py:36
  214.1 8.5 %collective-permute-start.33 = (bf16[256,256]{1,0:T(8,128)(2,1)S(1)}, bf16[256,256]{1,0:T(8,128)(2,1)S(1)}, u32[]{:S(2)}, u32[]{:S(2)}) collective-permute-start(bf16[256,256]{1,0:T(8,128)(2,1)S(1)} %get-tuple-element.78), channel_id=1, source_target_pairs={{8,0},{36,4},{16,8},{44,12},{24,16},{52,20},{0,24},{60,28},{40,32}... | collective-permute-start | bytes 393224 | tf_op jit(solution)/shard_map/ppermute | solution.py:36
  222.6 0.7 copy-start.16
  222.6 0.7 copy-start.17
  223.3 0.7 copy-start.18
  225.1 1.4 collective-permute-start.34
Sparse Core Ops, SparseCore 0:
  58.2 48.5 all-gather.2

commit v11 on v9

--- a/solution.py
+++ b/solution.py
@@ -72,6 +72,29 @@
 
 SUB = 256
 CUT = VOC // 2
+
+
+def onward_body(ep, em, *refs):
+    low, high = refs[-2:]
+    low[...] = ep[...]
+    high[...] = em[...]
+
+
+def onward(ep, em, *others):
+    n = len(others)
+    half = jax.ShapeDtypeStruct((CUT, ROWS), BF)
+    part = lambda first: pl.BlockSpec((SUB, ROWS), lambda i: (i + first, 0))
+    return pl.pallas_call(
+        onward_body,
+        grid=(CUT // SUB,),
+        in_specs=[part(0), part(CUT // SUB)] + [HBM] * n,
+        out_specs=[HBM] * n + [part(0), part(0)],
+        out_shape=[jax.ShapeDtypeStruct(a.shape, a.dtype) for a in others] + [half, half],
+        input_output_aliases={i + 2: i for i in range(n)},
+        compiler_params=params(),
+        cost_estimate=SMALL,
+        name="onward",
+    )(ep, em, *others)
 
 
 def gather_pieces(block, *early):
@@ -279,13 +302,13 @@
     return sum(x.astype(F32) for x in xs)
 
 
-def scatter(keep, recv, c, first, second, others):
+def scatter(keep, recv, c, first, second):
     b = [add(keep[d], recv[d // 2][d % 2]) for d in range(4)]
     u = [cross(b[d].astype(BF), 0, 4 - d) for d in (1, 2, 3)]
-    u1, u2, u3, work, *others = gate(*u, first(), *others)
+    u1, u2, u3, work = gate(*u, first())
     t = add(b[0], u1, u2, u3)
     u = [cross(t[d].astype(BF), 1, 4 - d) for d in (1, 2, 3)]
-    *u, work = gate(*u, second(work, *others))
+    *u, work = gate(*u, second(work))
     f = add(t[0], *u)
     low, high = f[:, :128], f[:, 128:]
     mine, other = jnp.where(c == 0, low, high), jnp.where(c == 0, high, low)
@@ -307,7 +330,7 @@
     for e, pack in ((ep, pack_p), (em, pack_m)):
         parts.append(token_grad(e[...], pack, pack[pl.ds(i, 1), :], i * TILE))
     q = jnp.concatenate([columns(f) for f in (f0, f1, f3)], axis=0)
-    acc[...] = dot_nn(jnp.concatenate(parts, axis=1), q)
+    acc[...] = dot_nn(jnp.concatenate(parts, axis=1), q).astype(BF)
 
 
 def embed_a_call(at, tgt, ep, em, packs, feats):
@@ -321,7 +344,7 @@
             in_specs=[tile, tile, tile, pack, pack] + [feature_spec(d) for d in (0, 1, 3)],
             out_specs=pl.BlockSpec((TILE, 1024), lambda i, at: (i, 0)),
         ),
-        out_shape=jax.ShapeDtypeStruct((VOC, 1024), F32),
+        out_shape=jax.ShapeDtypeStruct((VOC, 1024), BF),
         compiler_params=params(),
         cost_estimate=SMALL,
         name="embed_a",
@@ -332,7 +355,7 @@
     i = pl.program_id(0)
     e = jnp.where(i < CUT // TILE, low[...], high[...])
     g = token_grad(e, pack, pack[pl.ds(i, 1), :], i * TILE)
-    out[...] = (acc[...] + dot_nn(g, columns(f2))).astype(BF)
+    out[...] = (acc[...].astype(F32) + dot_nn(g, columns(f2))).astype(BF)
 
 
 def embed_b_call(at, acc, low, high, pack, feats):
@@ -384,17 +407,16 @@
     pack, grad_mix = finish_call(s, sibling(s), st, tid, mix, weight.reshape(1, 128))
     packs = [shift(pack, "y", d) for d in (1, 3, 2)]
     keep, send0, send1, tgt = hidden_call(at, e, pack, embed)
-    send0, send1, ep, em, *packs = gate(send0, send1, ep, em, *packs)
-    low, high = shift(ep[:CUT], "y", 1), shift(em[CUT:], "y", 3)
+    pack_p, pack_m, low, high = onward(ep, em, packs[0], packs[1])
+    low, high = shift(low, "y", 1), shift(high, "y", 3)
     recv = sibling(send0), sibling(send1)
 
     grad_hidden, grad_embed = scatter(
         keep,
         recv,
         c,
-        lambda: embed_a_call(at, tgt, ep, em, packs[:2], feats),
-        lambda acc, low, high: embed_b_call(at, acc, low, high, packs[2], feats),
-        (low, high),
+        lambda: embed_a_call(at, tgt, ep, em, (pack_p, pack_m), feats),
+        lambda acc: embed_b_call(at, acc, low, high, packs[2], feats),
     )
     return grad_hidden.reshape(4, 128, 128), grad_embed, grad_mix
 

time: 174 us -> 175 us (level)
  waiting for transfers between devices: 32.6 us -> 38.2 us
  starting transfers between devices: 48.9 us -> 43.4 us
  local copies, waits for them, and re-layouts: 11.3 us -> 8.81 us
  Pallas kernels: 55.5 us -> 57.6 us
    ppermute x9, waiting for transfers between devices: 3.29 us -> 7.88 us  [sibling(): return lax.ppermute(a, 'c', [(0, 1), (1, 0)])]
    pallas_call x0 -> x1, Pallas kernels: none -> 3.78 us  [onward(): pl.pallas_call(onward_body, grid=(CUT // SUB,), in_specs=[part(0), part(C...]
    slice x2 -> x0, local copies, waits for them, and re-layouts: 3.5 us -> none  [local(): low, high = (shift(ep[:CUT], 'y', 1), shift(em[CUT:], 'y', 3))]
    ppermute x12, starting transfers between devices: 21.9 us -> 19.2 us  [cross(): return lax.ppermute(a, ('x', 'z', 'c'), pairs)]
    ppermute x13, starting transfers between devices: 23.5 us -> 21.2 us  [shift(): return lax.ppermute(a, axis, [((i + d) % 4, i) for i in range(4)])]
    unnamed x56 -> x54, local copies, waits for them, and re-layouts: 7.08 us -> 8.08 us
  transfers between devices with their start and end apart: 36 -> 36, of which waited for: 14 -> 15; matrix products, arithmetic and copies ran while one was open for 5% -> 4% of each run, Pallas kernels for 32% -> 33%
where the time goes in v11:
time: 175 us; the launch traced here: 173 us
  Pallas kernels  57.6 us (33%)
  starting transfers between devices  43.4 us (25%)
  waiting for transfers between devices  38.2 us (22%)
  between operations  14.3 us (8%)
  other arithmetic  10.8 us (6%)
  local copies, waits for them, and re-layouts  8.81 us (5%)
    ppermute x13, starting transfers between devices, shift(): return lax.ppermute(a, axis, [((i + d) % 4, i) for i in range(4)])  21.2 us
    ppermute x12, starting transfers between devices, cross(): return lax.ppermute(a, ('x', 'z', 'c'), pairs)  19.2 us
    pallas_call x1, Pallas kernels, hidden_call(): pl.pallas_call(hidden_body, grid_spec=pltpu.PrefetchScalarGridSpec(num_sc...  16.7 us
    ppermute x12, waiting for transfers between devices, cross(): return lax.ppermute(a, ('x', 'z', 'c'), pairs)  16.4 us
    pallas_call x1, Pallas kernels, logits_call(): pl.pallas_call(logits_body, grid_spec=pltpu.PrefetchScalarGridSpec(num_sc...  16.3 us
    ppermute x13, waiting for transfers between devices, shift(): return lax.ppermute(a, axis, [((i + d) % 4, i) for i in range(4)])  13.9 us
    pallas_call x1, Pallas kernels, embed_a_call(): pl.pallas_call(embed_a_body, grid_spec=pltpu.PrefetchScalarGridSpec(num_s...  11.6 us
    unnamed x54, local copies, waits for them, and re-layouts  8.08 us
  transfers between devices with their start and end apart: 36, of which 15 were waited for; matrix products, arithmetic and copies ran while one was open for 4% of the time, Pallas kernels for 33%

profile of v11, /device:TPU:0, one launch (start us, length us, event | category | flops | bytes accessed | tf_op | source)
XLA Modules:
  0.0 173.1 jit_solution(3662675960421943204)
XLA Ops:
  7.2 0.9 broadcast_select_fusion.1
  8.2 0.7 broadcast_subtract_fusion
  8.9 0.6 collective-permute-done
  9.5 3.2 %collective-permute-start.3 = (bf16[256,256]{1,0:T(8,128)(2,1)S(1)}, bf16[256,256]{1,0:T(8,128)(2,1)S(1)}, u32[]{:S(2)}, u32[]{:S(2)}) collective-permute-start(bf16[256,256]{1,0:T(8,128)(2,1)S(1)} %maximum_select_fusion.1), channel_id=1, source_target_pairs={{64,0},{20,4},{72,8},{28,12},{80,16},{4,20},{88,24},{12,28},{96,32... | collective-permute-start | bytes 393224 | tf_op jit(solution)/shard_map/ppermute | solution.py:36
  12.7 1.1 collective-permute-start.2
  13.8 0.9 collective-permute-start.1
  14.7 0.6 pad_add_fusion.refs_1_
  15.3 4.7 %collective-permute-done.1.refs_0_ = bf16[256,256]{1,0:T(8,128)(2,1)S(1)} collective-permute-done((bf16[256,256]{1,0:T(8,128)(2,1)S(1)}, bf16[256,256]{1,0:T(8,128)(2,1)S(1)}, u32[]{:S(2)}, u32[]{:S(2)}) %collective-permute-start.1) | collective-permute-done | bytes 131104 | tf_op jit(solution)/shard_map/ppermute | solution.py:36
  20.0 0.6 tile.2
  20.7 1.0 pad_maximum_fusion.refs_0_
  21.6 2.0 %collective-permute-start.6 = (bf16[4,256,256]{2,1,0:T(8,128)(2,1)S(1)}, bf16[4,256,256]{2,1,0:T(8,128)(2,1)S(1)}, u32[]{:S(2)}, u32[]{:S(2)}) collective-permute-start(bf16[4,256,256]{2,1,0:T(8,128)(2,1)S(1)} %pad_maximum_fusion.refs_0_), channel_id=1, source_target_pairs={{24,0},{100,4},{0,8},{108,12},{8,16},{116,20},{16,24},{124,28},{56... | collective-permute-start | bytes 1572872 | tf_op jit(solution)/shard_map/ppermute | solution.py:36
  23.6 3.6 %collective-permute-start.5 = (bf16[4,256,256]{2,1,0:T(8,128)(2,1)S(1)}, bf16[4,256,256]{2,1,0:T(8,128)(2,1)S(1)}, u32[]{:S(2)}, u32[]{:S(2)}) collective-permute-start(bf16[4,256,256]{2,1,0:T(8,128)(2,1)S(1)} %pad_maximum_fusion.refs_0_), channel_id=1, source_target_pairs={{16,0},{68,4},{24,8},{76,12},{0,16},{84,20},{8,24},{92,28},{48,32}... | collective-permute-start | bytes 1572872 | tf_op jit(solution)/shard_map/ppermute | solution.py:36
  27.2 1.0 collective-permute-start.4
  28.2 4.7 %collective-permute-done.6.refs_3_ = bf16[4,256,256]{2,1,0:T(8,128)(2,1)S(1)} collective-permute-done((bf16[4,256,256]{2,1,0:T(8,128)(2,1)S(1)}, bf16[4,256,256]{2,1,0:T(8,128)(2,1)S(1)}, u32[]{:S(2)}, u32[]{:S(2)}) %collective-permute-start.6) | collective-permute-done | bytes 524320 | tf_op jit(solution)/shard_map/ppermute | solution.py:36
  32.9 7.1 %collective-permute-done.5.refs_2_ = bf16[4,256,256]{2,1,0:T(8,128)(2,1)S(1)} collective-permute-done((bf16[4,256,256]{2,1,0:T(8,128)(2,1)S(1)}, bf16[4,256,256]{2,1,0:T(8,128)(2,1)S(1)}, u32[]{:S(2)}, u32[]{:S(2)}) %collective-permute-start.5) | collective-permute-done | bytes 524320 | tf_op jit(solution)/shard_map/ppermute | solution.py:36
  40.0 0.5 collective-permute-start.8
  40.5 1.6 collective-permute-start.11
  42.1 0.5 collective-permute-done.8.refs_5_
  43.4 16.3 %logits.1 = (bf16[2048,512]{1,0:T(8,128)(2,1)}, f32[8,512]{1,0:T(8,128)}, f32[8,512]{1,0:T(8,128)}) custom-call(s32[4]{0:T(128)} %get-tuple-element.29.at, bf16[4,256,256]{2,1,0:T(8,128)(2,1)} %copy-done.2, bf16[4,256,256]{2,1,0:T(8,128)(2,1)} %copy-done.11, bf16[4,256,256]{2,1,0:T(8,128)(2,1)} %copy-done.10, bf16[4,256,256]{2,1,0:T(8,128)(2,1)} %copy-done.9, ...), custom_call_target="tpu_custom_call" | custom-call | flops 1000 | bytes 1000 | tf_op jit(solution)/shard_map/logits/pallas_call | solution.py:157
  59.8 0.6 copy-done.19
  60.5 3.4 %collective-permute-start.14 = (f32[8,512]{1,0:T(8,128)}, f32[8,512]{1,0:T(8,128)S(1)}, u32[]{:S(2)}, u32[]{:S(2)}) collective-permute-start(f32[8,512]{1,0:T(8,128)} %get-tuple-element.34), channel_id=1, source_target_pairs={{96,0},{0,32},{32,64},{64,96},{97,1},{1,33},{33,65},{65,97},{98,2}... | collective-permute-start | bytes 49160 | tf_op jit(solution)/shard_map/ppermute | solution.py:21
  63.9 4.1 %collective-permute-start.13 = (f32[8,512]{1,0:T(8,128)}, f32[8,512]{1,0:T(8,128)S(1)}, u32[]{:S(2)}, u32[]{:S(2)}) collective-permute-start(f32[8,512]{1,0:T(8,128)} %get-tuple-element.34), channel_id=1, source_target_pairs={{64,0},{96,32},{0,64},{32,96},{65,1},{97,33},{1,65},{33,97},{66,2}... | collective-permute-start | bytes 49160 | tf_op jit(solution)/shard_map/ppermute | solution.py:21
  68.0 1.6 collective-permute-start.12
  69.8 3.2 %collective-permute-start.24 = (bf16[2048,512]{1,0:T(8,128)(2,1)}, bf16[2048,512]{1,0:T(8,128)(2,1)S(1)}, u32[]{:S(2)}, u32[]{:S(2)}) collective-permute-start(bf16[2048,512]{1,0:T(8,128)(2,1)} %get-tuple-element.32.e), channel_id=1, source_target_pairs={{1,0},{2,1},{3,2},{0,3},{5,4},{6,5},{7,6},{4,7},{9,8},{10,9},{11,1... | collective-permute-start | bytes 6291464 | tf_op jit(solution)/shard_map/ppermute | solution.py:21
  73.0 0.9 fusion.11
  73.9 1.0 collective-permute-start.17
  75.0 2.1 %collective-permute-start.16 = (f32[8,512]{1,0:T(8,128)S(1)}, f32[8,512]{1,0:T(8,128)S(1)}, u32[]{:S(2)}, u32[]{:S(2)}) collective-permute-start(f32[8,512]{1,0:T(8,128)S(1)} %maximum_maximum_fusion), channel_id=1, source_target_pairs={{16,0},{24,8},{0,16},{8,24},{17,1},{25,9},{1,17},{9,25},{18,2},{26... | collective-permute-start | bytes 49160 | tf_op jit(solution)/shard_map/ppermute | solution.py:21
  77.1 1.5 collective-permute-start.15
  78.6 0.3 collective-permute-done.17
  78.9 1.4 collective-permute-done.16
  80.3 0.5 collective-permute-done.15
  81.1 1.2 collective-permute-done.18.b
  82.3 0.6 copy-done.25
  82.9 1.4 finish.1
  84.3 16.7 %hidden.1 = (bf16[4,4,256,256]{3,2,1,0:T(8,128)(2,1)}, bf16[2,4,256,256]{3,2,1,0:T(8,128)(2,1)}, bf16[2,4,256,256]{3,2,1,0:T(8,128)(2,1)}, bf16[2048,512]{1,0:T(8,128)(2,1)}) custom-call(s32[4]{0:T(128)} %get-tuple-element.29.at, bf16[2048,512]{1,0:T(8,128)(2,1)} %get-tuple-element.32.e, f32[8,512]{1,0:T(8,128)} %get-tuple-element.36.pack, ...), custom_call_target="tpu_custom_call" | custom-call | flops 1000 | bytes 1000 | tf_op jit(solution)/shard_map/hidden/pallas_call | solution.py:275
  101.3 0.3 collective-permute-start.21
  101.6 2.9 %collective-permute-done.19 = bf16[2,4,256,256]{3,2,1,0:T(8,128)(2,1)S(1)} collective-permute-done((bf16[2,4,256,256]{3,2,1,0:T(8,128)(2,1)}, bf16[2,4,256,256]{3,2,1,0:T(8,128)(2,1)S(1)}, u32[]{:S(2)}, u32[]{:S(2)}) %collective-permute-start.19) | collective-permute-done | bytes 1048608 | tf_op jit(solution)/shard_map/ppermute | solution.py:25
  104.5 0.3 collective-permute-start.26
  104.8 1.4 collective-permute-done.21
  106.2 2.9 %fusion.4 = (bf16[4,256,256]{2,1,0:T(8,128)(2,1)}, bf16[4,256,256]{2,1,0:T(8,128)(2,1)}, bf16[4,256,256]{2,1,0:T(8,128)(2,1)S(1)}) fusion(bf16[2,4,256,256]{3,2,1,0:T(8,128)(2,1)S(1)} %collective-permute-done.21, bf16[4,4,256,256]{3,2,1,0:T(8,128)(2,1)} %get-tuple-element.37, bf16[2,4,256,256]{3,2,1,0:T(8,128)(2,1)S(1)} %collective-permute-done.19), kind=kLoop, calls=%fused_computation.8 | loop fusion | flops 3145728 | bytes 4718592 | tf_op jit(solution)/shard_map/convert_element_type | solution.py:307
  109.1 1.7 collective-permute-start.23
  110.8 7.3 %collective-permute-done.27.refs_1_ = f32[8,512]{1,0:T(8,128)S(1)} collective-permute-done((f32[8,512]{1,0:T(8,128)S(1)}, f32[8,512]{1,0:T(8,128)S(1)}, u32[]{:S(2)}, u32[]{:S(2)}) %collective-permute-start.27) | collective-permute-done | bytes 16416 | tf_op jit(solution)/shard_map/ppermute | solution.py:21
  118.2 1.0 collective-permute-start.20
  119.2 1.3 copy-done
  120.5 1.3 copy-done.1
  121.8 3.8 %onward.1 = (f32[8,512]{1,0:T(8,128)}, f32[8,512]{1,0:T(8,128)}, bf16[1024,512]{1,0:T(8,128)(2,1)}, bf16[1024,512]{1,0:T(8,128)(2,1)}) custom-call(bf16[2048,512]{1,0:T(8,128)(2,1)} %copy-done.1, bf16[2048,512]{1,0:T(8,128)(2,1)} %copy-done, f32[8,512]{1,0:T(8,128)} %copy-done.22, f32[8,512]{1,0:T(8,128)} %copy-done.21), custom_call_target="tpu_custom_call", output_to_operand_aliasing={{0}: (2, {}), {1}: (3, {})} | custom-call | flops 1000 | bytes 1000 | tf_op jit(solution)/shard_map/onward/pallas_call | solution.py:87
  125.6 2.2 %collective-permute-start.31 = (bf16[1024,512]{1,0:T(8,128)(2,1)}, bf16[1024,512]{1,0:T(8,128)(2,1)S(1)}, u32[]{:S(2)}, u32[]{:S(2)}) collective-permute-start(bf16[1024,512]{1,0:T(8,128)(2,1)} %get-tuple-element.48), channel_id=1, source_target_pairs={{1,0},{2,1},{3,2},{0,3},{5,4},{6,5},{7,6},{4,7},{9,8},{10,9},{11,1... | collective-permute-start | bytes 3145736 | tf_op jit(solution)/shard_map/ppermute | solution.py:21
  127.8 11.6 %embed_a.1.refs_3_ = bf16[2048,1024]{1,0:T(8,128)(2,1)} custom-call(s32[4]{0:T(128)} %get-tuple-element.29.at, bf16[2048,512]{1,0:T(8,128)(2,1)} %get-tuple-element.40.tgt, bf16[2048,512]{1,0:T(8,128)(2,1)} %copy-done.1, bf16[2048,512]{1,0:T(8,128)(2,1)} %copy-done, f32[8,512]{1,0:T(8,128)} %get-tuple-element.41.pack_p, f32[8,512]{1,0:T(8,128)} %get-tuple-element.42.pack_m, ...), custom_call_target="tpu_custom_call" | custom-call | flops 1000 | bytes 1000 | tf_op jit(solution)/shard_map/embed_a/pallas_call | solution.py:339
  139.4 1.6 collective-permute-start.33
  141.0 0.8 copy-done.4
  141.8 0.8 copy-done.5
  142.6 1.8 %fusion.14 = (bf16[4,256,256]{2,1,0:T(8,128)(2,1)S(1)}, f32[4,256,256]{2,1,0:T(8,128)S(1)}) fusion(bf16[4,256,256]{2,1,0:T(8,128)(2,1)} %get-tuple-element.46, bf16[4,256,256]{2,1,0:T(8,128)(2,1)} %get-tuple-element.45, bf16[4,256,256]{2,1,0:T(8,128)(2,1)} %get-tuple-element.44, bf16[2,4,256,256]{3,2,1,0:T(8,128)(2,1)S(1)} %copy-done.8, ...), kind=kLoop, calls=%fused_computation.48 | loop fusion | flops 2621440 | bytes 4194304 | tf_op jit(solution)/shard_map/convert.2
  144.5 2.1 %collective-permute-start.30 = (bf16[256,256]{1,0:T(8,128)(2,1)S(1)}, bf16[256,256]{1,0:T(8,128)(2,1)S(1)}, u32[]{:S(2)}, u32[]{:S(2)}) collective-permute-start(bf16[256,256]{1,0:T(8,128)(2,1)S(1)} %get-tuple-element.64), channel_id=1, source_target_pairs={{8,0},{36,4},{16,8},{44,12},{24,16},{52,20},{0,24},{60,28},{40,32}... | collective-permute-start | bytes 393224 | tf_op jit(solution)/shard_map/ppermute | solution.py:36
  146.6 1.4 collective-permute-start.29
  148.0 3.9 %collective-permute-done.33.pack = f32[8,512]{1,0:T(8,128)S(1)} collective-permute-done((f32[8,512]{1,0:T(8,128)S(1)}, f32[8,512]{1,0:T(8,128)S(1)}, u32[]{:S(2)}, u32[]{:S(2)}) %collective-permute-start.33) | collective-permute-done | bytes 16416 | tf_op jit(solution)/shard_map/ppermute | solution.py:21
  151.9 1.0 collective-permute-start.28
  152.9 0.5 collective-permute-done.32.high
  153.4 0.5 copy-done.6
  153.9 7.7 %embed_b.1.refs_3_ = bf16[2048,1024]{1,0:T(8,128)(2,1)} custom-call(s32[4]{0:T(128)} %get-tuple-element.29.at, bf16[2048,1024]{1,0:T(8,128)(2,1)} %get-tuple-element.47.acc, bf16[1024,512]{1,0:T(8,128)(2,1)} %copy-done.6, bf16[1024,512]{1,0:T(8,128)(2,1)} %collective-permute-done.32.high, f32[8,512]{1,0:T(8,128)} %copy-done.24, ...), custom_call_target="tpu_custom_call" | custom-call | flops 1000 | bytes 1000 | tf_op jit(solution)/shard_map/embed_b/pallas_call | solution.py:363
  161.6 0.6 copy-done.16
  162.3 0.7 copy-done.18
  163.0 1.1 fusion.7
  164.2 1.3 collective-permute-done.34
  165.5 0.7 maximum_select_fusion
  (92 shorter events, 2.3 us)
Async XLA Ops:
  7.2 120.6 %all-gather.3.cloned.1.call-start = ((), (), s32[]{:S(2)}) async-start(), calls=%async_computation | async-start | bytes 4325376 | tf_op jit(solution)/shard_map/all_gather | solution.py:402
  8.1 1.3 collective-permute-start
  9.5 11.2 %collective-permute-start.3 = (bf16[256,256]{1,0:T(8,128)(2,1)S(1)}, bf16[256,256]{1,0:T(8,128)(2,1)S(1)}, u32[]{:S(2)}, u32[]{:S(2)}) collective-permute-start(bf16[256,256]{1,0:T(8,128)(2,1)S(1)} %maximum_select_fusion.1), channel_id=1, source_target_pairs={{64,0},{20,4},{72,8},{28,12},{80,16},{4,20},{88,24},{12,28},{96,32... | collective-permute-start | bytes 393224 | tf_op jit(solution)/shard_map/ppermute | solution.py:36
  12.7 8.0 %collective-permute-start.2 = (bf16[256,256]{1,0:T(8,128)(2,1)S(1)}, bf16[256,256]{1,0:T(8,128)(2,1)S(1)}, u32[]{:S(2)}, u32[]{:S(2)}) collective-permute-start(bf16[256,256]{1,0:T(8,128)(2,1)S(1)} %maximum_select_fusion.1), channel_id=1, source_target_pairs={{32,0},{12,4},{40,8},{20,12},{48,16},{28,20},{56,24},{4,28},{64,32... | collective-permute-start | bytes 393224 | tf_op jit(solution)/shard_map/ppermute | solution.py:36
  13.8 6.2 %collective-permute-start.1 = (bf16[256,256]{1,0:T(8,128)(2,1)S(1)}, bf16[256,256]{1,0:T(8,128)(2,1)S(1)}, u32[]{:S(2)}, u32[]{:S(2)}) collective-permute-start(bf16[256,256]{1,0:T(8,128)(2,1)S(1)} %maximum_select_fusion.1), channel_id=1, source_target_pairs={{96,0},{28,4},{104,8},{4,12},{112,16},{12,20},{120,24},{20,28},{0,... | collective-permute-start | bytes 393224 | tf_op jit(solution)/shard_map/ppermute | solution.py:36
  20.0 0.7 copy-start.20
  21.6 21.0 %copy-start.2 = (bf16[4,256,256]{2,1,0:T(8,128)(2,1)}, bf16[4,256,256]{2,1,0:T(8,128)(2,1)S(1)}, u32[]{:S(2)}) copy-start(bf16[4,256,256]{2,1,0:T(8,128)(2,1)S(1)} %pad_maximum_fusion.refs_0_) | copy-start | bytes 1572868
  21.6 11.3 %collective-permute-start.6 = (bf16[4,256,256]{2,1,0:T(8,128)(2,1)S(1)}, bf16[4,256,256]{2,1,0:T(8,128)(2,1)S(1)}, u32[]{:S(2)}, u32[]{:S(2)}) collective-permute-start(bf16[4,256,256]{2,1,0:T(8,128)(2,1)S(1)} %pad_maximum_fusion.refs_0_), channel_id=1, source_target_pairs={{24,0},{100,4},{0,8},{108,12},{8,16},{116,20},{16,24},{124,28},{56... | collective-permute-start | bytes 1572872 | tf_op jit(solution)/shard_map/ppermute | solution.py:36
  23.6 16.4 %collective-permute-start.5 = (bf16[4,256,256]{2,1,0:T(8,128)(2,1)S(1)}, bf16[4,256,256]{2,1,0:T(8,128)(2,1)S(1)}, u32[]{:S(2)}, u32[]{:S(2)}) collective-permute-start(bf16[4,256,256]{2,1,0:T(8,128)(2,1)S(1)} %pad_maximum_fusion.refs_0_), channel_id=1, source_target_pairs={{16,0},{68,4},{24,8},{76,12},{0,16},{84,20},{8,24},{92,28},{48,32}... | collective-permute-start | bytes 1572872 | tf_op jit(solution)/shard_map/ppermute | solution.py:36
  27.2 12.8 %collective-permute-start.4 = (bf16[4,256,256]{2,1,0:T(8,128)(2,1)S(1)}, bf16[4,256,256]{2,1,0:T(8,128)(2,1)S(1)}, u32[]{:S(2)}, u32[]{:S(2)}) collective-permute-start(bf16[4,256,256]{2,1,0:T(8,128)(2,1)S(1)} %pad_maximum_fusion.refs_0_), channel_id=1, source_target_pairs={{8,0},{36,4},{16,8},{44,12},{24,16},{52,20},{0,24},{60,28},{40,32}... | collective-permute-start | bytes 1572872 | tf_op jit(solution)/shard_map/ppermute | solution.py:36
  28.2 13.8 %collective-permute-start.7 = (bf16[4,256,256]{2,1,0:T(8,128)(2,1)S(1)}, bf16[4,256,256]{2,1,0:T(8,128)(2,1)S(1)}, u32[]{:S(2)}, u32[]{:S(2)}) collective-permute-start(bf16[4,256,256]{2,1,0:T(8,128)(2,1)S(1)} %pad_maximum_fusion.refs_0_), channel_id=1, source_target_pairs={{0,4},{4,0},{1,5},{5,1},{2,6},{6,2},{3,7},{7,3},{8,12},{12,8},{9,1... | collective-permute-start | bytes 1572872 | tf_op jit(solution)/shard_map/ppermute | solution.py:25
  32.9 9.7 %copy-start.9 = (bf16[4,256,256]{2,1,0:T(8,128)(2,1)}, bf16[4,256,256]{2,1,0:T(8,128)(2,1)S(1)}, u32[]{:S(2)}) copy-start(bf16[4,256,256]{2,1,0:T(8,128)(2,1)S(1)} %collective-permute-done.6.refs_3_) | copy-start | bytes 1572868
  32.9 9.2 %collective-permute-start.10 = (bf16[4,256,256]{2,1,0:T(8,128)(2,1)S(1)}, bf16[4,256,256]{2,1,0:T(8,128)(2,1)S(1)}, u32[]{:S(2)}, u32[]{:S(2)}) collective-permute-start(bf16[4,256,256]{2,1,0:T(8,128)(2,1)S(1)} %collective-permute-done.6.refs_3_), channel_id=1, source_target_pairs={{0,4},{4,0},{1,5},{5,1},{2,6},{6,2},{3,7},{7,3},{8,12},{12,8},{9,1... | collective-permute-start | bytes 1572872 | tf_op jit(solution)/shard_map/ppermute | solution.py:25
  40.0 2.7 %copy-start.10 = (bf16[4,256,256]{2,1,0:T(8,128)(2,1)}, bf16[4,256,256]{2,1,0:T(8,128)(2,1)S(1)}, u32[]{:S(2)}) copy-start(bf16[4,256,256]{2,1,0:T(8,128)(2,1)S(1)} %collective-permute-done.5.refs_2_) | copy-start | bytes 1572868
  40.0 2.1 %collective-permute-start.9 = (bf16[4,256,256]{2,1,0:T(8,128)(2,1)S(1)}, bf16[4,256,256]{2,1,0:T(8,128)(2,1)S(1)}, u32[]{:S(2)}, u32[]{:S(2)}) collective-permute-start(bf16[4,256,256]{2,1,0:T(8,128)(2,1)S(1)} %collective-permute-done.5.refs_2_), channel_id=1, source_target_pairs={{0,4},{4,0},{1,5},{5,1},{2,6},{6,2},{3,7},{7,3},{8,12},{12,8},{9,1... | collective-permute-start | bytes 1572872 | tf_op jit(solution)/shard_map/ppermute | solution.py:25
  40.0 2.7 %copy-start.11 = (bf16[4,256,256]{2,1,0:T(8,128)(2,1)}, bf16[4,256,256]{2,1,0:T(8,128)(2,1)S(1)}, u32[]{:S(2)}) copy-start(bf16[4,256,256]{2,1,0:T(8,128)(2,1)S(1)} %collective-permute-done.4.refs_1_) | copy-start | bytes 1572868
  40.0 2.6 %collective-permute-start.8 = (bf16[4,256,256]{2,1,0:T(8,128)(2,1)S(1)}, bf16[4,256,256]{2,1,0:T(8,128)(2,1)S(1)}, u32[]{:S(2)}, u32[]{:S(2)}) collective-permute-start(bf16[4,256,256]{2,1,0:T(8,128)(2,1)S(1)} %collective-permute-done.4.refs_1_), channel_id=1, source_target_pairs={{0,4},{4,0},{1,5},{5,1},{2,6},{6,2},{3,7},{7,3},{8,12},{12,8},{9,1... | collective-permute-start | bytes 1572872 | tf_op jit(solution)/shard_map/ppermute | solution.py:25
  40.5 19.3 %collective-permute-start.11 = (bf16[512,128]{1,0:T(8,128)(2,1)}, bf16[512,128]{1,0:T(8,128)(2,1)S(1)}, u32[]{:S(2)}, u32[]{:S(2)}) collective-permute-start(bf16[512,128]{1,0:T(8,128)(2,1)} %bitcast.52), channel_id=1, source_target_pairs={{0,0},{1,32},{2,64},{3,96},{32,1},{33,33},{34,65},{35,97},{64,2},{... | collective-permute-start | bytes 393224 | tf_op jit(solution)/shard_map/ppermute | solution.py:391
  42.1 0.8 copy-start.12
  42.1 1.0 copy-start.13
  42.1 1.1 copy-start.14
  42.6 0.8 copy-start.15
  59.8 0.7 copy-start.19
  60.5 12.5 %collective-permute-start.14 = (f32[8,512]{1,0:T(8,128)}, f32[8,512]{1,0:T(8,128)S(1)}, u32[]{:S(2)}, u32[]{:S(2)}) collective-permute-start(f32[8,512]{1,0:T(8,128)} %get-tuple-element.34), channel_id=1, source_target_pairs={{96,0},{0,32},{32,64},{64,96},{97,1},{1,33},{33,65},{65,97},{98,2}... | collective-permute-start | bytes 49160 | tf_op jit(solution)/shard_map/ppermute | solution.py:21
  63.9 9.1 %collective-permute-start.13 = (f32[8,512]{1,0:T(8,128)}, f32[8,512]{1,0:T(8,128)S(1)}, u32[]{:S(2)}, u32[]{:S(2)}) collective-permute-start(f32[8,512]{1,0:T(8,128)} %get-tuple-element.34), channel_id=1, source_target_pairs={{64,0},{96,32},{0,64},{32,96},{65,1},{97,33},{1,65},{33,97},{66,2}... | collective-permute-start | bytes 49160 | tf_op jit(solution)/shard_map/ppermute | solution.py:21
  68.0 5.0 %collective-permute-start.12 = (f32[8,512]{1,0:T(8,128)}, f32[8,512]{1,0:T(8,128)S(1)}, u32[]{:S(2)}, u32[]{:S(2)}) collective-permute-start(f32[8,512]{1,0:T(8,128)} %get-tuple-element.34), channel_id=1, source_target_pairs={{32,0},{64,32},{96,64},{0,96},{33,1},{65,33},{97,65},{1,97},{34,2}... | collective-permute-start | bytes 49160 | tf_op jit(solution)/shard_map/ppermute | solution.py:21
  69.8 49.4 %collective-permute-start.25 = (bf16[2048,512]{1,0:T(8,128)(2,1)}, bf16[2048,512]{1,0:T(8,128)(2,1)S(1)}, u32[]{:S(2)}, u32[]{:S(2)}) collective-permute-start(bf16[2048,512]{1,0:T(8,128)(2,1)} %get-tuple-element.32.e), channel_id=1, source_target_pairs={{3,0},{0,1},{1,2},{2,3},{7,4},{4,5},{5,6},{6,7},{11,8},{8,9},{9,10... | collective-permute-start | bytes 6291464 | tf_op jit(solution)/shard_map/ppermute | solution.py:21
  69.8 49.4 %collective-permute-start.24 = (bf16[2048,512]{1,0:T(8,128)(2,1)}, bf16[2048,512]{1,0:T(8,128)(2,1)S(1)}, u32[]{:S(2)}, u32[]{:S(2)}) collective-permute-start(bf16[2048,512]{1,0:T(8,128)(2,1)} %get-tuple-element.32.e), channel_id=1, source_target_pairs={{1,0},{2,1},{3,2},{0,3},{5,4},{6,5},{7,6},{4,7},{9,8},{10,9},{11,1... | collective-permute-start | bytes 6291464 | tf_op jit(solution)/shard_map/ppermute | solution.py:21
  73.9 5.0 %collective-permute-start.17 = (f32[8,512]{1,0:T(8,128)S(1)}, f32[8,512]{1,0:T(8,128)S(1)}, u32[]{:S(2)}, u32[]{:S(2)}) collective-permute-start(f32[8,512]{1,0:T(8,128)S(1)} %maximum_maximum_fusion), channel_id=1, source_target_pairs={{24,0},{0,8},{8,16},{16,24},{25,1},{1,9},{9,17},{17,25},{26,2},{2,... | collective-permute-start | bytes 49160 | tf_op jit(solution)/shard_map/ppermute | solution.py:21
  75.0 5.4 %collective-permute-start.16 = (f32[8,512]{1,0:T(8,128)S(1)}, f32[8,512]{1,0:T(8,128)S(1)}, u32[]{:S(2)}, u32[]{:S(2)}) collective-permute-start(f32[8,512]{1,0:T(8,128)S(1)} %maximum_maximum_fusion), channel_id=1, source_target_pairs={{16,0},{24,8},{0,16},{8,24},{17,1},{25,9},{1,17},{9,25},{18,2},{26... | collective-permute-start | bytes 49160 | tf_op jit(solution)/shard_map/ppermute | solution.py:21
  77.1 3.7 %collective-permute-start.15 = (f32[8,512]{1,0:T(8,128)S(1)}, f32[8,512]{1,0:T(8,128)S(1)}, u32[]{:S(2)}, u32[]{:S(2)}) collective-permute-start(f32[8,512]{1,0:T(8,128)S(1)} %maximum_maximum_fusion), channel_id=1, source_target_pairs={{8,0},{16,8},{24,16},{0,24},{9,1},{17,9},{25,17},{1,25},{10,2},{18... | collective-permute-start | bytes 49160 | tf_op jit(solution)/shard_map/ppermute | solution.py:21
  80.9 1.4 copy-start.23
  80.9 1.4 collective-permute-start.18
  82.3 0.6 copy-start.25
  84.3 17.3 %copy-start.26 = (f32[8,512]{1,0:T(8,128)S(1)}, f32[8,512]{1,0:T(8,128)}, u32[]{:S(2)}) copy-start(f32[8,512]{1,0:T(8,128)} %get-tuple-element.36.pack) | copy-start | bytes 49156
  101.0 3.5 %collective-permute-start.19 = (bf16[2,4,256,256]{3,2,1,0:T(8,128)(2,1)}, bf16[2,4,256,256]{3,2,1,0:T(8,128)(2,1)S(1)}, u32[]{:S(2)}, u32[]{:S(2)}) collective-permute-start(bf16[2,4,256,256]{3,2,1,0:T(8,128)(2,1)} %get-tuple-element.38), channel_id=1, source_target_pairs={{0,4},{4,0},{1,5},{5,1},{2,6},{6,2},{3,7},{7,3},{8,12},{12,8},{9,1... | collective-permute-start | bytes 3145736 | tf_op jit(solution)/shard_map/ppermute | solution.py:25
  101.3 4.9 %collective-permute-start.21 = (bf16[2,4,256,256]{3,2,1,0:T(8,128)(2,1)}, bf16[2,4,256,256]{3,2,1,0:T(8,128)(2,1)S(1)}, u32[]{:S(2)}, u32[]{:S(2)}) collective-permute-start(bf16[2,4,256,256]{3,2,1,0:T(8,128)(2,1)} %get-tuple-element.39), channel_id=1, source_target_pairs={{0,4},{4,0},{1,5},{5,1},{2,6},{6,2},{3,7},{7,3},{8,12},{12,8},{9,1... | collective-permute-start | bytes 3145736 | tf_op jit(solution)/shard_map/ppermute | solution.py:25
  101.6 16.4 %collective-permute-start.27 = (f32[8,512]{1,0:T(8,128)S(1)}, f32[8,512]{1,0:T(8,128)S(1)}, u32[]{:S(2)}, u32[]{:S(2)}) collective-permute-start(f32[8,512]{1,0:T(8,128)S(1)} %copy-done.26), channel_id=1, source_target_pairs={{3,0},{0,1},{1,2},{2,3},{7,4},{4,5},{5,6},{6,7},{11,8},{8,9},{9,10... | collective-permute-start | bytes 49160 | tf_op jit(solution)/shard_map/ppermute | solution.py:21
  104.5 4.6 %copy-start.7 = (bf16[2,4,256,256]{3,2,1,0:T(8,128)(2,1)}, bf16[2,4,256,256]{3,2,1,0:T(8,128)(2,1)S(1)}, u32[]{:S(2)}) copy-start(bf16[2,4,256,256]{3,2,1,0:T(8,128)(2,1)S(1)} %collective-permute-done.19) | copy-start | bytes 3145732
  104.5 13.7 %collective-permute-start.26 = (f32[8,512]{1,0:T(8,128)S(1)}, f32[8,512]{1,0:T(8,128)S(1)}, u32[]{:S(2)}, u32[]{:S(2)}) collective-permute-start(f32[8,512]{1,0:T(8,128)S(1)} %copy-done.26), channel_id=1, source_target_pairs={{1,0},{2,1},{3,2},{0,3},{5,4},{6,5},{7,6},{4,7},{9,8},{10,9},{11,1... | collective-permute-start | bytes 49160 | tf_op jit(solution)/shard_map/ppermute | solution.py:21
  109.1 30.3 %collective-permute-start.23 = (bf16[4,256,256]{2,1,0:T(8,128)(2,1)}, bf16[4,256,256]{2,1,0:T(8,128)(2,1)S(1)}, u32[]{:S(2)}, u32[]{:S(2)}) collective-permute-start(bf16[4,256,256]{2,1,0:T(8,128)(2,1)} %get-tuple-element.61), channel_id=1, source_target_pairs={{32,0},{12,4},{40,8},{20,12},{48,16},{28,20},{56,24},{4,28},{64,32... | collective-permute-start | bytes 1572872 | tf_op jit(solution)/shard_map/ppermute | solution.py:36
  118.1 1.2 copy-start.21
  118.1 22.9 %collective-permute-start.22 = (bf16[4,256,256]{2,1,0:T(8,128)(2,1)}, bf16[4,256,256]{2,1,0:T(8,128)(2,1)S(1)}, u32[]{:S(2)}, u32[]{:S(2)}) collective-permute-start(bf16[4,256,256]{2,1,0:T(8,128)(2,1)} %get-tuple-element.62), channel_id=1, source_target_pairs={{64,0},{20,4},{72,8},{28,12},{80,16},{4,20},{88,24},{12,28},{96,32... | collective-permute-start | bytes 1572872 | tf_op jit(solution)/shard_map/ppermute | solution.py:36
  118.2 1.0 copy-start.22
  118.2 22.8 %collective-permute-start.20 = (bf16[4,256,256]{2,1,0:T(8,128)(2,1)S(1)}, bf16[4,256,256]{2,1,0:T(8,128)(2,1)S(1)}, u32[]{:S(2)}, u32[]{:S(2)}) collective-permute-start(bf16[4,256,256]{2,1,0:T(8,128)(2,1)S(1)} %get-tuple-element.63), channel_id=1, source_target_pairs={{96,0},{28,4},{104,8},{4,12},{112,16},{12,20},{120,24},{20,28},{0,... | collective-permute-start | bytes 1572872 | tf_op jit(solution)/shard_map/ppermute | solution.py:36
  119.2 1.3 copy-start
  120.5 1.3 copy-start.1
  125.6 27.3 %collective-permute-start.31 = (bf16[1024,512]{1,0:T(8,128)(2,1)}, bf16[1024,512]{1,0:T(8,128)(2,1)S(1)}, u32[]{:S(2)}, u32[]{:S(2)}) collective-permute-start(bf16[1024,512]{1,0:T(8,128)(2,1)} %get-tuple-element.48), channel_id=1, source_target_pairs={{1,0},{2,1},{3,2},{0,3},{5,4},{6,5},{7,6},{4,7},{9,8},{10,9},{11,1... | collective-permute-start | bytes 3145736 | tf_op jit(solution)/shard_map/ppermute | solution.py:21
  127.8 25.6 %collective-permute-start.32 = (bf16[1024,512]{1,0:T(8,128)(2,1)}, bf16[1024,512]{1,0:T(8,128)(2,1)}, u32[]{:S(2)}, u32[]{:S(2)}) collective-permute-start(bf16[1024,512]{1,0:T(8,128)(2,1)} %get-tuple-element.49), channel_id=1, source_target_pairs={{3,0},{0,1},{1,2},{2,3},{7,4},{4,5},{5,6},{6,7},{11,8},{8,9},{9,10... | collective-permute-start | bytes 3145736 | tf_op jit(solution)/shard_map/ppermute | solution.py:21
  139.4 3.2 %copy-start.8 = (bf16[2,4,256,256]{3,2,1,0:T(8,128)(2,1)S(1)}, bf16[2,4,256,256]{3,2,1,0:T(8,128)(2,1)}, u32[]{:S(2)}) copy-start(bf16[2,4,256,256]{3,2,1,0:T(8,128)(2,1)} %copy-done.7) | copy-start | bytes 3145732
  139.4 1.6 copy-start.3
  139.4 12.5 %collective-permute-start.33 = (f32[8,512]{1,0:T(8,128)S(1)}, f32[8,512]{1,0:T(8,128)S(1)}, u32[]{:S(2)}, u32[]{:S(2)}) collective-permute-start(f32[8,512]{1,0:T(8,128)S(1)} %copy-done.26), channel_id=1, source_target_pairs={{2,0},{3,1},{0,2},{1,3},{6,4},{7,5},{4,6},{5,7},{10,8},{11,9},{8,1... | collective-permute-start | bytes 49160 | tf_op jit(solution)/shard_map/ppermute | solution.py:21
  141.0 0.8 copy-start.4
  141.8 0.8 copy-start.5
  144.5 17.1 %collective-permute-start.30 = (bf16[256,256]{1,0:T(8,128)(2,1)S(1)}, bf16[256,256]{1,0:T(8,128)(2,1)S(1)}, u32[]{:S(2)}, u32[]{:S(2)}) collective-permute-start(bf16[256,256]{1,0:T(8,128)(2,1)S(1)} %get-tuple-element.64), channel_id=1, source_target_pairs={{8,0},{36,4},{16,8},{44,12},{24,16},{52,20},{0,24},{60,28},{40,32}... | collective-permute-start | bytes 393224 | tf_op jit(solution)/shard_map/ppermute | solution.py:36
  146.6 15.0 %collective-permute-start.29 = (bf16[256,256]{1,0:T(8,128)(2,1)S(1)}, bf16[256,256]{1,0:T(8,128)(2,1)S(1)}, u32[]{:S(2)}, u32[]{:S(2)}) collective-permute-start(bf16[256,256]{1,0:T(8,128)(2,1)S(1)} %get-tuple-element.65), channel_id=1, source_target_pairs={{16,0},{68,4},{24,8},{76,12},{0,16},{84,20},{8,24},{92,28},{48,32}... | collective-permute-start | bytes 393224 | tf_op jit(solution)/shard_map/ppermute | solution.py:36
  151.9 1.5 copy-start.24
  151.9 9.7 %collective-permute-start.28 = (bf16[256,256]{1,0:T(8,128)(2,1)S(1)}, bf16[256,256]{1,0:T(8,128)(2,1)S(1)}, u32[]{:S(2)}, u32[]{:S(2)}) collective-permute-start(bf16[256,256]{1,0:T(8,128)(2,1)S(1)} %get-tuple-element.66), channel_id=1, source_target_pairs={{24,0},{100,4},{0,8},{108,12},{8,16},{116,20},{16,24},{124,28},{56... | collective-permute-start | bytes 393224 | tf_op jit(solution)/shard_map/ppermute | solution.py:36
  152.9 1.0 copy-start.6
  161.6 0.7 copy-start.16
  161.6 0.7 copy-start.17
  162.3 0.7 copy-start.18
  164.1 1.4 collective-permute-start.34
Sparse Core Ops, SparseCore 0:
  60.6 47.5 all-gather.2

commit v12 on v11

--- a/solution.py
+++ b/solution.py
@@ -75,22 +75,39 @@
 
 
 def onward_body(ep, em, *refs):
-    low, high = refs[-2:]
-    low[...] = ep[...]
-    high[...] = em[...]
+    low, high, held, get_sem, put_sem = refs[-5:]
+    gets, puts = [], []
+    for n in range(2 * CUT // SUB):
+        k = n // 2
+        rows = pl.ds(k * SUB, SUB)
+        src = ep.at[rows] if n % 2 == 0 else em.at[pl.ds(CUT + k * SUB, SUB)]
+        dst = (low, high)[n % 2].at[rows]
+        gets.append(pltpu.make_async_copy(src, held.at[n], get_sem.at[n]))
+        puts.append(pltpu.make_async_copy(held.at[n], dst, put_sem.at[n]))
+    for copy in gets:
+        copy.start()
+    for get, put in zip(gets, puts):
+        get.wait()
+        put.start()
+    for copy in puts:
+        copy.wait()
 
 
 def onward(ep, em, *others):
     n = len(others)
+    chunks = 2 * CUT // SUB
     half = jax.ShapeDtypeStruct((CUT, ROWS), BF)
-    part = lambda first: pl.BlockSpec((SUB, ROWS), lambda i: (i + first, 0))
     return pl.pallas_call(
         onward_body,
-        grid=(CUT // SUB,),
-        in_specs=[part(0), part(CUT // SUB)] + [HBM] * n,
-        out_specs=[HBM] * n + [part(0), part(0)],
+        in_specs=[HBM] * (n + 2),
+        out_specs=[HBM] * (n + 2),
         out_shape=[jax.ShapeDtypeStruct(a.shape, a.dtype) for a in others] + [half, half],
         input_output_aliases={i + 2: i for i in range(n)},
+        scratch_shapes=[
+            pltpu.VMEM((chunks, SUB, ROWS), BF),
+            pltpu.SemaphoreType.DMA((chunks,)),
+            pltpu.SemaphoreType.DMA((chunks,)),
+        ],
         compiler_params=params(),
         cost_estimate=SMALL,
         name="onward",
@@ -406,14 +423,13 @@
     s = merge_call(s, *(shift(s, "z", d) for d in (1, 2, 3)))
     pack, grad_mix = finish_call(s, sibling(s), st, tid, mix, weight.reshape(1, 128))
     packs = [shift(pack, "y", d) for d in (1, 3, 2)]
-    keep, send0, send1, tgt = hidden_call(at, e, pack, embed)
+    keep, *send, tgt = hidden_call(at, e, pack, embed)
     pack_p, pack_m, low, high = onward(ep, em, packs[0], packs[1])
     low, high = shift(low, "y", 1), shift(high, "y", 3)
-    recv = sibling(send0), sibling(send1)
 
     grad_hidden, grad_embed = scatter(
         keep,
-        recv,
+        [sibling(t) for t in send],
         c,
         lambda: embed_a_call(at, tgt, ep, em, (pack_p, pack_m), feats),
         lambda acc: embed_b_call(at, acc, low, high, packs[2], feats),

time: 175 us -> 174 us (level)
  transfers between devices with their start and end apart: 36 -> 36, of which waited for: 15 -> 15; matrix products, arithmetic and copies ran while one was open for 4% -> 5% of each run, Pallas kernels for 33% -> 33%
where the time goes in v12:
time: 174 us; the launch traced here: 172 us
  Pallas kernels  56.2 us (32%)
  starting transfers between devices  43.6 us (25%)
  waiting for transfers between devices  38.1 us (22%)
  between operations  14.3 us (8%)
  other arithmetic  10.8 us (6%)
  local copies, waits for them, and re-layouts  8.87 us (5%)
    ppermute x13, starting transfers between devices, shift(): return lax.ppermute(a, axis, [((i + d) % 4, i) for i in range(4)])  21.3 us
    ppermute x12, starting transfers between devices, cross(): return lax.ppermute(a, ('x', 'z', 'c'), pairs)  19.2 us
    pallas_call x1, Pallas kernels, hidden_call(): pl.pallas_call(hidden_body, grid_spec=pltpu.PrefetchScalarGridSpec(num_sc...  16.7 us
    ppermute x12, waiting for transfers between devices, cross(): return lax.ppermute(a, ('x', 'z', 'c'), pairs)  16.4 us
    pallas_call x1, Pallas kernels, logits_call(): pl.pallas_call(logits_body, grid_spec=pltpu.PrefetchScalarGridSpec(num_sc...  16.3 us
    ppermute x13, waiting for transfers between devices, shift(): return lax.ppermute(a, axis, [((i + d) % 4, i) for i in range(4)])  13.8 us
    pallas_call x1, Pallas kernels, embed_a_call(): pl.pallas_call(embed_a_body, grid_spec=pltpu.PrefetchScalarGridSpec(num_s...  11.6 us
    unnamed x54, local copies, waits for them, and re-layouts  8.15 us
  transfers between devices with their start and end apart: 36, of which 15 were waited for; matrix products, arithmetic and copies ran while one was open for 5% of the time, Pallas kernels for 33%

profile of v12, /device:TPU:0, one launch (start us, length us, event | category | flops | bytes accessed | tf_op | source)
XLA Modules:
  0.0 171.9 jit_solution(3569241843414596843)
XLA Ops:
  7.2 0.9 broadcast_select_fusion.1
  8.2 0.7 broadcast_subtract_fusion
  8.9 0.6 collective-permute-done
  9.5 3.2 %collective-permute-start.3 = (bf16[256,256]{1,0:T(8,128)(2,1)S(1)}, bf16[256,256]{1,0:T(8,128)(2,1)S(1)}, u32[]{:S(2)}, u32[]{:S(2)}) collective-permute-start(bf16[256,256]{1,0:T(8,128)(2,1)S(1)} %maximum_select_fusion.1), channel_id=1, source_target_pairs={{64,0},{20,4},{72,8},{28,12},{80,16},{4,20},{88,24},{12,28},{96,32... | collective-permute-start | bytes 393224 | tf_op jit(solution)/shard_map/ppermute | solution.py:36
  12.7 1.1 collective-permute-start.2
  13.8 0.9 collective-permute-start.1
  14.7 0.6 pad_add_fusion.refs_1_
  15.3 4.7 %collective-permute-done.1.refs_0_ = bf16[256,256]{1,0:T(8,128)(2,1)S(1)} collective-permute-done((bf16[256,256]{1,0:T(8,128)(2,1)S(1)}, bf16[256,256]{1,0:T(8,128)(2,1)S(1)}, u32[]{:S(2)}, u32[]{:S(2)}) %collective-permute-start.1) | collective-permute-done | bytes 131104 | tf_op jit(solution)/shard_map/ppermute | solution.py:36
  20.0 0.6 tile.2
  20.7 1.0 pad_maximum_fusion.refs_0_
  21.6 2.0 %collective-permute-start.6 = (bf16[4,256,256]{2,1,0:T(8,128)(2,1)S(1)}, bf16[4,256,256]{2,1,0:T(8,128)(2,1)S(1)}, u32[]{:S(2)}, u32[]{:S(2)}) collective-permute-start(bf16[4,256,256]{2,1,0:T(8,128)(2,1)S(1)} %pad_maximum_fusion.refs_0_), channel_id=1, source_target_pairs={{24,0},{100,4},{0,8},{108,12},{8,16},{116,20},{16,24},{124,28},{56... | collective-permute-start | bytes 1572872 | tf_op jit(solution)/shard_map/ppermute | solution.py:36
  23.6 3.6 %collective-permute-start.5 = (bf16[4,256,256]{2,1,0:T(8,128)(2,1)S(1)}, bf16[4,256,256]{2,1,0:T(8,128)(2,1)S(1)}, u32[]{:S(2)}, u32[]{:S(2)}) collective-permute-start(bf16[4,256,256]{2,1,0:T(8,128)(2,1)S(1)} %pad_maximum_fusion.refs_0_), channel_id=1, source_target_pairs={{16,0},{68,4},{24,8},{76,12},{0,16},{84,20},{8,24},{92,28},{48,32}... | collective-permute-start | bytes 1572872 | tf_op jit(solution)/shard_map/ppermute | solution.py:36
  27.2 1.0 collective-permute-start.4
  28.2 4.7 %collective-permute-done.6.refs_3_ = bf16[4,256,256]{2,1,0:T(8,128)(2,1)S(1)} collective-permute-done((bf16[4,256,256]{2,1,0:T(8,128)(2,1)S(1)}, bf16[4,256,256]{2,1,0:T(8,128)(2,1)S(1)}, u32[]{:S(2)}, u32[]{:S(2)}) %collective-permute-start.6) | collective-permute-done | bytes 524320 | tf_op jit(solution)/shard_map/ppermute | solution.py:36
  32.9 7.1 %collective-permute-done.5.refs_2_ = bf16[4,256,256]{2,1,0:T(8,128)(2,1)S(1)} collective-permute-done((bf16[4,256,256]{2,1,0:T(8,128)(2,1)S(1)}, bf16[4,256,256]{2,1,0:T(8,128)(2,1)S(1)}, u32[]{:S(2)}, u32[]{:S(2)}) %collective-permute-start.5) | collective-permute-done | bytes 524320 | tf_op jit(solution)/shard_map/ppermute | solution.py:36
  40.0 0.5 collective-permute-start.8
  40.5 1.6 collective-permute-start.11
  42.1 0.5 collective-permute-done.8.refs_5_
  43.4 16.3 %logits.1 = (bf16[2048,512]{1,0:T(8,128)(2,1)}, f32[8,512]{1,0:T(8,128)}, f32[8,512]{1,0:T(8,128)}) custom-call(s32[4]{0:T(128)} %get-tuple-element.29.at, bf16[4,256,256]{2,1,0:T(8,128)(2,1)} %copy-done.2, bf16[4,256,256]{2,1,0:T(8,128)(2,1)} %copy-done.11, bf16[4,256,256]{2,1,0:T(8,128)(2,1)} %copy-done.10, bf16[4,256,256]{2,1,0:T(8,128)(2,1)} %copy-done.9, ...), custom_call_target="tpu_custom_call" | custom-call | flops 1000 | bytes 1000 | tf_op jit(solution)/shard_map/logits/pallas_call | solution.py:174
  59.8 0.6 copy-done.19
  60.5 3.4 %collective-permute-start.14 = (f32[8,512]{1,0:T(8,128)}, f32[8,512]{1,0:T(8,128)S(1)}, u32[]{:S(2)}, u32[]{:S(2)}) collective-permute-start(f32[8,512]{1,0:T(8,128)} %get-tuple-element.34), channel_id=1, source_target_pairs={{96,0},{0,32},{32,64},{64,96},{97,1},{1,33},{33,65},{65,97},{98,2}... | collective-permute-start | bytes 49160 | tf_op jit(solution)/shard_map/ppermute | solution.py:21
  63.9 4.1 %collective-permute-start.13 = (f32[8,512]{1,0:T(8,128)}, f32[8,512]{1,0:T(8,128)S(1)}, u32[]{:S(2)}, u32[]{:S(2)}) collective-permute-start(f32[8,512]{1,0:T(8,128)} %get-tuple-element.34), channel_id=1, source_target_pairs={{64,0},{96,32},{0,64},{32,96},{65,1},{97,33},{1,65},{33,97},{66,2}... | collective-permute-start | bytes 49160 | tf_op jit(solution)/shard_map/ppermute | solution.py:21
  68.0 1.6 collective-permute-start.12
  69.8 3.2 %collective-permute-start.24 = (bf16[2048,512]{1,0:T(8,128)(2,1)}, bf16[2048,512]{1,0:T(8,128)(2,1)S(1)}, u32[]{:S(2)}, u32[]{:S(2)}) collective-permute-start(bf16[2048,512]{1,0:T(8,128)(2,1)} %get-tuple-element.32.e), channel_id=1, source_target_pairs={{1,0},{2,1},{3,2},{0,3},{5,4},{6,5},{7,6},{4,7},{9,8},{10,9},{11,1... | collective-permute-start | bytes 6291464 | tf_op jit(solution)/shard_map/ppermute | solution.py:21
  73.0 0.9 fusion.11
  73.9 1.0 collective-permute-start.17
  75.0 2.1 %collective-permute-start.16 = (f32[8,512]{1,0:T(8,128)S(1)}, f32[8,512]{1,0:T(8,128)S(1)}, u32[]{:S(2)}, u32[]{:S(2)}) collective-permute-start(f32[8,512]{1,0:T(8,128)S(1)} %maximum_maximum_fusion), channel_id=1, source_target_pairs={{16,0},{24,8},{0,16},{8,24},{17,1},{25,9},{1,17},{9,25},{18,2},{26... | collective-permute-start | bytes 49160 | tf_op jit(solution)/shard_map/ppermute | solution.py:21
  77.1 1.5 collective-permute-start.15
  78.6 0.3 collective-permute-done.17
  78.9 1.4 collective-permute-done.16
  80.3 0.5 collective-permute-done.15
  81.1 1.2 collective-permute-done.18.b
  82.3 0.6 copy-done.25
  82.9 1.4 finish.1
  84.3 16.7 %hidden.1 = (bf16[4,4,256,256]{3,2,1,0:T(8,128)(2,1)}, bf16[2,4,256,256]{3,2,1,0:T(8,128)(2,1)}, bf16[2,4,256,256]{3,2,1,0:T(8,128)(2,1)}, bf16[2048,512]{1,0:T(8,128)(2,1)}) custom-call(s32[4]{0:T(128)} %get-tuple-element.29.at, bf16[2048,512]{1,0:T(8,128)(2,1)} %get-tuple-element.32.e, f32[8,512]{1,0:T(8,128)} %get-tuple-element.36.pack, ...), custom_call_target="tpu_custom_call" | custom-call | flops 1000 | bytes 1000 | tf_op jit(solution)/shard_map/hidden/pallas_call | solution.py:292
  101.3 0.3 collective-permute-start.21
  101.6 2.9 %collective-permute-done.19 = bf16[2,4,256,256]{3,2,1,0:T(8,128)(2,1)S(1)} collective-permute-done((bf16[2,4,256,256]{3,2,1,0:T(8,128)(2,1)}, bf16[2,4,256,256]{3,2,1,0:T(8,128)(2,1)S(1)}, u32[]{:S(2)}, u32[]{:S(2)}) %collective-permute-start.19) | collective-permute-done | bytes 1048608 | tf_op jit(solution)/shard_map/ppermute | solution.py:25
  104.5 0.3 collective-permute-start.26
  104.8 1.4 collective-permute-done.21
  106.2 2.9 %fusion.4 = (bf16[4,256,256]{2,1,0:T(8,128)(2,1)}, bf16[4,256,256]{2,1,0:T(8,128)(2,1)}, bf16[4,256,256]{2,1,0:T(8,128)(2,1)S(1)}) fusion(bf16[2,4,256,256]{3,2,1,0:T(8,128)(2,1)S(1)} %collective-permute-done.21, bf16[4,4,256,256]{3,2,1,0:T(8,128)(2,1)} %get-tuple-element.37, bf16[2,4,256,256]{3,2,1,0:T(8,128)(2,1)S(1)} %collective-permute-done.19), kind=kLoop, calls=%fused_computation.8 | loop fusion | flops 3145728 | bytes 4718592 | tf_op jit(solution)/shard_map/convert_element_type | solution.py:324
  109.1 1.7 collective-permute-start.23
  110.8 7.3 %collective-permute-done.27.refs_1_ = f32[8,512]{1,0:T(8,128)S(1)} collective-permute-done((f32[8,512]{1,0:T(8,128)S(1)}, f32[8,512]{1,0:T(8,128)S(1)}, u32[]{:S(2)}, u32[]{:S(2)}) %collective-permute-start.27) | collective-permute-done | bytes 16416 | tf_op jit(solution)/shard_map/ppermute | solution.py:21
  118.2 1.0 collective-permute-start.20
  119.2 1.3 copy-done
  120.5 1.3 copy-done.1
  121.8 2.4 %onward.1 = (f32[8,512]{1,0:T(8,128)}, f32[8,512]{1,0:T(8,128)}, bf16[1024,512]{1,0:T(8,128)(2,1)}, bf16[1024,512]{1,0:T(8,128)(2,1)}) custom-call(bf16[2048,512]{1,0:T(8,128)(2,1)} %copy-done.1, bf16[2048,512]{1,0:T(8,128)(2,1)} %copy-done, f32[8,512]{1,0:T(8,128)} %copy-done.22, f32[8,512]{1,0:T(8,128)} %copy-done.21), custom_call_target="tpu_custom_call", output_to_operand_aliasing={{0}: (2, {}), {1}: (3, {})} | custom-call | flops 1000 | bytes 1000 | tf_op jit(solution)/shard_map/onward/pallas_call | solution.py:100
  124.3 2.2 %collective-permute-start.31 = (bf16[1024,512]{1,0:T(8,128)(2,1)}, bf16[1024,512]{1,0:T(8,128)(2,1)S(1)}, u32[]{:S(2)}, u32[]{:S(2)}) collective-permute-start(bf16[1024,512]{1,0:T(8,128)(2,1)} %get-tuple-element.48), channel_id=1, source_target_pairs={{1,0},{2,1},{3,2},{0,3},{5,4},{6,5},{7,6},{4,7},{9,8},{10,9},{11,1... | collective-permute-start | bytes 3145736 | tf_op jit(solution)/shard_map/ppermute | solution.py:21
  126.5 11.6 %embed_a.1.refs_3_ = bf16[2048,1024]{1,0:T(8,128)(2,1)} custom-call(s32[4]{0:T(128)} %get-tuple-element.29.at, bf16[2048,512]{1,0:T(8,128)(2,1)} %get-tuple-element.40.tgt, bf16[2048,512]{1,0:T(8,128)(2,1)} %copy-done.1, bf16[2048,512]{1,0:T(8,128)(2,1)} %copy-done, f32[8,512]{1,0:T(8,128)} %get-tuple-element.41.pack_p, f32[8,512]{1,0:T(8,128)} %get-tuple-element.42.pack_m, ...), custom_call_target="tpu_custom_call" | custom-call | flops 1000 | bytes 1000 | tf_op jit(solution)/shard_map/embed_a/pallas_call | solution.py:356
  138.2 1.6 collective-permute-start.33
  139.8 0.8 copy-done.4
  140.6 0.8 copy-done.5
  141.4 1.8 %fusion.14 = (bf16[4,256,256]{2,1,0:T(8,128)(2,1)S(1)}, f32[4,256,256]{2,1,0:T(8,128)S(1)}) fusion(bf16[4,256,256]{2,1,0:T(8,128)(2,1)} %get-tuple-element.46, bf16[4,256,256]{2,1,0:T(8,128)(2,1)} %get-tuple-element.45, bf16[4,256,256]{2,1,0:T(8,128)(2,1)} %get-tuple-element.44, bf16[2,4,256,256]{3,2,1,0:T(8,128)(2,1)S(1)} %copy-done.8, ...), kind=kLoop, calls=%fused_computation.48 | loop fusion | flops 2621440 | bytes 4194304 | tf_op jit(solution)/shard_map/convert.2
  143.3 2.1 %collective-permute-start.30 = (bf16[256,256]{1,0:T(8,128)(2,1)S(1)}, bf16[256,256]{1,0:T(8,128)(2,1)S(1)}, u32[]{:S(2)}, u32[]{:S(2)}) collective-permute-start(bf16[256,256]{1,0:T(8,128)(2,1)S(1)} %get-tuple-element.64), channel_id=1, source_target_pairs={{8,0},{36,4},{16,8},{44,12},{24,16},{52,20},{0,24},{60,28},{40,32}... | collective-permute-start | bytes 393224 | tf_op jit(solution)/shard_map/ppermute | solution.py:36
  145.4 1.4 collective-permute-start.29
  146.8 3.9 %collective-permute-done.33.pack = f32[8,512]{1,0:T(8,128)S(1)} collective-permute-done((f32[8,512]{1,0:T(8,128)S(1)}, f32[8,512]{1,0:T(8,128)S(1)}, u32[]{:S(2)}, u32[]{:S(2)}) %collective-permute-start.33) | collective-permute-done | bytes 16416 | tf_op jit(solution)/shard_map/ppermute | solution.py:21
  150.7 1.0 collective-permute-start.28
  151.7 0.4 collective-permute-done.32.high
  152.1 0.5 copy-done.6
  152.7 7.7 %embed_b.1.refs_3_ = bf16[2048,1024]{1,0:T(8,128)(2,1)} custom-call(s32[4]{0:T(128)} %get-tuple-element.29.at, bf16[2048,1024]{1,0:T(8,128)(2,1)} %get-tuple-element.47.acc, bf16[1024,512]{1,0:T(8,128)(2,1)} %copy-done.6, bf16[1024,512]{1,0:T(8,128)(2,1)} %collective-permute-done.32.high, f32[8,512]{1,0:T(8,128)} %copy-done.24, ...), custom_call_target="tpu_custom_call" | custom-call | flops 1000 | bytes 1000 | tf_op jit(solution)/shard_map/embed_b/pallas_call | solution.py:380
  160.4 0.6 copy-done.16
  161.1 0.7 copy-done.18
  161.8 1.1 fusion.7
  163.0 1.3 collective-permute-done.34
  164.3 0.7 maximum_select_fusion
  (92 shorter events, 2.3 us)
Async XLA Ops:
  7.2 119.4 %all-gather.3.cloned.1.call-start = ((), (), s32[]{:S(2)}) async-start(), calls=%async_computation | async-start | bytes 4325376 | tf_op jit(solution)/shard_map/all_gather | solution.py:419
  8.1 1.3 collective-permute-start
  9.5 11.2 %collective-permute-start.3 = (bf16[256,256]{1,0:T(8,128)(2,1)S(1)}, bf16[256,256]{1,0:T(8,128)(2,1)S(1)}, u32[]{:S(2)}, u32[]{:S(2)}) collective-permute-start(bf16[256,256]{1,0:T(8,128)(2,1)S(1)} %maximum_select_fusion.1), channel_id=1, source_target_pairs={{64,0},{20,4},{72,8},{28,12},{80,16},{4,20},{88,24},{12,28},{96,32... | collective-permute-start | bytes 393224 | tf_op jit(solution)/shard_map/ppermute | solution.py:36
  12.7 8.0 %collective-permute-start.2 = (bf16[256,256]{1,0:T(8,128)(2,1)S(1)}, bf16[256,256]{1,0:T(8,128)(2,1)S(1)}, u32[]{:S(2)}, u32[]{:S(2)}) collective-permute-start(bf16[256,256]{1,0:T(8,128)(2,1)S(1)} %maximum_select_fusion.1), channel_id=1, source_target_pairs={{32,0},{12,4},{40,8},{20,12},{48,16},{28,20},{56,24},{4,28},{64,32... | collective-permute-start | bytes 393224 | tf_op jit(solution)/shard_map/ppermute | solution.py:36
  13.8 6.2 %collective-permute-start.1 = (bf16[256,256]{1,0:T(8,128)(2,1)S(1)}, bf16[256,256]{1,0:T(8,128)(2,1)S(1)}, u32[]{:S(2)}, u32[]{:S(2)}) collective-permute-start(bf16[256,256]{1,0:T(8,128)(2,1)S(1)} %maximum_select_fusion.1), channel_id=1, source_target_pairs={{96,0},{28,4},{104,8},{4,12},{112,16},{12,20},{120,24},{20,28},{0,... | collective-permute-start | bytes 393224 | tf_op jit(solution)/shard_map/ppermute | solution.py:36
  20.0 0.7 copy-start.20
  21.6 21.0 %copy-start.2 = (bf16[4,256,256]{2,1,0:T(8,128)(2,1)}, bf16[4,256,256]{2,1,0:T(8,128)(2,1)S(1)}, u32[]{:S(2)}) copy-start(bf16[4,256,256]{2,1,0:T(8,128)(2,1)S(1)} %pad_maximum_fusion.refs_0_) | copy-start | bytes 1572868
  21.6 11.3 %collective-permute-start.6 = (bf16[4,256,256]{2,1,0:T(8,128)(2,1)S(1)}, bf16[4,256,256]{2,1,0:T(8,128)(2,1)S(1)}, u32[]{:S(2)}, u32[]{:S(2)}) collective-permute-start(bf16[4,256,256]{2,1,0:T(8,128)(2,1)S(1)} %pad_maximum_fusion.refs_0_), channel_id=1, source_target_pairs={{24,0},{100,4},{0,8},{108,12},{8,16},{116,20},{16,24},{124,28},{56... | collective-permute-start | bytes 1572872 | tf_op jit(solution)/shard_map/ppermute | solution.py:36
  23.6 16.4 %collective-permute-start.5 = (bf16[4,256,256]{2,1,0:T(8,128)(2,1)S(1)}, bf16[4,256,256]{2,1,0:T(8,128)(2,1)S(1)}, u32[]{:S(2)}, u32[]{:S(2)}) collective-permute-start(bf16[4,256,256]{2,1,0:T(8,128)(2,1)S(1)} %pad_maximum_fusion.refs_0_), channel_id=1, source_target_pairs={{16,0},{68,4},{24,8},{76,12},{0,16},{84,20},{8,24},{92,28},{48,32}... | collective-permute-start | bytes 1572872 | tf_op jit(solution)/shard_map/ppermute | solution.py:36
  27.2 12.8 %collective-permute-start.4 = (bf16[4,256,256]{2,1,0:T(8,128)(2,1)S(1)}, bf16[4,256,256]{2,1,0:T(8,128)(2,1)S(1)}, u32[]{:S(2)}, u32[]{:S(2)}) collective-permute-start(bf16[4,256,256]{2,1,0:T(8,128)(2,1)S(1)} %pad_maximum_fusion.refs_0_), channel_id=1, source_target_pairs={{8,0},{36,4},{16,8},{44,12},{24,16},{52,20},{0,24},{60,28},{40,32}... | collective-permute-start | bytes 1572872 | tf_op jit(solution)/shard_map/ppermute | solution.py:36
  28.2 13.8 %collective-permute-start.7 = (bf16[4,256,256]{2,1,0:T(8,128)(2,1)S(1)}, bf16[4,256,256]{2,1,0:T(8,128)(2,1)S(1)}, u32[]{:S(2)}, u32[]{:S(2)}) collective-permute-start(bf16[4,256,256]{2,1,0:T(8,128)(2,1)S(1)} %pad_maximum_fusion.refs_0_), channel_id=1, source_target_pairs={{0,4},{4,0},{1,5},{5,1},{2,6},{6,2},{3,7},{7,3},{8,12},{12,8},{9,1... | collective-permute-start | bytes 1572872 | tf_op jit(solution)/shard_map/ppermute | solution.py:25
  32.9 9.7 %copy-start.9 = (bf16[4,256,256]{2,1,0:T(8,128)(2,1)}, bf16[4,256,256]{2,1,0:T(8,128)(2,1)S(1)}, u32[]{:S(2)}) copy-start(bf16[4,256,256]{2,1,0:T(8,128)(2,1)S(1)} %collective-permute-done.6.refs_3_) | copy-start | bytes 1572868
  32.9 9.2 %collective-permute-start.10 = (bf16[4,256,256]{2,1,0:T(8,128)(2,1)S(1)}, bf16[4,256,256]{2,1,0:T(8,128)(2,1)S(1)}, u32[]{:S(2)}, u32[]{:S(2)}) collective-permute-start(bf16[4,256,256]{2,1,0:T(8,128)(2,1)S(1)} %collective-permute-done.6.refs_3_), channel_id=1, source_target_pairs={{0,4},{4,0},{1,5},{5,1},{2,6},{6,2},{3,7},{7,3},{8,12},{12,8},{9,1... | collective-permute-start | bytes 1572872 | tf_op jit(solution)/shard_map/ppermute | solution.py:25
  40.0 2.7 %copy-start.10 = (bf16[4,256,256]{2,1,0:T(8,128)(2,1)}, bf16[4,256,256]{2,1,0:T(8,128)(2,1)S(1)}, u32[]{:S(2)}) copy-start(bf16[4,256,256]{2,1,0:T(8,128)(2,1)S(1)} %collective-permute-done.5.refs_2_) | copy-start | bytes 1572868
  40.0 2.1 %collective-permute-start.9 = (bf16[4,256,256]{2,1,0:T(8,128)(2,1)S(1)}, bf16[4,256,256]{2,1,0:T(8,128)(2,1)S(1)}, u32[]{:S(2)}, u32[]{:S(2)}) collective-permute-start(bf16[4,256,256]{2,1,0:T(8,128)(2,1)S(1)} %collective-permute-done.5.refs_2_), channel_id=1, source_target_pairs={{0,4},{4,0},{1,5},{5,1},{2,6},{6,2},{3,7},{7,3},{8,12},{12,8},{9,1... | collective-permute-start | bytes 1572872 | tf_op jit(solution)/shard_map/ppermute | solution.py:25
  40.0 2.7 %copy-start.11 = (bf16[4,256,256]{2,1,0:T(8,128)(2,1)}, bf16[4,256,256]{2,1,0:T(8,128)(2,1)S(1)}, u32[]{:S(2)}) copy-start(bf16[4,256,256]{2,1,0:T(8,128)(2,1)S(1)} %collective-permute-done.4.refs_1_) | copy-start | bytes 1572868
  40.0 2.6 %collective-permute-start.8 = (bf16[4,256,256]{2,1,0:T(8,128)(2,1)S(1)}, bf16[4,256,256]{2,1,0:T(8,128)(2,1)S(1)}, u32[]{:S(2)}, u32[]{:S(2)}) collective-permute-start(bf16[4,256,256]{2,1,0:T(8,128)(2,1)S(1)} %collective-permute-done.4.refs_1_), channel_id=1, source_target_pairs={{0,4},{4,0},{1,5},{5,1},{2,6},{6,2},{3,7},{7,3},{8,12},{12,8},{9,1... | collective-permute-start | bytes 1572872 | tf_op jit(solution)/shard_map/ppermute | solution.py:25
  40.5 19.3 %collective-permute-start.11 = (bf16[512,128]{1,0:T(8,128)(2,1)}, bf16[512,128]{1,0:T(8,128)(2,1)S(1)}, u32[]{:S(2)}, u32[]{:S(2)}) collective-permute-start(bf16[512,128]{1,0:T(8,128)(2,1)} %bitcast.52), channel_id=1, source_target_pairs={{0,0},{1,32},{2,64},{3,96},{32,1},{33,33},{34,65},{35,97},{64,2},{... | collective-permute-start | bytes 393224 | tf_op jit(solution)/shard_map/ppermute | solution.py:408
  42.1 0.8 copy-start.12
  42.1 1.0 copy-start.13
  42.1 1.1 copy-start.14
  42.6 0.8 copy-start.15
  59.8 0.7 copy-start.19
  60.5 12.5 %collective-permute-start.14 = (f32[8,512]{1,0:T(8,128)}, f32[8,512]{1,0:T(8,128)S(1)}, u32[]{:S(2)}, u32[]{:S(2)}) collective-permute-start(f32[8,512]{1,0:T(8,128)} %get-tuple-element.34), channel_id=1, source_target_pairs={{96,0},{0,32},{32,64},{64,96},{97,1},{1,33},{33,65},{65,97},{98,2}... | collective-permute-start | bytes 49160 | tf_op jit(solution)/shard_map/ppermute | solution.py:21
  63.9 9.1 %collective-permute-start.13 = (f32[8,512]{1,0:T(8,128)}, f32[8,512]{1,0:T(8,128)S(1)}, u32[]{:S(2)}, u32[]{:S(2)}) collective-permute-start(f32[8,512]{1,0:T(8,128)} %get-tuple-element.34), channel_id=1, source_target_pairs={{64,0},{96,32},{0,64},{32,96},{65,1},{97,33},{1,65},{33,97},{66,2}... | collective-permute-start | bytes 49160 | tf_op jit(solution)/shard_map/ppermute | solution.py:21
  68.0 5.0 %collective-permute-start.12 = (f32[8,512]{1,0:T(8,128)}, f32[8,512]{1,0:T(8,128)S(1)}, u32[]{:S(2)}, u32[]{:S(2)}) collective-permute-start(f32[8,512]{1,0:T(8,128)} %get-tuple-element.34), channel_id=1, source_target_pairs={{32,0},{64,32},{96,64},{0,96},{33,1},{65,33},{97,65},{1,97},{34,2}... | collective-permute-start | bytes 49160 | tf_op jit(solution)/shard_map/ppermute | solution.py:21
  69.8 49.4 %collective-permute-start.25 = (bf16[2048,512]{1,0:T(8,128)(2,1)}, bf16[2048,512]{1,0:T(8,128)(2,1)S(1)}, u32[]{:S(2)}, u32[]{:S(2)}) collective-permute-start(bf16[2048,512]{1,0:T(8,128)(2,1)} %get-tuple-element.32.e), channel_id=1, source_target_pairs={{3,0},{0,1},{1,2},{2,3},{7,4},{4,5},{5,6},{6,7},{11,8},{8,9},{9,10... | collective-permute-start | bytes 6291464 | tf_op jit(solution)/shard_map/ppermute | solution.py:21
  69.8 49.4 %collective-permute-start.24 = (bf16[2048,512]{1,0:T(8,128)(2,1)}, bf16[2048,512]{1,0:T(8,128)(2,1)S(1)}, u32[]{:S(2)}, u32[]{:S(2)}) collective-permute-start(bf16[2048,512]{1,0:T(8,128)(2,1)} %get-tuple-element.32.e), channel_id=1, source_target_pairs={{1,0},{2,1},{3,2},{0,3},{5,4},{6,5},{7,6},{4,7},{9,8},{10,9},{11,1... | collective-permute-start | bytes 6291464 | tf_op jit(solution)/shard_map/ppermute | solution.py:21
  73.9 5.0 %collective-permute-start.17 = (f32[8,512]{1,0:T(8,128)S(1)}, f32[8,512]{1,0:T(8,128)S(1)}, u32[]{:S(2)}, u32[]{:S(2)}) collective-permute-start(f32[8,512]{1,0:T(8,128)S(1)} %maximum_maximum_fusion), channel_id=1, source_target_pairs={{24,0},{0,8},{8,16},{16,24},{25,1},{1,9},{9,17},{17,25},{26,2},{2,... | collective-permute-start | bytes 49160 | tf_op jit(solution)/shard_map/ppermute | solution.py:21
  75.0 5.4 %collective-permute-start.16 = (f32[8,512]{1,0:T(8,128)S(1)}, f32[8,512]{1,0:T(8,128)S(1)}, u32[]{:S(2)}, u32[]{:S(2)}) collective-permute-start(f32[8,512]{1,0:T(8,128)S(1)} %maximum_maximum_fusion), channel_id=1, source_target_pairs={{16,0},{24,8},{0,16},{8,24},{17,1},{25,9},{1,17},{9,25},{18,2},{26... | collective-permute-start | bytes 49160 | tf_op jit(solution)/shard_map/ppermute | solution.py:21
  77.1 3.7 %collective-permute-start.15 = (f32[8,512]{1,0:T(8,128)S(1)}, f32[8,512]{1,0:T(8,128)S(1)}, u32[]{:S(2)}, u32[]{:S(2)}) collective-permute-start(f32[8,512]{1,0:T(8,128)S(1)} %maximum_maximum_fusion), channel_id=1, source_target_pairs={{8,0},{16,8},{24,16},{0,24},{9,1},{17,9},{25,17},{1,25},{10,2},{18... | collective-permute-start | bytes 49160 | tf_op jit(solution)/shard_map/ppermute | solution.py:21
  80.9 1.4 copy-start.23
  80.9 1.4 collective-permute-start.18
  82.3 0.6 copy-start.25
  84.3 17.3 %copy-start.26 = (f32[8,512]{1,0:T(8,128)S(1)}, f32[8,512]{1,0:T(8,128)}, u32[]{:S(2)}) copy-start(f32[8,512]{1,0:T(8,128)} %get-tuple-element.36.pack) | copy-start | bytes 49156
  101.0 3.5 %collective-permute-start.19 = (bf16[2,4,256,256]{3,2,1,0:T(8,128)(2,1)}, bf16[2,4,256,256]{3,2,1,0:T(8,128)(2,1)S(1)}, u32[]{:S(2)}, u32[]{:S(2)}) collective-permute-start(bf16[2,4,256,256]{3,2,1,0:T(8,128)(2,1)} %get-tuple-element.38), channel_id=1, source_target_pairs={{0,4},{4,0},{1,5},{5,1},{2,6},{6,2},{3,7},{7,3},{8,12},{12,8},{9,1... | collective-permute-start | bytes 3145736 | tf_op jit(solution)/shard_map/ppermute | solution.py:25
  101.3 4.9 %collective-permute-start.21 = (bf16[2,4,256,256]{3,2,1,0:T(8,128)(2,1)}, bf16[2,4,256,256]{3,2,1,0:T(8,128)(2,1)S(1)}, u32[]{:S(2)}, u32[]{:S(2)}) collective-permute-start(bf16[2,4,256,256]{3,2,1,0:T(8,128)(2,1)} %get-tuple-element.39), channel_id=1, source_target_pairs={{0,4},{4,0},{1,5},{5,1},{2,6},{6,2},{3,7},{7,3},{8,12},{12,8},{9,1... | collective-permute-start | bytes 3145736 | tf_op jit(solution)/shard_map/ppermute | solution.py:25
  101.6 16.4 %collective-permute-start.27 = (f32[8,512]{1,0:T(8,128)S(1)}, f32[8,512]{1,0:T(8,128)S(1)}, u32[]{:S(2)}, u32[]{:S(2)}) collective-permute-start(f32[8,512]{1,0:T(8,128)S(1)} %copy-done.26), channel_id=1, source_target_pairs={{3,0},{0,1},{1,2},{2,3},{7,4},{4,5},{5,6},{6,7},{11,8},{8,9},{9,10... | collective-permute-start | bytes 49160 | tf_op jit(solution)/shard_map/ppermute | solution.py:21
  104.5 4.6 %copy-start.7 = (bf16[2,4,256,256]{3,2,1,0:T(8,128)(2,1)}, bf16[2,4,256,256]{3,2,1,0:T(8,128)(2,1)S(1)}, u32[]{:S(2)}) copy-start(bf16[2,4,256,256]{3,2,1,0:T(8,128)(2,1)S(1)} %collective-permute-done.19) | copy-start | bytes 3145732
  104.5 13.7 %collective-permute-start.26 = (f32[8,512]{1,0:T(8,128)S(1)}, f32[8,512]{1,0:T(8,128)S(1)}, u32[]{:S(2)}, u32[]{:S(2)}) collective-permute-start(f32[8,512]{1,0:T(8,128)S(1)} %copy-done.26), channel_id=1, source_target_pairs={{1,0},{2,1},{3,2},{0,3},{5,4},{6,5},{7,6},{4,7},{9,8},{10,9},{11,1... | collective-permute-start | bytes 49160 | tf_op jit(solution)/shard_map/ppermute | solution.py:21
  109.1 29.1 %collective-permute-start.23 = (bf16[4,256,256]{2,1,0:T(8,128)(2,1)}, bf16[4,256,256]{2,1,0:T(8,128)(2,1)S(1)}, u32[]{:S(2)}, u32[]{:S(2)}) collective-permute-start(bf16[4,256,256]{2,1,0:T(8,128)(2,1)} %get-tuple-element.61), channel_id=1, source_target_pairs={{32,0},{12,4},{40,8},{20,12},{48,16},{28,20},{56,24},{4,28},{64,32... | collective-permute-start | bytes 1572872 | tf_op jit(solution)/shard_map/ppermute | solution.py:36
  118.1 1.2 copy-start.21
  118.1 21.7 %collective-permute-start.22 = (bf16[4,256,256]{2,1,0:T(8,128)(2,1)}, bf16[4,256,256]{2,1,0:T(8,128)(2,1)S(1)}, u32[]{:S(2)}, u32[]{:S(2)}) collective-permute-start(bf16[4,256,256]{2,1,0:T(8,128)(2,1)} %get-tuple-element.62), channel_id=1, source_target_pairs={{64,0},{20,4},{72,8},{28,12},{80,16},{4,20},{88,24},{12,28},{96,32... | collective-permute-start | bytes 1572872 | tf_op jit(solution)/shard_map/ppermute | solution.py:36
  118.2 1.0 copy-start.22
  118.2 21.6 %collective-permute-start.20 = (bf16[4,256,256]{2,1,0:T(8,128)(2,1)S(1)}, bf16[4,256,256]{2,1,0:T(8,128)(2,1)S(1)}, u32[]{:S(2)}, u32[]{:S(2)}) collective-permute-start(bf16[4,256,256]{2,1,0:T(8,128)(2,1)S(1)} %get-tuple-element.63), channel_id=1, source_target_pairs={{96,0},{28,4},{104,8},{4,12},{112,16},{12,20},{120,24},{20,28},{0,... | collective-permute-start | bytes 1572872 | tf_op jit(solution)/shard_map/ppermute | solution.py:36
  119.2 1.3 copy-start
  120.5 1.3 copy-start.1
  124.3 27.4 %collective-permute-start.31 = (bf16[1024,512]{1,0:T(8,128)(2,1)}, bf16[1024,512]{1,0:T(8,128)(2,1)S(1)}, u32[]{:S(2)}, u32[]{:S(2)}) collective-permute-start(bf16[1024,512]{1,0:T(8,128)(2,1)} %get-tuple-element.48), channel_id=1, source_target_pairs={{1,0},{2,1},{3,2},{0,3},{5,4},{6,5},{7,6},{4,7},{9,8},{10,9},{11,1... | collective-permute-start | bytes 3145736 | tf_op jit(solution)/shard_map/ppermute | solution.py:21
  126.5 25.6 %collective-permute-start.32 = (bf16[1024,512]{1,0:T(8,128)(2,1)}, bf16[1024,512]{1,0:T(8,128)(2,1)}, u32[]{:S(2)}, u32[]{:S(2)}) collective-permute-start(bf16[1024,512]{1,0:T(8,128)(2,1)} %get-tuple-element.49), channel_id=1, source_target_pairs={{3,0},{0,1},{1,2},{2,3},{7,4},{4,5},{5,6},{6,7},{11,8},{8,9},{9,10... | collective-permute-start | bytes 3145736 | tf_op jit(solution)/shard_map/ppermute | solution.py:21
  138.1 3.2 %copy-start.8 = (bf16[2,4,256,256]{3,2,1,0:T(8,128)(2,1)S(1)}, bf16[2,4,256,256]{3,2,1,0:T(8,128)(2,1)}, u32[]{:S(2)}) copy-start(bf16[2,4,256,256]{3,2,1,0:T(8,128)(2,1)} %copy-done.7) | copy-start | bytes 3145732
  138.2 1.6 copy-start.3
  138.2 12.6 %collective-permute-start.33 = (f32[8,512]{1,0:T(8,128)S(1)}, f32[8,512]{1,0:T(8,128)S(1)}, u32[]{:S(2)}, u32[]{:S(2)}) collective-permute-start(f32[8,512]{1,0:T(8,128)S(1)} %copy-done.26), channel_id=1, source_target_pairs={{2,0},{3,1},{0,2},{1,3},{6,4},{7,5},{4,6},{5,7},{10,8},{11,9},{8,1... | collective-permute-start | bytes 49160 | tf_op jit(solution)/shard_map/ppermute | solution.py:21
  139.8 0.8 copy-start.4
  140.6 0.8 copy-start.5
  143.3 17.1 %collective-permute-start.30 = (bf16[256,256]{1,0:T(8,128)(2,1)S(1)}, bf16[256,256]{1,0:T(8,128)(2,1)S(1)}, u32[]{:S(2)}, u32[]{:S(2)}) collective-permute-start(bf16[256,256]{1,0:T(8,128)(2,1)S(1)} %get-tuple-element.64), channel_id=1, source_target_pairs={{8,0},{36,4},{16,8},{44,12},{24,16},{52,20},{0,24},{60,28},{40,32}... | collective-permute-start | bytes 393224 | tf_op jit(solution)/shard_map/ppermute | solution.py:36
  145.4 15.0 %collective-permute-start.29 = (bf16[256,256]{1,0:T(8,128)(2,1)S(1)}, bf16[256,256]{1,0:T(8,128)(2,1)S(1)}, u32[]{:S(2)}, u32[]{:S(2)}) collective-permute-start(bf16[256,256]{1,0:T(8,128)(2,1)S(1)} %get-tuple-element.65), channel_id=1, source_target_pairs={{16,0},{68,4},{24,8},{76,12},{0,16},{84,20},{8,24},{92,28},{48,32}... | collective-permute-start | bytes 393224 | tf_op jit(solution)/shard_map/ppermute | solution.py:36
  150.7 1.4 copy-start.24
  150.7 9.7 %collective-permute-start.28 = (bf16[256,256]{1,0:T(8,128)(2,1)S(1)}, bf16[256,256]{1,0:T(8,128)(2,1)S(1)}, u32[]{:S(2)}, u32[]{:S(2)}) collective-permute-start(bf16[256,256]{1,0:T(8,128)(2,1)S(1)} %get-tuple-element.66), channel_id=1, source_target_pairs={{24,0},{100,4},{0,8},{108,12},{8,16},{116,20},{16,24},{124,28},{56... | collective-permute-start | bytes 393224 | tf_op jit(solution)/shard_map/ppermute | solution.py:36
  151.7 1.0 copy-start.6
  160.4 0.7 copy-start.16
  160.4 0.7 copy-start.17
  161.1 0.7 copy-start.18
  162.9 1.4 collective-permute-start.34
Sparse Core Ops, SparseCore 0:
  60.6 47.5 all-gather.2

commit v13 on v12

--- a/solution.py
+++ b/solution.py
@@ -15,6 +15,7 @@
 TILE = 512
 TILES = VOC // TILE
 VMEM = 56 * 2**20
+MOST = 63 * 2**20
 
 
 def shift(a, axis, d):
@@ -44,8 +45,8 @@
     return lax.dot_general(a, b, (((1,), (0,)), ((), ())), preferred_element_type=F32)
 
 
-def params(**kw):
-    return pltpu.CompilerParams(vmem_limit_bytes=VMEM, **kw)
+def params(limit=VMEM):
+    return pltpu.CompilerParams(vmem_limit_bytes=limit)
 
 
 SMALL = pl.CostEstimate(flops=1000, bytes_accessed=1000, transcendentals=0)
@@ -108,7 +109,7 @@
             pltpu.SemaphoreType.DMA((chunks,)),
             pltpu.SemaphoreType.DMA((chunks,)),
         ],
-        compiler_params=params(),
+        compiler_params=params(MOST),
         cost_estimate=SMALL,
         name="onward",
     )(ep, em, *others)
@@ -319,16 +320,40 @@
     return sum(x.astype(F32) for x in xs)
 
 
-def scatter(keep, recv, c, first, second):
+def second_sum_body(at, t, u1, u2, u3, _, mine, other, _out):
+    total = add(t[0], u1[...], u2[...], u3[...])
+    low, high = total[:, :128], total[:, 128:]
+    first = at[2] == 0
+    mine[...] = jnp.where(first, low, high)
+    other[...] = jnp.where(first, high, low)
+
+
+def second_sum(at, t, us, work):
+    part = pl.BlockSpec((HALF, 256), lambda i, at: (0, 0))
+    out = pl.BlockSpec((HALF, 128), lambda i, at: (0, 0))
+    return pl.pallas_call(
+        second_sum_body,
+        grid_spec=pltpu.PrefetchScalarGridSpec(
+            num_scalar_prefetch=1,
+            grid=(1,),
+            in_specs=[pl.BlockSpec((1, HALF, 256), lambda i, at: (0, 0, 0)), part, part, part, HBM],
+            out_specs=[out, out, HBM],
+        ),
+        out_shape=[jax.ShapeDtypeStruct((HALF, 128), F32)] * 2 + [jax.ShapeDtypeStruct(work.shape, work.dtype)],
+        input_output_aliases={5: 2},
+        compiler_params=params(MOST),
+        cost_estimate=SMALL,
+        name="second_sum",
+    )(at, t, *us, work)
+
+
+def scatter(at, keep, recv, c, first, second):
     b = [add(keep[d], recv[d // 2][d % 2]) for d in range(4)]
     u = [cross(b[d].astype(BF), 0, 4 - d) for d in (1, 2, 3)]
     u1, u2, u3, work = gate(*u, first())
     t = add(b[0], u1, u2, u3)
     u = [cross(t[d].astype(BF), 1, 4 - d) for d in (1, 2, 3)]
-    *u, work = gate(*u, second(work))
-    f = add(t[0], *u)
-    low, high = f[:, :128], f[:, 128:]
-    mine, other = jnp.where(c == 0, low, high), jnp.where(c == 0, high, low)
+    mine, other, work = second_sum(at, t, u, second(work))
     got = sibling(other)
     return jnp.where(c == 0, jnp.concatenate([mine, got]), jnp.concatenate([got, mine])), work
 
@@ -362,7 +387,7 @@
             out_specs=pl.BlockSpec((TILE, 1024), lambda i, at: (i, 0)),
         ),
         out_shape=jax.ShapeDtypeStruct((VOC, 1024), BF),
-        compiler_params=params(),
+        compiler_params=params(MOST),
         cost_estimate=SMALL,
         name="embed_a",
     )(at, tgt, ep, em, *packs, feats, feats, feats)
@@ -392,7 +417,7 @@
             out_specs=pl.BlockSpec((TILE, 1024), lambda i, at: (i, 0)),
         ),
         out_shape=jax.ShapeDtypeStruct((VOC, 1024), BF),
-        compiler_params=params(),
+        compiler_params=params(MOST),
         cost_estimate=SMALL,
         name="embed_b",
     )(at, acc, low, high, pack, feats)
@@ -428,6 +453,7 @@
     low, high = shift(low, "y", 1), shift(high, "y", 3)
 
     grad_hidden, grad_embed = scatter(
+        at,
         keep,
         [sibling(t) for t in send],
         c,

time: 174 us -> 172 us (0.989)
  local copies, waits for them, and re-layouts: 8.87 us -> 3.52 us
  Pallas kernels: 56.2 us -> 58.6 us
    unnamed x54 -> x44, local copies, waits for them, and re-layouts: 8.15 us -> 2.8 us
    pallas_call x0 -> x1, Pallas kernels: none -> 2.53 us  [second_sum(): pl.pallas_call(second_sum_body, grid_spec=pltpu.PrefetchScalarGridSpec(nu...]
where the time goes in v13:
time: 172 us; the launch traced here: 171 us
  Pallas kernels  58.6 us (34%)
  starting transfers between devices  44 us (26%)
  waiting for transfers between devices  38.8 us (23%)
  between operations  14.3 us (8%)
  other arithmetic  11.6 us (7%)
  local copies, waits for them, and re-layouts  3.52 us (2%)
    ppermute x13, starting transfers between devices, shift(): return lax.ppermute(a, axis, [((i + d) % 4, i) for i in range(4)])  22 us
    ppermute x12, starting transfers between devices, cross(): return lax.ppermute(a, ('x', 'z', 'c'), pairs)  18.9 us
    pallas_call x1, Pallas kernels, hidden_call(): pl.pallas_call(hidden_body, grid_spec=pltpu.PrefetchScalarGridSpec(num_sc...  16.5 us
    ppermute x12, waiting for transfers between devices, cross(): return lax.ppermute(a, ('x', 'z', 'c'), pairs)  16.4 us
    pallas_call x1, Pallas kernels, logits_call(): pl.pallas_call(logits_body, grid_spec=pltpu.PrefetchScalarGridSpec(num_sc...  16.3 us
    ppermute x13, waiting for transfers between devices, shift(): return lax.ppermute(a, axis, [((i + d) % 4, i) for i in range(4)])  14.6 us
    pallas_call x1, Pallas kernels, embed_a_call(): pl.pallas_call(embed_a_body, grid_spec=pltpu.PrefetchScalarGridSpec(num_s...  11.6 us
    ppermute x9, waiting for transfers between devices, sibling(): return lax.ppermute(a, 'c', [(0, 1), (1, 0)])  7.76 us
  transfers between devices with their start and end apart: 36, of which 15 were waited for; matrix products, arithmetic and copies ran while one was open for 5% of the time, Pallas kernels for 33%

profile of v13, /device:TPU:0, one launch (start us, length us, event | category | flops | bytes accessed | tf_op | source)
XLA Modules:
  0.0 170.7 jit_solution(11705639502152727466)
XLA Ops:
  7.2 0.9 broadcast_select_fusion.1
  8.2 0.7 broadcast_subtract_fusion
  8.9 0.6 collective-permute-done
  9.5 3.2 %collective-permute-start.3 = (bf16[256,256]{1,0:T(8,128)(2,1)S(1)}, bf16[256,256]{1,0:T(8,128)(2,1)S(1)}, u32[]{:S(2)}, u32[]{:S(2)}) collective-permute-start(bf16[256,256]{1,0:T(8,128)(2,1)S(1)} %maximum_select_fusion.1), channel_id=1, source_target_pairs={{64,0},{20,4},{72,8},{28,12},{80,16},{4,20},{88,24},{12,28},{96,32... | collective-permute-start | bytes 393224 | tf_op jit(solution)/shard_map/ppermute | solution.py:37
  12.7 1.1 collective-permute-start.2
  13.8 0.9 collective-permute-start.1
  14.7 0.6 pad_add_fusion.refs_1_
  15.4 4.6 %collective-permute-done.1.refs_0_ = bf16[256,256]{1,0:T(8,128)(2,1)S(1)} collective-permute-done((bf16[256,256]{1,0:T(8,128)(2,1)S(1)}, bf16[256,256]{1,0:T(8,128)(2,1)S(1)}, u32[]{:S(2)}, u32[]{:S(2)}) %collective-permute-start.1) | collective-permute-done | bytes 131104 | tf_op jit(solution)/shard_map/ppermute | solution.py:37
  20.0 0.6 tile.2
  20.7 1.0 pad_maximum_fusion.refs_0_
  21.6 2.0 %collective-permute-start.6 = (bf16[4,256,256]{2,1,0:T(8,128)(2,1)S(1)}, bf16[4,256,256]{2,1,0:T(8,128)(2,1)S(1)}, u32[]{:S(2)}, u32[]{:S(2)}) collective-permute-start(bf16[4,256,256]{2,1,0:T(8,128)(2,1)S(1)} %pad_maximum_fusion.refs_0_), channel_id=1, source_target_pairs={{24,0},{100,4},{0,8},{108,12},{8,16},{116,20},{16,24},{124,28},{56... | collective-permute-start | bytes 1572872 | tf_op jit(solution)/shard_map/ppermute | solution.py:37
  23.6 3.6 %collective-permute-start.5 = (bf16[4,256,256]{2,1,0:T(8,128)(2,1)S(1)}, bf16[4,256,256]{2,1,0:T(8,128)(2,1)S(1)}, u32[]{:S(2)}, u32[]{:S(2)}) collective-permute-start(bf16[4,256,256]{2,1,0:T(8,128)(2,1)S(1)} %pad_maximum_fusion.refs_0_), channel_id=1, source_target_pairs={{16,0},{68,4},{24,8},{76,12},{0,16},{84,20},{8,24},{92,28},{48,32}... | collective-permute-start | bytes 1572872 | tf_op jit(solution)/shard_map/ppermute | solution.py:37
  27.2 1.0 collective-permute-start.4
  28.2 4.7 %collective-permute-done.6.refs_3_ = bf16[4,256,256]{2,1,0:T(8,128)(2,1)S(1)} collective-permute-done((bf16[4,256,256]{2,1,0:T(8,128)(2,1)S(1)}, bf16[4,256,256]{2,1,0:T(8,128)(2,1)S(1)}, u32[]{:S(2)}, u32[]{:S(2)}) %collective-permute-start.6) | collective-permute-done | bytes 524320 | tf_op jit(solution)/shard_map/ppermute | solution.py:37
  32.9 7.1 %collective-permute-done.5.refs_2_ = bf16[4,256,256]{2,1,0:T(8,128)(2,1)S(1)} collective-permute-done((bf16[4,256,256]{2,1,0:T(8,128)(2,1)S(1)}, bf16[4,256,256]{2,1,0:T(8,128)(2,1)S(1)}, u32[]{:S(2)}, u32[]{:S(2)}) %collective-permute-start.5) | collective-permute-done | bytes 524320 | tf_op jit(solution)/shard_map/ppermute | solution.py:37
  40.0 0.5 collective-permute-start.8
  40.5 1.6 collective-permute-start.11
  42.1 0.5 collective-permute-done.8.refs_5_
  42.7 0.2 copy-done.7
  42.9 0.2 copy-done.8
  43.2 0.2 copy-done.10
  43.4 16.3 %logits.1 = (bf16[2048,512]{1,0:T(8,128)(2,1)}, f32[8,512]{1,0:T(8,128)}, f32[8,512]{1,0:T(8,128)}) custom-call(s32[4]{0:T(128)} %get-tuple-element.28.at, bf16[4,256,256]{2,1,0:T(8,128)(2,1)} %copy-done, bf16[4,256,256]{2,1,0:T(8,128)(2,1)} %copy-done.6, bf16[4,256,256]{2,1,0:T(8,128)(2,1)} %copy-done.5, bf16[4,256,256]{2,1,0:T(8,128)(2,1)} %copy-done.4, ...), custom_call_target="tpu_custom_call" | custom-call | flops 1000 | bytes 1000 | tf_op jit(solution)/shard_map/logits/pallas_call | solution.py:175
  59.8 0.6 copy-done.11
  60.5 3.4 %collective-permute-start.14 = (f32[8,512]{1,0:T(8,128)}, f32[8,512]{1,0:T(8,128)S(1)}, u32[]{:S(2)}, u32[]{:S(2)}) collective-permute-start(f32[8,512]{1,0:T(8,128)} %get-tuple-element.33), channel_id=1, source_target_pairs={{96,0},{0,32},{32,64},{64,96},{97,1},{1,33},{33,65},{65,97},{98,2}... | collective-permute-start | bytes 49160 | tf_op jit(solution)/shard_map/ppermute | solution.py:22
  63.9 4.1 %collective-permute-start.13 = (f32[8,512]{1,0:T(8,128)}, f32[8,512]{1,0:T(8,128)S(1)}, u32[]{:S(2)}, u32[]{:S(2)}) collective-permute-start(f32[8,512]{1,0:T(8,128)} %get-tuple-element.33), channel_id=1, source_target_pairs={{64,0},{96,32},{0,64},{32,96},{65,1},{97,33},{1,65},{33,97},{66,2}... | collective-permute-start | bytes 49160 | tf_op jit(solution)/shard_map/ppermute | solution.py:22
  68.0 1.7 collective-permute-start.12
  69.8 3.2 %collective-permute-start.24 = (bf16[2048,512]{1,0:T(8,128)(2,1)}, bf16[2048,512]{1,0:T(8,128)(2,1)}, u32[]{:S(2)}, u32[]{:S(2)}) collective-permute-start(bf16[2048,512]{1,0:T(8,128)(2,1)} %get-tuple-element.31.e), channel_id=1, source_target_pairs={{1,0},{2,1},{3,2},{0,3},{5,4},{6,5},{7,6},{4,7},{9,8},{10,9},{11,1... | collective-permute-start | bytes 6291464 | tf_op jit(solution)/shard_map/ppermute | solution.py:22
  73.0 0.9 fusion.8
  73.9 1.0 collective-permute-start.17
  74.9 2.1 %collective-permute-start.16 = (f32[8,512]{1,0:T(8,128)S(1)}, f32[8,512]{1,0:T(8,128)S(1)}, u32[]{:S(2)}, u32[]{:S(2)}) collective-permute-start(f32[8,512]{1,0:T(8,128)S(1)} %maximum_maximum_fusion), channel_id=1, source_target_pairs={{16,0},{24,8},{0,16},{8,24},{17,1},{25,9},{1,17},{9,25},{18,2},{26... | collective-permute-start | bytes 49160 | tf_op jit(solution)/shard_map/ppermute | solution.py:22
  77.0 1.5 collective-permute-start.15
  78.6 0.3 collective-permute-done.17
  78.9 1.4 collective-permute-done.16
  80.3 0.4 collective-permute-done.15
  80.9 0.2 collective-permute-start.18
  81.1 1.2 collective-permute-done.18.b
  82.3 0.6 copy-done.20
  82.9 1.4 finish.1
  84.3 16.5 %hidden.1 = (bf16[4,4,256,256]{3,2,1,0:T(8,128)(2,1)}, bf16[2,4,256,256]{3,2,1,0:T(8,128)(2,1)}, bf16[2,4,256,256]{3,2,1,0:T(8,128)(2,1)}, bf16[2048,512]{1,0:T(8,128)(2,1)}) custom-call(s32[4]{0:T(128)} %get-tuple-element.28.at, bf16[2048,512]{1,0:T(8,128)(2,1)} %get-tuple-element.31.e, f32[8,512]{1,0:T(8,128)} %get-tuple-element.35.pack, ...), custom_call_target="tpu_custom_call" | custom-call | flops 1000 | bytes 1000 | tf_op jit(solution)/shard_map/hidden/pallas_call | solution.py:293
  100.8 0.3 collective-permute-start.19
  101.1 0.3 collective-permute-start.21
  101.4 2.4 %collective-permute-done.19 = bf16[2,4,256,256]{3,2,1,0:T(8,128)(2,1)S(1)} collective-permute-done((bf16[2,4,256,256]{3,2,1,0:T(8,128)(2,1)}, bf16[2,4,256,256]{3,2,1,0:T(8,128)(2,1)S(1)}, u32[]{:S(2)}, u32[]{:S(2)}) %collective-permute-start.19) | collective-permute-done | bytes 1048608 | tf_op jit(solution)/shard_map/ppermute | solution.py:26
  103.8 0.9 collective-permute-start.26
  104.7 1.6 collective-permute-done.21
  106.2 2.8 %fusion.4 = (bf16[4,256,256]{2,1,0:T(8,128)(2,1)}, bf16[4,256,256]{2,1,0:T(8,128)(2,1)}, bf16[4,256,256]{2,1,0:T(8,128)(2,1)}) fusion(bf16[2,4,256,256]{3,2,1,0:T(8,128)(2,1)S(1)} %collective-permute-done.21, bf16[4,4,256,256]{3,2,1,0:T(8,128)(2,1)} %get-tuple-element.36, bf16[2,4,256,256]{3,2,1,0:T(8,128)(2,1)S(1)} %collective-permute-done.19), kind=kLoop, calls=%fused_computation.8 | loop fusion | flops 3145728 | bytes 4718592 | tf_op jit(solution)/shard_map/convert_element_type | solution.py:352
  109.0 1.5 collective-permute-start.23
  110.5 7.5 %collective-permute-done.27.refs_1_ = f32[8,512]{1,0:T(8,128)S(1)} collective-permute-done((f32[8,512]{1,0:T(8,128)S(1)}, f32[8,512]{1,0:T(8,128)S(1)}, u32[]{:S(2)}, u32[]{:S(2)}) %collective-permute-start.27) | collective-permute-done | bytes 16416 | tf_op jit(solution)/shard_map/ppermute | solution.py:22
  118.0 0.2 collective-permute-start.22
  118.2 1.0 collective-permute-start.20
  119.2 2.4 %onward.1 = (f32[8,512]{1,0:T(8,128)}, f32[8,512]{1,0:T(8,128)}, bf16[1024,512]{1,0:T(8,128)(2,1)}, bf16[1024,512]{1,0:T(8,128)(2,1)}) custom-call(bf16[2048,512]{1,0:T(8,128)(2,1)} %collective-permute-done.24.ep, bf16[2048,512]{1,0:T(8,128)(2,1)} %collective-permute-done.25.em, f32[8,512]{1,0:T(8,128)} %copy-done.17, ...), custom_call_target="tpu_custom_call", output_to_operand_aliasing={{0}: (2, {}), {1}: (3, {})} | custom-call | flops 1000 | bytes 1000 | tf_op jit(solution)/shard_map/onward/pallas_call | solution.py:101
  121.6 2.5 %collective-permute-start.31 = (bf16[1024,512]{1,0:T(8,128)(2,1)}, bf16[1024,512]{1,0:T(8,128)(2,1)}, u32[]{:S(2)}, u32[]{:S(2)}) collective-permute-start(bf16[1024,512]{1,0:T(8,128)(2,1)} %get-tuple-element.47), channel_id=1, source_target_pairs={{1,0},{2,1},{3,2},{0,3},{5,4},{6,5},{7,6},{4,7},{9,8},{10,9},{11,1... | collective-permute-start | bytes 3145736 | tf_op jit(solution)/shard_map/ppermute | solution.py:22
  124.1 11.6 %embed_a.1.refs_3_ = bf16[2048,1024]{1,0:T(8,128)(2,1)} custom-call(s32[4]{0:T(128)} %get-tuple-element.28.at, bf16[2048,512]{1,0:T(8,128)(2,1)} %get-tuple-element.39.tgt, bf16[2048,512]{1,0:T(8,128)(2,1)} %collective-permute-done.24.ep, bf16[2048,512]{1,0:T(8,128)(2,1)} %collective-permute-done.25.em, f32[8,512]{1,0:T(8,128)} %get-tuple-element.40.pack_p, ...), custom_call_target="tpu_custom_call" | custom-call | flops 1000 | bytes 1000 | tf_op jit(solution)/shard_map/embed_a/pallas_call | solution.py:381
  135.7 1.6 collective-permute-start.33
  137.4 2.9 %fusion.11 = (bf16[4,256,256]{2,1,0:T(8,128)(2,1)S(1)}, f32[4,256,256]{2,1,0:T(8,128)}) fusion(bf16[4,256,256]{2,1,0:T(8,128)(2,1)} %get-tuple-element.45, bf16[4,256,256]{2,1,0:T(8,128)(2,1)} %get-tuple-element.44, bf16[4,256,256]{2,1,0:T(8,128)(2,1)} %get-tuple-element.43, bf16[2,4,256,256]{3,2,1,0:T(8,128)(2,1)S(1)} %copy-done.3, ...), kind=kLoop, calls=%fused_computation.42 | loop fusion | flops 2621440 | bytes 4194304 | tf_op jit(solution)/shard_map/convert.2
  140.2 2.1 %collective-permute-start.30 = (bf16[256,256]{1,0:T(8,128)(2,1)S(1)}, bf16[256,256]{1,0:T(8,128)(2,1)S(1)}, u32[]{:S(2)}, u32[]{:S(2)}) collective-permute-start(bf16[256,256]{1,0:T(8,128)(2,1)S(1)} %get-tuple-element.62), channel_id=1, source_target_pairs={{8,0},{36,4},{16,8},{44,12},{24,16},{52,20},{0,24},{60,28},{40,32}... | collective-permute-start | bytes 393224 | tf_op jit(solution)/shard_map/ppermute | solution.py:37
  142.4 1.4 collective-permute-start.29
  143.8 4.4 %collective-permute-done.33.pack = f32[8,512]{1,0:T(8,128)S(1)} collective-permute-done((f32[8,512]{1,0:T(8,128)S(1)}, f32[8,512]{1,0:T(8,128)S(1)}, u32[]{:S(2)}, u32[]{:S(2)}) %collective-permute-start.33) | collective-permute-done | bytes 16416 | tf_op jit(solution)/shard_map/ppermute | solution.py:22
  148.2 0.9 collective-permute-start.28
  149.1 0.5 collective-permute-done.32.high
  149.6 7.7 %embed_b.1._ = bf16[2048,1024]{1,0:T(8,128)(2,1)} custom-call(s32[4]{0:T(128)} %get-tuple-element.28.at, bf16[2048,1024]{1,0:T(8,128)(2,1)} %get-tuple-element.46.acc, bf16[1024,512]{1,0:T(8,128)(2,1)} %collective-permute-done.31.low, bf16[1024,512]{1,0:T(8,128)(2,1)} %collective-permute-done.32.high, f32[8,512]{1,0:T(8,128)} %copy-done.19, ...), custom_call_target="tpu_custom_call" | custom-call | flops 1000 | bytes 1000 | tf_op jit(solution)/shard_map/embed_b/pallas_call | solution.py:405
  157.4 0.6 copy-done.13
  158.1 2.5 %second_sum.1 = (f32[256,128]{1,0:T(8,128)}, f32[256,128]{1,0:T(8,128)}, bf16[2048,1024]{1,0:T(8,128)(2,1)}) custom-call(s32[4]{0:T(128)} %get-tuple-element.28.at, f32[4,256,256]{2,1,0:T(8,128)} %get-tuple-element.54.t, bf16[256,256]{1,0:T(8,128)(2,1)} %copy-done.15, bf16[256,256]{1,0:T(8,128)(2,1)} %copy-done.14, ...), custom_call_target="tpu_custom_call", output_to_operand_aliasing={{2}: (5, {})} | custom-call | flops 1000 | bytes 1000 | tf_op jit(solution)/shard_map/second_sum/pallas_call | solution.py:334
  160.6 1.6 collective-permute-done.34
  162.2 1.7 %maximum_select_fusion = f32[512,128]{1,0:T(8,128)} fusion(f32[256,128]{1,0:T(8,128)S(1)} %collective-permute-done.34, f32[256,128]{1,0:T(8,128)} %get-tuple-element.49, pred[]{:T(512)S(6)} %eq.2), kind=kLoop, calls=%fused_computation.10 | loop fusion | flops 196608 | bytes 524289 | tf_op jit(solution)/shard_map/jit(_where)/select_n | solution.py:358
  (80 shorter events, 0.9 us)
Async XLA Ops:
  7.2 116.9 %all-gather.3.cloned.1.call-start = ((), (), s32[]{:S(2)}) async-start(), calls=%async_computation | async-start | bytes 4325376 | tf_op jit(solution)/shard_map/all_gather | solution.py:444
  8.1 1.3 collective-permute-start
  9.5 11.2 %collective-permute-start.3 = (bf16[256,256]{1,0:T(8,128)(2,1)S(1)}, bf16[256,256]{1,0:T(8,128)(2,1)S(1)}, u32[]{:S(2)}, u32[]{:S(2)}) collective-permute-start(bf16[256,256]{1,0:T(8,128)(2,1)S(1)} %maximum_select_fusion.1), channel_id=1, source_target_pairs={{64,0},{20,4},{72,8},{28,12},{80,16},{4,20},{88,24},{12,28},{96,32... | collective-permute-start | bytes 393224 | tf_op jit(solution)/shard_map/ppermute | solution.py:37
  12.7 8.0 %collective-permute-start.2 = (bf16[256,256]{1,0:T(8,128)(2,1)S(1)}, bf16[256,256]{1,0:T(8,128)(2,1)S(1)}, u32[]{:S(2)}, u32[]{:S(2)}) collective-permute-start(bf16[256,256]{1,0:T(8,128)(2,1)S(1)} %maximum_select_fusion.1), channel_id=1, source_target_pairs={{32,0},{12,4},{40,8},{20,12},{48,16},{28,20},{56,24},{4,28},{64,32... | collective-permute-start | bytes 393224 | tf_op jit(solution)/shard_map/ppermute | solution.py:37
  13.8 6.2 %collective-permute-start.1 = (bf16[256,256]{1,0:T(8,128)(2,1)S(1)}, bf16[256,256]{1,0:T(8,128)(2,1)S(1)}, u32[]{:S(2)}, u32[]{:S(2)}) collective-permute-start(bf16[256,256]{1,0:T(8,128)(2,1)S(1)} %maximum_select_fusion.1), channel_id=1, source_target_pairs={{96,0},{28,4},{104,8},{4,12},{112,16},{12,20},{120,24},{20,28},{0,... | collective-permute-start | bytes 393224 | tf_op jit(solution)/shard_map/ppermute | solution.py:37
  20.0 0.7 copy-start.12
  21.6 21.0 %copy-start = (bf16[4,256,256]{2,1,0:T(8,128)(2,1)}, bf16[4,256,256]{2,1,0:T(8,128)(2,1)S(1)}, u32[]{:S(2)}) copy-start(bf16[4,256,256]{2,1,0:T(8,128)(2,1)S(1)} %pad_maximum_fusion.refs_0_) | copy-start | bytes 1572868
  21.6 11.3 %collective-permute-start.6 = (bf16[4,256,256]{2,1,0:T(8,128)(2,1)S(1)}, bf16[4,256,256]{2,1,0:T(8,128)(2,1)S(1)}, u32[]{:S(2)}, u32[]{:S(2)}) collective-permute-start(bf16[4,256,256]{2,1,0:T(8,128)(2,1)S(1)} %pad_maximum_fusion.refs_0_), channel_id=1, source_target_pairs={{24,0},{100,4},{0,8},{108,12},{8,16},{116,20},{16,24},{124,28},{56... | collective-permute-start | bytes 1572872 | tf_op jit(solution)/shard_map/ppermute | solution.py:37
  23.6 16.4 %collective-permute-start.5 = (bf16[4,256,256]{2,1,0:T(8,128)(2,1)S(1)}, bf16[4,256,256]{2,1,0:T(8,128)(2,1)S(1)}, u32[]{:S(2)}, u32[]{:S(2)}) collective-permute-start(bf16[4,256,256]{2,1,0:T(8,128)(2,1)S(1)} %pad_maximum_fusion.refs_0_), channel_id=1, source_target_pairs={{16,0},{68,4},{24,8},{76,12},{0,16},{84,20},{8,24},{92,28},{48,32}... | collective-permute-start | bytes 1572872 | tf_op jit(solution)/shard_map/ppermute | solution.py:37
  27.2 12.8 %collective-permute-start.4 = (bf16[4,256,256]{2,1,0:T(8,128)(2,1)S(1)}, bf16[4,256,256]{2,1,0:T(8,128)(2,1)S(1)}, u32[]{:S(2)}, u32[]{:S(2)}) collective-permute-start(bf16[4,256,256]{2,1,0:T(8,128)(2,1)S(1)} %pad_maximum_fusion.refs_0_), channel_id=1, source_target_pairs={{8,0},{36,4},{16,8},{44,12},{24,16},{52,20},{0,24},{60,28},{40,32}... | collective-permute-start | bytes 1572872 | tf_op jit(solution)/shard_map/ppermute | solution.py:37
  28.2 13.8 %collective-permute-start.7 = (bf16[4,256,256]{2,1,0:T(8,128)(2,1)S(1)}, bf16[4,256,256]{2,1,0:T(8,128)(2,1)S(1)}, u32[]{:S(2)}, u32[]{:S(2)}) collective-permute-start(bf16[4,256,256]{2,1,0:T(8,128)(2,1)S(1)} %pad_maximum_fusion.refs_0_), channel_id=1, source_target_pairs={{0,4},{4,0},{1,5},{5,1},{2,6},{6,2},{3,7},{7,3},{8,12},{12,8},{9,1... | collective-permute-start | bytes 1572872 | tf_op jit(solution)/shard_map/ppermute | solution.py:26
  32.9 9.7 %copy-start.4 = (bf16[4,256,256]{2,1,0:T(8,128)(2,1)}, bf16[4,256,256]{2,1,0:T(8,128)(2,1)S(1)}, u32[]{:S(2)}) copy-start(bf16[4,256,256]{2,1,0:T(8,128)(2,1)S(1)} %collective-permute-done.6.refs_3_) | copy-start | bytes 1572868
  32.9 9.2 %collective-permute-start.10 = (bf16[4,256,256]{2,1,0:T(8,128)(2,1)S(1)}, bf16[4,256,256]{2,1,0:T(8,128)(2,1)S(1)}, u32[]{:S(2)}, u32[]{:S(2)}) collective-permute-start(bf16[4,256,256]{2,1,0:T(8,128)(2,1)S(1)} %collective-permute-done.6.refs_3_), channel_id=1, source_target_pairs={{0,4},{4,0},{1,5},{5,1},{2,6},{6,2},{3,7},{7,3},{8,12},{12,8},{9,1... | collective-permute-start | bytes 1572872 | tf_op jit(solution)/shard_map/ppermute | solution.py:26
  40.0 2.7 %copy-start.5 = (bf16[4,256,256]{2,1,0:T(8,128)(2,1)}, bf16[4,256,256]{2,1,0:T(8,128)(2,1)S(1)}, u32[]{:S(2)}) copy-start(bf16[4,256,256]{2,1,0:T(8,128)(2,1)S(1)} %collective-permute-done.5.refs_2_) | copy-start | bytes 1572868
  40.0 2.1 %collective-permute-start.9 = (bf16[4,256,256]{2,1,0:T(8,128)(2,1)S(1)}, bf16[4,256,256]{2,1,0:T(8,128)(2,1)S(1)}, u32[]{:S(2)}, u32[]{:S(2)}) collective-permute-start(bf16[4,256,256]{2,1,0:T(8,128)(2,1)S(1)} %collective-permute-done.5.refs_2_), channel_id=1, source_target_pairs={{0,4},{4,0},{1,5},{5,1},{2,6},{6,2},{3,7},{7,3},{8,12},{12,8},{9,1... | collective-permute-start | bytes 1572872 | tf_op jit(solution)/shard_map/ppermute | solution.py:26
  40.0 2.7 %copy-start.6 = (bf16[4,256,256]{2,1,0:T(8,128)(2,1)}, bf16[4,256,256]{2,1,0:T(8,128)(2,1)S(1)}, u32[]{:S(2)}) copy-start(bf16[4,256,256]{2,1,0:T(8,128)(2,1)S(1)} %collective-permute-done.4.refs_1_) | copy-start | bytes 1572868
  40.0 2.6 %collective-permute-start.8 = (bf16[4,256,256]{2,1,0:T(8,128)(2,1)S(1)}, bf16[4,256,256]{2,1,0:T(8,128)(2,1)S(1)}, u32[]{:S(2)}, u32[]{:S(2)}) collective-permute-start(bf16[4,256,256]{2,1,0:T(8,128)(2,1)S(1)} %collective-permute-done.4.refs_1_), channel_id=1, source_target_pairs={{0,4},{4,0},{1,5},{5,1},{2,6},{6,2},{3,7},{7,3},{8,12},{12,8},{9,1... | collective-permute-start | bytes 1572872 | tf_op jit(solution)/shard_map/ppermute | solution.py:26
  40.5 19.3 %collective-permute-start.11 = (bf16[512,128]{1,0:T(8,128)(2,1)}, bf16[512,128]{1,0:T(8,128)(2,1)S(1)}, u32[]{:S(2)}, u32[]{:S(2)}) collective-permute-start(bf16[512,128]{1,0:T(8,128)(2,1)} %bitcast.44), channel_id=1, source_target_pairs={{0,0},{1,32},{2,64},{3,96},{32,1},{33,33},{34,65},{35,97},{64,2},{... | collective-permute-start | bytes 393224 | tf_op jit(solution)/shard_map/ppermute | solution.py:433
  42.1 0.8 copy-start.7
  42.1 1.0 copy-start.8
  42.1 1.1 copy-start.9
  42.6 0.8 copy-start.10
  59.8 0.7 copy-start.11
  60.5 12.5 %collective-permute-start.14 = (f32[8,512]{1,0:T(8,128)}, f32[8,512]{1,0:T(8,128)S(1)}, u32[]{:S(2)}, u32[]{:S(2)}) collective-permute-start(f32[8,512]{1,0:T(8,128)} %get-tuple-element.33), channel_id=1, source_target_pairs={{96,0},{0,32},{32,64},{64,96},{97,1},{1,33},{33,65},{65,97},{98,2}... | collective-permute-start | bytes 49160 | tf_op jit(solution)/shard_map/ppermute | solution.py:22
  63.9 9.1 %collective-permute-start.13 = (f32[8,512]{1,0:T(8,128)}, f32[8,512]{1,0:T(8,128)S(1)}, u32[]{:S(2)}, u32[]{:S(2)}) collective-permute-start(f32[8,512]{1,0:T(8,128)} %get-tuple-element.33), channel_id=1, source_target_pairs={{64,0},{96,32},{0,64},{32,96},{65,1},{97,33},{1,65},{33,97},{66,2}... | collective-permute-start | bytes 49160 | tf_op jit(solution)/shard_map/ppermute | solution.py:22
  68.0 5.0 %collective-permute-start.12 = (f32[8,512]{1,0:T(8,128)}, f32[8,512]{1,0:T(8,128)S(1)}, u32[]{:S(2)}, u32[]{:S(2)}) collective-permute-start(f32[8,512]{1,0:T(8,128)} %get-tuple-element.33), channel_id=1, source_target_pairs={{32,0},{64,32},{96,64},{0,96},{33,1},{65,33},{97,65},{1,97},{34,2}... | collective-permute-start | bytes 49160 | tf_op jit(solution)/shard_map/ppermute | solution.py:22
  69.7 49.4 %collective-permute-start.25 = (bf16[2048,512]{1,0:T(8,128)(2,1)}, bf16[2048,512]{1,0:T(8,128)(2,1)}, u32[]{:S(2)}, u32[]{:S(2)}) collective-permute-start(bf16[2048,512]{1,0:T(8,128)(2,1)} %get-tuple-element.31.e), channel_id=1, source_target_pairs={{3,0},{0,1},{1,2},{2,3},{7,4},{4,5},{5,6},{6,7},{11,8},{8,9},{9,10... | collective-permute-start | bytes 6291464 | tf_op jit(solution)/shard_map/ppermute | solution.py:22
  69.8 49.4 %collective-permute-start.24 = (bf16[2048,512]{1,0:T(8,128)(2,1)}, bf16[2048,512]{1,0:T(8,128)(2,1)}, u32[]{:S(2)}, u32[]{:S(2)}) collective-permute-start(bf16[2048,512]{1,0:T(8,128)(2,1)} %get-tuple-element.31.e), channel_id=1, source_target_pairs={{1,0},{2,1},{3,2},{0,3},{5,4},{6,5},{7,6},{4,7},{9,8},{10,9},{11,1... | collective-permute-start | bytes 6291464 | tf_op jit(solution)/shard_map/ppermute | solution.py:22
  73.9 5.0 %collective-permute-start.17 = (f32[8,512]{1,0:T(8,128)S(1)}, f32[8,512]{1,0:T(8,128)S(1)}, u32[]{:S(2)}, u32[]{:S(2)}) collective-permute-start(f32[8,512]{1,0:T(8,128)S(1)} %maximum_maximum_fusion), channel_id=1, source_target_pairs={{24,0},{0,8},{8,16},{16,24},{25,1},{1,9},{9,17},{17,25},{26,2},{2,... | collective-permute-start | bytes 49160 | tf_op jit(solution)/shard_map/ppermute | solution.py:22
  74.9 5.4 %collective-permute-start.16 = (f32[8,512]{1,0:T(8,128)S(1)}, f32[8,512]{1,0:T(8,128)S(1)}, u32[]{:S(2)}, u32[]{:S(2)}) collective-permute-start(f32[8,512]{1,0:T(8,128)S(1)} %maximum_maximum_fusion), channel_id=1, source_target_pairs={{16,0},{24,8},{0,16},{8,24},{17,1},{25,9},{1,17},{9,25},{18,2},{26... | collective-permute-start | bytes 49160 | tf_op jit(solution)/shard_map/ppermute | solution.py:22
  77.0 3.7 %collective-permute-start.15 = (f32[8,512]{1,0:T(8,128)S(1)}, f32[8,512]{1,0:T(8,128)S(1)}, u32[]{:S(2)}, u32[]{:S(2)}) collective-permute-start(f32[8,512]{1,0:T(8,128)S(1)} %maximum_maximum_fusion), channel_id=1, source_target_pairs={{8,0},{16,8},{24,16},{0,24},{9,1},{17,9},{25,17},{1,25},{10,2},{18... | collective-permute-start | bytes 49160 | tf_op jit(solution)/shard_map/ppermute | solution.py:22
  80.9 1.4 copy-start.18
  80.9 1.4 collective-permute-start.18
  82.3 0.6 copy-start.20
  84.3 17.1 %copy-start.21 = (f32[8,512]{1,0:T(8,128)S(1)}, f32[8,512]{1,0:T(8,128)}, u32[]{:S(2)}) copy-start(f32[8,512]{1,0:T(8,128)} %get-tuple-element.35.pack) | copy-start | bytes 49156
  100.8 3.0 %collective-permute-start.19 = (bf16[2,4,256,256]{3,2,1,0:T(8,128)(2,1)}, bf16[2,4,256,256]{3,2,1,0:T(8,128)(2,1)S(1)}, u32[]{:S(2)}, u32[]{:S(2)}) collective-permute-start(bf16[2,4,256,256]{3,2,1,0:T(8,128)(2,1)} %get-tuple-element.37), channel_id=1, source_target_pairs={{0,4},{4,0},{1,5},{5,1},{2,6},{6,2},{3,7},{7,3},{8,12},{12,8},{9,1... | collective-permute-start | bytes 3145736 | tf_op jit(solution)/shard_map/ppermute | solution.py:26
  101.1 5.1 %collective-permute-start.21 = (bf16[2,4,256,256]{3,2,1,0:T(8,128)(2,1)}, bf16[2,4,256,256]{3,2,1,0:T(8,128)(2,1)S(1)}, u32[]{:S(2)}, u32[]{:S(2)}) collective-permute-start(bf16[2,4,256,256]{3,2,1,0:T(8,128)(2,1)} %get-tuple-element.38), channel_id=1, source_target_pairs={{0,4},{4,0},{1,5},{5,1},{2,6},{6,2},{3,7},{7,3},{8,12},{12,8},{9,1... | collective-permute-start | bytes 3145736 | tf_op jit(solution)/shard_map/ppermute | solution.py:26
  101.4 16.6 %collective-permute-start.27 = (f32[8,512]{1,0:T(8,128)S(1)}, f32[8,512]{1,0:T(8,128)S(1)}, u32[]{:S(2)}, u32[]{:S(2)}) collective-permute-start(f32[8,512]{1,0:T(8,128)S(1)} %copy-done.21), channel_id=1, source_target_pairs={{3,0},{0,1},{1,2},{2,3},{7,4},{4,5},{5,6},{6,7},{11,8},{8,9},{9,10... | collective-permute-start | bytes 49160 | tf_op jit(solution)/shard_map/ppermute | solution.py:22
  103.8 5.2 %copy-start.2 = (bf16[2,4,256,256]{3,2,1,0:T(8,128)(2,1)}, bf16[2,4,256,256]{3,2,1,0:T(8,128)(2,1)S(1)}, u32[]{:S(2)}) copy-start(bf16[2,4,256,256]{3,2,1,0:T(8,128)(2,1)S(1)} %collective-permute-done.19) | copy-start | bytes 3145732
  103.8 14.4 %collective-permute-start.26 = (f32[8,512]{1,0:T(8,128)S(1)}, f32[8,512]{1,0:T(8,128)S(1)}, u32[]{:S(2)}, u32[]{:S(2)}) collective-permute-start(f32[8,512]{1,0:T(8,128)S(1)} %copy-done.21), channel_id=1, source_target_pairs={{1,0},{2,1},{3,2},{0,3},{5,4},{6,5},{7,6},{4,7},{9,8},{10,9},{11,1... | collective-permute-start | bytes 49160 | tf_op jit(solution)/shard_map/ppermute | solution.py:22
  109.0 26.7 %collective-permute-start.23 = (bf16[4,256,256]{2,1,0:T(8,128)(2,1)}, bf16[4,256,256]{2,1,0:T(8,128)(2,1)S(1)}, u32[]{:S(2)}, u32[]{:S(2)}) collective-permute-start(bf16[4,256,256]{2,1,0:T(8,128)(2,1)} %get-tuple-element.59), channel_id=1, source_target_pairs={{32,0},{12,4},{40,8},{20,12},{48,16},{28,20},{56,24},{4,28},{64,32... | collective-permute-start | bytes 1572872 | tf_op jit(solution)/shard_map/ppermute | solution.py:37
  118.0 1.2 copy-start.16
  118.0 19.3 %collective-permute-start.22 = (bf16[4,256,256]{2,1,0:T(8,128)(2,1)}, bf16[4,256,256]{2,1,0:T(8,128)(2,1)}, u32[]{:S(2)}, u32[]{:S(2)}) collective-permute-start(bf16[4,256,256]{2,1,0:T(8,128)(2,1)} %get-tuple-element.60), channel_id=1, source_target_pairs={{64,0},{20,4},{72,8},{28,12},{80,16},{4,20},{88,24},{12,28},{96,32... | collective-permute-start | bytes 1572872 | tf_op jit(solution)/shard_map/ppermute | solution.py:37
  118.2 1.0 copy-start.17
  118.2 19.1 %collective-permute-start.20 = (bf16[4,256,256]{2,1,0:T(8,128)(2,1)}, bf16[4,256,256]{2,1,0:T(8,128)(2,1)}, u32[]{:S(2)}, u32[]{:S(2)}) collective-permute-start(bf16[4,256,256]{2,1,0:T(8,128)(2,1)} %get-tuple-element.61), channel_id=1, source_target_pairs={{96,0},{28,4},{104,8},{4,12},{112,16},{12,20},{120,24},{20,28},{0,... | collective-permute-start | bytes 1572872 | tf_op jit(solution)/shard_map/ppermute | solution.py:37
  121.6 27.5 %collective-permute-start.31 = (bf16[1024,512]{1,0:T(8,128)(2,1)}, bf16[1024,512]{1,0:T(8,128)(2,1)}, u32[]{:S(2)}, u32[]{:S(2)}) collective-permute-start(bf16[1024,512]{1,0:T(8,128)(2,1)} %get-tuple-element.47), channel_id=1, source_target_pairs={{1,0},{2,1},{3,2},{0,3},{5,4},{6,5},{7,6},{4,7},{9,8},{10,9},{11,1... | collective-permute-start | bytes 3145736 | tf_op jit(solution)/shard_map/ppermute | solution.py:22
  124.1 25.5 %collective-permute-start.32 = (bf16[1024,512]{1,0:T(8,128)(2,1)}, bf16[1024,512]{1,0:T(8,128)(2,1)}, u32[]{:S(2)}, u32[]{:S(2)}) collective-permute-start(bf16[1024,512]{1,0:T(8,128)(2,1)} %get-tuple-element.48), channel_id=1, source_target_pairs={{3,0},{0,1},{1,2},{2,3},{7,4},{4,5},{5,6},{6,7},{11,8},{8,9},{9,10... | collective-permute-start | bytes 3145736 | tf_op jit(solution)/shard_map/ppermute | solution.py:22
  135.7 1.7 copy-start.3
  135.7 1.6 copy-start.1
  135.7 12.5 %collective-permute-start.33 = (f32[8,512]{1,0:T(8,128)S(1)}, f32[8,512]{1,0:T(8,128)S(1)}, u32[]{:S(2)}, u32[]{:S(2)}) collective-permute-start(f32[8,512]{1,0:T(8,128)S(1)} %copy-done.21), channel_id=1, source_target_pairs={{2,0},{3,1},{0,2},{1,3},{6,4},{7,5},{4,6},{5,7},{10,8},{11,9},{8,1... | collective-permute-start | bytes 49160 | tf_op jit(solution)/shard_map/ppermute | solution.py:22
  140.2 17.1 %collective-permute-start.30 = (bf16[256,256]{1,0:T(8,128)(2,1)S(1)}, bf16[256,256]{1,0:T(8,128)(2,1)S(1)}, u32[]{:S(2)}, u32[]{:S(2)}) collective-permute-start(bf16[256,256]{1,0:T(8,128)(2,1)S(1)} %get-tuple-element.62), channel_id=1, source_target_pairs={{8,0},{36,4},{16,8},{44,12},{24,16},{52,20},{0,24},{60,28},{40,32}... | collective-permute-start | bytes 393224 | tf_op jit(solution)/shard_map/ppermute | solution.py:37
  142.4 15.0 %collective-permute-start.29 = (bf16[256,256]{1,0:T(8,128)(2,1)S(1)}, bf16[256,256]{1,0:T(8,128)(2,1)S(1)}, u32[]{:S(2)}, u32[]{:S(2)}) collective-permute-start(bf16[256,256]{1,0:T(8,128)(2,1)S(1)} %get-tuple-element.63), channel_id=1, source_target_pairs={{16,0},{68,4},{24,8},{76,12},{0,16},{84,20},{8,24},{92,28},{48,32}... | collective-permute-start | bytes 393224 | tf_op jit(solution)/shard_map/ppermute | solution.py:37
  148.2 1.4 copy-start.19
  148.2 9.2 %collective-permute-start.28 = (bf16[256,256]{1,0:T(8,128)(2,1)S(1)}, bf16[256,256]{1,0:T(8,128)(2,1)S(1)}, u32[]{:S(2)}, u32[]{:S(2)}) collective-permute-start(bf16[256,256]{1,0:T(8,128)(2,1)S(1)} %get-tuple-element.64), channel_id=1, source_target_pairs={{24,0},{100,4},{0,8},{108,12},{8,16},{116,20},{16,24},{124,28},{56... | collective-permute-start | bytes 393224 | tf_op jit(solution)/shard_map/ppermute | solution.py:37
  157.3 0.7 copy-start.13
  157.3 0.7 copy-start.14
  157.4 0.7 copy-start.15
  160.6 1.6 collective-permute-start.34
Sparse Core Ops, SparseCore 0:
  60.6 47.5 all-gather.2

commit v14 on v12

--- a/solution.py
+++ b/solution.py
@@ -15,6 +15,7 @@
 TILE = 512
 TILES = VOC // TILE
 VMEM = 56 * 2**20
+MOST = 63 * 2**20
 
 
 def shift(a, axis, d):
@@ -44,8 +45,8 @@
     return lax.dot_general(a, b, (((1,), (0,)), ((), ())), preferred_element_type=F32)
 
 
-def params(**kw):
-    return pltpu.CompilerParams(vmem_limit_bytes=VMEM, **kw)
+def params(limit=VMEM):
+    return pltpu.CompilerParams(vmem_limit_bytes=limit)
 
 
 SMALL = pl.CostEstimate(flops=1000, bytes_accessed=1000, transcendentals=0)
@@ -108,7 +109,7 @@
             pltpu.SemaphoreType.DMA((chunks,)),
             pltpu.SemaphoreType.DMA((chunks,)),
         ],
-        compiler_params=params(),
+        compiler_params=params(MOST),
         cost_estimate=SMALL,
         name="onward",
     )(ep, em, *others)
@@ -325,8 +326,8 @@
     u1, u2, u3, work = gate(*u, first())
     t = add(b[0], u1, u2, u3)
     u = [cross(t[d].astype(BF), 1, 4 - d) for d in (1, 2, 3)]
-    *u, work = gate(*u, second(work))
-    f = add(t[0], *u)
+    u1, u2, u3, work = gate(*u, second(work))
+    f = add(t[0], u1, u2, u3)
     low, high = f[:, :128], f[:, 128:]
     mine, other = jnp.where(c == 0, low, high), jnp.where(c == 0, high, low)
     got = sibling(other)
@@ -362,7 +363,7 @@
             out_specs=pl.BlockSpec((TILE, 1024), lambda i, at: (i, 0)),
         ),
         out_shape=jax.ShapeDtypeStruct((VOC, 1024), BF),
-        compiler_params=params(),
+        compiler_params=params(MOST),
         cost_estimate=SMALL,
         name="embed_a",
     )(at, tgt, ep, em, *packs, feats, feats, feats)
@@ -392,7 +393,7 @@
             out_specs=pl.BlockSpec((TILE, 1024), lambda i, at: (i, 0)),
         ),
         out_shape=jax.ShapeDtypeStruct((VOC, 1024), BF),
-        compiler_params=params(),
+        compiler_params=params(MOST),
         cost_estimate=SMALL,
         name="embed_b",
     )(at, acc, low, high, pack, feats)

time: 174 us -> 171 us (0.983)
  local copies, waits for them, and re-layouts: 8.87 us -> 4.15 us
    unnamed x54 -> x44, local copies, waits for them, and re-layouts: 8.15 us -> 3.43 us
where the time goes in v14:
time: 171 us; the launch traced here: 169 us
  Pallas kernels  56 us (33%)
  starting transfers between devices  44.2 us (26%)
  waiting for transfers between devices  38.3 us (22%)
  between operations  14.3 us (8%)
  other arithmetic  11.9 us (7%)
  local copies, waits for them, and re-layouts  4.15 us (2%)
    ppermute x13, starting transfers between devices, shift(): return lax.ppermute(a, axis, [((i + d) % 4, i) for i in range(4)])  22 us
    ppermute x12, starting transfers between devices, cross(): return lax.ppermute(a, ('x', 'z', 'c'), pairs)  19.1 us
    pallas_call x1, Pallas kernels, hidden_call(): pl.pallas_call(hidden_body, grid_spec=pltpu.PrefetchScalarGridSpec(num_sc...  16.5 us
    ppermute x12, waiting for transfers between devices, cross(): return lax.ppermute(a, ('x', 'z', 'c'), pairs)  16.4 us
    pallas_call x1, Pallas kernels, logits_call(): pl.pallas_call(logits_body, grid_spec=pltpu.PrefetchScalarGridSpec(num_sc...  16.3 us
    ppermute x13, waiting for transfers between devices, shift(): return lax.ppermute(a, axis, [((i + d) % 4, i) for i in range(4)])  14.4 us
    pallas_call x1, Pallas kernels, embed_a_call(): pl.pallas_call(embed_a_body, grid_spec=pltpu.PrefetchScalarGridSpec(num_s...  11.6 us
    pallas_call x1, Pallas kernels, embed_b_call(): pl.pallas_call(embed_b_body, grid_spec=pltpu.PrefetchScalarGridSpec(num_s...  7.72 us
  transfers between devices with their start and end apart: 36, of which 15 were waited for; matrix products, arithmetic and copies ran while one was open for 5% of the time, Pallas kernels for 33%

profile of v14, /device:TPU:0, one launch (start us, length us, event | category | flops | bytes accessed | tf_op | source)
XLA Modules:
  0.0 168.9 jit_solution(6805811097952298753)
XLA Ops:
  7.2 0.9 broadcast_select_fusion.1
  8.2 0.7 broadcast_subtract_fusion
  8.9 0.6 collective-permute-done
  9.5 3.2 %collective-permute-start.3 = (bf16[256,256]{1,0:T(8,128)(2,1)S(1)}, bf16[256,256]{1,0:T(8,128)(2,1)S(1)}, u32[]{:S(2)}, u32[]{:S(2)}) collective-permute-start(bf16[256,256]{1,0:T(8,128)(2,1)S(1)} %maximum_select_fusion.1), channel_id=1, source_target_pairs={{64,0},{20,4},{72,8},{28,12},{80,16},{4,20},{88,24},{12,28},{96,32... | collective-permute-start | bytes 393224 | tf_op jit(solution)/shard_map/ppermute | solution.py:37
  12.7 1.1 collective-permute-start.2
  13.8 0.9 collective-permute-start.1
  14.7 0.7 pad_add_fusion.refs_1_
  15.4 4.6 %collective-permute-done.1.refs_0_ = bf16[256,256]{1,0:T(8,128)(2,1)S(1)} collective-permute-done((bf16[256,256]{1,0:T(8,128)(2,1)S(1)}, bf16[256,256]{1,0:T(8,128)(2,1)S(1)}, u32[]{:S(2)}, u32[]{:S(2)}) %collective-permute-start.1) | collective-permute-done | bytes 131104 | tf_op jit(solution)/shard_map/ppermute | solution.py:37
  20.0 0.6 tile.2
  20.7 1.0 pad_maximum_fusion.refs_0_
  21.6 2.0 %collective-permute-start.6 = (bf16[4,256,256]{2,1,0:T(8,128)(2,1)S(1)}, bf16[4,256,256]{2,1,0:T(8,128)(2,1)S(1)}, u32[]{:S(2)}, u32[]{:S(2)}) collective-permute-start(bf16[4,256,256]{2,1,0:T(8,128)(2,1)S(1)} %pad_maximum_fusion.refs_0_), channel_id=1, source_target_pairs={{24,0},{100,4},{0,8},{108,12},{8,16},{116,20},{16,24},{124,28},{56... | collective-permute-start | bytes 1572872 | tf_op jit(solution)/shard_map/ppermute | solution.py:37
  23.6 3.6 %collective-permute-start.5 = (bf16[4,256,256]{2,1,0:T(8,128)(2,1)S(1)}, bf16[4,256,256]{2,1,0:T(8,128)(2,1)S(1)}, u32[]{:S(2)}, u32[]{:S(2)}) collective-permute-start(bf16[4,256,256]{2,1,0:T(8,128)(2,1)S(1)} %pad_maximum_fusion.refs_0_), channel_id=1, source_target_pairs={{16,0},{68,4},{24,8},{76,12},{0,16},{84,20},{8,24},{92,28},{48,32}... | collective-permute-start | bytes 1572872 | tf_op jit(solution)/shard_map/ppermute | solution.py:37
  27.2 1.0 collective-permute-start.4
  28.2 4.7 %collective-permute-done.6.refs_3_ = bf16[4,256,256]{2,1,0:T(8,128)(2,1)S(1)} collective-permute-done((bf16[4,256,256]{2,1,0:T(8,128)(2,1)S(1)}, bf16[4,256,256]{2,1,0:T(8,128)(2,1)S(1)}, u32[]{:S(2)}, u32[]{:S(2)}) %collective-permute-start.6) | collective-permute-done | bytes 524320 | tf_op jit(solution)/shard_map/ppermute | solution.py:37
  32.9 7.1 %collective-permute-done.5.refs_2_ = bf16[4,256,256]{2,1,0:T(8,128)(2,1)S(1)} collective-permute-done((bf16[4,256,256]{2,1,0:T(8,128)(2,1)S(1)}, bf16[4,256,256]{2,1,0:T(8,128)(2,1)S(1)}, u32[]{:S(2)}, u32[]{:S(2)}) %collective-permute-start.5) | collective-permute-done | bytes 524320 | tf_op jit(solution)/shard_map/ppermute | solution.py:37
  40.0 0.5 collective-permute-start.8
  40.5 1.6 collective-permute-start.11
  42.1 0.5 collective-permute-done.8.refs_5_
  42.7 0.2 copy-done.7
  43.2 0.2 copy-done.10
  43.4 16.3 %logits.1 = (bf16[2048,512]{1,0:T(8,128)(2,1)}, f32[8,512]{1,0:T(8,128)}, f32[8,512]{1,0:T(8,128)}) custom-call(s32[4]{0:T(128)} %get-tuple-element.29.at, bf16[4,256,256]{2,1,0:T(8,128)(2,1)} %copy-done, bf16[4,256,256]{2,1,0:T(8,128)(2,1)} %copy-done.6, bf16[4,256,256]{2,1,0:T(8,128)(2,1)} %copy-done.5, bf16[4,256,256]{2,1,0:T(8,128)(2,1)} %copy-done.4, ...), custom_call_target="tpu_custom_call" | custom-call | flops 1000 | bytes 1000 | tf_op jit(solution)/shard_map/logits/pallas_call | solution.py:175
  59.8 0.6 copy-done.14
  60.5 3.4 %collective-permute-start.14 = (f32[8,512]{1,0:T(8,128)}, f32[8,512]{1,0:T(8,128)S(1)}, u32[]{:S(2)}, u32[]{:S(2)}) collective-permute-start(f32[8,512]{1,0:T(8,128)} %get-tuple-element.34), channel_id=1, source_target_pairs={{96,0},{0,32},{32,64},{64,96},{97,1},{1,33},{33,65},{65,97},{98,2}... | collective-permute-start | bytes 49160 | tf_op jit(solution)/shard_map/ppermute | solution.py:22
  63.9 4.1 %collective-permute-start.13 = (f32[8,512]{1,0:T(8,128)}, f32[8,512]{1,0:T(8,128)S(1)}, u32[]{:S(2)}, u32[]{:S(2)}) collective-permute-start(f32[8,512]{1,0:T(8,128)} %get-tuple-element.34), channel_id=1, source_target_pairs={{64,0},{96,32},{0,64},{32,96},{65,1},{97,33},{1,65},{33,97},{66,2}... | collective-permute-start | bytes 49160 | tf_op jit(solution)/shard_map/ppermute | solution.py:22
  68.0 1.6 collective-permute-start.12
  69.7 3.2 %collective-permute-start.24 = (bf16[2048,512]{1,0:T(8,128)(2,1)}, bf16[2048,512]{1,0:T(8,128)(2,1)}, u32[]{:S(2)}, u32[]{:S(2)}) collective-permute-start(bf16[2048,512]{1,0:T(8,128)(2,1)} %get-tuple-element.32.e), channel_id=1, source_target_pairs={{1,0},{2,1},{3,2},{0,3},{5,4},{6,5},{7,6},{4,7},{9,8},{10,9},{11,1... | collective-permute-start | bytes 6291464 | tf_op jit(solution)/shard_map/ppermute | solution.py:22
  73.0 0.9 fusion.11
  73.9 1.0 collective-permute-start.17
  74.9 2.1 %collective-permute-start.16 = (f32[8,512]{1,0:T(8,128)S(1)}, f32[8,512]{1,0:T(8,128)S(1)}, u32[]{:S(2)}, u32[]{:S(2)}) collective-permute-start(f32[8,512]{1,0:T(8,128)S(1)} %maximum_maximum_fusion), channel_id=1, source_target_pairs={{16,0},{24,8},{0,16},{8,24},{17,1},{25,9},{1,17},{9,25},{18,2},{26... | collective-permute-start | bytes 49160 | tf_op jit(solution)/shard_map/ppermute | solution.py:22
  77.0 1.5 collective-permute-start.15
  78.6 0.3 collective-permute-done.17
  78.9 1.4 collective-permute-done.16
  80.3 0.5 collective-permute-done.15
  80.9 0.2 collective-permute-start.18
  81.1 1.2 collective-permute-done.18.b
  82.3 0.6 copy-done.20
  82.9 1.4 finish.1
  84.3 16.5 %hidden.1 = (bf16[4,4,256,256]{3,2,1,0:T(8,128)(2,1)}, bf16[2,4,256,256]{3,2,1,0:T(8,128)(2,1)}, bf16[2,4,256,256]{3,2,1,0:T(8,128)(2,1)}, bf16[2048,512]{1,0:T(8,128)(2,1)}) custom-call(s32[4]{0:T(128)} %get-tuple-element.29.at, bf16[2048,512]{1,0:T(8,128)(2,1)} %get-tuple-element.32.e, f32[8,512]{1,0:T(8,128)} %get-tuple-element.36.pack, ...), custom_call_target="tpu_custom_call" | custom-call | flops 1000 | bytes 1000 | tf_op jit(solution)/shard_map/hidden/pallas_call | solution.py:293
  100.8 0.3 collective-permute-start.19
  101.1 0.3 collective-permute-start.21
  101.4 2.4 %collective-permute-done.19 = bf16[2,4,256,256]{3,2,1,0:T(8,128)(2,1)S(1)} collective-permute-done((bf16[2,4,256,256]{3,2,1,0:T(8,128)(2,1)}, bf16[2,4,256,256]{3,2,1,0:T(8,128)(2,1)S(1)}, u32[]{:S(2)}, u32[]{:S(2)}) %collective-permute-start.19) | collective-permute-done | bytes 1048608 | tf_op jit(solution)/shard_map/ppermute | solution.py:26
  103.8 0.9 collective-permute-start.26
  104.7 1.6 collective-permute-done.21
  106.2 2.8 %fusion.4 = (bf16[4,256,256]{2,1,0:T(8,128)(2,1)}, bf16[4,256,256]{2,1,0:T(8,128)(2,1)}, bf16[4,256,256]{2,1,0:T(8,128)(2,1)}) fusion(bf16[2,4,256,256]{3,2,1,0:T(8,128)(2,1)S(1)} %collective-permute-done.21, bf16[4,4,256,256]{3,2,1,0:T(8,128)(2,1)} %get-tuple-element.37, bf16[2,4,256,256]{3,2,1,0:T(8,128)(2,1)S(1)} %collective-permute-done.19), kind=kLoop, calls=%fused_computation.8 | loop fusion | flops 3145728 | bytes 4718592 | tf_op jit(solution)/shard_map/convert_element_type | solution.py:325
  109.1 1.7 collective-permute-start.23
  110.7 7.3 %collective-permute-done.27.refs_1_ = f32[8,512]{1,0:T(8,128)S(1)} collective-permute-done((f32[8,512]{1,0:T(8,128)S(1)}, f32[8,512]{1,0:T(8,128)S(1)}, u32[]{:S(2)}, u32[]{:S(2)}) %collective-permute-start.27) | collective-permute-done | bytes 16416 | tf_op jit(solution)/shard_map/ppermute | solution.py:22
  118.0 0.2 collective-permute-start.22
  118.2 1.0 collective-permute-start.20
  119.2 2.4 %onward.1 = (f32[8,512]{1,0:T(8,128)}, f32[8,512]{1,0:T(8,128)}, bf16[1024,512]{1,0:T(8,128)(2,1)}, bf16[1024,512]{1,0:T(8,128)(2,1)}) custom-call(bf16[2048,512]{1,0:T(8,128)(2,1)} %collective-permute-done.24.ep, bf16[2048,512]{1,0:T(8,128)(2,1)} %collective-permute-done.25.em, f32[8,512]{1,0:T(8,128)} %copy-done.17, ...), custom_call_target="tpu_custom_call", output_to_operand_aliasing={{0}: (2, {}), {1}: (3, {})} | custom-call | flops 1000 | bytes 1000 | tf_op jit(solution)/shard_map/onward/pallas_call | solution.py:101
  121.6 2.5 %collective-permute-start.31 = (bf16[1024,512]{1,0:T(8,128)(2,1)}, bf16[1024,512]{1,0:T(8,128)(2,1)}, u32[]{:S(2)}, u32[]{:S(2)}) collective-permute-start(bf16[1024,512]{1,0:T(8,128)(2,1)} %get-tuple-element.48), channel_id=1, source_target_pairs={{1,0},{2,1},{3,2},{0,3},{5,4},{6,5},{7,6},{4,7},{9,8},{10,9},{11,1... | collective-permute-start | bytes 3145736 | tf_op jit(solution)/shard_map/ppermute | solution.py:22
  124.0 11.6 %embed_a.1.refs_3_ = bf16[2048,1024]{1,0:T(8,128)(2,1)} custom-call(s32[4]{0:T(128)} %get-tuple-element.29.at, bf16[2048,512]{1,0:T(8,128)(2,1)} %get-tuple-element.40.tgt, bf16[2048,512]{1,0:T(8,128)(2,1)} %collective-permute-done.24.ep, bf16[2048,512]{1,0:T(8,128)(2,1)} %collective-permute-done.25.em, f32[8,512]{1,0:T(8,128)} %get-tuple-element.41.pack_p, ...), custom_call_target="tpu_custom_call" | custom-call | flops 1000 | bytes 1000 | tf_op jit(solution)/shard_map/embed_a/pallas_call | solution.py:357
  135.7 1.6 collective-permute-start.33
  137.3 2.8 %fusion.14 = (bf16[4,256,256]{2,1,0:T(8,128)(2,1)S(1)}, f32[4,256,256]{2,1,0:T(8,128)}) fusion(bf16[4,256,256]{2,1,0:T(8,128)(2,1)} %get-tuple-element.46, bf16[4,256,256]{2,1,0:T(8,128)(2,1)} %get-tuple-element.45, bf16[4,256,256]{2,1,0:T(8,128)(2,1)} %get-tuple-element.44, bf16[2,4,256,256]{3,2,1,0:T(8,128)(2,1)S(1)} %copy-done.3, ...), kind=kLoop, calls=%fused_computation.48 | loop fusion | flops 2621440 | bytes 4194304 | tf_op jit(solution)/shard_map/convert.2
  140.2 2.1 %collective-permute-start.30 = (bf16[256,256]{1,0:T(8,128)(2,1)S(1)}, bf16[256,256]{1,0:T(8,128)(2,1)S(1)}, u32[]{:S(2)}, u32[]{:S(2)}) collective-permute-start(bf16[256,256]{1,0:T(8,128)(2,1)S(1)} %get-tuple-element.64), channel_id=1, source_target_pairs={{8,0},{36,4},{16,8},{44,12},{24,16},{52,20},{0,24},{60,28},{40,32}... | collective-permute-start | bytes 393224 | tf_op jit(solution)/shard_map/ppermute | solution.py:37
  142.4 1.4 collective-permute-start.29
  143.8 4.4 %collective-permute-done.33.pack = f32[8,512]{1,0:T(8,128)S(1)} collective-permute-done((f32[8,512]{1,0:T(8,128)S(1)}, f32[8,512]{1,0:T(8,128)S(1)}, u32[]{:S(2)}, u32[]{:S(2)}) %collective-permute-start.33) | collective-permute-done | bytes 16416 | tf_op jit(solution)/shard_map/ppermute | solution.py:22
  148.2 1.0 collective-permute-start.28
  149.1 0.4 collective-permute-done.32.high
  149.6 7.7 %embed_b.1.refs_3_ = bf16[2048,1024]{1,0:T(8,128)(2,1)} custom-call(s32[4]{0:T(128)} %get-tuple-element.29.at, bf16[2048,1024]{1,0:T(8,128)(2,1)} %get-tuple-element.47.acc, bf16[1024,512]{1,0:T(8,128)(2,1)} %collective-permute-done.31.low, bf16[1024,512]{1,0:T(8,128)(2,1)} %collective-permute-done.32.high, f32[8,512]{1,0:T(8,128)} %copy-done.19, ...), custom_call_target="tpu_custom_call" | custom-call | flops 1000 | bytes 1000 | tf_op jit(solution)/shard_map/embed_b/pallas_call | solution.py:381
  157.3 0.6 copy-done.11
  158.0 0.7 copy-done.13
  158.7 1.2 fusion.7
  159.9 1.3 collective-permute-done.34
  161.3 0.7 maximum_select_fusion
  (82 shorter events, 1.2 us)
Async XLA Ops:
  7.2 116.9 %all-gather.3.cloned.1.call-start = ((), (), s32[]{:S(2)}) async-start(), calls=%async_computation | async-start | bytes 4325376 | tf_op jit(solution)/shard_map/all_gather | solution.py:420
  8.1 1.3 collective-permute-start
  9.5 11.2 %collective-permute-start.3 = (bf16[256,256]{1,0:T(8,128)(2,1)S(1)}, bf16[256,256]{1,0:T(8,128)(2,1)S(1)}, u32[]{:S(2)}, u32[]{:S(2)}) collective-permute-start(bf16[256,256]{1,0:T(8,128)(2,1)S(1)} %maximum_select_fusion.1), channel_id=1, source_target_pairs={{64,0},{20,4},{72,8},{28,12},{80,16},{4,20},{88,24},{12,28},{96,32... | collective-permute-start | bytes 393224 | tf_op jit(solution)/shard_map/ppermute | solution.py:37
  12.7 8.0 %collective-permute-start.2 = (bf16[256,256]{1,0:T(8,128)(2,1)S(1)}, bf16[256,256]{1,0:T(8,128)(2,1)S(1)}, u32[]{:S(2)}, u32[]{:S(2)}) collective-permute-start(bf16[256,256]{1,0:T(8,128)(2,1)S(1)} %maximum_select_fusion.1), channel_id=1, source_target_pairs={{32,0},{12,4},{40,8},{20,12},{48,16},{28,20},{56,24},{4,28},{64,32... | collective-permute-start | bytes 393224 | tf_op jit(solution)/shard_map/ppermute | solution.py:37
  13.8 6.2 %collective-permute-start.1 = (bf16[256,256]{1,0:T(8,128)(2,1)S(1)}, bf16[256,256]{1,0:T(8,128)(2,1)S(1)}, u32[]{:S(2)}, u32[]{:S(2)}) collective-permute-start(bf16[256,256]{1,0:T(8,128)(2,1)S(1)} %maximum_select_fusion.1), channel_id=1, source_target_pairs={{96,0},{28,4},{104,8},{4,12},{112,16},{12,20},{120,24},{20,28},{0,... | collective-permute-start | bytes 393224 | tf_op jit(solution)/shard_map/ppermute | solution.py:37
  20.0 0.7 copy-start.15
  21.6 21.0 %copy-start = (bf16[4,256,256]{2,1,0:T(8,128)(2,1)}, bf16[4,256,256]{2,1,0:T(8,128)(2,1)S(1)}, u32[]{:S(2)}) copy-start(bf16[4,256,256]{2,1,0:T(8,128)(2,1)S(1)} %pad_maximum_fusion.refs_0_) | copy-start | bytes 1572868
  21.6 11.3 %collective-permute-start.6 = (bf16[4,256,256]{2,1,0:T(8,128)(2,1)S(1)}, bf16[4,256,256]{2,1,0:T(8,128)(2,1)S(1)}, u32[]{:S(2)}, u32[]{:S(2)}) collective-permute-start(bf16[4,256,256]{2,1,0:T(8,128)(2,1)S(1)} %pad_maximum_fusion.refs_0_), channel_id=1, source_target_pairs={{24,0},{100,4},{0,8},{108,12},{8,16},{116,20},{16,24},{124,28},{56... | collective-permute-start | bytes 1572872 | tf_op jit(solution)/shard_map/ppermute | solution.py:37
  23.6 16.4 %collective-permute-start.5 = (bf16[4,256,256]{2,1,0:T(8,128)(2,1)S(1)}, bf16[4,256,256]{2,1,0:T(8,128)(2,1)S(1)}, u32[]{:S(2)}, u32[]{:S(2)}) collective-permute-start(bf16[4,256,256]{2,1,0:T(8,128)(2,1)S(1)} %pad_maximum_fusion.refs_0_), channel_id=1, source_target_pairs={{16,0},{68,4},{24,8},{76,12},{0,16},{84,20},{8,24},{92,28},{48,32}... | collective-permute-start | bytes 1572872 | tf_op jit(solution)/shard_map/ppermute | solution.py:37
  27.2 12.8 %collective-permute-start.4 = (bf16[4,256,256]{2,1,0:T(8,128)(2,1)S(1)}, bf16[4,256,256]{2,1,0:T(8,128)(2,1)S(1)}, u32[]{:S(2)}, u32[]{:S(2)}) collective-permute-start(bf16[4,256,256]{2,1,0:T(8,128)(2,1)S(1)} %pad_maximum_fusion.refs_0_), channel_id=1, source_target_pairs={{8,0},{36,4},{16,8},{44,12},{24,16},{52,20},{0,24},{60,28},{40,32}... | collective-permute-start | bytes 1572872 | tf_op jit(solution)/shard_map/ppermute | solution.py:37
  28.2 13.8 %collective-permute-start.7 = (bf16[4,256,256]{2,1,0:T(8,128)(2,1)S(1)}, bf16[4,256,256]{2,1,0:T(8,128)(2,1)S(1)}, u32[]{:S(2)}, u32[]{:S(2)}) collective-permute-start(bf16[4,256,256]{2,1,0:T(8,128)(2,1)S(1)} %pad_maximum_fusion.refs_0_), channel_id=1, source_target_pairs={{0,4},{4,0},{1,5},{5,1},{2,6},{6,2},{3,7},{7,3},{8,12},{12,8},{9,1... | collective-permute-start | bytes 1572872 | tf_op jit(solution)/shard_map/ppermute | solution.py:26
  32.9 9.7 %copy-start.4 = (bf16[4,256,256]{2,1,0:T(8,128)(2,1)}, bf16[4,256,256]{2,1,0:T(8,128)(2,1)S(1)}, u32[]{:S(2)}) copy-start(bf16[4,256,256]{2,1,0:T(8,128)(2,1)S(1)} %collective-permute-done.6.refs_3_) | copy-start | bytes 1572868
  32.9 9.2 %collective-permute-start.10 = (bf16[4,256,256]{2,1,0:T(8,128)(2,1)S(1)}, bf16[4,256,256]{2,1,0:T(8,128)(2,1)S(1)}, u32[]{:S(2)}, u32[]{:S(2)}) collective-permute-start(bf16[4,256,256]{2,1,0:T(8,128)(2,1)S(1)} %collective-permute-done.6.refs_3_), channel_id=1, source_target_pairs={{0,4},{4,0},{1,5},{5,1},{2,6},{6,2},{3,7},{7,3},{8,12},{12,8},{9,1... | collective-permute-start | bytes 1572872 | tf_op jit(solution)/shard_map/ppermute | solution.py:26
  40.0 2.7 %copy-start.5 = (bf16[4,256,256]{2,1,0:T(8,128)(2,1)}, bf16[4,256,256]{2,1,0:T(8,128)(2,1)S(1)}, u32[]{:S(2)}) copy-start(bf16[4,256,256]{2,1,0:T(8,128)(2,1)S(1)} %collective-permute-done.5.refs_2_) | copy-start | bytes 1572868
  40.0 2.1 %collective-permute-start.9 = (bf16[4,256,256]{2,1,0:T(8,128)(2,1)S(1)}, bf16[4,256,256]{2,1,0:T(8,128)(2,1)S(1)}, u32[]{:S(2)}, u32[]{:S(2)}) collective-permute-start(bf16[4,256,256]{2,1,0:T(8,128)(2,1)S(1)} %collective-permute-done.5.refs_2_), channel_id=1, source_target_pairs={{0,4},{4,0},{1,5},{5,1},{2,6},{6,2},{3,7},{7,3},{8,12},{12,8},{9,1... | collective-permute-start | bytes 1572872 | tf_op jit(solution)/shard_map/ppermute | solution.py:26
  40.0 2.7 %copy-start.6 = (bf16[4,256,256]{2,1,0:T(8,128)(2,1)}, bf16[4,256,256]{2,1,0:T(8,128)(2,1)S(1)}, u32[]{:S(2)}) copy-start(bf16[4,256,256]{2,1,0:T(8,128)(2,1)S(1)} %collective-permute-done.4.refs_1_) | copy-start | bytes 1572868
  40.0 2.6 %collective-permute-start.8 = (bf16[4,256,256]{2,1,0:T(8,128)(2,1)S(1)}, bf16[4,256,256]{2,1,0:T(8,128)(2,1)S(1)}, u32[]{:S(2)}, u32[]{:S(2)}) collective-permute-start(bf16[4,256,256]{2,1,0:T(8,128)(2,1)S(1)} %collective-permute-done.4.refs_1_), channel_id=1, source_target_pairs={{0,4},{4,0},{1,5},{5,1},{2,6},{6,2},{3,7},{7,3},{8,12},{12,8},{9,1... | collective-permute-start | bytes 1572872 | tf_op jit(solution)/shard_map/ppermute | solution.py:26
  40.5 19.3 %collective-permute-start.11 = (bf16[512,128]{1,0:T(8,128)(2,1)}, bf16[512,128]{1,0:T(8,128)(2,1)S(1)}, u32[]{:S(2)}, u32[]{:S(2)}) collective-permute-start(bf16[512,128]{1,0:T(8,128)(2,1)} %bitcast.52), channel_id=1, source_target_pairs={{0,0},{1,32},{2,64},{3,96},{32,1},{33,33},{34,65},{35,97},{64,2},{... | collective-permute-start | bytes 393224 | tf_op jit(solution)/shard_map/ppermute | solution.py:409
  42.1 0.8 copy-start.7
  42.1 1.0 copy-start.8
  42.1 1.1 copy-start.9
  42.6 0.8 copy-start.10
  59.8 0.7 copy-start.14
  60.5 12.5 %collective-permute-start.14 = (f32[8,512]{1,0:T(8,128)}, f32[8,512]{1,0:T(8,128)S(1)}, u32[]{:S(2)}, u32[]{:S(2)}) collective-permute-start(f32[8,512]{1,0:T(8,128)} %get-tuple-element.34), channel_id=1, source_target_pairs={{96,0},{0,32},{32,64},{64,96},{97,1},{1,33},{33,65},{65,97},{98,2}... | collective-permute-start | bytes 49160 | tf_op jit(solution)/shard_map/ppermute | solution.py:22
  63.9 9.1 %collective-permute-start.13 = (f32[8,512]{1,0:T(8,128)}, f32[8,512]{1,0:T(8,128)S(1)}, u32[]{:S(2)}, u32[]{:S(2)}) collective-permute-start(f32[8,512]{1,0:T(8,128)} %get-tuple-element.34), channel_id=1, source_target_pairs={{64,0},{96,32},{0,64},{32,96},{65,1},{97,33},{1,65},{33,97},{66,2}... | collective-permute-start | bytes 49160 | tf_op jit(solution)/shard_map/ppermute | solution.py:22
  68.0 5.0 %collective-permute-start.12 = (f32[8,512]{1,0:T(8,128)}, f32[8,512]{1,0:T(8,128)S(1)}, u32[]{:S(2)}, u32[]{:S(2)}) collective-permute-start(f32[8,512]{1,0:T(8,128)} %get-tuple-element.34), channel_id=1, source_target_pairs={{32,0},{64,32},{96,64},{0,96},{33,1},{65,33},{97,65},{1,97},{34,2}... | collective-permute-start | bytes 49160 | tf_op jit(solution)/shard_map/ppermute | solution.py:22
  69.7 49.4 %collective-permute-start.25 = (bf16[2048,512]{1,0:T(8,128)(2,1)}, bf16[2048,512]{1,0:T(8,128)(2,1)}, u32[]{:S(2)}, u32[]{:S(2)}) collective-permute-start(bf16[2048,512]{1,0:T(8,128)(2,1)} %get-tuple-element.32.e), channel_id=1, source_target_pairs={{3,0},{0,1},{1,2},{2,3},{7,4},{4,5},{5,6},{6,7},{11,8},{8,9},{9,10... | collective-permute-start | bytes 6291464 | tf_op jit(solution)/shard_map/ppermute | solution.py:22
  69.7 49.4 %collective-permute-start.24 = (bf16[2048,512]{1,0:T(8,128)(2,1)}, bf16[2048,512]{1,0:T(8,128)(2,1)}, u32[]{:S(2)}, u32[]{:S(2)}) collective-permute-start(bf16[2048,512]{1,0:T(8,128)(2,1)} %get-tuple-element.32.e), channel_id=1, source_target_pairs={{1,0},{2,1},{3,2},{0,3},{5,4},{6,5},{7,6},{4,7},{9,8},{10,9},{11,1... | collective-permute-start | bytes 6291464 | tf_op jit(solution)/shard_map/ppermute | solution.py:22
  73.9 5.0 %collective-permute-start.17 = (f32[8,512]{1,0:T(8,128)S(1)}, f32[8,512]{1,0:T(8,128)S(1)}, u32[]{:S(2)}, u32[]{:S(2)}) collective-permute-start(f32[8,512]{1,0:T(8,128)S(1)} %maximum_maximum_fusion), channel_id=1, source_target_pairs={{24,0},{0,8},{8,16},{16,24},{25,1},{1,9},{9,17},{17,25},{26,2},{2,... | collective-permute-start | bytes 49160 | tf_op jit(solution)/shard_map/ppermute | solution.py:22
  74.9 5.4 %collective-permute-start.16 = (f32[8,512]{1,0:T(8,128)S(1)}, f32[8,512]{1,0:T(8,128)S(1)}, u32[]{:S(2)}, u32[]{:S(2)}) collective-permute-start(f32[8,512]{1,0:T(8,128)S(1)} %maximum_maximum_fusion), channel_id=1, source_target_pairs={{16,0},{24,8},{0,16},{8,24},{17,1},{25,9},{1,17},{9,25},{18,2},{26... | collective-permute-start | bytes 49160 | tf_op jit(solution)/shard_map/ppermute | solution.py:22
  77.0 3.7 %collective-permute-start.15 = (f32[8,512]{1,0:T(8,128)S(1)}, f32[8,512]{1,0:T(8,128)S(1)}, u32[]{:S(2)}, u32[]{:S(2)}) collective-permute-start(f32[8,512]{1,0:T(8,128)S(1)} %maximum_maximum_fusion), channel_id=1, source_target_pairs={{8,0},{16,8},{24,16},{0,24},{9,1},{17,9},{25,17},{1,25},{10,2},{18... | collective-permute-start | bytes 49160 | tf_op jit(solution)/shard_map/ppermute | solution.py:22
  80.9 1.4 copy-start.18
  80.9 1.4 collective-permute-start.18
  82.3 0.6 copy-start.20
  84.3 17.1 %copy-start.21 = (f32[8,512]{1,0:T(8,128)S(1)}, f32[8,512]{1,0:T(8,128)}, u32[]{:S(2)}) copy-start(f32[8,512]{1,0:T(8,128)} %get-tuple-element.36.pack) | copy-start | bytes 49156
  100.8 3.0 %collective-permute-start.19 = (bf16[2,4,256,256]{3,2,1,0:T(8,128)(2,1)}, bf16[2,4,256,256]{3,2,1,0:T(8,128)(2,1)S(1)}, u32[]{:S(2)}, u32[]{:S(2)}) collective-permute-start(bf16[2,4,256,256]{3,2,1,0:T(8,128)(2,1)} %get-tuple-element.38), channel_id=1, source_target_pairs={{0,4},{4,0},{1,5},{5,1},{2,6},{6,2},{3,7},{7,3},{8,12},{12,8},{9,1... | collective-permute-start | bytes 3145736 | tf_op jit(solution)/shard_map/ppermute | solution.py:26
  101.1 5.1 %collective-permute-start.21 = (bf16[2,4,256,256]{3,2,1,0:T(8,128)(2,1)}, bf16[2,4,256,256]{3,2,1,0:T(8,128)(2,1)S(1)}, u32[]{:S(2)}, u32[]{:S(2)}) collective-permute-start(bf16[2,4,256,256]{3,2,1,0:T(8,128)(2,1)} %get-tuple-element.39), channel_id=1, source_target_pairs={{0,4},{4,0},{1,5},{5,1},{2,6},{6,2},{3,7},{7,3},{8,12},{12,8},{9,1... | collective-permute-start | bytes 3145736 | tf_op jit(solution)/shard_map/ppermute | solution.py:26
  101.4 16.6 %collective-permute-start.27 = (f32[8,512]{1,0:T(8,128)S(1)}, f32[8,512]{1,0:T(8,128)S(1)}, u32[]{:S(2)}, u32[]{:S(2)}) collective-permute-start(f32[8,512]{1,0:T(8,128)S(1)} %copy-done.21), channel_id=1, source_target_pairs={{3,0},{0,1},{1,2},{2,3},{7,4},{4,5},{5,6},{6,7},{11,8},{8,9},{9,10... | collective-permute-start | bytes 49160 | tf_op jit(solution)/shard_map/ppermute | solution.py:22
  103.8 5.3 %copy-start.2 = (bf16[2,4,256,256]{3,2,1,0:T(8,128)(2,1)}, bf16[2,4,256,256]{3,2,1,0:T(8,128)(2,1)S(1)}, u32[]{:S(2)}) copy-start(bf16[2,4,256,256]{3,2,1,0:T(8,128)(2,1)S(1)} %collective-permute-done.19) | copy-start | bytes 3145732
  103.8 14.4 %collective-permute-start.26 = (f32[8,512]{1,0:T(8,128)S(1)}, f32[8,512]{1,0:T(8,128)S(1)}, u32[]{:S(2)}, u32[]{:S(2)}) collective-permute-start(f32[8,512]{1,0:T(8,128)S(1)} %copy-done.21), channel_id=1, source_target_pairs={{1,0},{2,1},{3,2},{0,3},{5,4},{6,5},{7,6},{4,7},{9,8},{10,9},{11,1... | collective-permute-start | bytes 49160 | tf_op jit(solution)/shard_map/ppermute | solution.py:22
  109.1 26.6 %collective-permute-start.23 = (bf16[4,256,256]{2,1,0:T(8,128)(2,1)}, bf16[4,256,256]{2,1,0:T(8,128)(2,1)S(1)}, u32[]{:S(2)}, u32[]{:S(2)}) collective-permute-start(bf16[4,256,256]{2,1,0:T(8,128)(2,1)} %get-tuple-element.61), channel_id=1, source_target_pairs={{32,0},{12,4},{40,8},{20,12},{48,16},{28,20},{56,24},{4,28},{64,32... | collective-permute-start | bytes 1572872 | tf_op jit(solution)/shard_map/ppermute | solution.py:37
  118.0 1.2 copy-start.16
  118.0 19.3 %collective-permute-start.22 = (bf16[4,256,256]{2,1,0:T(8,128)(2,1)}, bf16[4,256,256]{2,1,0:T(8,128)(2,1)}, u32[]{:S(2)}, u32[]{:S(2)}) collective-permute-start(bf16[4,256,256]{2,1,0:T(8,128)(2,1)} %get-tuple-element.62), channel_id=1, source_target_pairs={{64,0},{20,4},{72,8},{28,12},{80,16},{4,20},{88,24},{12,28},{96,32... | collective-permute-start | bytes 1572872 | tf_op jit(solution)/shard_map/ppermute | solution.py:37
  118.2 1.0 copy-start.17
  118.2 19.1 %collective-permute-start.20 = (bf16[4,256,256]{2,1,0:T(8,128)(2,1)}, bf16[4,256,256]{2,1,0:T(8,128)(2,1)}, u32[]{:S(2)}, u32[]{:S(2)}) collective-permute-start(bf16[4,256,256]{2,1,0:T(8,128)(2,1)} %get-tuple-element.63), channel_id=1, source_target_pairs={{96,0},{28,4},{104,8},{4,12},{112,16},{12,20},{120,24},{20,28},{0,... | collective-permute-start | bytes 1572872 | tf_op jit(solution)/shard_map/ppermute | solution.py:37
  121.6 27.5 %collective-permute-start.31 = (bf16[1024,512]{1,0:T(8,128)(2,1)}, bf16[1024,512]{1,0:T(8,128)(2,1)}, u32[]{:S(2)}, u32[]{:S(2)}) collective-permute-start(bf16[1024,512]{1,0:T(8,128)(2,1)} %get-tuple-element.48), channel_id=1, source_target_pairs={{1,0},{2,1},{3,2},{0,3},{5,4},{6,5},{7,6},{4,7},{9,8},{10,9},{11,1... | collective-permute-start | bytes 3145736 | tf_op jit(solution)/shard_map/ppermute | solution.py:22
  124.0 25.5 %collective-permute-start.32 = (bf16[1024,512]{1,0:T(8,128)(2,1)}, bf16[1024,512]{1,0:T(8,128)(2,1)}, u32[]{:S(2)}, u32[]{:S(2)}) collective-permute-start(bf16[1024,512]{1,0:T(8,128)(2,1)} %get-tuple-element.49), channel_id=1, source_target_pairs={{3,0},{0,1},{1,2},{2,3},{7,4},{4,5},{5,6},{6,7},{11,8},{8,9},{9,10... | collective-permute-start | bytes 3145736 | tf_op jit(solution)/shard_map/ppermute | solution.py:22
  135.7 1.7 copy-start.3
  135.7 1.6 copy-start.1
  135.7 12.5 %collective-permute-start.33 = (f32[8,512]{1,0:T(8,128)S(1)}, f32[8,512]{1,0:T(8,128)S(1)}, u32[]{:S(2)}, u32[]{:S(2)}) collective-permute-start(f32[8,512]{1,0:T(8,128)S(1)} %copy-done.21), channel_id=1, source_target_pairs={{2,0},{3,1},{0,2},{1,3},{6,4},{7,5},{4,6},{5,7},{10,8},{11,9},{8,1... | collective-permute-start | bytes 49160 | tf_op jit(solution)/shard_map/ppermute | solution.py:22
  140.2 17.1 %collective-permute-start.30 = (bf16[256,256]{1,0:T(8,128)(2,1)S(1)}, bf16[256,256]{1,0:T(8,128)(2,1)S(1)}, u32[]{:S(2)}, u32[]{:S(2)}) collective-permute-start(bf16[256,256]{1,0:T(8,128)(2,1)S(1)} %get-tuple-element.64), channel_id=1, source_target_pairs={{8,0},{36,4},{16,8},{44,12},{24,16},{52,20},{0,24},{60,28},{40,32}... | collective-permute-start | bytes 393224 | tf_op jit(solution)/shard_map/ppermute | solution.py:37
  142.4 14.9 %collective-permute-start.29 = (bf16[256,256]{1,0:T(8,128)(2,1)S(1)}, bf16[256,256]{1,0:T(8,128)(2,1)S(1)}, u32[]{:S(2)}, u32[]{:S(2)}) collective-permute-start(bf16[256,256]{1,0:T(8,128)(2,1)S(1)} %get-tuple-element.65), channel_id=1, source_target_pairs={{16,0},{68,4},{24,8},{76,12},{0,16},{84,20},{8,24},{92,28},{48,32}... | collective-permute-start | bytes 393224 | tf_op jit(solution)/shard_map/ppermute | solution.py:37
  148.2 1.4 copy-start.19
  148.2 9.2 %collective-permute-start.28 = (bf16[256,256]{1,0:T(8,128)(2,1)S(1)}, bf16[256,256]{1,0:T(8,128)(2,1)S(1)}, u32[]{:S(2)}, u32[]{:S(2)}) collective-permute-start(bf16[256,256]{1,0:T(8,128)(2,1)S(1)} %get-tuple-element.66), channel_id=1, source_target_pairs={{24,0},{100,4},{0,8},{108,12},{8,16},{116,20},{16,24},{124,28},{56... | collective-permute-start | bytes 393224 | tf_op jit(solution)/shard_map/ppermute | solution.py:37
  157.3 0.7 copy-start.11
  157.3 0.7 copy-start.12
  158.0 0.7 copy-start.13
  159.9 1.4 collective-permute-start.34
Sparse Core Ops, SparseCore 0:
  60.6 47.5 all-gather.2
